TPU v7x, 32 devices: a whole 2x2x4 slice. The times are simulated.
32 devices in a mesh: slab: 4 (over y, x), seq: 8 (over z, core).
Axes of the slice: x: 2, y: 2, z: 4, core: 2. Of those that a mesh axis runs over, the one named last changes fastest.
Arguments:
- video_tokens: bfloat16 [128, 128, 1152], P(('slab', 'seq')), may hold values from -40 to 40
- modulation: float32 [128, 3, 1152], P(('slab', 'seq')), may hold values from -3 to 3
- qkv_weight: bfloat16 [1152, 3456], P(None, 'seq'), may hold values from -1.5 to 1.5
- out_weight: bfloat16 [1152, 1152], P(None, 'seq'), may hold values from -0.1875 to 0.1875
Outputs:
- restored: bfloat16 [128, 128, 1152], P(('slab', 'seq'))
All inputs are finite; a program needn't handle non-finite values.
Results may differ from a plain program's by a relative error of at most 0.004.
Values may be sent and summed in bfloat16 or wider, within the bound.
No kernel may reach another device: no remote copies, remote signals or barrier semaphores. Data moves between devices by JAX's collectives and lax.ppermute only.
A program may use at most 128 MiB of HBM per device.

v0:
```python
import jax
import jax.numpy as jnp
from jax import lax
from jax.sharding import PartitionSpec as P

H = 16
FRS = 32


epsilon = 1e-06


def shifted_2(value, axis, steps):
    count = lax.axis_size(axis)
    pairs = [(source, (source + steps) % count) for source in range(count)]
    return lax.ppermute(value, axis, pairs)


def modulate(tokens, modulation):
    values = tokens.astype(jnp.float32)
    average = jnp.mean(values, axis=-1, keepdims=True)
    centered = values - average
    variance = jnp.mean(centered * centered, axis=-1, keepdims=True)
    normed = centered * lax.rsqrt(variance + epsilon)
    return (normed * (1.0 + modulation[:, 1][:, None, :]) + modulation[:, 0][:, None, :]).astype(
        jnp.bfloat16
    )


def attend(queries, key_rows, value_rows):
    scores = jnp.einsum("wtphd,wsphd->wphts", queries, key_rows, preferred_element_type=jnp.float32)
    scores = scores * queries.shape[-1] ** (-0.5)
    scores = scores - jnp.max(scores, axis=-1, keepdims=True)
    exponent = jnp.exp(scores)
    softmaxed = (exponent / jnp.sum(exponent, axis=-1, keepdims=True)).astype(jnp.bfloat16)
    result = jnp.einsum(
        "wphts,wsphd->wtphd", softmaxed, value_rows, preferred_element_type=jnp.float32
    )
    return result.astype(jnp.bfloat16)


def per_device(video_tokens, modulation, qkv_weight, out_weight):
    width = video_tokens.shape[2]
    head_size = width // H
    heads_half = H // 2
    normed = modulate(video_tokens, modulation)
    position_major = lax.all_to_all(normed, "seq", split_axis=1, concat_axis=0, tiled=True)
    window_len = position_major.shape[0]
    pos_dev = position_major.shape[1]
    half_frames = FRS // 2
    token_rows = position_major.reshape(window_len * pos_dev, width)
    projected = jnp.dot(
        token_rows,
        lax.all_gather(qkv_weight, "seq", axis=1, tiled=True),
        preferred_element_type=jnp.float32,
    ).astype(jnp.bfloat16)
    grouped = projected.reshape(window_len, pos_dev, 6, heads_half, head_size)
    windowed = attend(grouped[None, :, :, 0], grouped[None, :, :, 1], grouped[None, :, :, 2])[0]
    shifted_group = grouped[:, :, 3:]
    query_part = shifted_group[:, :, 0]
    keyval = shifted_group[:, :, 1:]
    earlier = shifted_2(keyval[half_frames:], "slab", 1)
    later_kv = shifted_2(keyval[:half_frames], "slab", -1)
    first_keys = jnp.concatenate([earlier, keyval[:half_frames]], axis=0)
    second_keys = jnp.concatenate([keyval[half_frames:], later_kv], axis=0)
    queries = jnp.stack([query_part[:half_frames], query_part[half_frames:]])
    stacked = jnp.stack([first_keys, second_keys])
    result = attend(queries, stacked[:, :, :, 0], stacked[:, :, :, 1])
    shifted = result.reshape(window_len, pos_dev, heads_half, head_size)
    attended = jnp.concatenate([windowed, shifted], axis=2).reshape(window_len * pos_dev, width)
    output_rows = jnp.dot(
        attended,
        lax.all_gather(out_weight, "seq", axis=1, tiled=True),
        preferred_element_type=jnp.float32,
    ).astype(jnp.bfloat16)
    frame_major = lax.all_to_all(
        output_rows.reshape(window_len, pos_dev, width),
        "seq",
        split_axis=0,
        concat_axis=1,
        tiled=True,
    )
    restored = video_tokens.astype(jnp.float32) + modulation[:, 2][:, None, :] * frame_major.astype(
        jnp.float32
    )
    return restored.astype(jnp.bfloat16)


def solution(mesh):
    return jax.shard_map(
        per_device,
        mesh=mesh,
        in_specs=(
            P(("slab", "seq"), None, None),
            P(("slab", "seq"), None, None),
            P(None, "seq"),
            P(None, "seq"),
        ),
        out_specs=P(("slab", "seq"), None, None),
        check_vma=False,
    )
```

profile of v0, /device:TPU:9, one launch (start us, length us, event | category | flops | bytes accessed | tf_op | source)
XLA Modules:
  0.0 249.3 jit_solution(4320385396942218214)
XLA Ops:
  6.5 0.0 copy-start.1
  6.5 0.0 copy-start.6
  6.5 0.0 all-gather.3.cloned.1.call-start
  6.5 0.7 all-gather.3.cloned.1.call-update
  7.3 2.2 convert_reduce_fusion
  9.4 0.0 copy-done.1
  9.5 1.1 fusion.4
  10.6 0.0 copy-done.6
  10.6 2.8 %fusion.7 = bf16[4,128,1152]{2,0,1:T(4,128)(2,1)} fusion(f32[4,1152]{1,0:T(4,128)S(1)} %get-tuple-element.13, f32[4,1152]{1,0:T(4,128)S(1)} %get-tuple-element.14, f32[4,128]{0,1:T(8,128)S(1)} %add_rsqrt_fusion, f32[4,128]{0,1:T(8,128)S(1)} %broadcast_multiply_fusion, bf16[4,128,1152]{2,1,0:T(8,128)(2,1)S(1)} %copy-done.1), kind=kLoop, calls=%fused_computation.14 | loop fusion | flops 3538944 | bytes 2400256 | tf_op jit(solution)/shard_map/convert_element_type | solution.py:25
  13.5 5.6 %all-to-all-start = ((bf16[4,128,1152]{2,0,1:T(4,128)(2,1)}), bf16[4,128,1152]{2,0,1:T(4,128)(2,1)S(1)}, u32[]{:S(2)}, u32[]{:S(2)}) async-start(bf16[4,128,1152]{2,0,1:T(4,128)(2,1)} %fusion.7), calls=%async_computation | async-start | bytes 2359296 | tf_op jit(solution)/shard_map/all_to_all | solution.py:47
  19.1 0.0 all-gather.5.cloned.1.call-start
  19.1 0.7 all-gather.5.cloned.1.call-update
  19.8 56.1 %all-to-all-done = bf16[4,128,1152]{2,0,1:T(4,128)(2,1)S(1)} async-done(((bf16[4,128,1152]{2,0,1:T(4,128)(2,1)}), bf16[4,128,1152]{2,0,1:T(4,128)(2,1)S(1)}, u32[]{:S(2)}, u32[]{:S(2)}) %all-to-all-start) | async-done | bytes 1179680 | tf_op jit(solution)/shard_map/all_to_all | solution.py:47
  75.9 0.1 copy.42
  76.1 0.1 copy.43
  76.2 32.6 %all-gather.3.cloned.1.call-done = bf16[1152,3456]{0,1:T(8,128)(2,1)} async-done(((bf16[1152,432]{0,1:T(8,128)(2,1)}), bf16[1152,3456]{0,1:T(8,128)(2,1)}) %all-gather.3.cloned.1.call-update) | async-done | bytes 7962640 | tf_op jit(solution)/shard_map/all_gather | solution.py:54
  108.7 9.6 %convolution_convert_fusion = bf16[512,3456]{1,0:T(8,128)(2,1)} fusion(bf16[512,1152]{1,0:T(8,128)(2,1)S(1)} %bitcast.90, bf16[1152,3456]{0,1:T(8,128)(2,1)} %all-gather.3.cloned.1.call-done), kind=kOutput, calls=%fused_computation.2 | convolution fusion | flops 4078632960 | bytes 12681216 | tf_op jit(solution)/shard_map/dot_general | solution.py:52
  118.3 13.6 %reshape.71 = bf16[32,16,6,8,72]{4,3,2,1,0:T(8,128)(2,1)} reshape(bf16[512,3456]{1,0:T(8,128)(2,1)} %convolution_convert_fusion) | data formatting | bytes 7077888 | tf_op jit(solution)/shard_map/reshape | solution.py:57
  132.0 0.0 copy-start
  132.0 2.1 fusion.54
  134.1 1.2 copy.62
  135.3 0.0 copy-start.2
  135.3 2.4 collective-permute-start.1
  137.7 2.2 copy.61
  139.9 0.0 collective-permute-start
  139.9 0.0 copy-done
  139.9 0.2 fusion.53
  140.1 0.0 copy-done.2
  140.1 2.1 fusion.52
  142.2 4.8 %fusion.60 = (f32[16,8,32]{2,1,0:T(8,128)S(1)}, f32[16,8,32,32]{2,3,1,0:T(8,128)}) fusion(bf16[32,16,1,8,72]{4,3,2,1,0:T(8,128)(2,1)} %get-tuple-element.6, bf16[32,16,1,8,72]{4,3,2,1,0:T(8,128)(2,1)} %get-tuple-element.7), kind=kOutput, calls=%fused_computation.66 | convolution fusion | flops 19267616 | bytes 1720320 | tf_op jit(solution)/shard_map/sub | solution.py:33
  147.0 0.0 copy-start.5
  147.0 2.2 copy_bitcast_fusion.6
  149.3 0.0 copy-done.5
  149.3 3.6 %fusion.22 = bf16[32,16,8,72]{3,0,2,1:T(8,128)(2,1)} fusion(f32[16,8,32,32]{2,3,1,0:T(8,128)} %get-tuple-element.18, bf16[32,16,1,8,72]{4,3,2,1,0:T(8,128)(2,1)S(1)} %copy-done.5, f32[16,8,32]{2,1,0:T(8,128)S(1)} %get-tuple-element.17), kind=kOutput, calls=%fused_computation.37 | convolution fusion | flops 19431424 | bytes 1720320 | tf_op jit(solution)/shard_map/wphts,wsphd->wtphd/dot_general | solution.py:36
  152.8 0.0 copy-start.3
  152.8 6.9 %collective-permute-done.1 = bf16[16,16,2,8,72]{4,0,3,1,2:T(8,128)(2,1)} collective-permute-done((bf16[16,16,2,8,72]{4,0,3,1,2:T(8,128)(2,1)S(1)}, bf16[16,16,2,8,72]{4,0,3,1,2:T(8,128)(2,1)}, u32[]{:S(2)}, u32[]{:S(2)}) %collective-permute-start.1) | collective-permute-done | bytes 589856 | tf_op jit(solution)/shard_map/ppermute | solution.py:16
  159.7 2.1 maximum_bitcast_fusion.1
  161.9 21.4 %collective-permute-done = bf16[16,16,2,8,72]{4,0,3,1,2:T(8,128)(2,1)} collective-permute-done((bf16[16,16,2,8,72]{4,0,3,1,2:T(8,128)(2,1)}, bf16[16,16,2,8,72]{4,0,3,1,2:T(8,128)(2,1)}, u32[]{:S(2)}, u32[]{:S(2)}) %collective-permute-start) | collective-permute-done | bytes 589856 | tf_op jit(solution)/shard_map/ppermute | solution.py:16
  183.3 0.0 copy-done.3
  183.3 3.2 %maximum_bitcast_fusion = bf16[1,32,16,2,8,72]{5,1,4,2,0,3:T(8,128)(2,1)} fusion(bf16[16,16,2,8,72]{4,0,3,1,2:T(8,128)(2,1)S(1)} %copy-done.3, bf16[16,16,2,8,72]{4,0,3,1,2:T(8,128)(2,1)} %collective-permute-done), kind=kLoop, calls=%fused_computation.24 | loop fusion | flops 2359296 | bytes 2359296 | tf_op jit(solution)/shard_map/stack | solution.py:67
  186.5 4.3 %fusion.55 = (f32[2,16,8,16]{3,2,1,0:T(8,128)S(1)}, f32[2,16,8,16,32]{4,3,2,1,0:T(8,128)}) fusion(bf16[1,32,16,2,8,72]{5,1,4,2,0,3:T(8,128)(2,1)S(1)} %maximum_bitcast_fusion.1, bf16[1,32,16,2,8,72]{5,1,4,2,0,3:T(8,128)(2,1)} %maximum_bitcast_fusion, bf16[1,16,16,8,72]{4,1,3,2,0:T(8,128)(2,1)} %get-tuple-element.19, ...), kind=kOutput, calls=%fused_computation.65 | convolution fusion | flops 20152352 | bytes 3489792 | tf_op jit(solution)/shard_map/sub | solution.py:33
  190.8 2.6 %fusion.23 = bf16[2,16,16,8,72]{4,1,3,2,0:T(8,128)(2,1)S(1)} fusion(bf16[1,32,16,2,8,72]{5,1,4,2,0,3:T(8,128)(2,1)} %maximum_bitcast_fusion, bf16[1,32,16,2,8,72]{5,1,4,2,0,3:T(8,128)(2,1)S(1)} %maximum_bitcast_fusion.1, f32[2,16,8,16,32]{4,3,2,1,0:T(8,128)} %get-tuple-element.16, f32[2,16,8,16]{3,2,1,0:T(8,128)S(1)} %get-tuple-element.15), kind=kOutput, calls=%fused_computation.38 | convolution fusion | flops 20021248 | bytes 3489792 | tf_op jit(solution)/shard_map/wphts,wsphd->wtphd/dot_general | solution.py:36
  193.4 0.0 copy-start.4
  193.4 0.2 copy.53
  193.6 1.0 copy-done.4
  194.7 0.4 pad_maximum_fusion.1
  195.1 0.8 copy.54
  195.9 3.6 %reshape.76 = bf16[512,1152]{1,0:T(8,128)(2,1)} reshape(bf16[32,16,16,72]{3,2,1,0:T(8,128)(2,1)S(1)} %copy.54) | data formatting | bytes 2359296 | tf_op jit(solution)/shard_map/reshape | solution.py:70
  199.5 0.0 all-gather.5.cloned.1.call-done
  199.5 4.0 %convolution_convert_fusion.1 = bf16[512,1152]{1,0:T(8,128)(2,1)S(1)} fusion(bf16[512,1152]{1,0:T(8,128)(2,1)} %reshape.76, bf16[1152,1152]{0,1:T(8,128)(2,1)} %all-gather.5.cloned.1.call-done), kind=kOutput, calls=%fused_computation.8 | convolution fusion | flops 1359544320 | bytes 5013504 | tf_op jit(solution)/shard_map/dot_general | solution.py:71
  203.5 36.0 %all_to_all.24 = bf16[32,16,1152]{2,1,0:T(8,128)(2,1)S(1)} all-to-all(bf16[32,16,1152]{2,1,0:T(8,128)(2,1)S(1)} %bitcast.91), channel_id=1, replica_groups=mesh['slab'=4,'seq'=8] {'seq'}, dimensions={0} | all-to-all | bytes 2359296 | tf_op jit(solution)/shard_map/all_to_all | solution.py:76
  239.5 0.5 copy.55
  240.0 1.3 fusion.8
  241.3 1.1 copy.56
  (3 shorter events, 0.0 us)
Async XLA Ops:
  6.5 2.9 %copy-start.1 = (bf16[4,128,1152]{2,1,0:T(8,128)(2,1)S(1)}, bf16[4,128,1152]{2,1,0:T(8,128)(2,1)}, u32[]{:S(2)}) copy-start(bf16[4,128,1152]{2,1,0:T(8,128)(2,1)} %param.4) | copy-start | bytes 3538948
  6.5 4.1 %copy-start.6 = (f32[4,3,1152]{2,0,1:T(4,128)S(1)}, f32[4,3,1152]{2,0,1:T(4,128)}, u32[]{:S(2)}) copy-start(f32[4,3,1152]{2,0,1:T(4,128)} %param.5) | copy-start | bytes 165892
  6.5 102.2 %all-gather.3.cloned.1.call-start = ((), (), s32[]{:S(2)}) async-start(), calls=%async_computation.2 | async-start | bytes 8957952 | tf_op jit(solution)/shard_map/all_gather | solution.py:54
  13.5 62.5 %all-to-all-start = ((bf16[4,128,1152]{2,0,1:T(4,128)(2,1)}), bf16[4,128,1152]{2,0,1:T(4,128)(2,1)S(1)}, u32[]{:S(2)}, u32[]{:S(2)}) async-start(bf16[4,128,1152]{2,0,1:T(4,128)(2,1)} %fusion.7), calls=%async_computation | async-start | bytes 2359296 | tf_op jit(solution)/shard_map/all_to_all | solution.py:47
  19.1 180.4 %all-gather.5.cloned.1.call-start = ((), (), s32[]{:S(2)}) async-start(), calls=%async_computation.3 | async-start | bytes 2985984 | tf_op jit(solution)/shard_map/all_gather | solution.py:73
  132.0 8.0 %copy-start = (bf16[32,16,6,8,72]{4,3,2,1,0:T(8,128)(2,1)S(1)}, bf16[32,16,6,8,72]{4,3,2,1,0:T(8,128)(2,1)}, u32[]{:S(2)}) copy-start(bf16[32,16,6,8,72]{4,3,2,1,0:T(8,128)(2,1)} %reshape.71) | copy-start | bytes 10616836
  135.3 4.8 %copy-start.2 = (bf16[16,16,2,8,72]{4,0,3,1,2:T(8,128)(2,1)}, bf16[16,16,2,8,72]{4,0,3,1,2:T(8,128)(2,1)S(1)}, u32[]{:S(2)}) copy-start(bf16[16,16,2,8,72]{4,0,3,1,2:T(8,128)(2,1)S(1)} %copy.62) | copy-start | bytes 1769476
  135.3 24.4 %collective-permute-start.1 = (bf16[16,16,2,8,72]{4,0,3,1,2:T(8,128)(2,1)S(1)}, bf16[16,16,2,8,72]{4,0,3,1,2:T(8,128)(2,1)}, u32[]{:S(2)}, u32[]{:S(2)}) collective-permute-start(bf16[16,16,2,8,72]{4,0,3,1,2:T(8,128)(2,1)S(1)} %copy.62), channel_id=1, source_target_pairs={{0,24},{8,0},{16,8},{24,16},{1,25},{9,1},{17,9},{25,17},{2,26},{10... | collective-permute-start | bytes 1769480 | tf_op jit(solution)/shard_map/ppermute | solution.py:16
  139.9 43.4 %collective-permute-start = (bf16[16,16,2,8,72]{4,0,3,1,2:T(8,128)(2,1)}, bf16[16,16,2,8,72]{4,0,3,1,2:T(8,128)(2,1)}, u32[]{:S(2)}, u32[]{:S(2)}) collective-permute-start(bf16[16,16,2,8,72]{4,0,3,1,2:T(8,128)(2,1)} %copy.61), channel_id=1, source_target_pairs={{0,8},{8,16},{16,24},{24,0},{1,9},{9,17},{17,25},{25,1},{2,10},{10... | collective-permute-start | bytes 1769480 | tf_op jit(solution)/shard_map/ppermute | solution.py:16
  147.0 2.2 copy-start.5
  152.8 30.5 %copy-start.3 = (bf16[16,16,2,8,72]{4,0,3,1,2:T(8,128)(2,1)S(1)}, bf16[16,16,2,8,72]{4,0,3,1,2:T(8,128)(2,1)}, u32[]{:S(2)}) copy-start(bf16[16,16,2,8,72]{4,0,3,1,2:T(8,128)(2,1)} %copy-done.2) | copy-start | bytes 1769476
  193.4 1.2 copy-start.4
Sparse Core Ops, SparseCore 0:
  9.0 99.6 all-gather.2
  110.4 37.4 all-gather.4
where the time goes:
time: 253 us; the launch traced here: 249 us
  waiting for transfers between devices  118 us (47%)
  blocking collectives  36 us (14%)
  local copies, waits for them, and re-layouts  31.2 us (12%)
  matrix products  28.9 us (11%)
  between operations  13.5 us (5%)
  other arithmetic  13.2 us (5%)
  starting transfers between devices  8.02 us (3%)
    all_to_all x1, waiting for transfers between devices, per_device(): lax.all_to_all(normed, 'seq', split_axis=1, concat_axis=0, tiled=True)  56.1 us
    all_to_all x1, blocking collectives, per_device(): lax.all_to_all(output_rows.reshape(window_len, pos_dev, width), 'seq', sp...  36 us
    all_gather x1, waiting for transfers between devices, per_device(): lax.all_gather(qkv_weight, 'seq', axis=1, tiled=True)  32.6 us
    ppermute x2, waiting for transfers between devices, shifted_2(): return lax.ppermute(value, axis, pairs)  28.3 us
    reshape x1, local copies, waits for them, and re-layouts, per_device(): grouped = projected.reshape(window_len, pos_dev, 6, heads_half, head_size)  13.6 us
    dot_general x1, matrix products, per_device(): jnp.dot(token_rows, lax.all_gather(qkv_weight, 'seq', axis=1, tiled=True)...  9.61 us
    sub x2, matrix products, attend(): scores = scores - jnp.max(scores, axis=-1, keepdims=True)  9.07 us
    dot_general x2, matrix products, attend(): jnp.einsum('wphts,wsphd->wtphd', softmaxed, value_rows, preferred_element...  6.21 us
  transfers between devices with their start and end apart: 5, of which 4 were waited for; matrix products, arithmetic and copies ran while one was open for 26% of the time, Pallas kernels for 0%

commit v1 on v0

v1 whole, which is shorter than its diff:
```python
import functools

import jax
import jax.numpy as jnp
from jax import lax
from jax.experimental import pallas as pl
from jax.experimental.pallas import tpu as pltpu
from jax.sharding import PartitionSpec as P

H = 16
FRS = 32
EPSILON = 1e-06
LANES = 128
ROWS = 16
VMEM_BYTES = 50 * 1024 * 1024


def padded(width):
    return -(-width // LANES) * LANES


def norm_kernel(index_ref, tokens_ref, modulation_ref, *refs):
    out_refs, mixed = refs[:-1], refs[-1]
    frames = tokens_ref.shape[0]
    groups, rows, width = out_refs[0].shape
    positions = groups * rows // frames
    index = index_ref[0]
    for d, out_ref in enumerate(out_refs):
        start = pl.multiple_of(lax.bitwise_xor(index, d) * positions, positions)
        for f in range(frames):
            values = tokens_ref[f, pl.ds(start, positions), :].astype(jnp.float32)
            average = jnp.mean(values, axis=-1, keepdims=True)
            centered = values - average
            variance = jnp.mean(centered * centered, axis=-1, keepdims=True)
            normed = centered * lax.rsqrt(variance + EPSILON)
            result = normed * (1.0 + modulation_ref[f, 1:2, :]) + modulation_ref[f, 0:1, :]
            for t in range(width // LANES):
                mixed[t, pl.ds(f, positions, stride=frames), :] = result[:, t * LANES : (t + 1) * LANES]
        for t in range(width // LANES):
            out_ref[:, :, t * LANES : (t + 1) * LANES] = mixed[t].astype(out_ref.dtype).reshape(groups, rows, LANES)


def restore_kernel(index_ref, tokens_ref, modulation_ref, *refs):
    in_refs, out_ref, mixed = refs[:-2], refs[-2], refs[-1]
    frames = tokens_ref.shape[0]
    groups, rows, width = in_refs[0].shape
    positions = groups * rows // frames
    index = index_ref[0]
    for d, in_ref in enumerate(in_refs):
        start = pl.multiple_of(lax.bitwise_xor(index, d) * positions, positions)
        for t in range(width // LANES):
            part = in_ref[:, :, t * LANES : (t + 1) * LANES]
            mixed[t] = part.reshape(groups * rows, LANES).astype(jnp.float32)
        for f in range(frames):
            values = tokens_ref[f, pl.ds(start, positions), :].astype(jnp.float32)
            projected = jnp.concatenate(
                [mixed[t, pl.ds(f, positions, stride=frames), :] for t in range(width // LANES)], axis=1
            )
            result = values + modulation_ref[f, 2:3, :] * projected
            out_ref[f, pl.ds(start, positions), :] = result.astype(out_ref.dtype)


def nt_dot(left, right):
    return lax.dot_general(left, right, (((1,), (1,)), ((), ())), preferred_element_type=jnp.float32)


def head_window(head, head_size, shift):
    first = shift + head * head_size
    last = first + head_size
    low = first // LANES * LANES
    return first, last, low, padded(last)


def masked(values, first, last, low):
    lane = lax.broadcasted_iota(jnp.int32, values.shape, 1) + low
    return jnp.where((lane >= first) & (lane < last), values, jnp.zeros_like(values))


def softmax(scores, same, scale):
    scores = jnp.where(same, scores, -jnp.inf)
    top = jnp.max(scores, axis=-1, keepdims=True)
    exponent = jnp.exp((scores - top) * scale)
    total = jnp.sum(exponent, axis=-1, keepdims=True)
    return (exponent * (1.0 / total)).astype(jnp.bfloat16)


def block_kernel(plan, frames, index_ref, *refs):
    count, extra, weights = plan["count"], plan["extra"], plan["weights"]
    refs = list(refs)
    x_refs = [refs.pop(0) for _ in range(count)]
    e_refs = [refs.pop(0) for _ in range(extra)]
    w_refs = [refs.pop(0) for _ in range(weights)]
    out_refs = [refs.pop(0) for _ in range(count)]
    xs, xe, wall, qkv, ext, att, ys, sems, wsems = refs
    groups, _, rows, width = xs.shape
    half, lanes = plan["half"], plan["lanes"]
    heads_half = H // 2
    head_size = width // H
    scale = head_size ** (-0.5)
    slot = count * rows
    index, slab = index_ref[0], index_ref[1]

    copies = []
    for d in range(count):
        owner = lax.bitwise_xor(index, d)
        copies.append((x_refs[d], xs.at[:, owner]))
        copies.append((e_refs[d // 2].at[d % 2], xe.at[:, owner]))
    copies = [pltpu.make_async_copy(a, b, sems.at[n]) for n, (a, b) in enumerate(copies)]
    moves = []
    for operand, at, size, owner, part in plan["moves"]:
        if owner is None:
            row = part * lanes + (lanes - half if part == 5 else 0)
            row = row if part < 6 else 6 * lanes + (part - 6) * half
            moves.append((w_refs[operand].at[at[0]], wall.at[pl.ds(row, size)]))
            continue
        device = lax.bitwise_xor(index, owner)
        piece = lax.bitwise_xor(slab, part[1]) if part[0] == "xor" else jnp.int32(part[1])
        column = device * plan["columns"] + piece * size
        block = column // half
        row = block * lanes + (column - block * half)
        row = row + jnp.where(block == 5, lanes - half, 0)
        row = jnp.where(piece * size < plan["columns"], row,
                        6 * lanes + device * plan["outs"] + piece * size - plan["columns"])
        source = w_refs[operand]
        for step in at:
            source = source.at[step]
        moves.append((source, wall.at[pl.ds(pl.multiple_of(row, ROWS), size)]))
    moves = [pltpu.make_async_copy(a, b, wsems.at[n]) for n, (a, b) in enumerate(moves)]
    for copy in moves + copies:
        copy.start()
    gap = lanes - half
    for block in range(6):
        edge = block * lanes + (0 if block == 5 else half)
        if gap:
            wall[edge : edge + gap, :] = jnp.zeros((gap, width), wall.dtype)
    for copy in moves + copies:
        copy.wait()

    tokens = groups * slot
    own = xs[...].reshape(tokens, width)
    for block in range(6):
        part = wall[block * lanes : (block + 1) * lanes, :]
        qkv[block] = nt_dot(own, part).astype(qkv.dtype)
        if block >= 4:
            ext[block - 4] = nt_dot(xe[...].reshape(tokens, width), part).astype(ext.dtype)

    def one_group(g, carry):
        here = pl.ds(pl.multiple_of(g * slot, slot), slot)
        row = lax.broadcasted_iota(jnp.int32, (slot, slot), 0)
        column = lax.broadcasted_iota(jnp.int32, (slot, slot), 1)
        same = (row % rows) // frames == (column % rows) // frames
        low_half = lax.broadcasted_iota(jnp.int32, (slot, 1), 0) < slot // 2
        tiles = [None] * (width // LANES)

        def add(first_tile, value):
            for n in range(value.shape[1] // LANES):
                piece = value[:, n * LANES : (n + 1) * LANES]
                t = first_tile + n
                tiles[t] = piece if tiles[t] is None else tiles[t] + piece

        for head in range(heads_half):
            first, last, low, high = head_window(head, head_size, 0)
            queries = qkv[0, here, low:high]
            keys = masked(qkv[1, here, low:high], first, last, low)
            values = masked(qkv[2, here, low:high], first, last, low)
            probs = softmax(nt_dot(queries, keys), same, scale)
            add(low // LANES, jnp.dot(probs, values, preferred_element_type=jnp.float32))
        for head in range(heads_half):
            first, last, low, high = head_window(head, head_size, 0)
            queries = qkv[3, here, low:high]
            own_keys = masked(qkv[4, here, low:high], first, last, low)
            ext_keys = masked(ext[0, here, low:high], first, last, low)
            first, last, low, high = head_window(head, head_size, gap)
            own_values = masked(qkv[5, here, low:high], first, last, low)
            ext_values = masked(ext[1, here, low:high], first, last, low)
            mid = slot // 2
            keys = jnp.where(low_half, own_keys, ext_keys)
            later = jnp.where(low_half, ext_keys, own_keys)
            values = jnp.where(low_half, own_values, ext_values)
            later_values = jnp.where(low_half, ext_values, own_values)
            scores = jnp.concatenate([nt_dot(queries[:mid], keys), nt_dot(queries[mid:], later)], axis=0)
            probs = softmax(scores, same, scale)
            result = jnp.concatenate([
                jnp.dot(probs[:mid], values, preferred_element_type=jnp.float32),
                jnp.dot(probs[mid:], later_values, preferred_element_type=jnp.float32),
            ], axis=0)
            add((width // 2 - gap + low) // LANES, result)
        att[here, :] = jnp.concatenate(tiles, axis=1).astype(att.dtype)
        return carry

    lax.fori_loop(0, groups, one_group, 0)
    y = nt_dot(att[...], wall[6 * lanes :, :]).astype(ys.dtype)
    ys[...] = y.reshape(ys.shape)
    for d in range(count):
        out_refs[d][...] = ys[:, lax.bitwise_xor(index, d)]


def per_device(video_tokens, modulation, qkv_weight, out_weight):
    frames, positions, width = video_tokens.shape
    count, slabs = lax.axis_size("seq"), lax.axis_size("slab")
    index, slab = lax.axis_index("seq"), lax.axis_index("slab")
    block_positions = positions // count
    block_rows = block_positions * frames
    groups = block_rows // ROWS
    block = jax.ShapeDtypeStruct((groups, ROWS, width), jnp.bfloat16)
    own_index = jnp.stack([index, slab]).astype(jnp.int32)
    smem = pl.BlockSpec(memory_space=pltpu.SMEM)
    vmem = pl.BlockSpec(memory_space=pltpu.VMEM)
    anywhere = pl.BlockSpec(memory_space=pl.ANY)
    params = pltpu.CompilerParams(vmem_limit_bytes=VMEM_BYTES)

    def hop(value, seq_xor, slab_xor=0):
        pairs = [(s * count + i, (s ^ slab_xor) * count + (i ^ seq_xor)) for s in range(slabs) for i in range(count)]
        return lax.ppermute(value, ("slab", "seq"), pairs)

    half = width // 2
    lanes = padded(half)
    columns, outs = qkv_weight.shape[1], out_weight.shape[1]
    shard = jnp.concatenate([qkv_weight.T, out_weight.T], axis=0)
    unit = (columns + outs) // slabs
    moves = []
    if unit % ROWS == 0 and columns % unit == 0 and half % unit == 0:
        parts = shard.reshape(slabs, unit, width)
        mine = lax.dynamic_index_in_dim(parts, slab, 0, keepdims=False)
        operands = [parts, hop(parts, 1)]
        for sibling in range(2):
            for n in range(slabs):
                moves.append((sibling, (n,), unit, sibling, ("at", n)))
        received = {z: hop(mine, 2 * z) for z in range(1, count // 2)}
        bundles = [([1], True)]
        if count > 4:
            bundles.append((list(range(2, count // 2)), False))
        for zs, reverse in bundles:
            base = jnp.stack([received[z] for z in zs])
            held = {0: base}
            bits = [1 << b for b in range(slabs.bit_length() - 1)]
            for bit in reversed(bits) if reverse else bits:
                for e in list(held):
                    held[e ^ bit] = hop(held[e], 0, bit)
            for e in sorted(held):
                for sibling in range(2):
                    operands.append(held[e] if sibling == 0 else hop(held[e], 1))
                    for n, z in enumerate(zs):
                        moves.append((len(operands) - 1, (n,), unit, (2 * z) ^ sibling, ("xor", e)))
        plan_columns, plan_outs = columns, outs
    else:
        full_qkv = lax.all_gather(qkv_weight.T, "seq", axis=0, tiled=True)
        full_out = lax.all_gather(out_weight.T, "seq", axis=0, tiled=True)
        operands = [full_qkv.reshape(6, half, width), full_out.reshape(2, half, width)]
        operands = [jnp.concatenate(operands, axis=0)]
        moves = [(0, (n,), half, None, n) for n in range(8)]
        plan_columns, plan_outs = columns, outs

    sent = pl.pallas_call(
        norm_kernel,
        out_shape=[block] * count,
        in_specs=[smem, vmem, vmem],
        out_specs=[vmem] * count,
        scratch_shapes=[pltpu.VMEM((width // LANES, block_rows, LANES), jnp.float32)],
        compiler_params=params,
        name="norm",
    )(own_index, video_tokens, modulation)
    blocks = [sent[0]] + [hop(sent[d], d) for d in range(1, count)]
    middle = count // 2
    extras = []
    for z in range(count // 2):
        pairs = []
        for s in range(slabs):
            for i in range(count):
                step = 1 if (i ^ (2 * z)) >= middle else -1
                pairs.append((s * count + i, (s + step) % slabs * count + i))
        extras.append(lax.ppermute(jnp.stack(blocks[2 * z : 2 * z + 2]), ("slab", "seq"), pairs))

    plan = dict(count=count, extra=len(extras), weights=len(operands), half=half, lanes=lanes, moves=moves,
                columns=plan_columns, outs=plan_outs)
    tokens = count * block_rows
    flops = 2 * tokens * width * (6 * lanes + 2 * lanes + width)
    projected = pl.pallas_call(
        functools.partial(block_kernel, plan, frames),
        out_shape=[block] * count,
        in_specs=[smem] + [anywhere] * (count + len(extras) + len(operands)),
        out_specs=[vmem] * count,
        scratch_shapes=[
            pltpu.VMEM((groups, count, ROWS, width), jnp.bfloat16),
            pltpu.VMEM((groups, count, ROWS, width), jnp.bfloat16),
            pltpu.VMEM((6 * lanes + width, width), jnp.bfloat16),
            pltpu.VMEM((6, tokens, lanes), jnp.bfloat16),
            pltpu.VMEM((2, tokens, lanes), jnp.bfloat16),
            pltpu.VMEM((tokens, width), jnp.bfloat16),
            pltpu.VMEM((groups, count, ROWS, width), jnp.bfloat16),
            pltpu.SemaphoreType.DMA((2 * count,)),
            pltpu.SemaphoreType.DMA((len(moves),)),
        ],
        compiler_params=params,
        cost_estimate=pl.CostEstimate(flops=flops, bytes_accessed=16 * 1024 * 1024, transcendentals=0),
        name="block",
    )(own_index, *blocks, *extras, *operands)
    returned = [projected[0]] + [hop(projected[d], d) for d in range(1, count)]
    return pl.pallas_call(
        restore_kernel,
        out_shape=jax.ShapeDtypeStruct(video_tokens.shape, video_tokens.dtype),
        in_specs=[smem, vmem, vmem] + [vmem] * count,
        out_specs=vmem,
        scratch_shapes=[pltpu.VMEM((width // LANES, block_rows, LANES), jnp.float32)],
        compiler_params=params,
        name="restore",
    )(own_index, video_tokens, modulation, *returned)


def solution(mesh):
    return jax.shard_map(
        per_device,
        mesh=mesh,
        in_specs=(
            P(("slab", "seq"), None, None),
            P(("slab", "seq"), None, None),
            P(None, "seq"),
            P(None, "seq"),
        ),
        out_specs=P(("slab", "seq"), None, None),
        check_vma=False,
    )
```

time: 253 us -> 204 us (0.81); the launches traced: 249 us -> 204 us
  starting transfers between devices: 8.02 us -> 50.2 us
  blocking collectives: 36 us -> 0 us
  Pallas kernels: 0 us -> 35.5 us
  matrix products: 28.9 us -> 0 us
  local copies, waits for them, and re-layouts: 31.2 us -> 4.54 us
  between operations: 13.5 us -> 0.24 us
  other arithmetic: 13.2 us -> 1.36 us
  waiting for transfers between devices: 118 us -> 112 us
    ppermute x2 -> x36, waiting for transfers between devices: 28.3 us -> 112 us  [the longest x32 82.5 us: hop(): return lax.ppermute(value, ('slab', 'seq'), pairs)]
    all_to_all x1 -> x0, waiting for transfers between devices: 56.1 us -> none  [per_device(): lax.all_to_all(normed, 'seq', split_axis=1, concat_axis=0, tiled=True)]
    ppermute x2 -> x36, starting transfers between devices: 2.38 us -> 50.2 us  [the longest x32 43.5 us: hop(): return lax.ppermute(value, ('slab', 'seq'), pairs)]
    all_to_all x1 -> x0, blocking collectives: 36 us -> none  [per_device(): lax.all_to_all(output_rows.reshape(window_len, pos_dev, width), 'seq', sp...]
    pallas_call x0 -> x3, Pallas kernels: none -> 35.5 us  [the longest x1 31.8 us: per_device(): pl.pallas_call(functools.partial(block_kernel, plan, frames), out_shape=[...]
    all_gather x2 -> x0, waiting for transfers between devices: 32.6 us -> none  [the longest x1 32.6 us: per_device(): lax.all_gather(qkv_weight, 'seq', axis=1, tiled=True)]
    dot_general x4 -> x0, matrix products: 19.8 us -> none  [the longest x1 9.61 us: per_device(): jnp.dot(token_rows, lax.all_gather(qkv_weight, 'seq', axis=1, tiled=True)...]
    reshape x2 -> x0, local copies, waits for them, and re-layouts: 17.2 us -> none  [the longest x1 13.6 us: per_device(): grouped = projected.reshape(window_len, pos_dev, 6, heads_half, head_size)]
  transfers between devices with their start and end apart: 5 -> 36, of which waited for: 4 -> 19; matrix products, arithmetic and copies ran while one was open for 26% -> 1% of each run, Pallas kernels for 0% -> 0%
where the time goes in v1:
time: 204 us
  waiting for transfers between devices  112 us (55%)
  starting transfers between devices  50.2 us (25%)
  Pallas kernels  35.5 us (17%)
  local copies, waits for them, and re-layouts  4.54 us (2%)
    ppermute x32, waiting for transfers between devices, hop(): return lax.ppermute(value, ('slab', 'seq'), pairs)  82.5 us
    ppermute x32, starting transfers between devices, hop(): return lax.ppermute(value, ('slab', 'seq'), pairs)  43.5 us
    pallas_call x1, Pallas kernels, per_device(): pl.pallas_call(functools.partial(block_kernel, plan, frames), out_shape=[...  31.8 us
    ppermute x4, waiting for transfers between devices, per_device(): lax.ppermute(jnp.stack(blocks[2 * z:2 * z + 2]), ('slab', 'seq'), pairs)  29.5 us
    ppermute x4, starting transfers between devices, per_device(): lax.ppermute(jnp.stack(blocks[2 * z:2 * z + 2]), ('slab', 'seq'), pairs)  6.76 us
    unnamed x39, local copies, waits for them, and re-layouts  4.5 us
  transfers between devices with their start and end apart: 36, of which 19 were waited for; matrix products, arithmetic and copies ran while one was open for 1% of the time, Pallas kernels for 0%

profile of v1, /device:TPU:9, one launch (start us, length us, event | category | flops | bytes accessed | tf_op | source)
XLA Modules:
  0.0 203.8 jit_solution(10600784714517028846)
XLA Ops:
  0.0 0.8 copy.6.modulation_ref
  0.8 0.1 pad_add_fusion.index_ref
  0.9 1.3 copy-done
  2.2 1.6 norm.1
  3.9 2.3 %collective-permute-start.2 = (bf16[4,16,1152]{2,1,0:T(8,128)(2,1)S(1)}, bf16[4,16,1152]{2,1,0:T(8,128)(2,1)S(1)}, u32[]{:S(2)}, u32[]{:S(2)}) collective-permute-start(bf16[4,16,1152]{2,1,0:T(8,128)(2,1)S(1)} %get-tuple-element.24), channel_id=1, source_target_pairs={{0,3},{1,2},{2,1},{3,0},{4,7},{5,6},{6,5},{7,4},{8,11},{9,10},{10,... | collective-permute-start | bytes 442376 | tf_op jit(solution)/shard_map/ppermute | solution.py:214
  6.2 1.1 pad_maximum_fusion
  7.4 1.4 collective-permute-start.21
  8.7 1.1 collective-permute-start.20
  9.8 1.1 collective-permute-start.12
  10.9 0.4 collective-permute-start
  11.3 2.3 %collective-permute-done.2.refs_3_ = bf16[4,16,1152]{2,1,0:T(8,128)(2,1)S(1)} collective-permute-done((bf16[4,16,1152]{2,1,0:T(8,128)(2,1)S(1)}, bf16[4,16,1152]{2,1,0:T(8,128)(2,1)S(1)}, u32[]{:S(2)}, u32[]{:S(2)}) %collective-permute-start.2) | collective-permute-done | bytes 147488 | tf_op jit(solution)/shard_map/ppermute | solution.py:214
  13.7 9.2 %collective-permute-start.3 = (bf16[4,16,1152]{2,1,0:T(8,128)(2,1)S(1)}, bf16[4,16,1152]{2,1,0:T(8,128)(2,1)S(1)}, u32[]{:S(2)}, u32[]{:S(2)}) collective-permute-start(bf16[4,16,1152]{2,1,0:T(8,128)(2,1)S(1)} %get-tuple-element.25), channel_id=1, source_target_pairs={{0,4},{1,5},{2,6},{3,7},{4,0},{5,1},{6,2},{7,3},{8,12},{9,13},{10,... | collective-permute-start | bytes 442376 | tf_op jit(solution)/shard_map/ppermute | solution.py:214
  23.1 8.4 %collective-permute-done.21 = bf16[144,1152]{1,0:T(8,128)(2,1)S(1)} collective-permute-done((bf16[144,1152]{1,0:T(8,128)(2,1)S(1)}, bf16[144,1152]{1,0:T(8,128)(2,1)S(1)}, u32[]{:S(2)}, u32[]{:S(2)}) %collective-permute-start.21) | collective-permute-done | bytes 331808 | tf_op jit(solution)/shard_map/ppermute | solution.py:214
  31.4 1.0 collective-permute-start.5
  32.4 14.4 %collective-permute-done.20 = bf16[144,1152]{1,0:T(8,128)(2,1)S(1)} collective-permute-done((bf16[144,1152]{1,0:T(8,128)(2,1)S(1)}, bf16[144,1152]{1,0:T(8,128)(2,1)S(1)}, u32[]{:S(2)}, u32[]{:S(2)}) %collective-permute-start.20) | collective-permute-done | bytes 331808 | tf_op jit(solution)/shard_map/ppermute | solution.py:214
  46.8 0.8 collective-permute-start.6
  47.7 2.3 %collective-permute-done.3.refs_4_ = bf16[4,16,1152]{2,1,0:T(8,128)(2,1)S(1)} collective-permute-done((bf16[4,16,1152]{2,1,0:T(8,128)(2,1)S(1)}, bf16[4,16,1152]{2,1,0:T(8,128)(2,1)S(1)}, u32[]{:S(2)}, u32[]{:S(2)}) %collective-permute-start.3) | collective-permute-done | bytes 147488 | tf_op jit(solution)/shard_map/ppermute | solution.py:214
  50.0 2.2 %collective-permute-start.7 = (bf16[2,4,16,1152]{3,2,1,0:T(8,128)(2,1)S(1)}, bf16[2,4,16,1152]{3,2,1,0:T(8,128)(2,1)S(1)}, u32[]{:S(2)}, u32[]{:S(2)}) collective-permute-start(bf16[2,4,16,1152]{3,2,1,0:T(8,128)(2,1)S(1)} %pad_maximum_fusion.2), channel_id=1, source_target_pairs={{0,24},{1,25},{2,26},{3,27},{4,12},{5,13},{6,14},{7,15},{8,0},{9,1... | collective-permute-start | bytes 884744 | tf_op jit(solution)/shard_map/ppermute | solution.py:272
  52.1 4.2 %collective-permute-done.4.refs_5_ = bf16[4,16,1152]{2,1,0:T(8,128)(2,1)S(1)} collective-permute-done((bf16[4,16,1152]{2,1,0:T(8,128)(2,1)S(1)}, bf16[4,16,1152]{2,1,0:T(8,128)(2,1)S(1)}, u32[]{:S(2)}, u32[]{:S(2)}) %collective-permute-start.4) | collective-permute-done | bytes 147488 | tf_op jit(solution)/shard_map/ppermute | solution.py:214
  56.3 2.2 %collective-permute-start.8 = (bf16[2,4,16,1152]{3,2,1,0:T(8,128)(2,1)S(1)}, bf16[2,4,16,1152]{3,2,1,0:T(8,128)(2,1)S(1)}, u32[]{:S(2)}, u32[]{:S(2)}) collective-permute-start(bf16[2,4,16,1152]{3,2,1,0:T(8,128)(2,1)S(1)} %pad_maximum_fusion.3), channel_id=1, source_target_pairs={{0,24},{1,25},{2,26},{3,27},{4,12},{5,13},{6,14},{7,15},{8,0},{9,1... | collective-permute-start | bytes 884744 | tf_op jit(solution)/shard_map/ppermute | solution.py:272
  58.5 2.2 %collective-permute-done.5.refs_6_ = bf16[4,16,1152]{2,1,0:T(8,128)(2,1)S(1)} collective-permute-done((bf16[4,16,1152]{2,1,0:T(8,128)(2,1)S(1)}, bf16[4,16,1152]{2,1,0:T(8,128)(2,1)S(1)}, u32[]{:S(2)}, u32[]{:S(2)}) %collective-permute-start.5) | collective-permute-done | bytes 147488 | tf_op jit(solution)/shard_map/ppermute | solution.py:214
  60.7 1.2 collective-permute-start.23
  61.9 1.9 collective-permute-done.6.refs_7_
  63.8 1.2 collective-permute-start.9
  65.1 1.2 collective-permute-start.16
  66.3 0.2 collective-permute-start.14
  66.5 1.2 collective-permute-start.13
  67.8 17.5 %collective-permute-done.9.refs_10_ = bf16[2,4,16,1152]{3,2,1,0:T(8,128)(2,1)S(1)} collective-permute-done((bf16[2,4,16,1152]{3,2,1,0:T(8,128)(2,1)S(1)}, bf16[2,4,16,1152]{3,2,1,0:T(8,128)(2,1)S(1)}, u32[]{:S(2)}, u32[]{:S(2)}) %collective-permute-start.9) | collective-permute-done | bytes 294944 | tf_op jit(solution)/shard_map/ppermute | solution.py:272
  85.3 1.2 collective-permute-start.10
  86.5 0.2 collective-permute-start.18
  86.7 12.0 %collective-permute-done.10.refs_11_ = bf16[2,4,16,1152]{3,2,1,0:T(8,128)(2,1)S(1)} collective-permute-done((bf16[2,4,16,1152]{3,2,1,0:T(8,128)(2,1)S(1)}, bf16[2,4,16,1152]{3,2,1,0:T(8,128)(2,1)S(1)}, u32[]{:S(2)}, u32[]{:S(2)}) %collective-permute-start.10) | collective-permute-done | bytes 294944 | tf_op jit(solution)/shard_map/ppermute | solution.py:272
  98.7 3.5 %collective-permute-start.17 = (bf16[1,144,1152]{2,1,0:T(8,128)(2,1)S(1)}, bf16[1,144,1152]{2,1,0:T(8,128)(2,1)S(1)}, u32[]{:S(2)}, u32[]{:S(2)}) collective-permute-start(bf16[1,144,1152]{2,1,0:T(8,128)(2,1)S(1)} %collective-permute-done.16.refs_18_), channel_id=1, source_target_pairs={{0,1},{1,0},{2,3},{3,2},{4,5},{5,4},{6,7},{7,6},{8,9},{9,8},{10,11... | collective-permute-start | bytes 995336 | tf_op jit(solution)/shard_map/ppermute | solution.py:214
  102.2 0.1 collective-permute-start.11
  102.3 0.3 collective-permute-start.25
  102.6 1.2 collective-permute-start.27
  103.8 1.0 collective-permute-done.18.refs_20_
  104.8 2.0 collective-permute-start.22
  106.8 0.1 collective-permute-start.15
  106.9 2.3 %collective-permute-done.15.refs_17_ = bf16[1,144,1152]{2,1,0:T(8,128)(2,1)} collective-permute-done((bf16[1,144,1152]{2,1,0:T(8,128)(2,1)S(1)}, bf16[1,144,1152]{2,1,0:T(8,128)(2,1)}, u32[]{:S(2)}, u32[]{:S(2)}) %collective-permute-start.15) | collective-permute-done | bytes 331808 | tf_op jit(solution)/shard_map/ppermute | solution.py:214
  109.1 0.4 collective-permute-start.24
  109.5 8.9 %collective-permute-done.25.refs_26_ = bf16[2,144,1152]{2,1,0:T(8,128)(2,1)S(1)} collective-permute-done((bf16[2,144,1152]{2,1,0:T(8,128)(2,1)S(1)}, bf16[2,144,1152]{2,1,0:T(8,128)(2,1)S(1)}, u32[]{:S(2)}, u32[]{:S(2)}) %collective-permute-start.25) | collective-permute-done | bytes 663584 | tf_op jit(solution)/shard_map/ppermute | solution.py:214
  118.5 2.1 %collective-permute-start.26 = (bf16[2,144,1152]{2,1,0:T(8,128)(2,1)S(1)}, bf16[2,144,1152]{2,1,0:T(8,128)(2,1)S(1)}, u32[]{:S(2)}, u32[]{:S(2)}) collective-permute-start(bf16[2,144,1152]{2,1,0:T(8,128)(2,1)S(1)} %collective-permute-done.25.refs_26_), channel_id=1, source_target_pairs={{0,1},{1,0},{2,3},{3,2},{4,5},{5,4},{6,7},{7,6},{8,9},{9,8},{10,11... | collective-permute-start | bytes 1990664 | tf_op jit(solution)/shard_map/ppermute | solution.py:214
  120.6 12.1 %collective-permute-done.27.refs_28_ = bf16[2,144,1152]{2,1,0:T(8,128)(2,1)S(1)} collective-permute-done((bf16[2,144,1152]{2,1,0:T(8,128)(2,1)S(1)}, bf16[2,144,1152]{2,1,0:T(8,128)(2,1)S(1)}, u32[]{:S(2)}, u32[]{:S(2)}) %collective-permute-start.27) | collective-permute-done | bytes 663584 | tf_op jit(solution)/shard_map/ppermute | solution.py:214
  132.7 1.3 collective-permute-start.28
  134.0 2.1 %collective-permute-done.19.refs_21_ = bf16[1,144,1152]{2,1,0:T(8,128)(2,1)S(1)} collective-permute-done((bf16[1,144,1152]{2,1,0:T(8,128)(2,1)S(1)}, bf16[1,144,1152]{2,1,0:T(8,128)(2,1)S(1)}, u32[]{:S(2)}, u32[]{:S(2)}) %collective-permute-start.19) | collective-permute-done | bytes 331808 | tf_op jit(solution)/shard_map/ppermute | solution.py:214
  136.2 0.7 copy-done.18
  136.9 0.4 copy-done.5
  137.3 0.3 copy-done.11
  137.5 0.2 copy-done.10
  137.8 0.8 copy-done.12
  138.6 31.8 %block.1 = (bf16[4,16,1152]{2,1,0:T(8,128)(2,1)S(1)}, bf16[4,16,1152]{2,1,0:T(8,128)(2,1)S(1)}, bf16[4,16,1152]{2,1,0:T(8,128)(2,1)S(1)}, bf16[4,16,1152]{2,1,0:...) custom-call(s32[2]{0:T(128)S(1)} %pad_add_fusion.index_ref, ...), custom_call_target="tpu_custom_call" | custom-call | flops 7398752256 | bytes 16777216 | tf_op jit(solution)/shard_map/block/pallas_call | solution.py:278
  170.5 0.4 collective-permute-start.29
  170.9 1.7 collective-permute-start.30
  172.6 0.1 collective-permute-start.31
  172.7 2.5 %collective-permute-start.32 = (bf16[4,16,1152]{2,1,0:T(8,128)(2,1)S(1)}, bf16[4,16,1152]{2,1,0:T(8,128)(2,1)S(1)}, u32[]{:S(2)}, u32[]{:S(2)}) collective-permute-start(bf16[4,16,1152]{2,1,0:T(8,128)(2,1)S(1)} %get-tuple-element.33), channel_id=1, source_target_pairs={{0,4},{1,5},{2,6},{3,7},{4,0},{5,1},{6,2},{7,3},{8,12},{9,13},{10,... | collective-permute-start | bytes 442376 | tf_op jit(solution)/shard_map/ppermute | solution.py:214
  175.1 0.4 collective-permute-start.33
  175.5 1.1 collective-permute-start.34
  176.6 4.9 %collective-permute-start.35 = (bf16[4,16,1152]{2,1,0:T(8,128)(2,1)S(1)}, bf16[4,16,1152]{2,1,0:T(8,128)(2,1)S(1)}, u32[]{:S(2)}, u32[]{:S(2)}) collective-permute-start(bf16[4,16,1152]{2,1,0:T(8,128)(2,1)S(1)} %get-tuple-element.36), channel_id=1, source_target_pairs={{0,7},{1,6},{2,5},{3,4},{4,3},{5,2},{6,1},{7,0},{8,15},{9,14},{10,... | collective-permute-start | bytes 442376 | tf_op jit(solution)/shard_map/ppermute | solution.py:214
  181.5 1.5 collective-permute-done.31.refs_3_
  183.0 0.8 collective-permute-done.32.refs_4_
  183.8 10.4 %collective-permute-done.33.refs_5_ = bf16[4,16,1152]{2,1,0:T(8,128)(2,1)S(1)} collective-permute-done((bf16[4,16,1152]{2,1,0:T(8,128)(2,1)S(1)}, bf16[4,16,1152]{2,1,0:T(8,128)(2,1)S(1)}, u32[]{:S(2)}, u32[]{:S(2)}) %collective-permute-start.33) | collective-permute-done | bytes 147488 | tf_op jit(solution)/shard_map/ppermute | solution.py:214
  194.2 4.3 %collective-permute-done.34.refs_6_ = bf16[4,16,1152]{2,1,0:T(8,128)(2,1)S(1)} collective-permute-done((bf16[4,16,1152]{2,1,0:T(8,128)(2,1)S(1)}, bf16[4,16,1152]{2,1,0:T(8,128)(2,1)S(1)}, u32[]{:S(2)}, u32[]{:S(2)}) %collective-permute-start.34) | collective-permute-done | bytes 147488 | tf_op jit(solution)/shard_map/ppermute | solution.py:214
  198.5 3.3 %collective-permute-done.35.refs_7_ = bf16[4,16,1152]{2,1,0:T(8,128)(2,1)S(1)} collective-permute-done((bf16[4,16,1152]{2,1,0:T(8,128)(2,1)S(1)}, bf16[4,16,1152]{2,1,0:T(8,128)(2,1)S(1)}, u32[]{:S(2)}, u32[]{:S(2)}) %collective-permute-start.35) | collective-permute-done | bytes 147488 | tf_op jit(solution)/shard_map/ppermute | solution.py:214
  201.8 2.0 restore.1
  (58 shorter events, 0.6 us)
Async XLA Ops:
  0.9 1.3 copy-start
  2.2 4.0 %copy-start.3 = (bf16[1152,432]{0,1:T(8,128)(2,1)S(1)}, bf16[1152,432]{0,1:T(8,128)(2,1)}, u32[]{:S(2)}) copy-start(bf16[1152,432]{0,1:T(8,128)(2,1)} %param.6) | copy-start | bytes 2985988
  3.8 7.1 %collective-permute-start.1 = (bf16[4,16,1152]{2,1,0:T(8,128)(2,1)S(1)}, bf16[4,16,1152]{2,1,0:T(8,128)(2,1)S(1)}, u32[]{:S(2)}, u32[]{:S(2)}) collective-permute-start(bf16[4,16,1152]{2,1,0:T(8,128)(2,1)S(1)} %get-tuple-element.23), channel_id=1, source_target_pairs={{0,2},{1,3},{2,0},{3,1},{4,6},{5,7},{6,4},{7,5},{8,10},{9,11},{10,... | collective-permute-start | bytes 442376 | tf_op jit(solution)/shard_map/ppermute | solution.py:214
  3.9 9.7 %collective-permute-start.2 = (bf16[4,16,1152]{2,1,0:T(8,128)(2,1)S(1)}, bf16[4,16,1152]{2,1,0:T(8,128)(2,1)S(1)}, u32[]{:S(2)}, u32[]{:S(2)}) collective-permute-start(bf16[4,16,1152]{2,1,0:T(8,128)(2,1)S(1)} %get-tuple-element.24), channel_id=1, source_target_pairs={{0,3},{1,2},{2,1},{3,0},{4,7},{5,6},{6,5},{7,4},{8,11},{9,10},{10,... | collective-permute-start | bytes 442376 | tf_op jit(solution)/shard_map/ppermute | solution.py:214
  7.3 94.9 %copy-start.2 = (bf16[576,1152]{1,0:T(8,128)(2,1)}, bf16[576,1152]{1,0:T(8,128)(2,1)S(1)}, u32[]{:S(2)}) copy-start(bf16[576,1152]{1,0:T(8,128)(2,1)S(1)} %pad_maximum_fusion) | copy-start | bytes 3981316
  7.4 24.1 %collective-permute-start.21 = (bf16[144,1152]{1,0:T(8,128)(2,1)S(1)}, bf16[144,1152]{1,0:T(8,128)(2,1)S(1)}, u32[]{:S(2)}, u32[]{:S(2)}) collective-permute-start(bf16[144,1152]{1,0:T(8,128)(2,1)S(1)} %dynamic-slice_bitcast_fusion), channel_id=1, source_target_pairs={{0,6},{1,7},{2,4},{3,5},{4,2},{5,3},{6,0},{7,1},{8,14},{9,15},{10,... | collective-permute-start | bytes 995336 | tf_op jit(solution)/shard_map/ppermute | solution.py:214
  8.7 38.1 %collective-permute-start.20 = (bf16[144,1152]{1,0:T(8,128)(2,1)S(1)}, bf16[144,1152]{1,0:T(8,128)(2,1)S(1)}, u32[]{:S(2)}, u32[]{:S(2)}) collective-permute-start(bf16[144,1152]{1,0:T(8,128)(2,1)S(1)} %dynamic-slice_bitcast_fusion), channel_id=1, source_target_pairs={{0,4},{1,5},{2,6},{3,7},{4,0},{5,1},{6,2},{7,3},{8,12},{9,13},{10,... | collective-permute-start | bytes 995336 | tf_op jit(solution)/shard_map/ppermute | solution.py:214
  9.8 55.2 %collective-permute-start.12 = (bf16[144,1152]{1,0:T(8,128)(2,1)S(1)}, bf16[144,1152]{1,0:T(8,128)(2,1)S(1)}, u32[]{:S(2)}, u32[]{:S(2)}) collective-permute-start(bf16[144,1152]{1,0:T(8,128)(2,1)S(1)} %dynamic-slice_bitcast_fusion), channel_id=1, source_target_pairs={{0,2},{1,3},{2,0},{3,1},{4,6},{5,7},{6,4},{7,5},{8,10},{9,11},{10,... | collective-permute-start | bytes 995336 | tf_op jit(solution)/shard_map/ppermute | solution.py:214
  10.9 12.0 %collective-permute-start = (bf16[4,16,1152]{2,1,0:T(8,128)(2,1)S(1)}, bf16[4,16,1152]{2,1,0:T(8,128)(2,1)S(1)}, u32[]{:S(2)}, u32[]{:S(2)}) collective-permute-start(bf16[4,16,1152]{2,1,0:T(8,128)(2,1)S(1)} %get-tuple-element.22), channel_id=1, source_target_pairs={{0,1},{1,0},{2,3},{3,2},{4,5},{5,4},{6,7},{7,6},{8,9},{9,8},{10,11... | collective-permute-start | bytes 442376 | tf_op jit(solution)/shard_map/ppermute | solution.py:214
  13.7 36.3 %collective-permute-start.3 = (bf16[4,16,1152]{2,1,0:T(8,128)(2,1)S(1)}, bf16[4,16,1152]{2,1,0:T(8,128)(2,1)S(1)}, u32[]{:S(2)}, u32[]{:S(2)}) collective-permute-start(bf16[4,16,1152]{2,1,0:T(8,128)(2,1)S(1)} %get-tuple-element.25), channel_id=1, source_target_pairs={{0,4},{1,5},{2,6},{3,7},{4,0},{5,1},{6,2},{7,3},{8,12},{9,13},{10,... | collective-permute-start | bytes 442376 | tf_op jit(solution)/shard_map/ppermute | solution.py:214
  22.9 33.4 %collective-permute-start.4 = (bf16[4,16,1152]{2,1,0:T(8,128)(2,1)S(1)}, bf16[4,16,1152]{2,1,0:T(8,128)(2,1)S(1)}, u32[]{:S(2)}, u32[]{:S(2)}) collective-permute-start(bf16[4,16,1152]{2,1,0:T(8,128)(2,1)S(1)} %get-tuple-element.26), channel_id=1, source_target_pairs={{0,5},{1,4},{2,7},{3,6},{4,1},{5,0},{6,3},{7,2},{8,13},{9,12},{10,... | collective-permute-start | bytes 442376 | tf_op jit(solution)/shard_map/ppermute | solution.py:214
  31.4 29.2 %collective-permute-start.5 = (bf16[4,16,1152]{2,1,0:T(8,128)(2,1)S(1)}, bf16[4,16,1152]{2,1,0:T(8,128)(2,1)S(1)}, u32[]{:S(2)}, u32[]{:S(2)}) collective-permute-start(bf16[4,16,1152]{2,1,0:T(8,128)(2,1)S(1)} %get-tuple-element.27), channel_id=1, source_target_pairs={{0,6},{1,7},{2,4},{3,5},{4,2},{5,3},{6,0},{7,1},{8,14},{9,15},{10,... | collective-permute-start | bytes 442376 | tf_op jit(solution)/shard_map/ppermute | solution.py:214
  46.8 17.0 %collective-permute-start.6 = (bf16[4,16,1152]{2,1,0:T(8,128)(2,1)S(1)}, bf16[4,16,1152]{2,1,0:T(8,128)(2,1)S(1)}, u32[]{:S(2)}, u32[]{:S(2)}) collective-permute-start(bf16[4,16,1152]{2,1,0:T(8,128)(2,1)S(1)} %get-tuple-element.28), channel_id=1, source_target_pairs={{0,7},{1,6},{2,5},{3,4},{4,3},{5,2},{6,1},{7,0},{8,15},{9,14},{10,... | collective-permute-start | bytes 442376 | tf_op jit(solution)/shard_map/ppermute | solution.py:214
  47.7 89.2 %copy-start.4 = (bf16[2,144,1152]{2,1,0:T(8,128)(2,1)}, bf16[2,144,1152]{2,1,0:T(8,128)(2,1)S(1)}, u32[]{:S(2)}) copy-start(bf16[2,144,1152]{2,1,0:T(8,128)(2,1)S(1)} %pad_maximum_fusion.1.refs_22_) | copy-start | bytes 1990660
  50.0 16.3 %collective-permute-start.7 = (bf16[2,4,16,1152]{3,2,1,0:T(8,128)(2,1)S(1)}, bf16[2,4,16,1152]{3,2,1,0:T(8,128)(2,1)S(1)}, u32[]{:S(2)}, u32[]{:S(2)}) collective-permute-start(bf16[2,4,16,1152]{3,2,1,0:T(8,128)(2,1)S(1)} %pad_maximum_fusion.2), channel_id=1, source_target_pairs={{0,24},{1,25},{2,26},{3,27},{4,12},{5,13},{6,14},{7,15},{8,0},{9,1... | collective-permute-start | bytes 884744 | tf_op jit(solution)/shard_map/ppermute | solution.py:272
  56.3 10.2 %collective-permute-start.8 = (bf16[2,4,16,1152]{3,2,1,0:T(8,128)(2,1)S(1)}, bf16[2,4,16,1152]{3,2,1,0:T(8,128)(2,1)S(1)}, u32[]{:S(2)}, u32[]{:S(2)}) collective-permute-start(bf16[2,4,16,1152]{3,2,1,0:T(8,128)(2,1)S(1)} %pad_maximum_fusion.3), channel_id=1, source_target_pairs={{0,24},{1,25},{2,26},{3,27},{4,12},{5,13},{6,14},{7,15},{8,0},{9,1... | collective-permute-start | bytes 884744 | tf_op jit(solution)/shard_map/ppermute | solution.py:272
  60.7 41.9 %collective-permute-start.23 = (bf16[2,144,1152]{2,1,0:T(8,128)(2,1)S(1)}, bf16[2,144,1152]{2,1,0:T(8,128)(2,1)S(1)}, u32[]{:S(2)}, u32[]{:S(2)}) collective-permute-start(bf16[2,144,1152]{2,1,0:T(8,128)(2,1)S(1)} %pad_maximum_fusion.1.refs_22_), channel_id=1, source_target_pairs={{0,8},{1,9},{2,10},{3,11},{4,12},{5,13},{6,14},{7,15},{8,0},{9,1},... | collective-permute-start | bytes 1990664 | tf_op jit(solution)/shard_map/ppermute | solution.py:214
  63.8 21.4 %collective-permute-start.9 = (bf16[2,4,16,1152]{3,2,1,0:T(8,128)(2,1)S(1)}, bf16[2,4,16,1152]{3,2,1,0:T(8,128)(2,1)S(1)}, u32[]{:S(2)}, u32[]{:S(2)}) collective-permute-start(bf16[2,4,16,1152]{3,2,1,0:T(8,128)(2,1)S(1)} %pad_maximum_fusion.4), channel_id=1, source_target_pairs={{0,8},{1,9},{2,10},{3,11},{4,28},{5,29},{6,30},{7,31},{8,16},{9,17... | collective-permute-start | bytes 884744 | tf_op jit(solution)/shard_map/ppermute | solution.py:272
  65.1 21.4 %collective-permute-start.16 = (bf16[1,144,1152]{2,1,0:T(8,128)(2,1)S(1)}, bf16[1,144,1152]{2,1,0:T(8,128)(2,1)S(1)}, u32[]{:S(2)}, u32[]{:S(2)}) collective-permute-start(bf16[1,144,1152]{2,1,0:T(8,128)(2,1)S(1)} %bitcast.26), channel_id=1, source_target_pairs={{0,16},{1,17},{2,18},{3,19},{4,20},{5,21},{6,22},{7,23},{8,24},{9,... | collective-permute-start | bytes 995336 | tf_op jit(solution)/shard_map/ppermute | solution.py:214
  66.3 35.9 %collective-permute-start.14 = (bf16[1,144,1152]{2,1,0:T(8,128)(2,1)S(1)}, bf16[1,144,1152]{2,1,0:T(8,128)(2,1)S(1)}, u32[]{:S(2)}, u32[]{:S(2)}) collective-permute-start(bf16[1,144,1152]{2,1,0:T(8,128)(2,1)S(1)} %bitcast.27), channel_id=1, source_target_pairs={{0,8},{1,9},{2,10},{3,11},{4,12},{5,13},{6,14},{7,15},{8,0},{9,1},... | collective-permute-start | bytes 995336 | tf_op jit(solution)/shard_map/ppermute | solution.py:214
  66.5 35.8 %collective-permute-start.13 = (bf16[1,144,1152]{2,1,0:T(8,128)(2,1)S(1)}, bf16[1,144,1152]{2,1,0:T(8,128)(2,1)S(1)}, u32[]{:S(2)}, u32[]{:S(2)}) collective-permute-start(bf16[1,144,1152]{2,1,0:T(8,128)(2,1)S(1)} %bitcast.28), channel_id=1, source_target_pairs={{0,1},{1,0},{2,3},{3,2},{4,5},{5,4},{6,7},{7,6},{8,9},{9,8},{10,11... | collective-permute-start | bytes 995336 | tf_op jit(solution)/shard_map/ppermute | solution.py:214
  67.8 134.1 %copy-start.1 = (bf16[4,128,1152]{2,1,0:T(8,128)(2,1)S(1)}, bf16[4,128,1152]{2,1,0:T(8,128)(2,1)}, u32[]{:S(2)}) copy-start(bf16[4,128,1152]{2,1,0:T(8,128)(2,1)} %tokens_ref.3) | copy-start | bytes 3538948
  85.3 13.4 %collective-permute-start.10 = (bf16[2,4,16,1152]{3,2,1,0:T(8,128)(2,1)S(1)}, bf16[2,4,16,1152]{3,2,1,0:T(8,128)(2,1)S(1)}, u32[]{:S(2)}, u32[]{:S(2)}) collective-permute-start(bf16[2,4,16,1152]{3,2,1,0:T(8,128)(2,1)S(1)} %pad_maximum_fusion.5), channel_id=1, source_target_pairs={{0,8},{1,9},{2,10},{3,11},{4,28},{5,29},{6,30},{7,31},{8,16},{9,17... | collective-permute-start | bytes 884744 | tf_op jit(solution)/shard_map/ppermute | solution.py:272
  86.5 50.4 %copy-start.13 = (bf16[1,144,1152]{2,1,0:T(8,128)(2,1)}, bf16[1,144,1152]{2,1,0:T(8,128)(2,1)S(1)}, u32[]{:S(2)}) copy-start(bf16[1,144,1152]{2,1,0:T(8,128)(2,1)S(1)} %collective-permute-done.16.refs_18_) | copy-start | bytes 995332
  86.5 18.4 %collective-permute-start.18 = (bf16[1,144,1152]{2,1,0:T(8,128)(2,1)S(1)}, bf16[1,144,1152]{2,1,0:T(8,128)(2,1)S(1)}, u32[]{:S(2)}, u32[]{:S(2)}) collective-permute-start(bf16[1,144,1152]{2,1,0:T(8,128)(2,1)S(1)} %collective-permute-done.16.refs_18_), channel_id=1, source_target_pairs={{0,8},{1,9},{2,10},{3,11},{4,12},{5,13},{6,14},{7,15},{8,0},{9,1},... | collective-permute-start | bytes 995336 | tf_op jit(solution)/shard_map/ppermute | solution.py:214
  98.7 8.1 %collective-permute-start.17 = (bf16[1,144,1152]{2,1,0:T(8,128)(2,1)S(1)}, bf16[1,144,1152]{2,1,0:T(8,128)(2,1)S(1)}, u32[]{:S(2)}, u32[]{:S(2)}) collective-permute-start(bf16[1,144,1152]{2,1,0:T(8,128)(2,1)S(1)} %collective-permute-done.16.refs_18_), channel_id=1, source_target_pairs={{0,1},{1,0},{2,3},{3,2},{4,5},{5,4},{6,7},{7,6},{8,9},{9,8},{10,11... | collective-permute-start | bytes 995336 | tf_op jit(solution)/shard_map/ppermute | solution.py:214
  102.2 34.7 %copy-start.14 = (bf16[1,144,1152]{2,1,0:T(8,128)(2,1)}, bf16[1,144,1152]{2,1,0:T(8,128)(2,1)S(1)}, u32[]{:S(2)}) copy-start(bf16[1,144,1152]{2,1,0:T(8,128)(2,1)S(1)} %collective-permute-done.14.refs_16_) | copy-start | bytes 995332
  102.2 33.9 %collective-permute-start.11 = (bf16[4,144,1152]{2,1,0:T(8,128)(2,1)S(1)}, bf16[4,144,1152]{2,1,0:T(8,128)(2,1)S(1)}, u32[]{:S(2)}, u32[]{:S(2)}) collective-permute-start(bf16[4,144,1152]{2,1,0:T(8,128)(2,1)S(1)} %bitcast.31), channel_id=1, source_target_pairs={{0,1},{1,0},{2,3},{3,2},{4,5},{5,4},{6,7},{7,6},{8,9},{9,8},{10,11... | collective-permute-start | bytes 3981320 | tf_op jit(solution)/shard_map/ppermute | solution.py:214
  102.3 34.6 %copy-start.15 = (bf16[1,144,1152]{2,1,0:T(8,128)(2,1)}, bf16[1,144,1152]{2,1,0:T(8,128)(2,1)S(1)}, u32[]{:S(2)}) copy-start(bf16[1,144,1152]{2,1,0:T(8,128)(2,1)S(1)} %collective-permute-done.13.refs_15_) | copy-start | bytes 995332
  102.3 16.1 %collective-permute-start.25 = (bf16[2,144,1152]{2,1,0:T(8,128)(2,1)S(1)}, bf16[2,144,1152]{2,1,0:T(8,128)(2,1)S(1)}, u32[]{:S(2)}, u32[]{:S(2)}) collective-permute-start(bf16[2,144,1152]{2,1,0:T(8,128)(2,1)S(1)} %pad_maximum_fusion.1.refs_22_), channel_id=1, source_target_pairs={{0,16},{1,17},{2,18},{3,19},{4,20},{5,21},{6,22},{7,23},{8,24},{9,... | collective-permute-start | bytes 1990664 | tf_op jit(solution)/shard_map/ppermute | solution.py:214
  102.6 34.3 %copy-start.6 = (bf16[2,144,1152]{2,1,0:T(8,128)(2,1)}, bf16[2,144,1152]{2,1,0:T(8,128)(2,1)S(1)}, u32[]{:S(2)}) copy-start(bf16[2,144,1152]{2,1,0:T(8,128)(2,1)S(1)} %collective-permute-done.23.refs_24_) | copy-start | bytes 1990660
  102.6 30.1 %collective-permute-start.27 = (bf16[2,144,1152]{2,1,0:T(8,128)(2,1)S(1)}, bf16[2,144,1152]{2,1,0:T(8,128)(2,1)S(1)}, u32[]{:S(2)}, u32[]{:S(2)}) collective-permute-start(bf16[2,144,1152]{2,1,0:T(8,128)(2,1)S(1)} %collective-permute-done.23.refs_24_), channel_id=1, source_target_pairs={{0,16},{1,17},{2,18},{3,19},{4,20},{5,21},{6,22},{7,23},{8,24},{9,... | collective-permute-start | bytes 1990664 | tf_op jit(solution)/shard_map/ppermute | solution.py:214
  104.8 31.3 %copy-start.16 = (bf16[1,144,1152]{2,1,0:T(8,128)(2,1)}, bf16[1,144,1152]{2,1,0:T(8,128)(2,1)S(1)}, u32[]{:S(2)}) copy-start(bf16[1,144,1152]{2,1,0:T(8,128)(2,1)S(1)} %collective-permute-done.18.refs_20_) | copy-start | bytes 995332
  104.8 29.1 %collective-permute-start.22 = (bf16[2,144,1152]{2,1,0:T(8,128)(2,1)S(1)}, bf16[2,144,1152]{2,1,0:T(8,128)(2,1)S(1)}, u32[]{:S(2)}, u32[]{:S(2)}) collective-permute-start(bf16[2,144,1152]{2,1,0:T(8,128)(2,1)S(1)} %pad_maximum_fusion.1.refs_22_), channel_id=1, source_target_pairs={{0,1},{1,0},{2,3},{3,2},{4,5},{5,4},{6,7},{7,6},{8,9},{9,8},{10,11... | collective-permute-start | bytes 1990664 | tf_op jit(solution)/shard_map/ppermute | solution.py:214
  106.8 29.4 %copy-start.17 = (bf16[1,144,1152]{2,1,0:T(8,128)(2,1)}, bf16[1,144,1152]{2,1,0:T(8,128)(2,1)S(1)}, u32[]{:S(2)}) copy-start(bf16[1,144,1152]{2,1,0:T(8,128)(2,1)S(1)} %collective-permute-done.17.refs_19_) | copy-start | bytes 995332
  106.8 2.3 %collective-permute-start.15 = (bf16[1,144,1152]{2,1,0:T(8,128)(2,1)S(1)}, bf16[1,144,1152]{2,1,0:T(8,128)(2,1)}, u32[]{:S(2)}, u32[]{:S(2)}) collective-permute-start(bf16[1,144,1152]{2,1,0:T(8,128)(2,1)S(1)} %collective-permute-done.14.refs_16_), channel_id=1, source_target_pairs={{0,1},{1,0},{2,3},{3,2},{4,5},{5,4},{6,7},{7,6},{8,9},{9,8},{10,11... | collective-permute-start | bytes 995336 | tf_op jit(solution)/shard_map/ppermute | solution.py:214
  109.1 27.0 %collective-permute-start.24 = (bf16[2,144,1152]{2,1,0:T(8,128)(2,1)S(1)}, bf16[2,144,1152]{2,1,0:T(8,128)(2,1)S(1)}, u32[]{:S(2)}, u32[]{:S(2)}) collective-permute-start(bf16[2,144,1152]{2,1,0:T(8,128)(2,1)S(1)} %collective-permute-done.23.refs_24_), channel_id=1, source_target_pairs={{0,1},{1,0},{2,3},{3,2},{4,5},{5,4},{6,7},{7,6},{8,9},{9,8},{10,11... | collective-permute-start | bytes 1990664 | tf_op jit(solution)/shard_map/ppermute | solution.py:214
  118.4 18.5 %copy-start.7 = (bf16[2,144,1152]{2,1,0:T(8,128)(2,1)}, bf16[2,144,1152]{2,1,0:T(8,128)(2,1)S(1)}, u32[]{:S(2)}) copy-start(bf16[2,144,1152]{2,1,0:T(8,128)(2,1)S(1)} %collective-permute-done.25.refs_26_) | copy-start | bytes 1990660
  118.5 17.7 %collective-permute-start.26 = (bf16[2,144,1152]{2,1,0:T(8,128)(2,1)S(1)}, bf16[2,144,1152]{2,1,0:T(8,128)(2,1)S(1)}, u32[]{:S(2)}, u32[]{:S(2)}) collective-permute-start(bf16[2,144,1152]{2,1,0:T(8,128)(2,1)S(1)} %collective-permute-done.25.refs_26_), channel_id=1, source_target_pairs={{0,1},{1,0},{2,3},{3,2},{4,5},{5,4},{6,7},{7,6},{8,9},{9,8},{10,11... | collective-permute-start | bytes 1990664 | tf_op jit(solution)/shard_map/ppermute | solution.py:214
  132.7 4.3 %copy-start.8 = (bf16[2,144,1152]{2,1,0:T(8,128)(2,1)}, bf16[2,144,1152]{2,1,0:T(8,128)(2,1)S(1)}, u32[]{:S(2)}) copy-start(bf16[2,144,1152]{2,1,0:T(8,128)(2,1)S(1)} %collective-permute-done.27.refs_28_) | copy-start | bytes 1990660
  132.7 4.2 %collective-permute-start.28 = (bf16[2,144,1152]{2,1,0:T(8,128)(2,1)S(1)}, bf16[2,144,1152]{2,1,0:T(8,128)(2,1)S(1)}, u32[]{:S(2)}, u32[]{:S(2)}) collective-permute-start(bf16[2,144,1152]{2,1,0:T(8,128)(2,1)S(1)} %collective-permute-done.27.refs_28_), channel_id=1, source_target_pairs={{0,1},{1,0},{2,3},{3,2},{4,5},{5,4},{6,7},{7,6},{8,9},{9,8},{10,11... | collective-permute-start | bytes 1990664 | tf_op jit(solution)/shard_map/ppermute | solution.py:214
  133.9 3.0 %copy-start.9 = (bf16[2,144,1152]{2,1,0:T(8,128)(2,1)}, bf16[2,144,1152]{2,1,0:T(8,128)(2,1)S(1)}, u32[]{:S(2)}) copy-start(bf16[2,144,1152]{2,1,0:T(8,128)(2,1)S(1)} %collective-permute-done.22.refs_23_) | copy-start | bytes 1990660
  133.9 2.2 %collective-permute-start.19 = (bf16[1,144,1152]{2,1,0:T(8,128)(2,1)S(1)}, bf16[1,144,1152]{2,1,0:T(8,128)(2,1)S(1)}, u32[]{:S(2)}, u32[]{:S(2)}) collective-permute-start(bf16[1,144,1152]{2,1,0:T(8,128)(2,1)S(1)} %collective-permute-done.18.refs_20_), channel_id=1, source_target_pairs={{0,1},{1,0},{2,3},{3,2},{4,5},{5,4},{6,7},{7,6},{8,9},{9,8},{10,11... | collective-permute-start | bytes 995336 | tf_op jit(solution)/shard_map/ppermute | solution.py:214
  136.1 0.7 copy-start.18
  136.1 1.2 copy-start.5
  136.1 1.4 copy-start.11
  136.9 0.9 copy-start.10
  137.8 0.8 copy-start.12
  170.5 5.1 %collective-permute-start.29 = (bf16[4,16,1152]{2,1,0:T(8,128)(2,1)S(1)}, bf16[4,16,1152]{2,1,0:T(8,128)(2,1)S(1)}, u32[]{:S(2)}, u32[]{:S(2)}) collective-permute-start(bf16[4,16,1152]{2,1,0:T(8,128)(2,1)S(1)} %get-tuple-element.30), channel_id=1, source_target_pairs={{0,1},{1,0},{2,3},{3,2},{4,5},{5,4},{6,7},{7,6},{8,9},{9,8},{10,11... | collective-permute-start | bytes 442376 | tf_op jit(solution)/shard_map/ppermute | solution.py:214
  170.9 5.7 %collective-permute-start.30 = (bf16[4,16,1152]{2,1,0:T(8,128)(2,1)S(1)}, bf16[4,16,1152]{2,1,0:T(8,128)(2,1)S(1)}, u32[]{:S(2)}, u32[]{:S(2)}) collective-permute-start(bf16[4,16,1152]{2,1,0:T(8,128)(2,1)S(1)} %get-tuple-element.31), channel_id=1, source_target_pairs={{0,2},{1,3},{2,0},{3,1},{4,6},{5,7},{6,4},{7,5},{8,10},{9,11},{10,... | collective-permute-start | bytes 442376 | tf_op jit(solution)/shard_map/ppermute | solution.py:214
  172.6 10.4 %collective-permute-start.31 = (bf16[4,16,1152]{2,1,0:T(8,128)(2,1)S(1)}, bf16[4,16,1152]{2,1,0:T(8,128)(2,1)S(1)}, u32[]{:S(2)}, u32[]{:S(2)}) collective-permute-start(bf16[4,16,1152]{2,1,0:T(8,128)(2,1)S(1)} %get-tuple-element.32), channel_id=1, source_target_pairs={{0,3},{1,2},{2,1},{3,0},{4,7},{5,6},{6,5},{7,4},{8,11},{9,10},{10,... | collective-permute-start | bytes 442376 | tf_op jit(solution)/shard_map/ppermute | solution.py:214
  172.7 11.1 %collective-permute-start.32 = (bf16[4,16,1152]{2,1,0:T(8,128)(2,1)S(1)}, bf16[4,16,1152]{2,1,0:T(8,128)(2,1)S(1)}, u32[]{:S(2)}, u32[]{:S(2)}) collective-permute-start(bf16[4,16,1152]{2,1,0:T(8,128)(2,1)S(1)} %get-tuple-element.33), channel_id=1, source_target_pairs={{0,4},{1,5},{2,6},{3,7},{4,0},{5,1},{6,2},{7,3},{8,12},{9,13},{10,... | collective-permute-start | bytes 442376 | tf_op jit(solution)/shard_map/ppermute | solution.py:214
  175.1 19.1 %collective-permute-start.33 = (bf16[4,16,1152]{2,1,0:T(8,128)(2,1)S(1)}, bf16[4,16,1152]{2,1,0:T(8,128)(2,1)S(1)}, u32[]{:S(2)}, u32[]{:S(2)}) collective-permute-start(bf16[4,16,1152]{2,1,0:T(8,128)(2,1)S(1)} %get-tuple-element.34), channel_id=1, source_target_pairs={{0,5},{1,4},{2,7},{3,6},{4,1},{5,0},{6,3},{7,2},{8,13},{9,12},{10,... | collective-permute-start | bytes 442376 | tf_op jit(solution)/shard_map/ppermute | solution.py:214
  175.5 22.9 %collective-permute-start.34 = (bf16[4,16,1152]{2,1,0:T(8,128)(2,1)S(1)}, bf16[4,16,1152]{2,1,0:T(8,128)(2,1)S(1)}, u32[]{:S(2)}, u32[]{:S(2)}) collective-permute-start(bf16[4,16,1152]{2,1,0:T(8,128)(2,1)S(1)} %get-tuple-element.35), channel_id=1, source_target_pairs={{0,6},{1,7},{2,4},{3,5},{4,2},{5,3},{6,0},{7,1},{8,14},{9,15},{10,... | collective-permute-start | bytes 442376 | tf_op jit(solution)/shard_map/ppermute | solution.py:214
  176.6 25.2 %collective-permute-start.35 = (bf16[4,16,1152]{2,1,0:T(8,128)(2,1)S(1)}, bf16[4,16,1152]{2,1,0:T(8,128)(2,1)S(1)}, u32[]{:S(2)}, u32[]{:S(2)}) collective-permute-start(bf16[4,16,1152]{2,1,0:T(8,128)(2,1)S(1)} %get-tuple-element.36), channel_id=1, source_target_pairs={{0,7},{1,6},{2,5},{3,4},{4,3},{5,2},{6,1},{7,0},{8,15},{9,14},{10,... | collective-permute-start | bytes 442376 | tf_op jit(solution)/shard_map/ppermute | solution.py:214

commit v2 on v1

v2 whole, which is shorter than its diff:
```python
import functools

import jax
import jax.numpy as jnp
from jax import lax
from jax.experimental import pallas as pl
from jax.experimental.pallas import tpu as pltpu
from jax.sharding import PartitionSpec as P

H = 16
FRS = 32
EPSILON = 1e-06
LANES = 128
ROWS = 16
VMEM_BYTES = 50 * 1024 * 1024


def padded(width):
    return -(-width // LANES) * LANES


def norm_kernel(index_ref, tokens_ref, modulation_ref, keep_ref, give_ref, mixed):
    frames = tokens_ref.shape[0]
    chips, groups, rows, width = keep_ref.shape
    positions = groups * rows // frames
    index = index_ref[0]
    for d in range(2 * chips):
        out_ref = (keep_ref, give_ref)[d % 2]
        start = pl.multiple_of(lax.bitwise_xor(index, d) * positions, positions)
        for f in range(frames):
            values = tokens_ref[f, pl.ds(start, positions), :].astype(jnp.float32)
            average = jnp.mean(values, axis=-1, keepdims=True)
            centered = values - average
            variance = jnp.mean(centered * centered, axis=-1, keepdims=True)
            normed = centered * lax.rsqrt(variance + EPSILON)
            result = normed * (1.0 + modulation_ref[f, 1:2, :]) + modulation_ref[f, 0:1, :]
            for t in range(width // LANES):
                mixed[t, pl.ds(f, positions, stride=frames), :] = result[:, t * LANES : (t + 1) * LANES]
        for t in range(width // LANES):
            part = mixed[t].astype(out_ref.dtype).reshape(groups, rows, LANES)
            out_ref[d // 2, :, :, t * LANES : (t + 1) * LANES] = part


def restore_kernel(index_ref, tokens_ref, modulation_ref, *refs):
    in_refs, out_ref, mixed = refs[:-2], refs[-2], refs[-1]
    frames = tokens_ref.shape[0]
    groups, rows, width = in_refs[0].shape
    positions = groups * rows // frames
    index = index_ref[0]
    for d, in_ref in enumerate(in_refs):
        start = pl.multiple_of(lax.bitwise_xor(index, d) * positions, positions)
        for t in range(width // LANES):
            part = in_ref[:, :, t * LANES : (t + 1) * LANES]
            mixed[t] = part.reshape(groups * rows, LANES).astype(jnp.float32)
        for f in range(frames):
            values = tokens_ref[f, pl.ds(start, positions), :].astype(jnp.float32)
            projected = jnp.concatenate(
                [mixed[t, pl.ds(f, positions, stride=frames), :] for t in range(width // LANES)], axis=1
            )
            result = values + modulation_ref[f, 2:3, :] * projected
            out_ref[f, pl.ds(start, positions), :] = result.astype(out_ref.dtype)


def nt_dot(left, right):
    return lax.dot_general(left, right, (((1,), (1,)), ((), ())), preferred_element_type=jnp.float32)


def head_window(head, head_size, shift):
    first = shift + head * head_size
    last = first + head_size
    low = first // LANES * LANES
    return first, last, low, padded(last)


def masked(values, first, last, low):
    lane = lax.broadcasted_iota(jnp.int32, values.shape, 1) + low
    return jnp.where((lane >= first) & (lane < last), values, jnp.zeros_like(values))


def softmax(scores, same, scale):
    scores = jnp.where(same, scores, -jnp.inf)
    top = jnp.max(scores, axis=0, keepdims=True)
    exponent = jnp.exp((scores - top) * scale)
    total = jnp.sum(exponent, axis=0, keepdims=True)
    return exponent * (1.0 / total)


def block_kernel(plan, frames, index_ref, *refs):
    count, extra, weights = plan["count"], plan["extra"], plan["weights"]
    refs = list(refs)
    x_refs = [refs.pop(0) for _ in range(extra)]
    e_refs = [refs.pop(0) for _ in range(extra)]
    w_refs = [refs.pop(0) for _ in range(weights)]
    out_refs = [refs.pop(0) for _ in range(count)]
    xs, xe, wall, qt, kn, vt, ken, vet, att, ys, sems, wsems = refs
    groups, _, rows, width = xs.shape
    half, lanes = plan["half"], plan["lanes"]
    heads_half = H // 2
    head_size = width // H
    scale = head_size ** (-0.5)
    slot = count * rows
    index, slab = index_ref[0], index_ref[1]

    copies = []
    for d in range(count):
        owner = lax.bitwise_xor(index, d)
        copies.append((x_refs[d // 2].at[d % 2], xs.at[:, owner]))
        copies.append((e_refs[d // 2].at[d % 2], xe.at[:, owner]))
    copies = [pltpu.make_async_copy(a, b, sems.at[n]) for n, (a, b) in enumerate(copies)]
    moves = []
    for operand, at, size, owner, part in plan["moves"]:
        if owner is None:
            row = part * size
        else:
            device = lax.bitwise_xor(index, owner)
            piece = lax.bitwise_xor(slab, part[1]) if part[0] == "xor" else jnp.int32(part[1])
            start = piece * size
            row = jnp.where(start < plan["columns"], device * plan["columns"] + start,
                            6 * half + device * plan["outs"] + start - plan["columns"])
        source = w_refs[operand]
        for step in at:
            source = source.at[step]
        moves.append((source, wall.at[pl.ds(pl.multiple_of(row, ROWS), size)]))
    moves = [pltpu.make_async_copy(a, b, wsems.at[n]) for n, (a, b) in enumerate(moves)]
    for copy in moves + copies:
        copy.start()
    gap = lanes - half
    if gap:
        for kind in range(2):
            qt[kind, half:, :] = jnp.zeros((gap, qt.shape[2]), qt.dtype)
            kn[kind, :, half:] = jnp.zeros((kn.shape[1], gap), kn.dtype)
        ken[:, half:] = jnp.zeros((ken.shape[0], gap), ken.dtype)
    for copy in moves + copies:
        copy.wait()

    tokens = groups * slot
    own = xs[...].reshape(tokens, width)
    for kind in range(2):
        parts = [wall[(3 * kind + n) * half : (3 * kind + n + 1) * half, :] for n in range(3)]
        qt[kind, :half, :] = nt_dot(parts[0], own).astype(qt.dtype)
        kn[kind, :, :half] = nt_dot(own, parts[1]).astype(kn.dtype)
        vt[kind] = nt_dot(parts[2], own).astype(vt.dtype)
        if kind == 1:
            others = xe[...].reshape(tokens, width)
            ken[:, :half] = nt_dot(others, parts[1]).astype(ken.dtype)
            vet[...] = nt_dot(parts[2], others).astype(vet.dtype)

    def one_group(g, carry):
        here = pl.ds(pl.multiple_of(g * slot, slot), slot)
        row = lax.broadcasted_iota(jnp.int32, (slot, slot), 0)
        column = lax.broadcasted_iota(jnp.int32, (slot, slot), 1)
        same = (row % rows) // frames == (column % rows) // frames
        near = (row < slot // 2) == (column < slot // 2)
        windows = [head_window(head, head_size, 0) for head in range(heads_half)]
        results = []
        scores = []
        for first, last, low, high in windows:
            keys = masked(kn[0, here, low:high], first, last, low)
            scores.append(jnp.dot(keys, qt[0, low:high, here], preferred_element_type=jnp.float32))
        probs = [softmax(score, same, scale).astype(jnp.bfloat16) for score in scores]
        for head, prob in enumerate(probs):
            values = vt[0, head * head_size : (head + 1) * head_size, here]
            results.append(jnp.dot(values, prob, preferred_element_type=jnp.float32))
        scores = []
        for first, last, low, high in windows:
            queries = qt[1, low:high, here]
            own_keys = masked(kn[1, here, low:high], first, last, low)
            other_keys = masked(ken[here, low:high], first, last, low)
            scores.append(jnp.where(
                near,
                jnp.dot(own_keys, queries, preferred_element_type=jnp.float32),
                jnp.dot(other_keys, queries, preferred_element_type=jnp.float32),
            ))
        probs = [softmax(score, same, scale) for score in scores]
        for head, prob in enumerate(probs):
            at = slice(head * head_size, (head + 1) * head_size)
            own_probs = jnp.where(near, prob, 0.0).astype(jnp.bfloat16)
            other_probs = jnp.where(near, 0.0, prob).astype(jnp.bfloat16)
            results.append(
                jnp.dot(vt[1, at, here], own_probs, preferred_element_type=jnp.float32)
                + jnp.dot(vet[at, here], other_probs, preferred_element_type=jnp.float32)
            )
        att[here, :] = jnp.concatenate(results, axis=0).T.astype(att.dtype)
        return carry

    lax.fori_loop(0, groups, one_group, 0)
    y = nt_dot(att[...], wall[6 * half :, :]).astype(ys.dtype)
    ys[...] = y.reshape(ys.shape)
    for d in range(count):
        out_refs[d][...] = ys[:, lax.bitwise_xor(index, d)]


def per_device(video_tokens, modulation, qkv_weight, out_weight):
    frames, positions, width = video_tokens.shape
    count, slabs = lax.axis_size("seq"), lax.axis_size("slab")
    index, slab = lax.axis_index("seq"), lax.axis_index("slab")
    block_positions = positions // count
    block_rows = block_positions * frames
    groups = block_rows // ROWS
    block = jax.ShapeDtypeStruct((groups, ROWS, width), jnp.bfloat16)
    own_index = jnp.stack([index, slab]).astype(jnp.int32)
    smem = pl.BlockSpec(memory_space=pltpu.SMEM)
    vmem = pl.BlockSpec(memory_space=pltpu.VMEM)
    anywhere = pl.BlockSpec(memory_space=pl.ANY)
    params = pltpu.CompilerParams(vmem_limit_bytes=VMEM_BYTES)

    def hop(value, seq_xor, slab_xor=0):
        pairs = [(s * count + i, (s ^ slab_xor) * count + (i ^ seq_xor)) for s in range(slabs) for i in range(count)]
        return lax.ppermute(value, ("slab", "seq"), pairs)

    half = width // 2
    lanes = padded(half)
    columns, outs = qkv_weight.shape[1], out_weight.shape[1]
    chips = count // 2
    unit = (columns + outs) // slabs
    moves = []
    if unit % ROWS == 0 and columns % unit == 0 and outs == unit and half % unit == 0:
        wide, narrow = qkv_weight.T, out_weight.T
        pieces = columns // unit
        first = lax.dynamic_slice_in_dim(wide, jnp.minimum(slab, pieces - 1) * unit, unit, 0)
        mine = jnp.where(slab < pieces, first, narrow)
        received = {0: mine}
        for bit in reversed(range(chips.bit_length() - 1)):
            for z in list(received):
                received[z ^ (1 << bit)] = hop(received[z], 2 << bit)
        operands = []

        def both_cores(value, entries):
            for sibling in range(2):
                operands.append(hop(value, 1) if sibling else value)
                for at, size, z, part in entries:
                    moves.append((len(operands) - 1, at, size, (2 * z) ^ sibling, part))

        both_cores(wide, [((pl.ds(n * unit, unit),), unit, 0, ("at", n)) for n in range(pieces)])
        both_cores(narrow, [((), unit, 0, ("at", pieces))])
        near = list(range(1, chips - 1)) or [1]
        bundles = [(near, False)] + ([([chips - 1], True)] if chips - 1 not in near else [])
        for zs, reverse in bundles:
            base = jnp.stack([received[z] for z in zs])
            held = {0: base}
            bits = [1 << b for b in range(slabs.bit_length() - 1)]
            for bit in reversed(bits) if reverse else bits:
                for e in list(held):
                    held[e ^ bit] = hop(held[e], 0, bit)
            for e in sorted(held):
                both_cores(held[e], [((n,), unit, z, ("xor", e)) for n, z in enumerate(zs)])
    else:
        full_qkv = lax.all_gather(qkv_weight.T, "seq", axis=0, tiled=True)
        full_out = lax.all_gather(out_weight.T, "seq", axis=0, tiled=True)
        operands = [full_qkv.reshape(6, half, width), full_out.reshape(2, half, width)]
        operands = [jnp.concatenate(operands, axis=0)]
        moves = [(0, (n,), half, None, n) for n in range(8)]

    keep, give = pl.pallas_call(
        norm_kernel,
        out_shape=[jax.ShapeDtypeStruct((chips,) + block.shape, block.dtype)] * 2,
        in_specs=[smem, vmem, vmem],
        out_specs=[vmem] * 2,
        scratch_shapes=[pltpu.VMEM((width // LANES, block_rows, LANES), jnp.float32)],
        compiler_params=params,
        name="norm",
    )(own_index, video_tokens, modulation)
    swapped = hop(give, 1)
    middle = count // 2
    blocks, extras = [], []
    for z in range(chips):
        pair = jnp.stack([keep[z], swapped[z]])
        blocks.append(hop(pair, 2 * z) if z else pair)
        pairs = []
        for s in range(slabs):
            for i in range(count):
                step = 1 if (i ^ (2 * z)) >= middle else -1
                pairs.append((s * count + i, (s + step) % slabs * count + i))
        extras.append(lax.ppermute(blocks[z], ("slab", "seq"), pairs))

    plan = dict(count=count, extra=len(extras), weights=len(operands), half=half, lanes=lanes, moves=moves,
                columns=columns, outs=outs)
    tokens = count * block_rows
    flops = 2 * tokens * width * (6 * lanes + 2 * lanes + width)
    projected = pl.pallas_call(
        functools.partial(block_kernel, plan, frames),
        out_shape=[block] * count,
        in_specs=[smem] + [anywhere] * (2 * len(extras) + len(operands)),
        out_specs=[vmem] * count,
        scratch_shapes=[
            pltpu.VMEM((groups, count, ROWS, width), jnp.bfloat16),
            pltpu.VMEM((groups, count, ROWS, width), jnp.bfloat16),
            pltpu.VMEM((6 * half + width, width), jnp.bfloat16),
            pltpu.VMEM((2, lanes, tokens), jnp.bfloat16),
            pltpu.VMEM((2, tokens, lanes), jnp.bfloat16),
            pltpu.VMEM((2, half, tokens), jnp.bfloat16),
            pltpu.VMEM((tokens, lanes), jnp.bfloat16),
            pltpu.VMEM((half, tokens), jnp.bfloat16),
            pltpu.VMEM((tokens, width), jnp.bfloat16),
            pltpu.VMEM((groups, count, ROWS, width), jnp.bfloat16),
            pltpu.SemaphoreType.DMA((2 * count,)),
            pltpu.SemaphoreType.DMA((len(moves),)),
        ],
        compiler_params=params,
        cost_estimate=pl.CostEstimate(flops=flops, bytes_accessed=16 * 1024 * 1024, transcendentals=0),
        name="block",
    )(own_index, *blocks, *extras, *operands)
    returned = [projected[0]] + [hop(projected[d], d) for d in range(1, count)]
    return pl.pallas_call(
        restore_kernel,
        out_shape=jax.ShapeDtypeStruct(video_tokens.shape, video_tokens.dtype),
        in_specs=[smem, vmem, vmem] + [vmem] * count,
        out_specs=vmem,
        scratch_shapes=[pltpu.VMEM((width // LANES, block_rows, LANES), jnp.float32)],
        compiler_params=params,
        name="restore",
    )(own_index, video_tokens, modulation, *returned)


def solution(mesh):
    return jax.shard_map(
        per_device,
        mesh=mesh,
        in_specs=(
            P(("slab", "seq"), None, None),
            P(("slab", "seq"), None, None),
            P(None, "seq"),
            P(None, "seq"),
        ),
        out_specs=P(("slab", "seq"), None, None),
        check_vma=False,
    )
```

time: 204 us -> 153 us (0.75)
  waiting for transfers between devices: 112 us -> 67.6 us
  Pallas kernels: 35.5 us -> 21.8 us
  starting transfers between devices: 50.2 us -> 58 us
    ppermute x4, waiting for transfers between devices: 29.5 us -> 0.01 us  [per_device(): extras.append(lax.ppermute(blocks[z], ('slab', 'seq'), pairs))]
    ppermute x32 -> x30, waiting for transfers between devices: 82.5 us -> 67.6 us  [hop(): return lax.ppermute(value, ('slab', 'seq'), pairs)]
    pallas_call x1, Pallas kernels: 31.8 us -> 18.1 us  [per_device(): pl.pallas_call(functools.partial(block_kernel, plan, frames), out_shape=[...]
    ppermute x32 -> x30, starting transfers between devices: 43.5 us -> 49 us  [hop(): return lax.ppermute(value, ('slab', 'seq'), pairs)]
    ppermute x4, starting transfers between devices: 6.76 us -> 8.97 us  [per_device(): extras.append(lax.ppermute(blocks[z], ('slab', 'seq'), pairs))]
    unnamed x39 -> x45, local copies, waits for them, and re-layouts: 4.5 us -> 4.09 us
  transfers between devices with their start and end apart: 36 -> 34, of which waited for: 19 -> 15; matrix products, arithmetic and copies ran while one was open for 1% -> 1% of each run, Pallas kernels for 0% -> 1%
where the time goes in v2:
time: 153 us
  waiting for transfers between devices  67.6 us (44%)
  starting transfers between devices  58 us (38%)
  Pallas kernels  21.8 us (14%)
  local copies, waits for them, and re-layouts  4.18 us (3%)
    ppermute x30, waiting for transfers between devices, hop(): return lax.ppermute(value, ('slab', 'seq'), pairs)  67.6 us
    ppermute x30, starting transfers between devices, hop(): return lax.ppermute(value, ('slab', 'seq'), pairs)  49 us
    pallas_call x1, Pallas kernels, per_device(): pl.pallas_call(functools.partial(block_kernel, plan, frames), out_shape=[...  18.1 us
    ppermute x4, starting transfers between devices, per_device(): extras.append(lax.ppermute(blocks[z], ('slab', 'seq'), pairs))  8.97 us
    unnamed x45, local copies, waits for them, and re-layouts  4.09 us
  transfers between devices with their start and end apart: 34, of which 15 were waited for; matrix products, arithmetic and copies ran while one was open for 1% of the time, Pallas kernels for 1%

profile of v2, /device:TPU:9, one launch (start us, length us, event | category | flops | bytes accessed | tf_op | source)
XLA Modules:
  0.0 153.2 jit_solution(3085434983925860560)
XLA Ops:
  0.0 1.2 bitcast_select_fusion
  1.2 2.4 %collective-permute-start.11 = (bf16[144,1152]{1,0:T(8,128)(2,1)S(1)}, bf16[144,1152]{1,0:T(8,128)(2,1)S(1)}, u32[]{:S(2)}, u32[]{:S(2)}) collective-permute-start(bf16[144,1152]{1,0:T(8,128)(2,1)S(1)} %bitcast_select_fusion), channel_id=1, source_target_pairs={{0,4},{1,5},{2,6},{3,7},{4,0},{5,1},{6,2},{7,3},{8,12},{9,13},{10,... | collective-permute-start | bytes 995336 | tf_op jit(solution)/shard_map/ppermute | solution.py:209
  3.5 0.2 collective-permute-start.10
  3.7 1.2 collective-permute-start.9
  4.9 0.8 copy.6.modulation_ref
  5.8 0.1 pad_add_fusion.index_ref
  5.9 1.3 copy-done
  7.1 1.7 %norm.1 = (bf16[4,4,16,1152]{3,2,1,0:T(8,128)(2,1)S(1)}, bf16[4,4,16,1152]{3,2,1,0:T(8,128)(2,1)S(1)}) custom-call(s32[2]{0:T(128)S(1)} %pad_add_fusion.index_ref, bf16[4,128,1152]{2,1,0:T(8,128)(2,1)S(1)} %copy-done, f32[4,3,1152]{2,1,0:T(4,128)S(1)} %copy.6.modulation_ref), custom_call_target="tpu_custom_call" | custom-call | tf_op jit(solution)/shard_map/norm/pallas_call | solution.py:254
  8.8 0.1 collective-permute-start
  8.9 9.1 %collective-permute-done.11 = bf16[144,1152]{1,0:T(8,128)(2,1)S(1)} collective-permute-done((bf16[144,1152]{1,0:T(8,128)(2,1)S(1)}, bf16[144,1152]{1,0:T(8,128)(2,1)S(1)}, u32[]{:S(2)}, u32[]{:S(2)}) %collective-permute-start.11) | collective-permute-done | bytes 331808 | tf_op jit(solution)/shard_map/ppermute | solution.py:209
  18.0 0.0 collective-permute-done.10
  18.1 0.1 pad_maximum_fusion.refs_12_
  18.1 1.3 collective-permute-start.13
  19.4 0.1 collective-permute-start.19
  19.6 0.0 copy-start.4
  19.6 0.0 copy-start.2
  19.6 1.4 collective-permute-start.1
  21.1 3.2 %collective-permute-start.2 = (bf16[2,4,16,1152]{3,2,1,0:T(8,128)(2,1)S(1)}, bf16[2,4,16,1152]{3,2,1,0:T(8,128)(2,1)S(1)}, u32[]{:S(2)}, u32[]{:S(2)}) collective-permute-start(bf16[2,4,16,1152]{3,2,1,0:T(8,128)(2,1)S(1)} %pad_maximum_fusion.3), channel_id=1, source_target_pairs={{0,4},{1,5},{2,6},{3,7},{4,0},{5,1},{6,2},{7,3},{8,12},{9,13},{10,... | collective-permute-start | bytes 884744 | tf_op jit(solution)/shard_map/ppermute | solution.py:209
  24.3 0.0 collective-permute-done.9.refs_11_
  24.3 1.3 collective-permute-start.4
  25.6 5.3 %collective-permute-done.19 = bf16[144,1152]{1,0:T(8,128)(2,1)S(1)} collective-permute-done((bf16[144,1152]{1,0:T(8,128)(2,1)S(1)}, bf16[144,1152]{1,0:T(8,128)(2,1)S(1)}, u32[]{:S(2)}, u32[]{:S(2)}) %collective-permute-start.19) | collective-permute-done | bytes 331808 | tf_op jit(solution)/shard_map/ppermute | solution.py:209
  30.9 1.2 collective-permute-start.23
  32.1 5.0 %collective-permute-done.1.refs_1_ = bf16[2,4,16,1152]{3,2,1,0:T(8,128)(2,1)S(1)} collective-permute-done((bf16[2,4,16,1152]{3,2,1,0:T(8,128)(2,1)S(1)}, bf16[2,4,16,1152]{3,2,1,0:T(8,128)(2,1)S(1)}, u32[]{:S(2)}, u32[]{:S(2)}) %collective-permute-start.1) | collective-permute-done | bytes 294944 | tf_op jit(solution)/shard_map/ppermute | solution.py:209
  37.2 4.6 %collective-permute-start.3 = (bf16[2,4,16,1152]{3,2,1,0:T(8,128)(2,1)S(1)}, bf16[2,4,16,1152]{3,2,1,0:T(8,128)(2,1)S(1)}, u32[]{:S(2)}, u32[]{:S(2)}) collective-permute-start(bf16[2,4,16,1152]{3,2,1,0:T(8,128)(2,1)S(1)} %pad_maximum_fusion.4), channel_id=1, source_target_pairs={{0,6},{1,7},{2,4},{3,5},{4,2},{5,3},{6,0},{7,1},{8,14},{9,15},{10,... | collective-permute-start | bytes 884744 | tf_op jit(solution)/shard_map/ppermute | solution.py:209
  41.8 0.8 collective-permute-done.2.refs_2_
  42.6 1.4 collective-permute-start.8
  44.0 0.3 collective-permute-start.21
  44.2 10.5 %collective-permute-done.3.refs_3_ = bf16[2,4,16,1152]{3,2,1,0:T(8,128)(2,1)S(1)} collective-permute-done((bf16[2,4,16,1152]{3,2,1,0:T(8,128)(2,1)S(1)}, bf16[2,4,16,1152]{3,2,1,0:T(8,128)(2,1)S(1)}, u32[]{:S(2)}, u32[]{:S(2)}) %collective-permute-start.3) | collective-permute-done | bytes 294944 | tf_op jit(solution)/shard_map/ppermute | solution.py:209
  54.7 1.2 collective-permute-start.15
  55.9 0.0 collective-permute-done.23.refs_24_
  56.0 2.2 %collective-permute-start.12 = (bf16[2,144,1152]{2,1,0:T(8,128)(2,1)S(1)}, bf16[2,144,1152]{2,1,0:T(8,128)(2,1)S(1)}, u32[]{:S(2)}, u32[]{:S(2)}) collective-permute-start(bf16[2,144,1152]{2,1,0:T(8,128)(2,1)S(1)} %pad_maximum_fusion.refs_12_), channel_id=1, source_target_pairs={{0,1},{1,0},{2,3},{3,2},{4,5},{5,4},{6,7},{7,6},{8,9},{9,8},{10,11... | collective-permute-start | bytes 1990664 | tf_op jit(solution)/shard_map/ppermute | solution.py:209
  58.1 0.2 collective-permute-start.17
  58.4 0.4 collective-permute-start.20
  58.7 1.6 %collective-permute-done.20.refs_21_ = bf16[1,144,1152]{2,1,0:T(8,128)(2,1)S(1)} collective-permute-done((bf16[1,144,1152]{2,1,0:T(8,128)(2,1)S(1)}, bf16[1,144,1152]{2,1,0:T(8,128)(2,1)S(1)}, u32[]{:S(2)}, u32[]{:S(2)}) %collective-permute-start.20) | collective-permute-done | bytes 331808 | tf_op jit(solution)/shard_map/ppermute | solution.py:209
  60.3 0.9 collective-permute-start.5
  61.2 8.0 %collective-permute-done.15.refs_16_ = bf16[2,144,1152]{2,1,0:T(8,128)(2,1)S(1)} collective-permute-done((bf16[2,144,1152]{2,1,0:T(8,128)(2,1)S(1)}, bf16[2,144,1152]{2,1,0:T(8,128)(2,1)S(1)}, u32[]{:S(2)}, u32[]{:S(2)}) %collective-permute-start.15) | collective-permute-done | bytes 663584 | tf_op jit(solution)/shard_map/ppermute | solution.py:209
  69.3 6.6 %collective-permute-start.6 = (bf16[2,4,16,1152]{3,2,1,0:T(8,128)(2,1)S(1)}, bf16[2,4,16,1152]{3,2,1,0:T(8,128)(2,1)S(1)}, u32[]{:S(2)}, u32[]{:S(2)}) collective-permute-start(bf16[2,4,16,1152]{3,2,1,0:T(8,128)(2,1)S(1)} %collective-permute-done.2.refs_2_), channel_id=1, source_target_pairs={{0,8},{1,9},{2,10},{3,11},{4,28},{5,29},{6,30},{7,31},{8,16},{9,17... | collective-permute-start | bytes 884744 | tf_op jit(solution)/shard_map/ppermute | solution.py:274
  75.9 0.2 collective-permute-start.7
  76.1 2.2 %collective-permute-start.25 = (bf16[1,144,1152]{2,1,0:T(8,128)(2,1)S(1)}, bf16[1,144,1152]{2,1,0:T(8,128)(2,1)S(1)}, u32[]{:S(2)}, u32[]{:S(2)}) collective-permute-start(bf16[1,144,1152]{2,1,0:T(8,128)(2,1)S(1)} %collective-permute-done.23.refs_24_), channel_id=1, source_target_pairs={{0,8},{1,9},{2,10},{3,11},{4,12},{5,13},{6,14},{7,15},{8,0},{9,1},... | collective-permute-start | bytes 995336 | tf_op jit(solution)/shard_map/ppermute | solution.py:209
  78.3 5.9 %collective-permute-start.24 = (bf16[1,144,1152]{2,1,0:T(8,128)(2,1)S(1)}, bf16[1,144,1152]{2,1,0:T(8,128)(2,1)S(1)}, u32[]{:S(2)}, u32[]{:S(2)}) collective-permute-start(bf16[1,144,1152]{2,1,0:T(8,128)(2,1)S(1)} %collective-permute-done.23.refs_24_), channel_id=1, source_target_pairs={{0,1},{1,0},{2,3},{3,2},{4,5},{5,4},{6,7},{7,6},{8,9},{9,8},{10,11... | collective-permute-start | bytes 995336 | tf_op jit(solution)/shard_map/ppermute | solution.py:209
  84.2 5.9 %collective-permute-start.14 = (bf16[2,144,1152]{2,1,0:T(8,128)(2,1)S(1)}, bf16[2,144,1152]{2,1,0:T(8,128)(2,1)S(1)}, u32[]{:S(2)}, u32[]{:S(2)}) collective-permute-start(bf16[2,144,1152]{2,1,0:T(8,128)(2,1)S(1)} %collective-permute-done.13.refs_14_), channel_id=1, source_target_pairs={{0,1},{1,0},{2,3},{3,2},{4,5},{5,4},{6,7},{7,6},{8,9},{9,8},{10,11... | collective-permute-start | bytes 1990664 | tf_op jit(solution)/shard_map/ppermute | solution.py:209
  90.1 4.6 %collective-permute-start.16 = (bf16[2,144,1152]{2,1,0:T(8,128)(2,1)S(1)}, bf16[2,144,1152]{2,1,0:T(8,128)(2,1)S(1)}, u32[]{:S(2)}, u32[]{:S(2)}) collective-permute-start(bf16[2,144,1152]{2,1,0:T(8,128)(2,1)S(1)} %collective-permute-done.15.refs_16_), channel_id=1, source_target_pairs={{0,1},{1,0},{2,3},{3,2},{4,5},{5,4},{6,7},{7,6},{8,9},{9,8},{10,11... | collective-permute-start | bytes 1990664 | tf_op jit(solution)/shard_map/ppermute | solution.py:209
  94.8 1.4 collective-permute-done.17.refs_18_
  96.1 2.8 %collective-permute-start.18 = (bf16[2,144,1152]{2,1,0:T(8,128)(2,1)S(1)}, bf16[2,144,1152]{2,1,0:T(8,128)(2,1)S(1)}, u32[]{:S(2)}, u32[]{:S(2)}) collective-permute-start(bf16[2,144,1152]{2,1,0:T(8,128)(2,1)S(1)} %collective-permute-done.17.refs_18_), channel_id=1, source_target_pairs={{0,1},{1,0},{2,3},{3,2},{4,5},{5,4},{6,7},{7,6},{8,9},{9,8},{10,11... | collective-permute-start | bytes 1990664 | tf_op jit(solution)/shard_map/ppermute | solution.py:209
  98.9 0.1 collective-permute-start.22
  99.0 0.4 collective-permute-start.26
  99.4 1.7 %collective-permute-done.22.refs_23_ = bf16[1,144,1152]{2,1,0:T(8,128)(2,1)S(1)} collective-permute-done((bf16[1,144,1152]{2,1,0:T(8,128)(2,1)S(1)}, bf16[1,144,1152]{2,1,0:T(8,128)(2,1)S(1)}, u32[]{:S(2)}, u32[]{:S(2)}) %collective-permute-start.22) | collective-permute-done | bytes 331808 | tf_op jit(solution)/shard_map/ppermute | solution.py:209
  101.1 0.5 collective-permute-done.26.refs_27_
  101.7 0.1 copy-done.20
  101.8 0.5 copy-done.21
  102.3 0.2 copy-done.11
  102.6 0.2 copy-done.10
  102.8 0.8 copy-done.12
  103.7 18.1 %block.1 = (bf16[4,16,1152]{2,1,0:T(8,128)(2,1)S(1)}, bf16[4,16,1152]{2,1,0:T(8,128)(2,1)S(1)}, bf16[4,16,1152]{2,1,0:T(8,128)(2,1)S(1)}, bf16[4,16,1152]{2,1,0:...) custom-call(s32[2]{0:T(128)S(1)} %pad_add_fusion.index_ref, ...), custom_call_target="tpu_custom_call" | custom-call | flops 7398752256 | bytes 16777216 | tf_op jit(solution)/shard_map/block/pallas_call | solution.py:280
  121.8 0.5 collective-permute-start.27
  122.2 1.8 %collective-permute-start.29 = (bf16[4,16,1152]{2,1,0:T(8,128)(2,1)S(1)}, bf16[4,16,1152]{2,1,0:T(8,128)(2,1)S(1)}, u32[]{:S(2)}, u32[]{:S(2)}) collective-permute-start(bf16[4,16,1152]{2,1,0:T(8,128)(2,1)S(1)} %get-tuple-element.20), channel_id=1, source_target_pairs={{0,3},{1,2},{2,1},{3,0},{4,7},{5,6},{6,5},{7,4},{8,11},{9,10},{10,... | collective-permute-start | bytes 442376 | tf_op jit(solution)/shard_map/ppermute | solution.py:209
  124.0 2.6 %collective-permute-start.31 = (bf16[4,16,1152]{2,1,0:T(8,128)(2,1)S(1)}, bf16[4,16,1152]{2,1,0:T(8,128)(2,1)S(1)}, u32[]{:S(2)}, u32[]{:S(2)}) collective-permute-start(bf16[4,16,1152]{2,1,0:T(8,128)(2,1)S(1)} %get-tuple-element.22), channel_id=1, source_target_pairs={{0,5},{1,4},{2,7},{3,6},{4,1},{5,0},{6,3},{7,2},{8,13},{9,12},{10,... | collective-permute-start | bytes 442376 | tf_op jit(solution)/shard_map/ppermute | solution.py:209
  126.6 0.9 collective-permute-done.28.refs_2_
  127.5 0.9 collective-permute-start.33
  128.4 3.4 %collective-permute-done.29.refs_3_ = bf16[4,16,1152]{2,1,0:T(8,128)(2,1)S(1)} collective-permute-done((bf16[4,16,1152]{2,1,0:T(8,128)(2,1)S(1)}, bf16[4,16,1152]{2,1,0:T(8,128)(2,1)S(1)}, u32[]{:S(2)}, u32[]{:S(2)}) %collective-permute-start.29) | collective-permute-done | bytes 147488 | tf_op jit(solution)/shard_map/ppermute | solution.py:209
  131.8 3.9 %collective-permute-done.31.refs_5_ = bf16[4,16,1152]{2,1,0:T(8,128)(2,1)S(1)} collective-permute-done((bf16[4,16,1152]{2,1,0:T(8,128)(2,1)S(1)}, bf16[4,16,1152]{2,1,0:T(8,128)(2,1)S(1)}, u32[]{:S(2)}, u32[]{:S(2)}) %collective-permute-start.31) | collective-permute-done | bytes 147488 | tf_op jit(solution)/shard_map/ppermute | solution.py:209
  135.8 11.8 %collective-permute-done.32.refs_6_ = bf16[4,16,1152]{2,1,0:T(8,128)(2,1)S(1)} collective-permute-done((bf16[4,16,1152]{2,1,0:T(8,128)(2,1)S(1)}, bf16[4,16,1152]{2,1,0:T(8,128)(2,1)S(1)}, u32[]{:S(2)}, u32[]{:S(2)}) %collective-permute-start.32) | collective-permute-done | bytes 147488 | tf_op jit(solution)/shard_map/ppermute | solution.py:209
  147.5 3.7 %collective-permute-done.33.refs_7_ = bf16[4,16,1152]{2,1,0:T(8,128)(2,1)S(1)} collective-permute-done((bf16[4,16,1152]{2,1,0:T(8,128)(2,1)S(1)}, bf16[4,16,1152]{2,1,0:T(8,128)(2,1)S(1)}, u32[]{:S(2)}, u32[]{:S(2)}) %collective-permute-start.33) | collective-permute-done | bytes 147488 | tf_op jit(solution)/shard_map/ppermute | solution.py:209
  151.2 2.0 %restore.1 = bf16[4,128,1152]{2,1,0:T(8,128)(2,1)} custom-call(s32[2]{0:T(128)S(1)} %pad_add_fusion.index_ref, bf16[4,128,1152]{2,1,0:T(8,128)(2,1)S(1)} %copy-done.1, f32[4,3,1152]{2,1,0:T(4,128)S(1)} %copy.6.modulation_ref, bf16[4,16,1152]{2,1,0:T(8,128)(2,1)S(1)} %get-tuple-element.17.refs_0_, bf16[4,16,1152]{2,1,0:T(8,128)(2,1)S(1)} %collective-permute-done.27.refs_1_, ...), custom_call_target="tpu_custom_call" | custom-call | tf_op jit(solution)/shard_map/restore/pallas_call | solution.py:304
  (61 shorter events, 0.3 us)
Async XLA Ops:
  1.2 16.9 %collective-permute-start.11 = (bf16[144,1152]{1,0:T(8,128)(2,1)S(1)}, bf16[144,1152]{1,0:T(8,128)(2,1)S(1)}, u32[]{:S(2)}, u32[]{:S(2)}) collective-permute-start(bf16[144,1152]{1,0:T(8,128)(2,1)S(1)} %bitcast_select_fusion), channel_id=1, source_target_pairs={{0,4},{1,5},{2,6},{3,7},{4,0},{5,1},{6,2},{7,3},{8,12},{9,13},{10,... | collective-permute-start | bytes 995336 | tf_op jit(solution)/shard_map/ppermute | solution.py:209
  3.5 14.5 %collective-permute-start.10 = (bf16[144,1152]{1,0:T(8,128)(2,1)S(1)}, bf16[144,1152]{1,0:T(8,128)(2,1)S(1)}, u32[]{:S(2)}, u32[]{:S(2)}) collective-permute-start(bf16[144,1152]{1,0:T(8,128)(2,1)S(1)} %bitcast_select_fusion), channel_id=1, source_target_pairs={{0,2},{1,3},{2,0},{3,1},{4,6},{5,7},{6,4},{7,5},{8,10},{9,11},{10,... | collective-permute-start | bytes 995336 | tf_op jit(solution)/shard_map/ppermute | solution.py:209
  3.7 20.6 %collective-permute-start.9 = (bf16[144,1152]{1,0:T(8,128)(2,1)}, bf16[144,1152]{1,0:T(8,128)(2,1)S(1)}, u32[]{:S(2)}, u32[]{:S(2)}) collective-permute-start(bf16[144,1152]{1,0:T(8,128)(2,1)} %bitcast.10), channel_id=1, source_target_pairs={{0,1},{1,0},{2,3},{3,2},{4,5},{5,4},{6,7},{7,6},{8,9},{9,8},{10,11... | collective-permute-start | bytes 995336 | tf_op jit(solution)/shard_map/ppermute | solution.py:209
  5.9 1.3 copy-start
  8.8 10.7 %collective-permute-start = (bf16[4,4,16,1152]{3,2,1,0:T(8,128)(2,1)S(1)}, bf16[4,4,16,1152]{3,2,1,0:T(8,128)(2,1)S(1)}, u32[]{:S(2)}, u32[]{:S(2)}) collective-permute-start(bf16[4,4,16,1152]{3,2,1,0:T(8,128)(2,1)S(1)} %get-tuple-element.16), channel_id=1, source_target_pairs={{0,1},{1,0},{2,3},{3,2},{4,5},{5,4},{6,7},{7,6},{8,9},{9,8},{10,11... | collective-permute-start | bytes 1769480 | tf_op jit(solution)/shard_map/ppermute | solution.py:209
  18.1 37.8 %copy-start.3 = (bf16[2,144,1152]{2,1,0:T(8,128)(2,1)}, bf16[2,144,1152]{2,1,0:T(8,128)(2,1)S(1)}, u32[]{:S(2)}) copy-start(bf16[2,144,1152]{2,1,0:T(8,128)(2,1)S(1)} %pad_maximum_fusion.refs_12_) | copy-start | bytes 1990660
  18.1 40.0 %collective-permute-start.13 = (bf16[2,144,1152]{2,1,0:T(8,128)(2,1)S(1)}, bf16[2,144,1152]{2,1,0:T(8,128)(2,1)S(1)}, u32[]{:S(2)}, u32[]{:S(2)}) collective-permute-start(bf16[2,144,1152]{2,1,0:T(8,128)(2,1)S(1)} %pad_maximum_fusion.refs_12_), channel_id=1, source_target_pairs={{0,8},{1,9},{2,10},{3,11},{4,12},{5,13},{6,14},{7,15},{8,0},{9,1},... | collective-permute-start | bytes 1990664 | tf_op jit(solution)/shard_map/ppermute | solution.py:209
  19.4 11.4 %collective-permute-start.19 = (bf16[144,1152]{1,0:T(8,128)(2,1)S(1)}, bf16[144,1152]{1,0:T(8,128)(2,1)S(1)}, u32[]{:S(2)}, u32[]{:S(2)}) collective-permute-start(bf16[144,1152]{1,0:T(8,128)(2,1)S(1)} %collective-permute-done.11), channel_id=1, source_target_pairs={{0,2},{1,3},{2,0},{3,1},{4,6},{5,7},{6,4},{7,5},{8,10},{9,11},{10,... | collective-permute-start | bytes 995336 | tf_op jit(solution)/shard_map/ppermute | solution.py:209
  19.6 23.0 %copy-start.4 = (bf16[1152,432]{0,1:T(8,128)(2,1)S(1)}, bf16[1152,432]{0,1:T(8,128)(2,1)}, u32[]{:S(2)}) copy-start(bf16[1152,432]{0,1:T(8,128)(2,1)} %param.6) | copy-start | bytes 2985988
  19.6 84.1 %copy-start.2 = (bf16[1152,144]{0,1:T(8,128)(2,1)S(1)}, bf16[1152,144]{0,1:T(8,128)(2,1)}, u32[]{:S(2)}) copy-start(bf16[1152,144]{0,1:T(8,128)(2,1)} %param.7) | copy-start | bytes 995332
  19.6 17.6 %collective-permute-start.1 = (bf16[2,4,16,1152]{3,2,1,0:T(8,128)(2,1)S(1)}, bf16[2,4,16,1152]{3,2,1,0:T(8,128)(2,1)S(1)}, u32[]{:S(2)}, u32[]{:S(2)}) collective-permute-start(bf16[2,4,16,1152]{3,2,1,0:T(8,128)(2,1)S(1)} %pad_maximum_fusion.2), channel_id=1, source_target_pairs={{0,2},{1,3},{2,0},{3,1},{4,6},{5,7},{6,4},{7,5},{8,10},{9,11},{10,... | collective-permute-start | bytes 884744 | tf_op jit(solution)/shard_map/ppermute | solution.py:209
  21.1 21.5 %collective-permute-start.2 = (bf16[2,4,16,1152]{3,2,1,0:T(8,128)(2,1)S(1)}, bf16[2,4,16,1152]{3,2,1,0:T(8,128)(2,1)S(1)}, u32[]{:S(2)}, u32[]{:S(2)}) collective-permute-start(bf16[2,4,16,1152]{3,2,1,0:T(8,128)(2,1)S(1)} %pad_maximum_fusion.3), channel_id=1, source_target_pairs={{0,4},{1,5},{2,6},{3,7},{4,0},{5,1},{6,2},{7,3},{8,12},{9,13},{10,... | collective-permute-start | bytes 884744 | tf_op jit(solution)/shard_map/ppermute | solution.py:209
  24.3 77.3 %copy-start.13 = (bf16[144,1152]{1,0:T(8,128)(2,1)}, bf16[144,1152]{1,0:T(8,128)(2,1)S(1)}, u32[]{:S(2)}) copy-start(bf16[144,1152]{1,0:T(8,128)(2,1)S(1)} %collective-permute-done.9.refs_11_) | copy-start | bytes 995332
  24.3 19.6 %collective-permute-start.4 = (bf16[2,4,16,1152]{3,2,1,0:T(8,128)(2,1)S(1)}, bf16[2,4,16,1152]{3,2,1,0:T(8,128)(2,1)S(1)}, u32[]{:S(2)}, u32[]{:S(2)}) collective-permute-start(bf16[2,4,16,1152]{3,2,1,0:T(8,128)(2,1)S(1)} %pad_maximum_fusion.1.refs_0_), channel_id=1, source_target_pairs={{0,24},{1,25},{2,26},{3,27},{4,12},{5,13},{6,14},{7,15},{8,0},{9,1... | collective-permute-start | bytes 884744 | tf_op jit(solution)/shard_map/ppermute | solution.py:274
  30.9 70.8 %copy-start.14 = (bf16[144,1152]{1,0:T(8,128)(2,1)}, bf16[144,1152]{1,0:T(8,128)(2,1)S(1)}, u32[]{:S(2)}) copy-start(bf16[144,1152]{1,0:T(8,128)(2,1)S(1)} %collective-permute-done.19) | copy-start | bytes 995332
  30.9 25.1 %collective-permute-start.23 = (bf16[1,144,1152]{2,1,0:T(8,128)(2,1)S(1)}, bf16[1,144,1152]{2,1,0:T(8,128)(2,1)S(1)}, u32[]{:S(2)}, u32[]{:S(2)}) collective-permute-start(bf16[1,144,1152]{2,1,0:T(8,128)(2,1)S(1)} %bitcast.16), channel_id=1, source_target_pairs={{0,16},{1,17},{2,18},{3,19},{4,20},{5,21},{6,22},{7,23},{8,24},{9,... | collective-permute-start | bytes 995336 | tf_op jit(solution)/shard_map/ppermute | solution.py:209
  37.2 17.5 %collective-permute-start.3 = (bf16[2,4,16,1152]{3,2,1,0:T(8,128)(2,1)S(1)}, bf16[2,4,16,1152]{3,2,1,0:T(8,128)(2,1)S(1)}, u32[]{:S(2)}, u32[]{:S(2)}) collective-permute-start(bf16[2,4,16,1152]{3,2,1,0:T(8,128)(2,1)S(1)} %pad_maximum_fusion.4), channel_id=1, source_target_pairs={{0,6},{1,7},{2,4},{3,5},{4,2},{5,3},{6,0},{7,1},{8,14},{9,15},{10,... | collective-permute-start | bytes 884744 | tf_op jit(solution)/shard_map/ppermute | solution.py:209
  42.6 108.7 %copy-start.1 = (bf16[4,128,1152]{2,1,0:T(8,128)(2,1)S(1)}, bf16[4,128,1152]{2,1,0:T(8,128)(2,1)}, u32[]{:S(2)}) copy-start(bf16[4,128,1152]{2,1,0:T(8,128)(2,1)} %tokens_ref.3) | copy-start | bytes 3538948
  42.6 33.5 %collective-permute-start.8 = (bf16[432,1152]{1,0:T(8,128)(2,1)S(1)}, bf16[432,1152]{1,0:T(8,128)(2,1)S(1)}, u32[]{:S(2)}, u32[]{:S(2)}) collective-permute-start(bf16[432,1152]{1,0:T(8,128)(2,1)S(1)} %bitcast.15), channel_id=1, source_target_pairs={{0,1},{1,0},{2,3},{3,2},{4,5},{5,4},{6,7},{7,6},{8,9},{9,8},{10,11... | collective-permute-start | bytes 2985992 | tf_op jit(solution)/shard_map/ppermute | solution.py:209
  44.0 14.4 %collective-permute-start.21 = (bf16[1,144,1152]{2,1,0:T(8,128)(2,1)S(1)}, bf16[1,144,1152]{2,1,0:T(8,128)(2,1)S(1)}, u32[]{:S(2)}, u32[]{:S(2)}) collective-permute-start(bf16[1,144,1152]{2,1,0:T(8,128)(2,1)S(1)} %bitcast.17), channel_id=1, source_target_pairs={{0,8},{1,9},{2,10},{3,11},{4,12},{5,13},{6,14},{7,15},{8,0},{9,1},... | collective-permute-start | bytes 995336 | tf_op jit(solution)/shard_map/ppermute | solution.py:209
  54.7 14.6 %collective-permute-start.15 = (bf16[2,144,1152]{2,1,0:T(8,128)(2,1)S(1)}, bf16[2,144,1152]{2,1,0:T(8,128)(2,1)S(1)}, u32[]{:S(2)}, u32[]{:S(2)}) collective-permute-start(bf16[2,144,1152]{2,1,0:T(8,128)(2,1)S(1)} %pad_maximum_fusion.refs_12_), channel_id=1, source_target_pairs={{0,16},{1,17},{2,18},{3,19},{4,20},{5,21},{6,22},{7,23},{8,24},{9,... | collective-permute-start | bytes 1990664 | tf_op jit(solution)/shard_map/ppermute | solution.py:209
  56.0 45.7 %copy-start.15 = (bf16[1,144,1152]{2,1,0:T(8,128)(2,1)}, bf16[1,144,1152]{2,1,0:T(8,128)(2,1)S(1)}, u32[]{:S(2)}) copy-start(bf16[1,144,1152]{2,1,0:T(8,128)(2,1)S(1)} %collective-permute-done.23.refs_24_) | copy-start | bytes 995332
  56.0 19.9 %collective-permute-start.12 = (bf16[2,144,1152]{2,1,0:T(8,128)(2,1)S(1)}, bf16[2,144,1152]{2,1,0:T(8,128)(2,1)S(1)}, u32[]{:S(2)}, u32[]{:S(2)}) collective-permute-start(bf16[2,144,1152]{2,1,0:T(8,128)(2,1)S(1)} %pad_maximum_fusion.refs_12_), channel_id=1, source_target_pairs={{0,1},{1,0},{2,3},{3,2},{4,5},{5,4},{6,7},{7,6},{8,9},{9,8},{10,11... | collective-permute-start | bytes 1990664 | tf_op jit(solution)/shard_map/ppermute | solution.py:209
  58.1 43.5 %copy-start.6 = (bf16[2,144,1152]{2,1,0:T(8,128)(2,1)}, bf16[2,144,1152]{2,1,0:T(8,128)(2,1)S(1)}, u32[]{:S(2)}) copy-start(bf16[2,144,1152]{2,1,0:T(8,128)(2,1)S(1)} %collective-permute-done.13.refs_14_) | copy-start | bytes 1990660
  58.1 38.0 %collective-permute-start.17 = (bf16[2,144,1152]{2,1,0:T(8,128)(2,1)S(1)}, bf16[2,144,1152]{2,1,0:T(8,128)(2,1)S(1)}, u32[]{:S(2)}, u32[]{:S(2)}) collective-permute-start(bf16[2,144,1152]{2,1,0:T(8,128)(2,1)S(1)} %collective-permute-done.13.refs_14_), channel_id=1, source_target_pairs={{0,16},{1,17},{2,18},{3,19},{4,20},{5,21},{6,22},{7,23},{8,24},{9,... | collective-permute-start | bytes 1990664 | tf_op jit(solution)/shard_map/ppermute | solution.py:209
  58.4 43.3 %copy-start.16 = (bf16[1,144,1152]{2,1,0:T(8,128)(2,1)}, bf16[1,144,1152]{2,1,0:T(8,128)(2,1)S(1)}, u32[]{:S(2)}) copy-start(bf16[1,144,1152]{2,1,0:T(8,128)(2,1)S(1)} %collective-permute-done.21.refs_22_) | copy-start | bytes 995332
  58.4 2.0 %collective-permute-start.20 = (bf16[1,144,1152]{2,1,0:T(8,128)(2,1)S(1)}, bf16[1,144,1152]{2,1,0:T(8,128)(2,1)S(1)}, u32[]{:S(2)}, u32[]{:S(2)}) collective-permute-start(bf16[1,144,1152]{2,1,0:T(8,128)(2,1)S(1)} %bitcast.18), channel_id=1, source_target_pairs={{0,1},{1,0},{2,3},{3,2},{4,5},{5,4},{6,7},{7,6},{8,9},{9,8},{10,11... | collective-permute-start | bytes 995336 | tf_op jit(solution)/shard_map/ppermute | solution.py:209
  60.3 41.3 %copy-start.17 = (bf16[1,144,1152]{2,1,0:T(8,128)(2,1)}, bf16[1,144,1152]{2,1,0:T(8,128)(2,1)S(1)}, u32[]{:S(2)}) copy-start(bf16[1,144,1152]{2,1,0:T(8,128)(2,1)S(1)} %collective-permute-done.20.refs_21_) | copy-start | bytes 995332
  60.3 18.0 %collective-permute-start.5 = (bf16[2,4,16,1152]{3,2,1,0:T(8,128)(2,1)S(1)}, bf16[2,4,16,1152]{3,2,1,0:T(8,128)(2,1)S(1)}, u32[]{:S(2)}, u32[]{:S(2)}) collective-permute-start(bf16[2,4,16,1152]{3,2,1,0:T(8,128)(2,1)S(1)} %collective-permute-done.1.refs_1_), channel_id=1, source_target_pairs={{0,24},{1,25},{2,26},{3,27},{4,12},{5,13},{6,14},{7,15},{8,0},{9,1... | collective-permute-start | bytes 884744 | tf_op jit(solution)/shard_map/ppermute | solution.py:274
  69.3 32.4 %copy-start.7 = (bf16[2,144,1152]{2,1,0:T(8,128)(2,1)}, bf16[2,144,1152]{2,1,0:T(8,128)(2,1)S(1)}, u32[]{:S(2)}) copy-start(bf16[2,144,1152]{2,1,0:T(8,128)(2,1)S(1)} %collective-permute-done.15.refs_16_) | copy-start | bytes 1990660
  69.3 15.0 %collective-permute-start.6 = (bf16[2,4,16,1152]{3,2,1,0:T(8,128)(2,1)S(1)}, bf16[2,4,16,1152]{3,2,1,0:T(8,128)(2,1)S(1)}, u32[]{:S(2)}, u32[]{:S(2)}) collective-permute-start(bf16[2,4,16,1152]{3,2,1,0:T(8,128)(2,1)S(1)} %collective-permute-done.2.refs_2_), channel_id=1, source_target_pairs={{0,8},{1,9},{2,10},{3,11},{4,28},{5,29},{6,30},{7,31},{8,16},{9,17... | collective-permute-start | bytes 884744 | tf_op jit(solution)/shard_map/ppermute | solution.py:274
  75.9 25.8 %copy-start.8 = (bf16[2,144,1152]{2,1,0:T(8,128)(2,1)}, bf16[2,144,1152]{2,1,0:T(8,128)(2,1)S(1)}, u32[]{:S(2)}) copy-start(bf16[2,144,1152]{2,1,0:T(8,128)(2,1)S(1)} %collective-permute-done.12.refs_13_) | copy-start | bytes 1990660
  75.9 14.3 %collective-permute-start.7 = (bf16[2,4,16,1152]{3,2,1,0:T(8,128)(2,1)S(1)}, bf16[2,4,16,1152]{3,2,1,0:T(8,128)(2,1)S(1)}, u32[]{:S(2)}, u32[]{:S(2)}) collective-permute-start(bf16[2,4,16,1152]{3,2,1,0:T(8,128)(2,1)S(1)} %collective-permute-done.3.refs_3_), channel_id=1, source_target_pairs={{0,8},{1,9},{2,10},{3,11},{4,28},{5,29},{6,30},{7,31},{8,16},{9,17... | collective-permute-start | bytes 884744 | tf_op jit(solution)/shard_map/ppermute | solution.py:274
  76.1 25.6 %copy-start.5 = (bf16[432,1152]{1,0:T(8,128)(2,1)}, bf16[432,1152]{1,0:T(8,128)(2,1)S(1)}, u32[]{:S(2)}) copy-start(bf16[432,1152]{1,0:T(8,128)(2,1)S(1)} %collective-permute-done.8.refs_9_) | copy-start | bytes 2985988
  76.1 22.8 %collective-permute-start.25 = (bf16[1,144,1152]{2,1,0:T(8,128)(2,1)S(1)}, bf16[1,144,1152]{2,1,0:T(8,128)(2,1)S(1)}, u32[]{:S(2)}, u32[]{:S(2)}) collective-permute-start(bf16[1,144,1152]{2,1,0:T(8,128)(2,1)S(1)} %collective-permute-done.23.refs_24_), channel_id=1, source_target_pairs={{0,8},{1,9},{2,10},{3,11},{4,12},{5,13},{6,14},{7,15},{8,0},{9,1},... | collective-permute-start | bytes 995336 | tf_op jit(solution)/shard_map/ppermute | solution.py:209
  78.3 20.7 %collective-permute-start.24 = (bf16[1,144,1152]{2,1,0:T(8,128)(2,1)S(1)}, bf16[1,144,1152]{2,1,0:T(8,128)(2,1)S(1)}, u32[]{:S(2)}, u32[]{:S(2)}) collective-permute-start(bf16[1,144,1152]{2,1,0:T(8,128)(2,1)S(1)} %collective-permute-done.23.refs_24_), channel_id=1, source_target_pairs={{0,1},{1,0},{2,3},{3,2},{4,5},{5,4},{6,7},{7,6},{8,9},{9,8},{10,11... | collective-permute-start | bytes 995336 | tf_op jit(solution)/shard_map/ppermute | solution.py:209
  84.2 17.3 %collective-permute-start.14 = (bf16[2,144,1152]{2,1,0:T(8,128)(2,1)S(1)}, bf16[2,144,1152]{2,1,0:T(8,128)(2,1)S(1)}, u32[]{:S(2)}, u32[]{:S(2)}) collective-permute-start(bf16[2,144,1152]{2,1,0:T(8,128)(2,1)S(1)} %collective-permute-done.13.refs_14_), channel_id=1, source_target_pairs={{0,1},{1,0},{2,3},{3,2},{4,5},{5,4},{6,7},{7,6},{8,9},{9,8},{10,11... | collective-permute-start | bytes 1990664 | tf_op jit(solution)/shard_map/ppermute | solution.py:209
  90.1 11.5 %collective-permute-start.16 = (bf16[2,144,1152]{2,1,0:T(8,128)(2,1)S(1)}, bf16[2,144,1152]{2,1,0:T(8,128)(2,1)S(1)}, u32[]{:S(2)}, u32[]{:S(2)}) collective-permute-start(bf16[2,144,1152]{2,1,0:T(8,128)(2,1)S(1)} %collective-permute-done.15.refs_16_), channel_id=1, source_target_pairs={{0,1},{1,0},{2,3},{3,2},{4,5},{5,4},{6,7},{7,6},{8,9},{9,8},{10,11... | collective-permute-start | bytes 1990664 | tf_op jit(solution)/shard_map/ppermute | solution.py:209
  96.1 5.6 %copy-start.9 = (bf16[2,144,1152]{2,1,0:T(8,128)(2,1)}, bf16[2,144,1152]{2,1,0:T(8,128)(2,1)S(1)}, u32[]{:S(2)}) copy-start(bf16[2,144,1152]{2,1,0:T(8,128)(2,1)S(1)} %collective-permute-done.17.refs_18_) | copy-start | bytes 1990660
  96.1 5.5 %collective-permute-start.18 = (bf16[2,144,1152]{2,1,0:T(8,128)(2,1)S(1)}, bf16[2,144,1152]{2,1,0:T(8,128)(2,1)S(1)}, u32[]{:S(2)}, u32[]{:S(2)}) collective-permute-start(bf16[2,144,1152]{2,1,0:T(8,128)(2,1)S(1)} %collective-permute-done.17.refs_18_), channel_id=1, source_target_pairs={{0,1},{1,0},{2,3},{3,2},{4,5},{5,4},{6,7},{7,6},{8,9},{9,8},{10,11... | collective-permute-start | bytes 1990664 | tf_op jit(solution)/shard_map/ppermute | solution.py:209
  98.9 2.8 %copy-start.18 = (bf16[1,144,1152]{2,1,0:T(8,128)(2,1)}, bf16[1,144,1152]{2,1,0:T(8,128)(2,1)S(1)}, u32[]{:S(2)}) copy-start(bf16[1,144,1152]{2,1,0:T(8,128)(2,1)S(1)} %collective-permute-done.25.refs_26_) | copy-start | bytes 995332
  98.9 2.2 %collective-permute-start.22 = (bf16[1,144,1152]{2,1,0:T(8,128)(2,1)S(1)}, bf16[1,144,1152]{2,1,0:T(8,128)(2,1)S(1)}, u32[]{:S(2)}, u32[]{:S(2)}) collective-permute-start(bf16[1,144,1152]{2,1,0:T(8,128)(2,1)S(1)} %collective-permute-done.21.refs_22_), channel_id=1, source_target_pairs={{0,1},{1,0},{2,3},{3,2},{4,5},{5,4},{6,7},{7,6},{8,9},{9,8},{10,11... | collective-permute-start | bytes 995336 | tf_op jit(solution)/shard_map/ppermute | solution.py:209
  99.0 2.7 %copy-start.19 = (bf16[1,144,1152]{2,1,0:T(8,128)(2,1)}, bf16[1,144,1152]{2,1,0:T(8,128)(2,1)S(1)}, u32[]{:S(2)}) copy-start(bf16[1,144,1152]{2,1,0:T(8,128)(2,1)S(1)} %collective-permute-done.24.refs_25_) | copy-start | bytes 995332
  99.0 2.6 %collective-permute-start.26 = (bf16[1,144,1152]{2,1,0:T(8,128)(2,1)S(1)}, bf16[1,144,1152]{2,1,0:T(8,128)(2,1)S(1)}, u32[]{:S(2)}, u32[]{:S(2)}) collective-permute-start(bf16[1,144,1152]{2,1,0:T(8,128)(2,1)S(1)} %collective-permute-done.25.refs_26_), channel_id=1, source_target_pairs={{0,1},{1,0},{2,3},{3,2},{4,5},{5,4},{6,7},{7,6},{8,9},{9,8},{10,11... | collective-permute-start | bytes 995336 | tf_op jit(solution)/shard_map/ppermute | solution.py:209
  101.1 0.7 copy-start.20
  101.6 0.8 copy-start.21
  101.6 1.0 copy-start.11
  101.6 1.2 copy-start.10
  102.8 0.8 copy-start.12
  121.8 4.8 %collective-permute-start.27 = (bf16[4,16,1152]{2,1,0:T(8,128)(2,1)S(1)}, bf16[4,16,1152]{2,1,0:T(8,128)(2,1)S(1)}, u32[]{:S(2)}, u32[]{:S(2)}) collective-permute-start(bf16[4,16,1152]{2,1,0:T(8,128)(2,1)S(1)} %get-tuple-element.18), channel_id=1, source_target_pairs={{0,1},{1,0},{2,3},{3,2},{4,5},{5,4},{6,7},{7,6},{8,9},{9,8},{10,11... | collective-permute-start | bytes 442376 | tf_op jit(solution)/shard_map/ppermute | solution.py:209
  122.2 5.3 %collective-permute-start.28 = (bf16[4,16,1152]{2,1,0:T(8,128)(2,1)S(1)}, bf16[4,16,1152]{2,1,0:T(8,128)(2,1)S(1)}, u32[]{:S(2)}, u32[]{:S(2)}) collective-permute-start(bf16[4,16,1152]{2,1,0:T(8,128)(2,1)S(1)} %get-tuple-element.19), channel_id=1, source_target_pairs={{0,2},{1,3},{2,0},{3,1},{4,6},{5,7},{6,4},{7,5},{8,10},{9,11},{10,... | collective-permute-start | bytes 442376 | tf_op jit(solution)/shard_map/ppermute | solution.py:209
  122.2 9.6 %collective-permute-start.29 = (bf16[4,16,1152]{2,1,0:T(8,128)(2,1)S(1)}, bf16[4,16,1152]{2,1,0:T(8,128)(2,1)S(1)}, u32[]{:S(2)}, u32[]{:S(2)}) collective-permute-start(bf16[4,16,1152]{2,1,0:T(8,128)(2,1)S(1)} %get-tuple-element.20), channel_id=1, source_target_pairs={{0,3},{1,2},{2,1},{3,0},{4,7},{5,6},{6,5},{7,4},{8,11},{9,10},{10,... | collective-permute-start | bytes 442376 | tf_op jit(solution)/shard_map/ppermute | solution.py:209
  124.0 7.8 %collective-permute-start.30 = (bf16[4,16,1152]{2,1,0:T(8,128)(2,1)S(1)}, bf16[4,16,1152]{2,1,0:T(8,128)(2,1)S(1)}, u32[]{:S(2)}, u32[]{:S(2)}) collective-permute-start(bf16[4,16,1152]{2,1,0:T(8,128)(2,1)S(1)} %get-tuple-element.21), channel_id=1, source_target_pairs={{0,4},{1,5},{2,6},{3,7},{4,0},{5,1},{6,2},{7,3},{8,12},{9,13},{10,... | collective-permute-start | bytes 442376 | tf_op jit(solution)/shard_map/ppermute | solution.py:209
  124.0 11.7 %collective-permute-start.31 = (bf16[4,16,1152]{2,1,0:T(8,128)(2,1)S(1)}, bf16[4,16,1152]{2,1,0:T(8,128)(2,1)S(1)}, u32[]{:S(2)}, u32[]{:S(2)}) collective-permute-start(bf16[4,16,1152]{2,1,0:T(8,128)(2,1)S(1)} %get-tuple-element.22), channel_id=1, source_target_pairs={{0,5},{1,4},{2,7},{3,6},{4,1},{5,0},{6,3},{7,2},{8,13},{9,12},{10,... | collective-permute-start | bytes 442376 | tf_op jit(solution)/shard_map/ppermute | solution.py:209
  126.6 20.9 %collective-permute-start.32 = (bf16[4,16,1152]{2,1,0:T(8,128)(2,1)S(1)}, bf16[4,16,1152]{2,1,0:T(8,128)(2,1)S(1)}, u32[]{:S(2)}, u32[]{:S(2)}) collective-permute-start(bf16[4,16,1152]{2,1,0:T(8,128)(2,1)S(1)} %get-tuple-element.23), channel_id=1, source_target_pairs={{0,6},{1,7},{2,4},{3,5},{4,2},{5,3},{6,0},{7,1},{8,14},{9,15},{10,... | collective-permute-start | bytes 442376 | tf_op jit(solution)/shard_map/ppermute | solution.py:209
  127.5 23.7 %collective-permute-start.33 = (bf16[4,16,1152]{2,1,0:T(8,128)(2,1)S(1)}, bf16[4,16,1152]{2,1,0:T(8,128)(2,1)S(1)}, u32[]{:S(2)}, u32[]{:S(2)}) collective-permute-start(bf16[4,16,1152]{2,1,0:T(8,128)(2,1)S(1)} %get-tuple-element.24), channel_id=1, source_target_pairs={{0,7},{1,6},{2,5},{3,4},{4,3},{5,2},{6,1},{7,0},{8,15},{9,14},{10,... | collective-permute-start | bytes 442376 | tf_op jit(solution)/shard_map/ppermute | solution.py:209

commit v3 on v2

v3 whole, which is shorter than its diff:
```python
import functools

import jax
import jax.numpy as jnp
from jax import lax
from jax.experimental import pallas as pl
from jax.experimental.pallas import tpu as pltpu
from jax.sharding import PartitionSpec as P

H = 16
FRS = 32
EPSILON = 1e-06
LANES = 128
ROWS = 16
SPACE_FLOPS = 40 * 10**9
VMEM_BYTES = 50 * 1024 * 1024


def padded(width):
    return -(-width // LANES) * LANES


def norm_kernel(index_ref, tokens_ref, modulation_ref, keep_ref, give_ref, mixed):
    frames = tokens_ref.shape[0]
    chips, groups, rows, width = keep_ref.shape
    positions = groups * rows // frames
    index = index_ref[0]
    for d in range(2 * chips):
        out_ref = (keep_ref, give_ref)[d % 2]
        start = pl.multiple_of(lax.bitwise_xor(index, d) * positions, positions)
        for f in range(frames):
            values = tokens_ref[f, pl.ds(start, positions), :].astype(jnp.float32)
            average = jnp.mean(values, axis=-1, keepdims=True)
            centered = values - average
            variance = jnp.mean(centered * centered, axis=-1, keepdims=True)
            normed = centered * lax.rsqrt(variance + EPSILON)
            result = normed * (1.0 + modulation_ref[f, 1:2, :]) + modulation_ref[f, 0:1, :]
            for t in range(width // LANES):
                mixed[t, pl.ds(f, positions, stride=frames), :] = result[:, t * LANES : (t + 1) * LANES]
        for t in range(width // LANES):
            part = mixed[t].astype(out_ref.dtype).reshape(groups, rows, LANES)
            out_ref[d // 2, :, :, t * LANES : (t + 1) * LANES] = part


def restore_kernel(index_ref, tokens_ref, modulation_ref, *refs):
    in_refs, out_ref, mixed = refs[:-2], refs[-2], refs[-1]
    frames = tokens_ref.shape[0]
    groups, rows, width = in_refs[0].shape
    positions = groups * rows // frames
    index = index_ref[0]
    for d, in_ref in enumerate(in_refs):
        start = pl.multiple_of(lax.bitwise_xor(index, d) * positions, positions)
        for t in range(width // LANES):
            part = in_ref[:, :, t * LANES : (t + 1) * LANES]
            mixed[t] = part.reshape(groups * rows, LANES).astype(jnp.float32)
        for f in range(frames):
            values = tokens_ref[f, pl.ds(start, positions), :].astype(jnp.float32)
            projected = jnp.concatenate(
                [mixed[t, pl.ds(f, positions, stride=frames), :] for t in range(width // LANES)], axis=1
            )
            result = values + modulation_ref[f, 2:3, :] * projected
            out_ref[f, pl.ds(start, positions), :] = result.astype(out_ref.dtype)


def nt_dot(left, right):
    return lax.dot_general(left, right, (((1,), (1,)), ((), ())), preferred_element_type=jnp.float32)


def head_window(head, head_size, shift):
    first = shift + head * head_size
    last = first + head_size
    low = first // LANES * LANES
    return first, last, low, padded(last)


def masked(values, first, last, low):
    lane = lax.broadcasted_iota(jnp.int32, values.shape, 1) + low
    return jnp.where((lane >= first) & (lane < last), values, jnp.zeros_like(values))


def softmax(scores, same, scale):
    scores = jnp.where(same, scores, -jnp.inf)
    top = jnp.max(scores, axis=0, keepdims=True)
    exponent = jnp.exp((scores - top) * scale)
    total = jnp.sum(exponent, axis=0, keepdims=True)
    return exponent * (1.0 / total)


def block_kernel(plan, frames, index_ref, *refs):
    kind, weights, half = plan["kind"], plan["weights"], plan["half"]
    refs = list(refs)
    x_refs = [refs.pop(0) for _ in range(plan["inputs"])]
    w_refs = [refs.pop(0) for _ in range(weights)]
    out_refs = [refs.pop(0) for _ in range(2)]
    xs, wall, qt, kn, vt, sems, wsems = refs
    groups, count, rows, width = xs.shape
    lanes = qt.shape[0]
    heads_half = H // 2
    head_size = width // H
    scale = head_size ** (-0.5)
    slot = count * rows
    index, slab = index_ref[0], index_ref[1]

    upper = index >= count // 2
    sources = []
    for d in range(count):
        owner = lax.bitwise_xor(index, d)
        source = x_refs[-1].at[d // 2, d % 2] if kind == 1 and d < count // 2 else x_refs[d // 2].at[d % 2]
        sources.append(pltpu.make_async_copy(source, xs.at[:, owner], sems.at[d]))
    choices = []
    for chosen, entries in plan["moves"]:
        moves = []
        for operand, at, size, owner, part in entries:
            source = w_refs[operand]
            for step in at:
                source = source.at[step]
            if owner is None:
                moves.append((source, wall.at[pl.ds(part * size, size)]))
                continue
            base = lax.bitwise_xor(index, owner) * plan["columns"] - kind * 3 * half
            if part is None:
                moves.append((source, wall.at[pl.ds(pl.multiple_of(base, ROWS), size)]))
                continue
            piece, over, spare = lax.bitwise_xor(slab, part[0]), plan["over"], part[1]
            ends = piece == plan["pieces"] - 1
            row = base + piece * size
            skip = jnp.where(ends, over, 0)
            moves.append((source.at[pl.ds(pl.multiple_of(skip, ROWS), size - over)],
                          wall.at[pl.ds(pl.multiple_of(row, ROWS), size - over)]))
            if over:
                row = jnp.where(ends, 3 * half + spare * over, row + size - over)
                moves.append((source.at[pl.ds(size - over, over)],
                              wall.at[pl.ds(pl.multiple_of(row, ROWS), over)]))
        moves = [pltpu.make_async_copy(a, b, wsems.at[n]) for n, (a, b) in enumerate(moves)]
        choices.append((None if chosen is None else upper == chosen, moves))

    def on_choice(act):
        for condition, moves in choices:
            if condition is None:
                for copy in moves:
                    act(copy)
            else:
                @pl.when(condition)
                def _():
                    for copy in moves:
                        act(copy)

    choices.append((None, sources))
    on_choice(lambda copy: copy.start())
    gap = lanes - half
    if gap:
        qt[half:, :] = jnp.zeros((gap, qt.shape[1]), qt.dtype)
        kn[:, half:] = jnp.zeros((kn.shape[0], gap), kn.dtype)
    on_choice(lambda copy: copy.wait())

    tokens = groups * slot
    own = xs[...].reshape(tokens, width)
    parts = [wall[n * half : (n + 1) * half, :] for n in range(3)]
    qt[:half, :] = nt_dot(parts[0], own).astype(qt.dtype)
    kn[:, :half] = nt_dot(own, parts[1]).astype(kn.dtype)
    vt[...] = nt_dot(parts[2], own).astype(vt.dtype)

    def one_group(g, carry):
        here = pl.ds(pl.multiple_of(g * slot, slot), slot)
        row = lax.broadcasted_iota(jnp.int32, (slot, slot), 0)
        column = lax.broadcasted_iota(jnp.int32, (slot, slot), 1)
        same = (row % rows) // frames == (column % rows) // frames
        scores = []
        for head in range(heads_half):
            first, last, low, high = head_window(head, head_size, 0)
            keys = masked(kn[here, low:high], first, last, low)
            scores.append(jnp.dot(keys, qt[low:high, here], preferred_element_type=jnp.float32))
        probs = [softmax(score, same, scale).astype(jnp.bfloat16) for score in scores]
        results = []
        for head, prob in enumerate(probs):
            values = vt[head * head_size : (head + 1) * head_size, here]
            results.append(jnp.dot(values, prob, preferred_element_type=jnp.float32))
        if gap:
            space = jnp.zeros((gap, slot), jnp.float32)
            results = [space] + results if kind else results + [space]
        result = jnp.concatenate(results, axis=0).T.astype(jnp.bfloat16)
        earlier, later = result[: slot // 2], result[slot // 2 :]
        out_refs[0][g] = jnp.where(upper, later, earlier).reshape(count // 2, rows, lanes)
        out_refs[1][g] = jnp.where(upper, earlier, later).reshape(count // 2, rows, lanes)
        return carry

    lax.fori_loop(0, groups, one_group, 0, unroll=True)


def project_kernel(plan, index_ref, first_near, first_far, second_near, second_far, *refs):
    count, moves = plan["count"], plan["moves"]
    refs = list(refs)
    w_refs = [refs.pop(0) for _ in range(plan["weights"])]
    out_refs = [refs.pop(0) for _ in range(count)]
    wall, ys, sems = refs
    index = index_ref[0]
    tokens = ys.shape[0] * ys.shape[1] * ys.shape[2]
    copies = []
    for n, (operand, at, owner) in enumerate(moves):
        source = w_refs[operand]
        for step in at:
            source = source.at[step]
        size = source.shape[0]
        row = pl.multiple_of(lax.bitwise_xor(index, owner[0]) * size, ROWS) if isinstance(owner, tuple) else owner * size
        copies.append(pltpu.make_async_copy(source, wall.at[pl.ds(row, size)], sems.at[n]))
    for copy in copies:
        copy.start()
    for copy in copies:
        copy.wait()
    upper = index >= count // 2

    def in_order(near_ref, far_ref):
        near, far = near_ref[...], far_ref[...]
        both = [jnp.where(upper, far, near), jnp.where(upper, near, far)]
        return jnp.concatenate(both, axis=1).reshape(tokens, -1)

    first, second = in_order(first_near, first_far), in_order(second_near, second_far)
    cut = 2 * first.shape[1] - wall.shape[1]
    parts = [first[:, : first.shape[1] - cut], first[:, first.shape[1] - cut :] + second[:, :cut], second[:, cut:]]
    attended = jnp.concatenate(parts if cut else [first, second], axis=1)
    ys[...] = nt_dot(attended, wall[...]).astype(ys.dtype).reshape(ys.shape)
    for d in range(count):
        out_refs[d][...] = ys[:, lax.bitwise_xor(index, d)]


def per_device(video_tokens, modulation, qkv_weight, out_weight):
    frames, positions, width = video_tokens.shape
    count, slabs = lax.axis_size("seq"), lax.axis_size("slab")
    index, slab = lax.axis_index("seq"), lax.axis_index("slab")
    block_positions = positions // count
    block_rows = block_positions * frames
    groups = block_rows // ROWS
    block = jax.ShapeDtypeStruct((groups, ROWS, width), jnp.bfloat16)
    own_index = jnp.stack([index, slab]).astype(jnp.int32)
    smem = pl.BlockSpec(memory_space=pltpu.SMEM)
    vmem = pl.BlockSpec(memory_space=pltpu.VMEM)
    anywhere = pl.BlockSpec(memory_space=pl.ANY)
    params = pltpu.CompilerParams(vmem_limit_bytes=VMEM_BYTES)

    def hop(value, seq_xor, slab_xor=0):
        pairs = [(s * count + i, (s ^ slab_xor) * count + (i ^ seq_xor)) for s in range(slabs) for i in range(count)]
        return lax.ppermute(value, ("slab", "seq"), pairs)

    half = width // 2
    lanes = padded(half)
    columns, outs = qkv_weight.shape[1], out_weight.shape[1]
    chips = count // 2
    middle = chips
    size = -(-columns // (slabs * ROWS)) * ROWS
    over = slabs * size - columns
    shared = columns % ROWS == 0 and outs % ROWS == 0 and over < size and chips == 4 and slabs == 4
    tie = lax.optimization_barrier

    keep, give = pl.pallas_call(
        norm_kernel,
        out_shape=[jax.ShapeDtypeStruct((chips,) + block.shape, block.dtype)] * 2,
        in_specs=[smem, vmem, vmem],
        out_specs=[vmem] * 2,
        scratch_shapes=[pltpu.VMEM((width // LANES, block_rows, LANES), jnp.float32)],
        compiler_params=params,
        name="norm",
    )(own_index, video_tokens, modulation)
    swapped = hop(give, 1)
    pair = [jnp.stack([keep[z], swapped[z]]) for z in range(chips)]

    def to_neighbour(value, step):
        pairs = [(s * count + i, (s + (step if i < middle else -step)) % slabs * count + i)
                 for s in range(slabs) for i in range(count)]
        return lax.ppermute(value, ("slab", "seq"), pairs)

    def following_of(values):
        return to_neighbour(jnp.stack(values), -1)

    wide, narrow = qkv_weight.T, out_weight.T
    out_operands, out_moves = [], []
    operands, moves = [], []
    if shared:
        mine = lax.dynamic_slice_in_dim(wide, jnp.minimum(slab * size, columns - size), size, 0)

        def with_sibling(value, entries, other):
            for sibling in range(2):
                operands.append(other if sibling else value)
                for at, length, z, part in entries:
                    part = part if part is None else (part, 2 * z + sibling)
                    moves.append((len(operands) - 1, at, length, (2 * z) ^ sibling, part))

        x, y = 1, 2
        blocks = [pair[0], None, None, None]
        far = hop(mine, 4)
        wide_other, narrow_other = hop(wide, 1), hop(narrow, 1)
        blocks[1] = hop(pair[1], 2)
        far, mine, pair, wide_other, narrow_other, blocks[1] = tie((far, mine, pair, wide_other, narrow_other, blocks[1]))
        ax, ay = hop(far, 0, x), hop(far, 0, y)
        rest = hop(jnp.stack([mine, far]), 2)
        blocks[2] = hop(pair[2], 4)
        following = following_of(blocks[:2])
        ax, ay, rest, blocks[2], following, pair[3] = tie((ax, ay, rest, blocks[2], following, pair[3]))
        bx, by = hop(rest, 0, x), hop(rest, 0, y)
        blocks[3] = hop(pair[3], 6)

        ay, bx, by, blocks[3], narrow = tie((ay, bx, by, blocks[3], narrow))
        axy = hop(ay, 0, x)
        bxy = hop(bx, 0, y)
        out_far = hop(narrow, 4)
        swaps = [hop(value, 1) for value in (far, ax, ay)]
        swaps += [None] + [hop(value, 1) for value in (rest, bx, by)]
        bxy, swaps = tie((bxy, swaps))
        swaps.append(hop(bxy, 1))
        swaps[3] = hop(axy, 1)
        with_sibling(wide, [((), columns, 0, None)], wide_other)
        for e, value in enumerate((far, ax, ay, axy)):
            with_sibling(value, [((), size, 2, e)], swaps[e])
        for e, value in enumerate((rest, bx, by, bxy)):
            with_sibling(value, [((n,), size, z, e) for n, z in enumerate((1, 3))], swaps[4 + e])
        near_half = [m for m in moves if m[3] < middle]
        far_half = [m for m in moves if m[3] >= middle]
        by_kind = [[(False, near_half), (True, far_half)], [(True, near_half), (False, far_half)]]
    else:
        operands = [lax.all_gather(wide, "seq", axis=0, tiled=True).reshape(6, half, width)]
        out_operands = [lax.all_gather(narrow, "seq", axis=0, tiled=True)]
        by_kind = [[(None, [(0, (3 * kind + n,), half, None, n) for n in range(3)])] for kind in range(2)]
        out_moves = [(0, (), 0)]
        blocks = [hop(pair[z], 2 * z) if z else pair[z] for z in range(chips)]
        following = following_of(blocks[: chips // 2])

    tokens = count * block_rows

    def attention(kind, inputs):
        plan = dict(kind=kind, weights=len(operands), inputs=len(inputs), half=half, moves=by_kind[kind],
                    columns=columns, over=over, pieces=slabs)
        copies = max(2 * len(entries) for _, entries in by_kind[kind])
        return pl.pallas_call(
            functools.partial(block_kernel, plan, frames),
            out_shape=[jax.ShapeDtypeStruct((groups, middle, ROWS, lanes), jnp.bfloat16)] * 2,
            in_specs=[smem] + [anywhere] * (len(inputs) + len(operands)),
            out_specs=[vmem] * 2,
            scratch_shapes=[
                pltpu.VMEM((groups, count, ROWS, width), jnp.bfloat16),
                pltpu.VMEM((3 * half + count * over, width), jnp.bfloat16),
                pltpu.VMEM((lanes, tokens), jnp.bfloat16),
                pltpu.VMEM((tokens, lanes), jnp.bfloat16),
                pltpu.VMEM((half, tokens), jnp.bfloat16),
                pltpu.SemaphoreType.DMA((count,)),
                pltpu.SemaphoreType.DMA((copies,)),
            ],
            compiler_params=params,
            cost_estimate=pl.CostEstimate(flops=SPACE_FLOPS, bytes_accessed=8 * 1024 * 1024,
                                          transcendentals=0),
            name=("windowed", "shifted")[kind],
        )(own_index, *inputs, *operands)

    second_near, second_far = attention(1, blocks + [following])
    if shared:
        out_rest = hop(jnp.stack([narrow, out_far]), 2)
    second_near = to_neighbour(second_near, 1)
    first_near, first_far = attention(0, blocks)
    if shared:
        out_rest, first_near, second_near = tie((out_rest, first_near, second_near))
        out_operands = [narrow, narrow_other, out_far, hop(out_far, 1), out_rest, hop(out_rest, 1)]
        out_moves = [(0, (), (0,)), (1, (), (1,)), (2, (), (4,)), (3, (), (5,)), (4, (0,), (2,)), (5, (0,), (3,)),
                     (4, (1,), (6,)), (5, (1,), (7,))]
    plan = dict(count=count, weights=len(out_operands), moves=out_moves)
    projected = pl.pallas_call(
        functools.partial(project_kernel, plan),
        out_shape=[block] * count,
        in_specs=[smem] + [vmem] * 4 + [anywhere] * len(out_operands),
        out_specs=[vmem] * count,
        scratch_shapes=[
            pltpu.VMEM((width, width), jnp.bfloat16),
            pltpu.VMEM((groups, count, ROWS, width), jnp.bfloat16),
            pltpu.SemaphoreType.DMA((len(out_moves),)),
        ],
        compiler_params=params,
        cost_estimate=pl.CostEstimate(flops=2 * tokens * width * width, bytes_accessed=4 * 1024 * 1024,
                                      transcendentals=0),
        name="project",
    )(own_index, first_near, first_far, second_near, second_far, *out_operands)
    returned = [projected[0]] + [hop(projected[d], d) for d in range(1, count)]
    return pl.pallas_call(
        restore_kernel,
        out_shape=jax.ShapeDtypeStruct(video_tokens.shape, video_tokens.dtype),
        in_specs=[smem, vmem, vmem] + [vmem] * count,
        out_specs=vmem,
        scratch_shapes=[pltpu.VMEM((width // LANES, block_rows, LANES), jnp.float32)],
        compiler_params=params,
        name="restore",
    )(own_index, video_tokens, modulation, *returned)


def solution(mesh):
    return jax.shard_map(
        per_device,
        mesh=mesh,
        in_specs=(
            P(("slab", "seq"), None, None),
            P(("slab", "seq"), None, None),
            P(None, "seq"),
            P(None, "seq"),
        ),
        out_specs=P(("slab", "seq"), None, None),
        check_vma=False,
    )
```

time: 153 us -> 140 us (0.915)
  starting transfers between devices: 58 us -> 28 us
  waiting for transfers between devices: 67.6 us -> 81.3 us
  Pallas kernels: 21.8 us -> 24.8 us
    ppermute x30 -> x33, starting transfers between devices: 49 us -> 25.3 us  [hop(): return lax.ppermute(value, ('slab', 'seq'), pairs)]
    ppermute x30 -> x33, waiting for transfers between devices: 67.6 us -> 79.9 us  [hop(): return lax.ppermute(value, ('slab', 'seq'), pairs)]
    ppermute x4 -> x2, starting transfers between devices: 8.97 us -> 2.69 us  [to_neighbour(): return lax.ppermute(value, ('slab', 'seq'), pairs)]
    pallas_call x1 -> x3, Pallas kernels: 18.1 us -> 21.2 us  [the longest x2 16.9 us: attention(): pl.pallas_call(functools.partial(block_kernel, plan, frames), out_shape=[...]
    unnamed x45 -> x33, local copies, waits for them, and re-layouts: 4.09 us -> 3.8 us
  transfers between devices with their start and end apart: 34 -> 35, of which waited for: 15 -> 17; matrix products, arithmetic and copies ran while one was open for 1% -> 1% of each run, Pallas kernels for 1% -> 12%
where the time goes in v3:
time: 140 us
  waiting for transfers between devices  81.3 us (58%)
  starting transfers between devices  28 us (20%)
  Pallas kernels  24.8 us (18%)
  local copies, waits for them, and re-layouts  4.91 us (4%)
    ppermute x33, waiting for transfers between devices, hop(): return lax.ppermute(value, ('slab', 'seq'), pairs)  79.9 us
    ppermute x33, starting transfers between devices, hop(): return lax.ppermute(value, ('slab', 'seq'), pairs)  25.3 us
    pallas_call x2, Pallas kernels, attention(): pl.pallas_call(functools.partial(block_kernel, plan, frames), out_shape=[...  16.9 us
    pallas_call x1, Pallas kernels, per_device(): pl.pallas_call(functools.partial(project_kernel, plan), out_shape=[block]...  4.3 us
    unnamed x33, local copies, waits for them, and re-layouts  3.8 us
  transfers between devices with their start and end apart: 35, of which 17 were waited for; matrix products, arithmetic and copies ran while one was open for 1% of the time, Pallas kernels for 12%

profile of v3, /device:TPU:9, one launch (start us, length us, event | category | flops | bytes accessed | tf_op | source)
XLA Modules:
  0.0 139.8 jit_solution(14667065753801035875)
XLA Ops:
  0.0 0.8 copy.6.modulation_ref
  0.8 0.1 pad_add_fusion.index_ref
  0.9 1.3 copy-done
  2.2 1.6 %norm.1 = (bf16[4,4,16,1152]{3,2,1,0:T(8,128)(2,1)S(1)}, bf16[4,4,16,1152]{3,2,1,0:T(8,128)(2,1)S(1)}) custom-call(s32[2]{0:T(128)S(1)} %pad_add_fusion.index_ref, bf16[4,128,1152]{2,1,0:T(8,128)(2,1)S(1)} %copy-done, f32[4,3,1152]{2,1,0:T(4,128)S(1)} %copy.6.modulation_ref), custom_call_target="tpu_custom_call" | custom-call | tf_op jit(solution)/shard_map/norm/pallas_call | solution.py:254
  3.8 0.7 collective-permute-start.1
  4.6 1.0 dynamic-slice_bitcast_fusion
  5.6 2.4 %collective-permute-start = (bf16[112,1152]{1,0:T(8,128)(2,1)S(1)}, bf16[112,1152]{1,0:T(8,128)(2,1)S(1)}, u32[]{:S(2)}, u32[]{:S(2)}) collective-permute-start(bf16[112,1152]{1,0:T(8,128)(2,1)S(1)} %dynamic-slice_bitcast_fusion), channel_id=1, source_target_pairs={{0,4},{1,5},{2,6},{3,7},{4,0},{5,1},{6,2},{7,3},{8,12},{9,13},{10,... | collective-permute-start | bytes 774152 | tf_op jit(solution)/shard_map/ppermute | solution.py:242
  8.0 0.3 collective-permute-start.2
  8.3 0.2 collective-permute-start.3
  8.5 0.0 collective-permute-done.1
  8.7 0.2 collective-permute-start.4
  8.9 0.1 pad_maximum_fusion.5
  9.0 10.4 %collective-permute-done.refs_6_.refs_7_ = bf16[112,1152]{1,0:T(8,128)(2,1)S(1)} collective-permute-done((bf16[112,1152]{1,0:T(8,128)(2,1)S(1)}, bf16[112,1152]{1,0:T(8,128)(2,1)S(1)}, u32[]{:S(2)}, u32[]{:S(2)}) %collective-permute-start) | collective-permute-done | bytes 258080 | tf_op jit(solution)/shard_map/ppermute | solution.py:242
  19.4 1.4 %collective-permute-done.4.refs_1_ = bf16[2,4,16,1152]{3,2,1,0:T(8,128)(2,1)S(1)} collective-permute-done((bf16[2,4,16,1152]{3,2,1,0:T(8,128)(2,1)S(1)}, bf16[2,4,16,1152]{3,2,1,0:T(8,128)(2,1)S(1)}, u32[]{:S(2)}, u32[]{:S(2)}) %collective-permute-start.4) | collective-permute-done | bytes 294944 | tf_op jit(solution)/shard_map/ppermute | solution.py:242
  20.9 0.1 pad_maximum_fusion.1
  20.9 2.2 %collective-permute-start.9 = (bf16[2,2,4,16,1152]{4,3,2,1,0:T(8,128)(2,1)S(1)}, bf16[2,2,4,16,1152]{4,3,2,1,0:T(8,128)(2,1)S(1)}, u32[]{:S(2)}, u32[]{:S(2)}) collective-permute-start(bf16[2,2,4,16,1152]{4,3,2,1,0:T(8,128)(2,1)S(1)} %pad_maximum_fusion.1), channel_id=1, source_target_pairs={{0,24},{1,25},{2,26},{3,27},{4,12},{5,13},{6,14},{7,15},{8,0},{9,1... | collective-permute-start | bytes 1769480 | tf_op jit(solution)/shard_map/ppermute | solution.py:269
  23.2 0.1 pad_maximum_fusion.2
  23.2 0.8 collective-permute-start.7
  24.0 0.3 collective-permute-start.8
  24.3 1.2 collective-permute-start.5
  25.5 0.2 collective-permute-start.6
  25.7 14.8 %collective-permute-done.5.refs_8_.refs_9_ = bf16[112,1152]{1,0:T(8,128)(2,1)S(1)} collective-permute-done((bf16[112,1152]{1,0:T(8,128)(2,1)S(1)}, bf16[112,1152]{1,0:T(8,128)(2,1)S(1)}, u32[]{:S(2)}, u32[]{:S(2)}) %collective-permute-start.5) | collective-permute-done | bytes 258080 | tf_op jit(solution)/shard_map/ppermute | solution.py:242
  40.6 0.7 collective-permute-done.8.refs_2_
  41.3 2.7 %collective-permute-start.10 = (bf16[2,112,1152]{2,1,0:T(8,128)(2,1)S(1)}, bf16[2,112,1152]{2,1,0:T(8,128)(2,1)S(1)}, u32[]{:S(2)}, u32[]{:S(2)}) collective-permute-start(bf16[2,112,1152]{2,1,0:T(8,128)(2,1)S(1)} %collective-permute-done.7.refs_14_.refs_15_), channel_id=1, source_target_pairs={{0,8},{1,9},{2,10},{3,11},{4,12},{5,13},{6,14},{7,15},{8,0},{9,1},... | collective-permute-start | bytes 1548296 | tf_op jit(solution)/shard_map/ppermute | solution.py:242
  44.0 1.2 collective-permute-start.11
  45.2 1.2 collective-permute-start.16
  46.4 12.6 %collective-permute-done.12.refs_3_ = bf16[2,4,16,1152]{3,2,1,0:T(8,128)(2,1)S(1)} collective-permute-done((bf16[2,4,16,1152]{3,2,1,0:T(8,128)(2,1)S(1)}, bf16[2,4,16,1152]{3,2,1,0:T(8,128)(2,1)S(1)}, u32[]{:S(2)}, u32[]{:S(2)}) %collective-permute-start.12) | collective-permute-done | bytes 294944 | tf_op jit(solution)/shard_map/ppermute | solution.py:242
  59.0 1.9 %collective-permute-start.17 = (bf16[112,1152]{1,0:T(8,128)(2,1)S(1)}, bf16[112,1152]{1,0:T(8,128)(2,1)S(1)}, u32[]{:S(2)}, u32[]{:S(2)}) collective-permute-start(bf16[112,1152]{1,0:T(8,128)(2,1)S(1)} %collective-permute-done.5.refs_8_.refs_9_), channel_id=1, source_target_pairs={{0,1},{1,0},{2,3},{3,2},{4,5},{5,4},{6,7},{7,6},{8,9},{9,8},{10,11... | collective-permute-start | bytes 774152 | tf_op jit(solution)/shard_map/ppermute | solution.py:242
  61.0 0.3 collective-permute-start.15
  61.3 0.3 collective-permute-start.20
  61.6 0.2 collective-permute-start.21
  61.8 0.3 collective-permute-done.17.refs_9_.refs_10_
  62.1 0.4 collective-permute-start.18
  62.5 1.8 %collective-permute-done.18.refs_11_.refs_12_ = bf16[112,1152]{1,0:T(8,128)(2,1)S(1)} collective-permute-done((bf16[112,1152]{1,0:T(8,128)(2,1)S(1)}, bf16[112,1152]{1,0:T(8,128)(2,1)S(1)}, u32[]{:S(2)}, u32[]{:S(2)}) %collective-permute-start.18) | collective-permute-done | bytes 258080 | tf_op jit(solution)/shard_map/ppermute | solution.py:242
  64.3 0.1 collective-permute-start.22
  64.4 10.1 %collective-permute-done.15.refs_20_.refs_21_ = bf16[2,112,1152]{2,1,0:T(8,128)(2,1)S(1)} collective-permute-done((bf16[2,112,1152]{2,1,0:T(8,128)(2,1)S(1)}, bf16[2,112,1152]{2,1,0:T(8,128)(2,1)S(1)}, u32[]{:S(2)}, u32[]{:S(2)}) %collective-permute-start.15) | collective-permute-done | bytes 516128 | tf_op jit(solution)/shard_map/ppermute | solution.py:242
  74.4 0.9 collective-permute-start.24
  75.3 0.1 collective-permute-start.23
  75.4 1.5 %collective-permute-done.13.refs_2_ = bf16[144,1152]{1,0:T(8,128)(2,1)S(1)} collective-permute-done((bf16[144,1152]{1,0:T(8,128)(2,1)S(1)}, bf16[144,1152]{1,0:T(8,128)(2,1)S(1)}, u32[]{:S(2)}, u32[]{:S(2)}) %collective-permute-start.13) | collective-permute-done | bytes 331808 | tf_op jit(solution)/shard_map/ppermute | solution.py:242
  76.9 0.1 pad_maximum_fusion
  77.0 2.0 %collective-permute-start.14 = (bf16[2,144,1152]{2,1,0:T(8,128)(2,1)S(1)}, bf16[2,144,1152]{2,1,0:T(8,128)(2,1)S(1)}, u32[]{:S(2)}, u32[]{:S(2)}) collective-permute-start(bf16[2,144,1152]{2,1,0:T(8,128)(2,1)S(1)} %pad_maximum_fusion), channel_id=1, source_target_pairs={{0,2},{1,3},{2,0},{3,1},{4,6},{5,7},{6,4},{7,5},{8,10},{9,11},{10,... | collective-permute-start | bytes 1990664 | tf_op jit(solution)/shard_map/ppermute | solution.py:242
  79.1 0.8 copy-done.15
  79.9 9.7 %shifted.1 = (bf16[4,4,16,640]{3,2,1,0:T(8,128)(2,1)S(1)}, bf16[4,4,16,640]{3,2,1,0:T(8,128)(2,1)S(1)}) custom-call(s32[2]{0:T(128)S(1)} %pad_add_fusion.index_ref, bf16[2,4,16,1152]{3,2,1,0:T(8,128)(2,1)S(1)} %get-tuple-element.98.refs_0_, bf16[2,4,16,1152]{3,2,1,0:T(8,128)(2,1)S(1)} %collective-permute-done.4.refs_1_, ...), custom_call_target="tpu_custom_call" | custom-call | flops 40000000000 | bytes 8388608 | tf_op jit(solution)/shard_map/shifted/pallas_call | solution.py:332
  89.5 0.5 collective-permute-start.25
  90.0 7.2 %windowed.1 = (bf16[4,4,16,640]{3,2,1,0:T(8,128)(2,1)S(1)}, bf16[4,4,16,640]{3,2,1,0:T(8,128)(2,1)S(1)}) custom-call(s32[2]{0:T(128)S(1)} %pad_add_fusion.index_ref, bf16[2,4,16,1152]{3,2,1,0:T(8,128)(2,1)S(1)} %get-tuple-element.98.refs_0_, bf16[2,4,16,1152]{3,2,1,0:T(8,128)(2,1)S(1)} %collective-permute-done.4.refs_1_, ...), custom_call_target="tpu_custom_call" | custom-call | flops 40000000000 | bytes 8388608 | tf_op jit(solution)/shard_map/windowed/pallas_call | solution.py:332
  97.2 0.0 copy-start.5
  97.2 1.5 %collective-permute-done.25.second_near = bf16[4,4,16,640]{3,2,1,0:T(8,128)(2,1)S(1)} collective-permute-done((bf16[4,4,16,640]{3,2,1,0:T(8,128)(2,1)S(1)}, bf16[4,4,16,640]{3,2,1,0:T(8,128)(2,1)S(1)}, u32[]{:S(2)}, u32[]{:S(2)}) %collective-permute-start.25) | collective-permute-done | bytes 327712 | tf_op jit(solution)/shard_map/ppermute | solution.py:269
  98.7 1.9 %collective-permute-start.27 = (bf16[2,144,1152]{2,1,0:T(8,128)(2,1)S(1)}, bf16[2,144,1152]{2,1,0:T(8,128)(2,1)S(1)}, u32[]{:S(2)}, u32[]{:S(2)}) collective-permute-start(bf16[2,144,1152]{2,1,0:T(8,128)(2,1)S(1)} %collective-permute-done.14.refs_4_), channel_id=1, source_target_pairs={{0,1},{1,0},{2,3},{3,2},{4,5},{5,4},{6,7},{7,6},{8,9},{9,8},{10,11... | collective-permute-start | bytes 1990664 | tf_op jit(solution)/shard_map/ppermute | solution.py:242
  100.6 0.0 collective-permute-start.26
  100.6 2.2 %collective-permute-done.26.refs_3_ = bf16[144,1152]{1,0:T(8,128)(2,1)S(1)} collective-permute-done((bf16[144,1152]{1,0:T(8,128)(2,1)S(1)}, bf16[144,1152]{1,0:T(8,128)(2,1)S(1)}, u32[]{:S(2)}, u32[]{:S(2)}) %collective-permute-start.26) | collective-permute-done | bytes 331808 | tf_op jit(solution)/shard_map/ppermute | solution.py:242
  102.8 0.8 copy-done.6
  103.7 4.3 %project.1 = (bf16[4,16,1152]{2,1,0:T(8,128)(2,1)S(1)}, bf16[4,16,1152]{2,1,0:T(8,128)(2,1)S(1)}, bf16[4,16,1152]{2,1,0:T(8,128)(2,1)S(1)}, bf16[4,16,1152]{2,1,...) custom-call(s32[2]{0:T(128)S(1)} %pad_add_fusion.index_ref, ...), custom_call_target="tpu_custom_call" | custom-call | flops 1358954496 | bytes 4194304 | tf_op jit(solution)/shard_map/project/pallas_call | solution.py:363
  108.0 0.4 collective-permute-start.28
  108.4 0.0 collective-permute-start.29
  108.5 1.8 %collective-permute-start.30 = (bf16[4,16,1152]{2,1,0:T(8,128)(2,1)S(1)}, bf16[4,16,1152]{2,1,0:T(8,128)(2,1)S(1)}, u32[]{:S(2)}, u32[]{:S(2)}) collective-permute-start(bf16[4,16,1152]{2,1,0:T(8,128)(2,1)S(1)} %get-tuple-element.84), channel_id=1, source_target_pairs={{0,3},{1,2},{2,1},{3,0},{4,7},{5,6},{6,5},{7,4},{8,11},{9,10},{10,... | collective-permute-start | bytes 442376 | tf_op jit(solution)/shard_map/ppermute | solution.py:242
  110.2 2.6 %collective-permute-start.32 = (bf16[4,16,1152]{2,1,0:T(8,128)(2,1)S(1)}, bf16[4,16,1152]{2,1,0:T(8,128)(2,1)S(1)}, u32[]{:S(2)}, u32[]{:S(2)}) collective-permute-start(bf16[4,16,1152]{2,1,0:T(8,128)(2,1)S(1)} %get-tuple-element.86), channel_id=1, source_target_pairs={{0,5},{1,4},{2,7},{3,6},{4,1},{5,0},{6,3},{7,2},{8,13},{9,12},{10,... | collective-permute-start | bytes 442376 | tf_op jit(solution)/shard_map/ppermute | solution.py:242
  112.8 0.9 collective-permute-done.29.refs_2_
  113.7 1.0 collective-permute-start.34
  114.7 4.1 %collective-permute-done.30.refs_3_ = bf16[4,16,1152]{2,1,0:T(8,128)(2,1)S(1)} collective-permute-done((bf16[4,16,1152]{2,1,0:T(8,128)(2,1)S(1)}, bf16[4,16,1152]{2,1,0:T(8,128)(2,1)S(1)}, u32[]{:S(2)}, u32[]{:S(2)}) %collective-permute-start.30) | collective-permute-done | bytes 147488 | tf_op jit(solution)/shard_map/ppermute | solution.py:242
  118.9 0.5 collective-permute-done.31.refs_4_
  119.4 4.1 %collective-permute-done.32.refs_5_ = bf16[4,16,1152]{2,1,0:T(8,128)(2,1)S(1)} collective-permute-done((bf16[4,16,1152]{2,1,0:T(8,128)(2,1)S(1)}, bf16[4,16,1152]{2,1,0:T(8,128)(2,1)S(1)}, u32[]{:S(2)}, u32[]{:S(2)}) %collective-permute-start.32) | collective-permute-done | bytes 147488 | tf_op jit(solution)/shard_map/ppermute | solution.py:242
  123.5 10.9 %collective-permute-done.33.refs_6_ = bf16[4,16,1152]{2,1,0:T(8,128)(2,1)S(1)} collective-permute-done((bf16[4,16,1152]{2,1,0:T(8,128)(2,1)S(1)}, bf16[4,16,1152]{2,1,0:T(8,128)(2,1)S(1)}, u32[]{:S(2)}, u32[]{:S(2)}) %collective-permute-start.33) | collective-permute-done | bytes 147488 | tf_op jit(solution)/shard_map/ppermute | solution.py:242
  134.4 3.3 %collective-permute-done.34.refs_7_ = bf16[4,16,1152]{2,1,0:T(8,128)(2,1)S(1)} collective-permute-done((bf16[4,16,1152]{2,1,0:T(8,128)(2,1)S(1)}, bf16[4,16,1152]{2,1,0:T(8,128)(2,1)S(1)}, u32[]{:S(2)}, u32[]{:S(2)}) %collective-permute-start.34) | collective-permute-done | bytes 147488 | tf_op jit(solution)/shard_map/ppermute | solution.py:242
  137.7 2.0 %restore.1 = bf16[4,128,1152]{2,1,0:T(8,128)(2,1)} custom-call(s32[2]{0:T(128)S(1)} %pad_add_fusion.index_ref, bf16[4,128,1152]{2,1,0:T(8,128)(2,1)S(1)} %copy-done.1, f32[4,3,1152]{2,1,0:T(4,128)S(1)} %copy.6.modulation_ref, bf16[4,16,1152]{2,1,0:T(8,128)(2,1)S(1)} %get-tuple-element.81.refs_0_, bf16[4,16,1152]{2,1,0:T(8,128)(2,1)S(1)} %collective-permute-done.28.refs_1_, ...), custom_call_target="tpu_custom_call" | custom-call | tf_op jit(solution)/shard_map/restore/pallas_call | solution.py:379
  (54 shorter events, 0.3 us)
Async XLA Ops:
  0.9 1.3 copy-start
  2.2 5.8 %copy-start.3 = (bf16[1152,432]{0,1:T(8,128)(2,1)S(1)}, bf16[1152,432]{0,1:T(8,128)(2,1)}, u32[]{:S(2)}) copy-start(bf16[1152,432]{0,1:T(8,128)(2,1)} %param.6) | copy-start | bytes 2985988
  2.2 6.1 %copy-start.2 = (bf16[1152,144]{0,1:T(8,128)(2,1)S(1)}, bf16[1152,144]{0,1:T(8,128)(2,1)}, u32[]{:S(2)}) copy-start(bf16[1152,144]{0,1:T(8,128)(2,1)} %param.7) | copy-start | bytes 995332
  3.8 4.7 %collective-permute-start.1 = (bf16[4,4,16,1152]{3,2,1,0:T(8,128)(2,1)S(1)}, bf16[4,4,16,1152]{3,2,1,0:T(8,128)(2,1)S(1)}, u32[]{:S(2)}, u32[]{:S(2)}) collective-permute-start(bf16[4,4,16,1152]{3,2,1,0:T(8,128)(2,1)S(1)} %get-tuple-element.48), channel_id=1, source_target_pairs={{0,1},{1,0},{2,3},{3,2},{4,5},{5,4},{6,7},{7,6},{8,9},{9,8},{10,11... | collective-permute-start | bytes 1769480 | tf_op jit(solution)/shard_map/ppermute | solution.py:242
  5.6 13.8 %collective-permute-start = (bf16[112,1152]{1,0:T(8,128)(2,1)S(1)}, bf16[112,1152]{1,0:T(8,128)(2,1)S(1)}, u32[]{:S(2)}, u32[]{:S(2)}) collective-permute-start(bf16[112,1152]{1,0:T(8,128)(2,1)S(1)} %dynamic-slice_bitcast_fusion), channel_id=1, source_target_pairs={{0,4},{1,5},{2,6},{3,7},{4,0},{5,1},{6,2},{7,3},{8,12},{9,13},{10,... | collective-permute-start | bytes 774152 | tf_op jit(solution)/shard_map/ppermute | solution.py:242
  8.0 12.9 %collective-permute-start.2 = (bf16[432,1152]{1,0:T(8,128)(2,1)S(1)}, bf16[432,1152]{1,0:T(8,128)(2,1)S(1)}, u32[]{:S(2)}, u32[]{:S(2)}) collective-permute-start(bf16[432,1152]{1,0:T(8,128)(2,1)S(1)} %bitcast.23), channel_id=1, source_target_pairs={{0,1},{1,0},{2,3},{3,2},{4,5},{5,4},{6,7},{7,6},{8,9},{9,8},{10,11... | collective-permute-start | bytes 2985992 | tf_op jit(solution)/shard_map/ppermute | solution.py:242
  8.3 11.1 %collective-permute-start.3 = (bf16[144,1152]{1,0:T(8,128)(2,1)S(1)}, bf16[144,1152]{1,0:T(8,128)(2,1)S(1)}, u32[]{:S(2)}, u32[]{:S(2)}) collective-permute-start(bf16[144,1152]{1,0:T(8,128)(2,1)S(1)} %bitcast.13), channel_id=1, source_target_pairs={{0,1},{1,0},{2,3},{3,2},{4,5},{5,4},{6,7},{7,6},{8,9},{9,8},{10,11... | collective-permute-start | bytes 995336 | tf_op jit(solution)/shard_map/ppermute | solution.py:242
  8.7 12.2 %collective-permute-start.4 = (bf16[2,4,16,1152]{3,2,1,0:T(8,128)(2,1)S(1)}, bf16[2,4,16,1152]{3,2,1,0:T(8,128)(2,1)S(1)}, u32[]{:S(2)}, u32[]{:S(2)}) collective-permute-start(bf16[2,4,16,1152]{3,2,1,0:T(8,128)(2,1)S(1)} %pad_maximum_fusion.4), channel_id=1, source_target_pairs={{0,2},{1,3},{2,0},{3,1},{4,6},{5,7},{6,4},{7,5},{8,10},{9,11},{10,... | collective-permute-start | bytes 884744 | tf_op jit(solution)/shard_map/ppermute | solution.py:242
  20.9 56.1 %copy-start.4 = (bf16[432,1152]{1,0:T(8,128)(2,1)}, bf16[432,1152]{1,0:T(8,128)(2,1)S(1)}, u32[]{:S(2)}) copy-start(bf16[432,1152]{1,0:T(8,128)(2,1)S(1)} %collective-permute-done.2.refs_5_.refs_6_) | copy-start | bytes 2985988
  20.9 20.3 %collective-permute-start.9 = (bf16[2,2,4,16,1152]{4,3,2,1,0:T(8,128)(2,1)S(1)}, bf16[2,2,4,16,1152]{4,3,2,1,0:T(8,128)(2,1)S(1)}, u32[]{:S(2)}, u32[]{:S(2)}) collective-permute-start(bf16[2,2,4,16,1152]{4,3,2,1,0:T(8,128)(2,1)S(1)} %pad_maximum_fusion.1), channel_id=1, source_target_pairs={{0,24},{1,25},{2,26},{3,27},{4,12},{5,13},{6,14},{7,15},{8,0},{9,1... | collective-permute-start | bytes 1769480 | tf_op jit(solution)/shard_map/ppermute | solution.py:269
  23.2 18.1 %collective-permute-start.7 = (bf16[2,112,1152]{2,1,0:T(8,128)(2,1)S(1)}, bf16[2,112,1152]{2,1,0:T(8,128)(2,1)S(1)}, u32[]{:S(2)}, u32[]{:S(2)}) collective-permute-start(bf16[2,112,1152]{2,1,0:T(8,128)(2,1)S(1)} %pad_maximum_fusion.2), channel_id=1, source_target_pairs={{0,2},{1,3},{2,0},{3,1},{4,6},{5,7},{6,4},{7,5},{8,10},{9,11},{10,... | collective-permute-start | bytes 1548296 | tf_op jit(solution)/shard_map/ppermute | solution.py:242
  24.0 17.3 %collective-permute-start.8 = (bf16[2,4,16,1152]{3,2,1,0:T(8,128)(2,1)S(1)}, bf16[2,4,16,1152]{3,2,1,0:T(8,128)(2,1)S(1)}, u32[]{:S(2)}, u32[]{:S(2)}) collective-permute-start(bf16[2,4,16,1152]{3,2,1,0:T(8,128)(2,1)S(1)} %get-tuple-element.51), channel_id=1, source_target_pairs={{0,4},{1,5},{2,6},{3,7},{4,0},{5,1},{6,2},{7,3},{8,12},{9,13},{10,... | collective-permute-start | bytes 884744 | tf_op jit(solution)/shard_map/ppermute | solution.py:242
  24.3 16.3 %collective-permute-start.5 = (bf16[112,1152]{1,0:T(8,128)(2,1)S(1)}, bf16[112,1152]{1,0:T(8,128)(2,1)S(1)}, u32[]{:S(2)}, u32[]{:S(2)}) collective-permute-start(bf16[112,1152]{1,0:T(8,128)(2,1)S(1)} %collective-permute-done.refs_6_.refs_7_), channel_id=1, source_target_pairs={{0,8},{1,9},{2,10},{3,11},{4,12},{5,13},{6,14},{7,15},{8,0},{9,1},... | collective-permute-start | bytes 774152 | tf_op jit(solution)/shard_map/ppermute | solution.py:242
  25.5 15.1 %collective-permute-start.6 = (bf16[112,1152]{1,0:T(8,128)(2,1)S(1)}, bf16[112,1152]{1,0:T(8,128)(2,1)S(1)}, u32[]{:S(2)}, u32[]{:S(2)}) collective-permute-start(bf16[112,1152]{1,0:T(8,128)(2,1)S(1)} %collective-permute-done.refs_6_.refs_7_), channel_id=1, source_target_pairs={{0,16},{1,17},{2,18},{3,19},{4,20},{5,21},{6,22},{7,23},{8,24},{9,... | collective-permute-start | bytes 774152 | tf_op jit(solution)/shard_map/ppermute | solution.py:242
  41.3 37.7 %copy-start.8 = (bf16[2,112,1152]{2,1,0:T(8,128)(2,1)}, bf16[2,112,1152]{2,1,0:T(8,128)(2,1)S(1)}, u32[]{:S(2)}) copy-start(bf16[2,112,1152]{2,1,0:T(8,128)(2,1)S(1)} %collective-permute-done.7.refs_14_.refs_15_) | copy-start | bytes 1548292
  41.3 37.7 %copy-start.7 = (bf16[2,2,4,16,1152]{4,3,2,1,0:T(8,128)(2,1)}, bf16[2,2,4,16,1152]{4,3,2,1,0:T(8,128)(2,1)S(1)}, u32[]{:S(2)}) copy-start(bf16[2,2,4,16,1152]{4,3,2,1,0:T(8,128)(2,1)S(1)} %collective-permute-done.9.refs_4_) | copy-start | bytes 1769476
  41.3 19.7 %collective-permute-start.10 = (bf16[2,112,1152]{2,1,0:T(8,128)(2,1)S(1)}, bf16[2,112,1152]{2,1,0:T(8,128)(2,1)S(1)}, u32[]{:S(2)}, u32[]{:S(2)}) collective-permute-start(bf16[2,112,1152]{2,1,0:T(8,128)(2,1)S(1)} %collective-permute-done.7.refs_14_.refs_15_), channel_id=1, source_target_pairs={{0,8},{1,9},{2,10},{3,11},{4,12},{5,13},{6,14},{7,15},{8,0},{9,1},... | collective-permute-start | bytes 1548296 | tf_op jit(solution)/shard_map/ppermute | solution.py:242
  44.0 17.0 %collective-permute-start.11 = (bf16[2,112,1152]{2,1,0:T(8,128)(2,1)S(1)}, bf16[2,112,1152]{2,1,0:T(8,128)(2,1)S(1)}, u32[]{:S(2)}, u32[]{:S(2)}) collective-permute-start(bf16[2,112,1152]{2,1,0:T(8,128)(2,1)S(1)} %collective-permute-done.7.refs_14_.refs_15_), channel_id=1, source_target_pairs={{0,16},{1,17},{2,18},{3,19},{4,20},{5,21},{6,22},{7,23},{8,24},{9,... | collective-permute-start | bytes 1548296 | tf_op jit(solution)/shard_map/ppermute | solution.py:242
  45.2 13.8 %collective-permute-start.12 = (bf16[2,4,16,1152]{3,2,1,0:T(8,128)(2,1)S(1)}, bf16[2,4,16,1152]{3,2,1,0:T(8,128)(2,1)S(1)}, u32[]{:S(2)}, u32[]{:S(2)}) collective-permute-start(bf16[2,4,16,1152]{3,2,1,0:T(8,128)(2,1)S(1)} %get-tuple-element.56), channel_id=1, source_target_pairs={{0,6},{1,7},{2,4},{3,5},{4,2},{5,3},{6,0},{7,1},{8,14},{9,15},{10,... | collective-permute-start | bytes 884744 | tf_op jit(solution)/shard_map/ppermute | solution.py:242
  45.2 16.4 %collective-permute-start.16 = (bf16[112,1152]{1,0:T(8,128)(2,1)S(1)}, bf16[112,1152]{1,0:T(8,128)(2,1)S(1)}, u32[]{:S(2)}, u32[]{:S(2)}) collective-permute-start(bf16[112,1152]{1,0:T(8,128)(2,1)S(1)} %collective-permute-done.refs_6_.refs_7_), channel_id=1, source_target_pairs={{0,1},{1,0},{2,3},{3,2},{4,5},{5,4},{6,7},{7,6},{8,9},{9,8},{10,11... | collective-permute-start | bytes 774152 | tf_op jit(solution)/shard_map/ppermute | solution.py:242
  46.4 16.1 %collective-permute-start.19 = (bf16[2,112,1152]{2,1,0:T(8,128)(2,1)S(1)}, bf16[2,112,1152]{2,1,0:T(8,128)(2,1)S(1)}, u32[]{:S(2)}, u32[]{:S(2)}) collective-permute-start(bf16[2,112,1152]{2,1,0:T(8,128)(2,1)S(1)} %collective-permute-done.7.refs_14_.refs_15_), channel_id=1, source_target_pairs={{0,1},{1,0},{2,3},{3,2},{4,5},{5,4},{6,7},{7,6},{8,9},{9,8},{10,11... | collective-permute-start | bytes 1548296 | tf_op jit(solution)/shard_map/ppermute | solution.py:242
  59.0 3.1 %collective-permute-start.17 = (bf16[112,1152]{1,0:T(8,128)(2,1)S(1)}, bf16[112,1152]{1,0:T(8,128)(2,1)S(1)}, u32[]{:S(2)}, u32[]{:S(2)}) collective-permute-start(bf16[112,1152]{1,0:T(8,128)(2,1)S(1)} %collective-permute-done.5.refs_8_.refs_9_), channel_id=1, source_target_pairs={{0,1},{1,0},{2,3},{3,2},{4,5},{5,4},{6,7},{7,6},{8,9},{9,8},{10,11... | collective-permute-start | bytes 774152 | tf_op jit(solution)/shard_map/ppermute | solution.py:242
  61.0 18.0 %copy-start.9 = (bf16[2,112,1152]{2,1,0:T(8,128)(2,1)}, bf16[2,112,1152]{2,1,0:T(8,128)(2,1)S(1)}, u32[]{:S(2)}) copy-start(bf16[2,112,1152]{2,1,0:T(8,128)(2,1)S(1)} %collective-permute-done.10.refs_16_.refs_17_) | copy-start | bytes 1548292
  61.0 18.0 %copy-start.10 = (bf16[2,112,1152]{2,1,0:T(8,128)(2,1)}, bf16[2,112,1152]{2,1,0:T(8,128)(2,1)S(1)}, u32[]{:S(2)}) copy-start(bf16[2,112,1152]{2,1,0:T(8,128)(2,1)S(1)} %collective-permute-done.11.refs_18_.refs_19_) | copy-start | bytes 1548292
  61.0 13.4 %collective-permute-start.15 = (bf16[2,112,1152]{2,1,0:T(8,128)(2,1)S(1)}, bf16[2,112,1152]{2,1,0:T(8,128)(2,1)S(1)}, u32[]{:S(2)}, u32[]{:S(2)}) collective-permute-start(bf16[2,112,1152]{2,1,0:T(8,128)(2,1)S(1)} %collective-permute-done.10.refs_16_.refs_17_), channel_id=1, source_target_pairs={{0,16},{1,17},{2,18},{3,19},{4,20},{5,21},{6,22},{7,23},{8,24},{9,... | collective-permute-start | bytes 1548296 | tf_op jit(solution)/shard_map/ppermute | solution.py:242
  61.3 13.1 %collective-permute-start.20 = (bf16[2,112,1152]{2,1,0:T(8,128)(2,1)S(1)}, bf16[2,112,1152]{2,1,0:T(8,128)(2,1)S(1)}, u32[]{:S(2)}, u32[]{:S(2)}) collective-permute-start(bf16[2,112,1152]{2,1,0:T(8,128)(2,1)S(1)} %collective-permute-done.10.refs_16_.refs_17_), channel_id=1, source_target_pairs={{0,1},{1,0},{2,3},{3,2},{4,5},{5,4},{6,7},{7,6},{8,9},{9,8},{10,11... | collective-permute-start | bytes 1548296 | tf_op jit(solution)/shard_map/ppermute | solution.py:242
  61.6 12.9 %collective-permute-start.21 = (bf16[2,112,1152]{2,1,0:T(8,128)(2,1)S(1)}, bf16[2,112,1152]{2,1,0:T(8,128)(2,1)S(1)}, u32[]{:S(2)}, u32[]{:S(2)}) collective-permute-start(bf16[2,112,1152]{2,1,0:T(8,128)(2,1)S(1)} %collective-permute-done.11.refs_18_.refs_19_), channel_id=1, source_target_pairs={{0,1},{1,0},{2,3},{3,2},{4,5},{5,4},{6,7},{7,6},{8,9},{9,8},{10,11... | collective-permute-start | bytes 1548296 | tf_op jit(solution)/shard_map/ppermute | solution.py:242
  62.1 2.2 %collective-permute-start.18 = (bf16[112,1152]{1,0:T(8,128)(2,1)S(1)}, bf16[112,1152]{1,0:T(8,128)(2,1)S(1)}, u32[]{:S(2)}, u32[]{:S(2)}) collective-permute-start(bf16[112,1152]{1,0:T(8,128)(2,1)S(1)} %collective-permute-done.6.refs_10_.refs_11_), channel_id=1, source_target_pairs={{0,1},{1,0},{2,3},{3,2},{4,5},{5,4},{6,7},{7,6},{8,9},{9,8},{10,11... | collective-permute-start | bytes 774152 | tf_op jit(solution)/shard_map/ppermute | solution.py:242
  62.5 16.5 %copy-start.11 = (bf16[2,112,1152]{2,1,0:T(8,128)(2,1)}, bf16[2,112,1152]{2,1,0:T(8,128)(2,1)S(1)}, u32[]{:S(2)}) copy-start(bf16[2,112,1152]{2,1,0:T(8,128)(2,1)S(1)} %collective-permute-done.19.refs_15_.refs_16_) | copy-start | bytes 1548292
  62.5 14.4 %collective-permute-start.13 = (bf16[144,1152]{1,0:T(8,128)(2,1)S(1)}, bf16[144,1152]{1,0:T(8,128)(2,1)S(1)}, u32[]{:S(2)}, u32[]{:S(2)}) collective-permute-start(bf16[144,1152]{1,0:T(8,128)(2,1)S(1)} %bitcast.14), channel_id=1, source_target_pairs={{0,4},{1,5},{2,6},{3,7},{4,0},{5,1},{6,2},{7,3},{8,12},{9,13},{10,... | collective-permute-start | bytes 995336 | tf_op jit(solution)/shard_map/ppermute | solution.py:242
  64.3 11.0 %collective-permute-start.22 = (bf16[112,1152]{1,0:T(8,128)(2,1)S(1)}, bf16[112,1152]{1,0:T(8,128)(2,1)S(1)}, u32[]{:S(2)}, u32[]{:S(2)}) collective-permute-start(bf16[112,1152]{1,0:T(8,128)(2,1)S(1)} %collective-permute-done.6.refs_10_.refs_11_), channel_id=1, source_target_pairs={{0,8},{1,9},{2,10},{3,11},{4,12},{5,13},{6,14},{7,15},{8,0},{9,1},... | collective-permute-start | bytes 774152 | tf_op jit(solution)/shard_map/ppermute | solution.py:242
  74.4 4.6 %copy-start.12 = (bf16[2,112,1152]{2,1,0:T(8,128)(2,1)}, bf16[2,112,1152]{2,1,0:T(8,128)(2,1)S(1)}, u32[]{:S(2)}) copy-start(bf16[2,112,1152]{2,1,0:T(8,128)(2,1)S(1)} %collective-permute-done.15.refs_20_.refs_21_) | copy-start | bytes 1548292
  74.4 4.6 %copy-start.13 = (bf16[2,112,1152]{2,1,0:T(8,128)(2,1)}, bf16[2,112,1152]{2,1,0:T(8,128)(2,1)S(1)}, u32[]{:S(2)}) copy-start(bf16[2,112,1152]{2,1,0:T(8,128)(2,1)S(1)} %collective-permute-done.20.refs_17_.refs_18_) | copy-start | bytes 1548292
  74.4 4.6 %copy-start.14 = (bf16[2,112,1152]{2,1,0:T(8,128)(2,1)}, bf16[2,112,1152]{2,1,0:T(8,128)(2,1)S(1)}, u32[]{:S(2)}) copy-start(bf16[2,112,1152]{2,1,0:T(8,128)(2,1)S(1)} %collective-permute-done.21.refs_19_.refs_20_) | copy-start | bytes 1548292
  74.4 4.5 %collective-permute-start.24 = (bf16[2,112,1152]{2,1,0:T(8,128)(2,1)S(1)}, bf16[2,112,1152]{2,1,0:T(8,128)(2,1)S(1)}, u32[]{:S(2)}, u32[]{:S(2)}) collective-permute-start(bf16[2,112,1152]{2,1,0:T(8,128)(2,1)S(1)} %collective-permute-done.15.refs_20_.refs_21_), channel_id=1, source_target_pairs={{0,1},{1,0},{2,3},{3,2},{4,5},{5,4},{6,7},{7,6},{8,9},{9,8},{10,11... | collective-permute-start | bytes 1548296 | tf_op jit(solution)/shard_map/ppermute | solution.py:242
  75.3 3.7 %collective-permute-start.23 = (bf16[112,1152]{1,0:T(8,128)(2,1)S(1)}, bf16[112,1152]{1,0:T(8,128)(2,1)S(1)}, u32[]{:S(2)}, u32[]{:S(2)}) collective-permute-start(bf16[112,1152]{1,0:T(8,128)(2,1)S(1)} %collective-permute-done.22.refs_12_.refs_13_), channel_id=1, source_target_pairs={{0,1},{1,0},{2,3},{3,2},{4,5},{5,4},{6,7},{7,6},{8,9},{9,8},{10,11... | collective-permute-start | bytes 774152 | tf_op jit(solution)/shard_map/ppermute | solution.py:242
  77.0 20.2 %collective-permute-start.14 = (bf16[2,144,1152]{2,1,0:T(8,128)(2,1)S(1)}, bf16[2,144,1152]{2,1,0:T(8,128)(2,1)S(1)}, u32[]{:S(2)}, u32[]{:S(2)}) collective-permute-start(bf16[2,144,1152]{2,1,0:T(8,128)(2,1)S(1)} %pad_maximum_fusion), channel_id=1, source_target_pairs={{0,2},{1,3},{2,0},{3,1},{4,6},{5,7},{6,4},{7,5},{8,10},{9,11},{10,... | collective-permute-start | bytes 1990664 | tf_op jit(solution)/shard_map/ppermute | solution.py:242
  79.1 0.8 copy-start.15
  89.5 9.2 %collective-permute-start.25 = (bf16[4,4,16,640]{3,2,1,0:T(8,128)(2,1)S(1)}, bf16[4,4,16,640]{3,2,1,0:T(8,128)(2,1)S(1)}, u32[]{:S(2)}, u32[]{:S(2)}) collective-permute-start(bf16[4,4,16,640]{3,2,1,0:T(8,128)(2,1)S(1)} %get-tuple-element.74), channel_id=1, source_target_pairs={{0,8},{1,9},{2,10},{3,11},{4,28},{5,29},{6,30},{7,31},{8,16},{9,17... | collective-permute-start | bytes 983048 | tf_op jit(solution)/shard_map/ppermute | solution.py:269
  97.2 5.6 %copy-start.5 = (bf16[2,144,1152]{2,1,0:T(8,128)(2,1)}, bf16[2,144,1152]{2,1,0:T(8,128)(2,1)S(1)}, u32[]{:S(2)}) copy-start(bf16[2,144,1152]{2,1,0:T(8,128)(2,1)S(1)} %collective-permute-done.14.refs_4_) | copy-start | bytes 1990660
  98.7 4.1 %collective-permute-start.27 = (bf16[2,144,1152]{2,1,0:T(8,128)(2,1)S(1)}, bf16[2,144,1152]{2,1,0:T(8,128)(2,1)S(1)}, u32[]{:S(2)}, u32[]{:S(2)}) collective-permute-start(bf16[2,144,1152]{2,1,0:T(8,128)(2,1)S(1)} %collective-permute-done.14.refs_4_), channel_id=1, source_target_pairs={{0,1},{1,0},{2,3},{3,2},{4,5},{5,4},{6,7},{7,6},{8,9},{9,8},{10,11... | collective-permute-start | bytes 1990664 | tf_op jit(solution)/shard_map/ppermute | solution.py:242
  100.6 2.2 %collective-permute-start.26 = (bf16[144,1152]{1,0:T(8,128)(2,1)S(1)}, bf16[144,1152]{1,0:T(8,128)(2,1)S(1)}, u32[]{:S(2)}, u32[]{:S(2)}) collective-permute-start(bf16[144,1152]{1,0:T(8,128)(2,1)S(1)} %collective-permute-done.13.refs_2_), channel_id=1, source_target_pairs={{0,1},{1,0},{2,3},{3,2},{4,5},{5,4},{6,7},{7,6},{8,9},{9,8},{10,11... | collective-permute-start | bytes 995336 | tf_op jit(solution)/shard_map/ppermute | solution.py:242
  102.8 0.9 copy-start.6
  103.7 34.0 %copy-start.1 = (bf16[4,128,1152]{2,1,0:T(8,128)(2,1)S(1)}, bf16[4,128,1152]{2,1,0:T(8,128)(2,1)}, u32[]{:S(2)}) copy-start(bf16[4,128,1152]{2,1,0:T(8,128)(2,1)} %tokens_ref.3) | copy-start | bytes 3538948
  108.0 4.8 %collective-permute-start.28 = (bf16[4,16,1152]{2,1,0:T(8,128)(2,1)S(1)}, bf16[4,16,1152]{2,1,0:T(8,128)(2,1)S(1)}, u32[]{:S(2)}, u32[]{:S(2)}) collective-permute-start(bf16[4,16,1152]{2,1,0:T(8,128)(2,1)S(1)} %get-tuple-element.82), channel_id=1, source_target_pairs={{0,1},{1,0},{2,3},{3,2},{4,5},{5,4},{6,7},{7,6},{8,9},{9,8},{10,11... | collective-permute-start | bytes 442376 | tf_op jit(solution)/shard_map/ppermute | solution.py:242
  108.4 5.3 %collective-permute-start.29 = (bf16[4,16,1152]{2,1,0:T(8,128)(2,1)S(1)}, bf16[4,16,1152]{2,1,0:T(8,128)(2,1)S(1)}, u32[]{:S(2)}, u32[]{:S(2)}) collective-permute-start(bf16[4,16,1152]{2,1,0:T(8,128)(2,1)S(1)} %get-tuple-element.83), channel_id=1, source_target_pairs={{0,2},{1,3},{2,0},{3,1},{4,6},{5,7},{6,4},{7,5},{8,10},{9,11},{10,... | collective-permute-start | bytes 442376 | tf_op jit(solution)/shard_map/ppermute | solution.py:242
  108.5 10.4 %collective-permute-start.30 = (bf16[4,16,1152]{2,1,0:T(8,128)(2,1)S(1)}, bf16[4,16,1152]{2,1,0:T(8,128)(2,1)S(1)}, u32[]{:S(2)}, u32[]{:S(2)}) collective-permute-start(bf16[4,16,1152]{2,1,0:T(8,128)(2,1)S(1)} %get-tuple-element.84), channel_id=1, source_target_pairs={{0,3},{1,2},{2,1},{3,0},{4,7},{5,6},{6,5},{7,4},{8,11},{9,10},{10,... | collective-permute-start | bytes 442376 | tf_op jit(solution)/shard_map/ppermute | solution.py:242
  110.2 9.2 %collective-permute-start.31 = (bf16[4,16,1152]{2,1,0:T(8,128)(2,1)S(1)}, bf16[4,16,1152]{2,1,0:T(8,128)(2,1)S(1)}, u32[]{:S(2)}, u32[]{:S(2)}) collective-permute-start(bf16[4,16,1152]{2,1,0:T(8,128)(2,1)S(1)} %get-tuple-element.85), channel_id=1, source_target_pairs={{0,4},{1,5},{2,6},{3,7},{4,0},{5,1},{6,2},{7,3},{8,12},{9,13},{10,... | collective-permute-start | bytes 442376 | tf_op jit(solution)/shard_map/ppermute | solution.py:242
  110.2 13.2 %collective-permute-start.32 = (bf16[4,16,1152]{2,1,0:T(8,128)(2,1)S(1)}, bf16[4,16,1152]{2,1,0:T(8,128)(2,1)S(1)}, u32[]{:S(2)}, u32[]{:S(2)}) collective-permute-start(bf16[4,16,1152]{2,1,0:T(8,128)(2,1)S(1)} %get-tuple-element.86), channel_id=1, source_target_pairs={{0,5},{1,4},{2,7},{3,6},{4,1},{5,0},{6,3},{7,2},{8,13},{9,12},{10,... | collective-permute-start | bytes 442376 | tf_op jit(solution)/shard_map/ppermute | solution.py:242
  112.8 21.6 %collective-permute-start.33 = (bf16[4,16,1152]{2,1,0:T(8,128)(2,1)S(1)}, bf16[4,16,1152]{2,1,0:T(8,128)(2,1)S(1)}, u32[]{:S(2)}, u32[]{:S(2)}) collective-permute-start(bf16[4,16,1152]{2,1,0:T(8,128)(2,1)S(1)} %get-tuple-element.87), channel_id=1, source_target_pairs={{0,6},{1,7},{2,4},{3,5},{4,2},{5,3},{6,0},{7,1},{8,14},{9,15},{10,... | collective-permute-start | bytes 442376 | tf_op jit(solution)/shard_map/ppermute | solution.py:242
  113.7 24.0 %collective-permute-start.34 = (bf16[4,16,1152]{2,1,0:T(8,128)(2,1)S(1)}, bf16[4,16,1152]{2,1,0:T(8,128)(2,1)S(1)}, u32[]{:S(2)}, u32[]{:S(2)}) collective-permute-start(bf16[4,16,1152]{2,1,0:T(8,128)(2,1)S(1)} %get-tuple-element.88), channel_id=1, source_target_pairs={{0,7},{1,6},{2,5},{3,4},{4,3},{5,2},{6,1},{7,0},{8,15},{9,14},{10,... | collective-permute-start | bytes 442376 | tf_op jit(solution)/shard_map/ppermute | solution.py:242

commit v4 on v3

--- a/solution.py
+++ b/solution.py
@@ -13,7 +13,7 @@
 LANES = 128
 ROWS = 16
 SPACE_FLOPS = 40 * 10**9
-VMEM_BYTES = 50 * 1024 * 1024
+VMEM_BYTES = 24 * 1024 * 1024
 
 
 def padded(width):
@@ -42,26 +42,6 @@
             out_ref[d // 2, :, :, t * LANES : (t + 1) * LANES] = part
 
 
-def restore_kernel(index_ref, tokens_ref, modulation_ref, *refs):
-    in_refs, out_ref, mixed = refs[:-2], refs[-2], refs[-1]
-    frames = tokens_ref.shape[0]
-    groups, rows, width = in_refs[0].shape
-    positions = groups * rows // frames
-    index = index_ref[0]
-    for d, in_ref in enumerate(in_refs):
-        start = pl.multiple_of(lax.bitwise_xor(index, d) * positions, positions)
-        for t in range(width // LANES):
-            part = in_ref[:, :, t * LANES : (t + 1) * LANES]
-            mixed[t] = part.reshape(groups * rows, LANES).astype(jnp.float32)
-        for f in range(frames):
-            values = tokens_ref[f, pl.ds(start, positions), :].astype(jnp.float32)
-            projected = jnp.concatenate(
-                [mixed[t, pl.ds(f, positions, stride=frames), :] for t in range(width // LANES)], axis=1
-            )
-            result = values + modulation_ref[f, 2:3, :] * projected
-            out_ref[f, pl.ds(start, positions), :] = result.astype(out_ref.dtype)
-
-
 def nt_dot(left, right):
     return lax.dot_general(left, right, (((1,), (1,)), ((), ())), preferred_element_type=jnp.float32)
 
@@ -86,13 +66,46 @@
     return exponent * (1.0 / total)
 
 
+def piece_moves(plan, index, slab, entries, w_refs, wall, first_row, rows):
+    moves = []
+    for operand, at, size, owner, part in entries:
+        source = w_refs[operand]
+        for step in at:
+            source = source.at[step]
+        base = lax.bitwise_xor(index, owner) * plan["columns"] - first_row
+        if part is None:
+            moves.append((source, wall.at[pl.ds(pl.multiple_of(base, ROWS), size)]))
+            continue
+        piece, over, spare = lax.bitwise_xor(slab, part[0]), plan["over"], part[1]
+        ends = piece == plan["pieces"] - 1
+        row = base + piece * size
+        skip = jnp.where(ends, over, 0)
+        moves.append((source.at[pl.ds(pl.multiple_of(skip, ROWS), size - over)],
+                      wall.at[pl.ds(pl.multiple_of(row, ROWS), size - over)]))
+        if over:
+            row = jnp.where(ends, rows + spare * over, row + size - over)
+            moves.append((source.at[pl.ds(size - over, over)], wall.at[pl.ds(pl.multiple_of(row, ROWS), over)]))
+    return moves
+
+
+def gather_kernel(plan, index_ref, *refs):
+    w_refs, wall, sems = refs[:-2], refs[-2], refs[-1]
+    moves = piece_moves(plan, index_ref[0], index_ref[1], plan["moves"], w_refs, wall, 0, 6 * plan["half"])
+    moves = [pltpu.make_async_copy(a, b, sems.at[n]) for n, (a, b) in enumerate(moves)]
+    for move in moves:
+        move.start()
+    for move in moves:
+        move.wait()
+
+
 def block_kernel(plan, frames, index_ref, *refs):
     kind, weights, half = plan["kind"], plan["weights"], plan["half"]
     refs = list(refs)
     x_refs = [refs.pop(0) for _ in range(plan["inputs"])]
+    full_ref = refs.pop(0)
     w_refs = [refs.pop(0) for _ in range(weights)]
     out_refs = [refs.pop(0) for _ in range(2)]
-    xs, wall, qt, kn, vt, sems, wsems = refs
+    xs, wall, qt, kn, vt, sems, full_sem, wsems = refs
     groups, count, rows, width = xs.shape
     lanes = qt.shape[0]
     heads_half = H // 2
@@ -100,57 +113,37 @@
     scale = head_size ** (-0.5)
     slot = count * rows
     index, slab = index_ref[0], index_ref[1]
-
     upper = index >= count // 2
+    full = pltpu.make_async_copy(full_ref.at[pl.ds(3 * kind * half, 3 * half)], wall.at[pl.ds(0, 3 * half)], full_sem.at[0])
+    full.start()
+
     sources = []
     for d in range(count):
         owner = lax.bitwise_xor(index, d)
         source = x_refs[-1].at[d // 2, d % 2] if kind == 1 and d < count // 2 else x_refs[d // 2].at[d % 2]
         sources.append(pltpu.make_async_copy(source, xs.at[:, owner], sems.at[d]))
+    for copy in sources:
+        copy.start()
+    full.wait()
     choices = []
     for chosen, entries in plan["moves"]:
-        moves = []
-        for operand, at, size, owner, part in entries:
-            source = w_refs[operand]
-            for step in at:
-                source = source.at[step]
-            if owner is None:
-                moves.append((source, wall.at[pl.ds(part * size, size)]))
-                continue
-            base = lax.bitwise_xor(index, owner) * plan["columns"] - kind * 3 * half
-            if part is None:
-                moves.append((source, wall.at[pl.ds(pl.multiple_of(base, ROWS), size)]))
-                continue
-            piece, over, spare = lax.bitwise_xor(slab, part[0]), plan["over"], part[1]
-            ends = piece == plan["pieces"] - 1
-            row = base + piece * size
-            skip = jnp.where(ends, over, 0)
-            moves.append((source.at[pl.ds(pl.multiple_of(skip, ROWS), size - over)],
-                          wall.at[pl.ds(pl.multiple_of(row, ROWS), size - over)]))
-            if over:
-                row = jnp.where(ends, 3 * half + spare * over, row + size - over)
-                moves.append((source.at[pl.ds(size - over, over)],
-                              wall.at[pl.ds(pl.multiple_of(row, ROWS), over)]))
-        moves = [pltpu.make_async_copy(a, b, wsems.at[n]) for n, (a, b) in enumerate(moves)]
-        choices.append((None if chosen is None else upper == chosen, moves))
+        moves = piece_moves(plan, index, slab, entries, w_refs, wall, 3 * kind * half, 3 * half)
+        choices.append((chosen, [pltpu.make_async_copy(a, b, wsems.at[n]) for n, (a, b) in enumerate(moves)]))
 
     def on_choice(act):
-        for condition, moves in choices:
-            if condition is None:
+        for chosen, moves in choices:
+            @pl.when(upper == chosen)
+            def _():
                 for copy in moves:
                     act(copy)
-            else:
-                @pl.when(condition)
-                def _():
-                    for copy in moves:
-                        act(copy)
-
-    choices.append((None, sources))
+
     on_choice(lambda copy: copy.start())
     gap = lanes - half
     if gap:
         qt[half:, :] = jnp.zeros((gap, qt.shape[1]), qt.dtype)
         kn[:, half:] = jnp.zeros((kn.shape[0], gap), kn.dtype)
+    for copy in sources:
+        copy.wait()
     on_choice(lambda copy: copy.wait())
 
     tokens = groups * slot
@@ -187,14 +180,29 @@
     lax.fori_loop(0, groups, one_group, 0, unroll=True)
 
 
-def project_kernel(plan, index_ref, first_near, first_far, second_near, second_far, *refs):
+def merge_kernel(first_d, index_ref, first_ref, second_ref, *out_refs):
+    index = index_ref[0]
+    for n, out_ref in enumerate(out_refs):
+        at = lax.rem(lax.bitwise_xor(index, first_d + n), len(out_refs))
+        first, second = first_ref[:, at], second_ref[:, at]
+        lanes = first.shape[-1]
+        cut = 2 * lanes - out_ref.shape[-1]
+        if cut:
+            out_ref[..., : lanes - cut] = first[..., : lanes - cut]
+            out_ref[..., lanes - cut : lanes] = first[..., lanes - cut :] + second[..., :cut]
+            out_ref[..., lanes:] = second[..., cut:]
+        else:
+            out_ref[..., :lanes] = first
+            out_ref[..., lanes:] = second
+
+
+def restore_kernel(plan, index_ref, tokens_ref, modulation_ref, *refs):
     count, moves = plan["count"], plan["moves"]
     refs = list(refs)
+    in_refs = [refs.pop(0) for _ in range(count)]
     w_refs = [refs.pop(0) for _ in range(plan["weights"])]
-    out_refs = [refs.pop(0) for _ in range(count)]
-    wall, ys, sems = refs
+    out_ref, wall, mixed, sems = refs
     index = index_ref[0]
-    tokens = ys.shape[0] * ys.shape[1] * ys.shape[2]
     copies = []
     for n, (operand, at, owner) in enumerate(moves):
         source = w_refs[operand]
@@ -207,20 +215,22 @@
         copy.start()
     for copy in copies:
         copy.wait()
-    upper = index >= count // 2
-
-    def in_order(near_ref, far_ref):
-        near, far = near_ref[...], far_ref[...]
-        both = [jnp.where(upper, far, near), jnp.where(upper, near, far)]
-        return jnp.concatenate(both, axis=1).reshape(tokens, -1)
-
-    first, second = in_order(first_near, first_far), in_order(second_near, second_far)
-    cut = 2 * first.shape[1] - wall.shape[1]
-    parts = [first[:, : first.shape[1] - cut], first[:, first.shape[1] - cut :] + second[:, :cut], second[:, cut:]]
-    attended = jnp.concatenate(parts if cut else [first, second], axis=1)
-    ys[...] = nt_dot(attended, wall[...]).astype(ys.dtype).reshape(ys.shape)
+    frames = tokens_ref.shape[0]
+    groups, rows, width = in_refs[0].shape
+    block_rows = groups * rows
+    positions = block_rows // frames
+    attended = jnp.concatenate([in_ref[...].reshape(block_rows, width) for in_ref in in_refs], axis=0)
+    projected = nt_dot(attended, wall[...]).astype(jnp.bfloat16).astype(jnp.float32)
+    for t in range(width // LANES):
+        mixed[t] = projected[:, t * LANES : (t + 1) * LANES]
     for d in range(count):
-        out_refs[d][...] = ys[:, lax.bitwise_xor(index, d)]
+        start = pl.multiple_of(lax.bitwise_xor(index, d) * positions, positions)
+        for f in range(frames):
+            values = tokens_ref[f, pl.ds(start, positions), :].astype(jnp.float32)
+            rows_of = pl.ds(d * block_rows + f, positions, stride=frames)
+            update = jnp.concatenate([mixed[t, rows_of, :] for t in range(width // LANES)], axis=1)
+            result = values + modulation_ref[f, 2:3, :] * update
+            out_ref[f, pl.ds(start, positions), :] = result.astype(out_ref.dtype)
 
 
 def per_device(video_tokens, modulation, qkv_weight, out_weight):
@@ -294,31 +304,46 @@
         rest = hop(jnp.stack([mine, far]), 2)
         blocks[2] = hop(pair[2], 4)
         following = following_of(blocks[:2])
-        ax, ay, rest, blocks[2], following, pair[3] = tie((ax, ay, rest, blocks[2], following, pair[3]))
+        ax, ay, rest, blocks[2], following, narrow = tie((ax, ay, rest, blocks[2], following, narrow))
         bx, by = hop(rest, 0, x), hop(rest, 0, y)
+        out_far = hop(narrow, 4)
+        ay, bx, by, pair[3], out_far = tie((ay, bx, by, pair[3], out_far))
         blocks[3] = hop(pair[3], 6)
-
-        ay, bx, by, blocks[3], narrow = tie((ay, bx, by, blocks[3], narrow))
         axy = hop(ay, 0, x)
         bxy = hop(bx, 0, y)
-        out_far = hop(narrow, 4)
         swaps = [hop(value, 1) for value in (far, ax, ay)]
         swaps += [None] + [hop(value, 1) for value in (rest, bx, by)]
-        bxy, swaps = tie((bxy, swaps))
+        with_sibling(wide, [((), columns, 0, None)], wide_other)
+        for e, value in enumerate((far, ax, ay)):
+            with_sibling(value, [((), size, 2, e)], swaps[e])
+        for e, value in enumerate((rest, bx, by)):
+            with_sibling(value, [((n,), size, z, e) for n, z in enumerate((1, 3))], swaps[4 + e])
+        full_rows = 6 * half + count * over
+        plan = dict(half=half, columns=columns, over=over, pieces=slabs, moves=moves)
+        full = pl.pallas_call(
+            functools.partial(gather_kernel, plan),
+            out_shape=jax.ShapeDtypeStruct((full_rows, width), jnp.bfloat16),
+            in_specs=[smem] + [anywhere] * len(operands),
+            out_specs=anywhere,
+            scratch_shapes=[pltpu.SemaphoreType.DMA((2 * len(moves),))],
+            compiler_params=params,
+            cost_estimate=pl.CostEstimate(flops=2 * 10**9, bytes_accessed=8 * 1024 * 1024, transcendentals=0),
+            name="gather",
+        )(own_index, *operands)
+        operands.clear()
+        moves.clear()
+        bxy, swaps, out_far, blocks[3], full = tie((bxy, swaps, out_far, blocks[3], full))
         swaps.append(hop(bxy, 1))
         swaps[3] = hop(axy, 1)
-        with_sibling(wide, [((), columns, 0, None)], wide_other)
-        for e, value in enumerate((far, ax, ay, axy)):
-            with_sibling(value, [((), size, 2, e)], swaps[e])
-        for e, value in enumerate((rest, bx, by, bxy)):
-            with_sibling(value, [((n,), size, z, e) for n, z in enumerate((1, 3))], swaps[4 + e])
+        with_sibling(axy, [((), size, 2, 3)], swaps[3])
+        with_sibling(bxy, [((n,), size, z, 3) for n, z in enumerate((1, 3))], swaps[7])
         near_half = [m for m in moves if m[3] < middle]
         far_half = [m for m in moves if m[3] >= middle]
         by_kind = [[(False, near_half), (True, far_half)], [(True, near_half), (False, far_half)]]
     else:
-        operands = [lax.all_gather(wide, "seq", axis=0, tiled=True).reshape(6, half, width)]
+        full = lax.all_gather(wide, "seq", axis=0, tiled=True)
+        by_kind = [[], []]
         out_operands = [lax.all_gather(narrow, "seq", axis=0, tiled=True)]
-        by_kind = [[(None, [(0, (3 * kind + n,), half, None, n) for n in range(3)])] for kind in range(2)]
         out_moves = [(0, (), 0)]
         blocks = [hop(pair[z], 2 * z) if z else pair[z] for z in range(chips)]
         following = following_of(blocks[: chips // 2])
@@ -328,11 +353,11 @@
     def attention(kind, inputs):
         plan = dict(kind=kind, weights=len(operands), inputs=len(inputs), half=half, moves=by_kind[kind],
                     columns=columns, over=over, pieces=slabs)
-        copies = max(2 * len(entries) for _, entries in by_kind[kind])
+        copies = max([1] + [2 * len(entries) for _, entries in by_kind[kind]])
         return pl.pallas_call(
             functools.partial(block_kernel, plan, frames),
             out_shape=[jax.ShapeDtypeStruct((groups, middle, ROWS, lanes), jnp.bfloat16)] * 2,
-            in_specs=[smem] + [anywhere] * (len(inputs) + len(operands)),
+            in_specs=[smem] + [anywhere] * (len(inputs) + 1 + len(operands)),
             out_specs=[vmem] * 2,
             scratch_shapes=[
                 pltpu.VMEM((groups, count, ROWS, width), jnp.bfloat16),
@@ -341,13 +366,14 @@
                 pltpu.VMEM((tokens, lanes), jnp.bfloat16),
                 pltpu.VMEM((half, tokens), jnp.bfloat16),
                 pltpu.SemaphoreType.DMA((count,)),
+                pltpu.SemaphoreType.DMA((1,)),
                 pltpu.SemaphoreType.DMA((copies,)),
             ],
             compiler_params=params,
             cost_estimate=pl.CostEstimate(flops=SPACE_FLOPS, bytes_accessed=8 * 1024 * 1024,
                                           transcendentals=0),
             name=("windowed", "shifted")[kind],
-        )(own_index, *inputs, *operands)
+        )(own_index, *inputs, full, *operands)
 
     second_near, second_far = attention(1, blocks + [following])
     if shared:
@@ -355,36 +381,41 @@
     second_near = to_neighbour(second_near, 1)
     first_near, first_far = attention(0, blocks)
     if shared:
-        out_rest, first_near, second_near = tie((out_rest, first_near, second_near))
+        out_rest, first_near, first_far, second_near = tie((out_rest, first_near, first_far, second_near))
         out_operands = [narrow, narrow_other, out_far, hop(out_far, 1), out_rest, hop(out_rest, 1)]
         out_moves = [(0, (), (0,)), (1, (), (1,)), (2, (), (4,)), (3, (), (5,)), (4, (0,), (2,)), (5, (0,), (3,)),
                      (4, (1,), (6,)), (5, (1,), (7,))]
+
+    def merged(first_d, first, second, flops):
+        return pl.pallas_call(
+            functools.partial(merge_kernel, first_d),
+            out_shape=[block] * middle,
+            in_specs=[smem] + [vmem] * 2,
+            out_specs=[vmem] * middle,
+            compiler_params=params,
+            cost_estimate=pl.CostEstimate(flops=flops, bytes_accessed=4 * 1024 * 1024, transcendentals=0),
+            name="merge",
+        )(own_index, first, second)
+
+    sent_far = merged(middle, first_far, second_far, 0)
+    sent_near = merged(0, first_near, second_near, 0)
+    sent_far, sent_near, out_operands = tie((sent_far, sent_near, out_operands))
+    returned = [sent_near[0]] + [hop(sent_near[d], d) for d in range(1, middle)]
+    returned += [hop(value, middle + n) for n, value in enumerate(sent_far)]
     plan = dict(count=count, weights=len(out_operands), moves=out_moves)
-    projected = pl.pallas_call(
-        functools.partial(project_kernel, plan),
-        out_shape=[block] * count,
-        in_specs=[smem] + [vmem] * 4 + [anywhere] * len(out_operands),
-        out_specs=[vmem] * count,
+    return pl.pallas_call(
+        functools.partial(restore_kernel, plan),
+        out_shape=jax.ShapeDtypeStruct(video_tokens.shape, video_tokens.dtype),
+        in_specs=[smem, vmem, vmem] + [vmem] * count + [anywhere] * len(out_operands),
+        out_specs=vmem,
         scratch_shapes=[
             pltpu.VMEM((width, width), jnp.bfloat16),
-            pltpu.VMEM((groups, count, ROWS, width), jnp.bfloat16),
+            pltpu.VMEM((width // LANES, tokens, LANES), jnp.float32),
             pltpu.SemaphoreType.DMA((len(out_moves),)),
         ],
         compiler_params=params,
-        cost_estimate=pl.CostEstimate(flops=2 * tokens * width * width, bytes_accessed=4 * 1024 * 1024,
-                                      transcendentals=0),
-        name="project",
-    )(own_index, first_near, first_far, second_near, second_far, *out_operands)
-    returned = [projected[0]] + [hop(projected[d], d) for d in range(1, count)]
-    return pl.pallas_call(
-        restore_kernel,
-        out_shape=jax.ShapeDtypeStruct(video_tokens.shape, video_tokens.dtype),
-        in_specs=[smem, vmem, vmem] + [vmem] * count,
-        out_specs=vmem,
-        scratch_shapes=[pltpu.VMEM((width // LANES, block_rows, LANES), jnp.float32)],
-        compiler_params=params,
         name="restore",
-    )(own_index, video_tokens, modulation, *returned)
+    )(own_index, video_tokens, modulation, *returned, *out_operands)
 
 
 def solution(mesh):

time: 140 us -> 135 us (0.964)
  waiting for transfers between devices: 81.3 us -> 72.6 us
  Pallas kernels: 24.8 us -> 28.8 us
  local copies, waits for them, and re-layouts: 4.91 us -> 2.28 us
  starting transfers between devices: 28 us -> 30 us
    ppermute x33, waiting for transfers between devices: 79.9 us -> 70.4 us  [hop(): return lax.ppermute(value, ('slab', 'seq'), pairs)]
    pallas_call x2 -> x4, Pallas kernels: 6.33 us -> 13.7 us  [the longest x1 7.9 us: per_device(): pl.pallas_call(functools.partial(gather_kernel, plan), out_shape=jax.Shap...]
    pallas_call x2, Pallas kernels: 16.9 us -> 13.4 us  [attention(): pl.pallas_call(functools.partial(block_kernel, plan, frames), out_shape=[...]
    unnamed x33 -> x9, local copies, waits for them, and re-layouts: 3.8 us -> 2.12 us
  transfers between devices with their start and end apart: 35 -> 35, of which waited for: 17 -> 16; matrix products, arithmetic and copies ran while one was open for 1% -> 0% of each run, Pallas kernels for 12% -> 17%
where the time goes in v4:
time: 135 us; the launch traced here: 134 us
  waiting for transfers between devices  72.6 us (54%)
  starting transfers between devices  30 us (22%)
  Pallas kernels  28.8 us (21%)
  local copies, waits for them, and re-layouts  2.28 us (2%)
    ppermute x33, waiting for transfers between devices, hop(): return lax.ppermute(value, ('slab', 'seq'), pairs)  70.4 us
    ppermute x33, starting transfers between devices, hop(): return lax.ppermute(value, ('slab', 'seq'), pairs)  26.6 us
    pallas_call x2, Pallas kernels, attention(): pl.pallas_call(functools.partial(block_kernel, plan, frames), out_shape=[...  13.4 us
    pallas_call x1, Pallas kernels, per_device(): pl.pallas_call(functools.partial(gather_kernel, plan), out_shape=jax.Shap...  7.9 us
    pallas_call x1, Pallas kernels, per_device(): pl.pallas_call(functools.partial(restore_kernel, plan), out_shape=jax.Sha...  4.63 us
    ppermute x2, starting transfers between devices, to_neighbour(): return lax.ppermute(value, ('slab', 'seq'), pairs)  3.4 us
  transfers between devices with their start and end apart: 35, of which 16 were waited for; matrix products, arithmetic and copies ran while one was open for 0% of the time, Pallas kernels for 17%

profile of v4, /device:TPU:9, one launch (start us, length us, event | category | flops | bytes accessed | tf_op | source)
XLA Modules:
  0.0 134.4 jit_solution(3526449470507056498)
XLA Ops:
  0.0 0.8 copy.6.modulation_ref
  0.8 0.1 pad_add_fusion.index_ref
  0.9 1.3 copy-done
  2.2 1.6 %norm.1 = (bf16[4,4,16,1152]{3,2,1,0:T(8,128)(2,1)S(1)}, bf16[4,4,16,1152]{3,2,1,0:T(8,128)(2,1)S(1)}) custom-call(s32[2]{0:T(128)S(1)} %pad_add_fusion.index_ref, bf16[4,128,1152]{2,1,0:T(8,128)(2,1)S(1)} %copy-done, f32[4,3,1152]{2,1,0:T(4,128)S(1)} %copy.6.modulation_ref), custom_call_target="tpu_custom_call" | custom-call | tf_op jit(solution)/shard_map/norm/pallas_call | solution.py:264
  3.8 0.7 collective-permute-start.1
  4.6 0.1 dynamic-slice_bitcast_fusion
  4.7 2.4 %collective-permute-start = (bf16[112,1152]{1,0:T(8,128)(2,1)S(1)}, bf16[112,1152]{1,0:T(8,128)(2,1)S(1)}, u32[]{:S(2)}, u32[]{:S(2)}) collective-permute-start(bf16[112,1152]{1,0:T(8,128)(2,1)S(1)} %dynamic-slice_bitcast_fusion), channel_id=1, source_target_pairs={{0,4},{1,5},{2,6},{3,7},{4,0},{5,1},{6,2},{7,3},{8,12},{9,13},{10,... | collective-permute-start | bytes 774152 | tf_op jit(solution)/shard_map/ppermute | solution.py:252
  7.0 0.3 collective-permute-start.2
  7.4 0.2 collective-permute-start.3
  7.7 0.2 collective-permute-start.4
  8.0 0.1 pad_maximum_fusion.5
  8.1 10.4 %collective-permute-done.refs_2_ = bf16[112,1152]{1,0:T(8,128)(2,1)S(1)} collective-permute-done((bf16[112,1152]{1,0:T(8,128)(2,1)S(1)}, bf16[112,1152]{1,0:T(8,128)(2,1)S(1)}, u32[]{:S(2)}, u32[]{:S(2)}) %collective-permute-start) | collective-permute-done | bytes 258080 | tf_op jit(solution)/shard_map/ppermute | solution.py:252
  18.5 1.4 %collective-permute-done.4.refs_1_ = bf16[2,4,16,1152]{3,2,1,0:T(8,128)(2,1)S(1)} collective-permute-done((bf16[2,4,16,1152]{3,2,1,0:T(8,128)(2,1)S(1)}, bf16[2,4,16,1152]{3,2,1,0:T(8,128)(2,1)S(1)}, u32[]{:S(2)}, u32[]{:S(2)}) %collective-permute-start.4) | collective-permute-done | bytes 294944 | tf_op jit(solution)/shard_map/ppermute | solution.py:252
  19.9 0.1 pad_maximum_fusion.1
  20.0 2.2 %collective-permute-start.9 = (bf16[2,2,4,16,1152]{4,3,2,1,0:T(8,128)(2,1)S(1)}, bf16[2,2,4,16,1152]{4,3,2,1,0:T(8,128)(2,1)S(1)}, u32[]{:S(2)}, u32[]{:S(2)}) collective-permute-start(bf16[2,2,4,16,1152]{4,3,2,1,0:T(8,128)(2,1)S(1)} %pad_maximum_fusion.1), channel_id=1, source_target_pairs={{0,24},{1,25},{2,26},{3,27},{4,12},{5,13},{6,14},{7,15},{8,0},{9,1... | collective-permute-start | bytes 1769480 | tf_op jit(solution)/shard_map/ppermute | solution.py:279
  22.2 0.1 pad_maximum_fusion.2
  22.3 0.8 collective-permute-start.7
  23.1 0.9 collective-permute-start.8
  23.9 1.2 collective-permute-start.5
  25.1 0.2 collective-permute-start.6
  25.4 14.2 %collective-permute-done.5.refs_4_ = bf16[112,1152]{1,0:T(8,128)(2,1)S(1)} collective-permute-done((bf16[112,1152]{1,0:T(8,128)(2,1)S(1)}, bf16[112,1152]{1,0:T(8,128)(2,1)S(1)}, u32[]{:S(2)}, u32[]{:S(2)}) %collective-permute-start.5) | collective-permute-done | bytes 258080 | tf_op jit(solution)/shard_map/ppermute | solution.py:252
  39.6 1.2 collective-permute-done.8.refs_2_
  40.8 2.2 %collective-permute-start.10 = (bf16[2,112,1152]{2,1,0:T(8,128)(2,1)S(1)}, bf16[2,112,1152]{2,1,0:T(8,128)(2,1)S(1)}, u32[]{:S(2)}, u32[]{:S(2)}) collective-permute-start(bf16[2,112,1152]{2,1,0:T(8,128)(2,1)S(1)} %collective-permute-done.7.refs_8_), channel_id=1, source_target_pairs={{0,8},{1,9},{2,10},{3,11},{4,12},{5,13},{6,14},{7,15},{8,0},{9,1},... | collective-permute-start | bytes 1548296 | tf_op jit(solution)/shard_map/ppermute | solution.py:252
  43.0 1.2 collective-permute-start.11
  44.2 1.3 %collective-permute-start.12 = (bf16[144,1152]{1,0:T(8,128)(2,1)S(1)}, bf16[144,1152]{1,0:T(8,128)(2,1)S(1)}, u32[]{:S(2)}, u32[]{:S(2)}) collective-permute-start(bf16[144,1152]{1,0:T(8,128)(2,1)S(1)} %bitcast.16), channel_id=1, source_target_pairs={{0,4},{1,5},{2,6},{3,7},{4,0},{5,1},{6,2},{7,3},{8,12},{9,13},{10,... | collective-permute-start | bytes 995336 | tf_op jit(solution)/shard_map/ppermute | solution.py:252
  45.6 1.6 %collective-permute-start.17 = (bf16[2,112,1152]{2,1,0:T(8,128)(2,1)S(1)}, bf16[2,112,1152]{2,1,0:T(8,128)(2,1)S(1)}, u32[]{:S(2)}, u32[]{:S(2)}) collective-permute-start(bf16[2,112,1152]{2,1,0:T(8,128)(2,1)S(1)} %collective-permute-done.7.refs_8_), channel_id=1, source_target_pairs={{0,1},{1,0},{2,3},{3,2},{4,5},{5,4},{6,7},{7,6},{8,9},{9,8},{10,11... | collective-permute-start | bytes 1548296 | tf_op jit(solution)/shard_map/ppermute | solution.py:252
  47.2 12.1 %collective-permute-done.12.refs_10_ = bf16[144,1152]{1,0:T(8,128)(2,1)S(1)} collective-permute-done((bf16[144,1152]{1,0:T(8,128)(2,1)S(1)}, bf16[144,1152]{1,0:T(8,128)(2,1)S(1)}, u32[]{:S(2)}, u32[]{:S(2)}) %collective-permute-start.12) | collective-permute-done | bytes 331808 | tf_op jit(solution)/shard_map/ppermute | solution.py:252
  59.3 0.5 collective-permute-start.15
  59.8 0.1 collective-permute-start.18
  59.9 0.4 collective-permute-start.19
  60.3 0.2 collective-permute-start.13
  60.6 0.4 collective-permute-done.15.refs_5_
  61.0 0.4 collective-permute-start.16
  61.3 1.5 %collective-permute-start.20 = (bf16[2,4,16,1152]{3,2,1,0:T(8,128)(2,1)S(1)}, bf16[2,4,16,1152]{3,2,1,0:T(8,128)(2,1)S(1)}, u32[]{:S(2)}, u32[]{:S(2)}) collective-permute-start(bf16[2,4,16,1152]{3,2,1,0:T(8,128)(2,1)S(1)} %get-tuple-element.74), channel_id=1, source_target_pairs={{0,6},{1,7},{2,4},{3,5},{4,2},{5,3},{6,0},{7,1},{8,14},{9,15},{10,... | collective-permute-start | bytes 884744 | tf_op jit(solution)/shard_map/ppermute | solution.py:252
  62.8 0.0 collective-permute-done.16.refs_7_
  62.8 1.1 collective-permute-start.22
  64.0 7.9 %gather.1.refs_4_.refs_5_ = bf16[3584,1152]{1,0:T(8,128)(2,1)S(1)} custom-call(s32[2]{0:T(128)S(1)} %pad_add_fusion.index_ref, bf16[432,1152]{1,0:T(8,128)(2,1)S(1)} %bitcast.14, bf16[432,1152]{1,0:T(8,128)(2,1)S(1)} %collective-permute-done.2.refs_1_, bf16[112,1152]{1,0:T(8,128)(2,1)S(1)} %collective-permute-done.refs_2_, ...), custom_call_target="tpu_custom_call" | custom-call | flops 2000000000 | bytes 8388608 | tf_op jit(solution)/shard_map/gather/pallas_call | solution.py:323
  71.9 4.3 %collective-permute-done.20.refs_3_ = bf16[2,4,16,1152]{3,2,1,0:T(8,128)(2,1)S(1)} collective-permute-done((bf16[2,4,16,1152]{3,2,1,0:T(8,128)(2,1)S(1)}, bf16[2,4,16,1152]{3,2,1,0:T(8,128)(2,1)S(1)}, u32[]{:S(2)}, u32[]{:S(2)}) %collective-permute-start.20) | collective-permute-done | bytes 294944 | tf_op jit(solution)/shard_map/ppermute | solution.py:252
  76.1 1.0 collective-permute-start.24
  77.1 0.1 collective-permute-start.23
  77.2 0.1 pad_maximum_fusion
  77.2 0.8 collective-permute-start.21
  78.0 1.0 collective-permute-done.23.refs_6_.refs_7_
  79.0 6.9 %shifted.1 = (bf16[4,4,16,640]{3,2,1,0:T(8,128)(2,1)S(1)}, bf16[4,4,16,640]{3,2,1,0:T(8,128)(2,1)S(1)}) custom-call(s32[2]{0:T(128)S(1)} %pad_add_fusion.index_ref, bf16[2,4,16,1152]{3,2,1,0:T(8,128)(2,1)S(1)} %get-tuple-element.122.refs_0_, bf16[2,4,16,1152]{3,2,1,0:T(8,128)(2,1)S(1)} %collective-permute-done.4.refs_1_, ...), custom_call_target="tpu_custom_call" | custom-call | flops 40000000000 | bytes 8388608 | tf_op jit(solution)/shard_map/shifted/pallas_call | solution.py:357
  85.9 1.2 collective-permute-start.25
  87.1 6.5 %windowed.1 = (bf16[4,4,16,640]{3,2,1,0:T(8,128)(2,1)S(1)}, bf16[4,4,16,640]{3,2,1,0:T(8,128)(2,1)S(1)}) custom-call(s32[2]{0:T(128)S(1)} %pad_add_fusion.index_ref, bf16[2,4,16,1152]{3,2,1,0:T(8,128)(2,1)S(1)} %get-tuple-element.122.refs_0_, bf16[2,4,16,1152]{3,2,1,0:T(8,128)(2,1)S(1)} %collective-permute-done.4.refs_1_, ...), custom_call_target="tpu_custom_call" | custom-call | flops 40000000000 | bytes 8388608 | tf_op jit(solution)/shard_map/windowed/pallas_call | solution.py:357
  93.6 0.0 copy-start.1
  93.6 2.2 %collective-permute-done.25.second_ref = bf16[4,4,16,640]{3,2,1,0:T(8,128)(2,1)S(1)} collective-permute-done((bf16[4,4,16,640]{3,2,1,0:T(8,128)(2,1)S(1)}, bf16[4,4,16,640]{3,2,1,0:T(8,128)(2,1)S(1)}, u32[]{:S(2)}, u32[]{:S(2)}) %collective-permute-start.25) | collective-permute-done | bytes 327712 | tf_op jit(solution)/shard_map/ppermute | solution.py:279
  95.8 1.2 collective-permute-start.27
  97.0 0.6 merge.3
  97.6 0.6 merge.2
  98.2 1.0 collective-permute-done.26.refs_11_
  99.2 0.4 collective-permute-start.28
  99.6 0.8 collective-permute-start.29
  100.4 1.0 collective-permute-start.30
  101.4 2.6 %collective-permute-start.32 = (bf16[4,16,1152]{2,1,0:T(8,128)(2,1)S(1)}, bf16[4,16,1152]{2,1,0:T(8,128)(2,1)S(1)}, u32[]{:S(2)}, u32[]{:S(2)}) collective-permute-start(bf16[4,16,1152]{2,1,0:T(8,128)(2,1)S(1)} %get-tuple-element.104), channel_id=1, source_target_pairs={{0,5},{1,4},{2,7},{3,6},{4,1},{5,0},{6,3},{7,2},{8,13},{9,12},{10,... | collective-permute-start | bytes 442376 | tf_op jit(solution)/shard_map/ppermute | solution.py:252
  104.0 0.9 collective-permute-done.29.refs_2_
  104.9 1.3 collective-permute-start.34
  106.2 4.1 %collective-permute-done.30.refs_3_ = bf16[4,16,1152]{2,1,0:T(8,128)(2,1)S(1)} collective-permute-done((bf16[4,16,1152]{2,1,0:T(8,128)(2,1)S(1)}, bf16[4,16,1152]{2,1,0:T(8,128)(2,1)S(1)}, u32[]{:S(2)}, u32[]{:S(2)}) %collective-permute-start.30) | collective-permute-done | bytes 147488 | tf_op jit(solution)/shard_map/ppermute | solution.py:252
  110.3 0.5 collective-permute-done.31.refs_4_
  110.8 4.1 %collective-permute-done.32.refs_5_ = bf16[4,16,1152]{2,1,0:T(8,128)(2,1)S(1)} collective-permute-done((bf16[4,16,1152]{2,1,0:T(8,128)(2,1)S(1)}, bf16[4,16,1152]{2,1,0:T(8,128)(2,1)S(1)}, u32[]{:S(2)}, u32[]{:S(2)}) %collective-permute-start.32) | collective-permute-done | bytes 147488 | tf_op jit(solution)/shard_map/ppermute | solution.py:252
  114.9 11.4 %collective-permute-done.33.refs_6_ = bf16[4,16,1152]{2,1,0:T(8,128)(2,1)S(1)} collective-permute-done((bf16[4,16,1152]{2,1,0:T(8,128)(2,1)S(1)}, bf16[4,16,1152]{2,1,0:T(8,128)(2,1)S(1)}, u32[]{:S(2)}, u32[]{:S(2)}) %collective-permute-start.33) | collective-permute-done | bytes 147488 | tf_op jit(solution)/shard_map/ppermute | solution.py:252
  126.3 3.3 %collective-permute-done.34.refs_7_ = bf16[4,16,1152]{2,1,0:T(8,128)(2,1)S(1)} collective-permute-done((bf16[4,16,1152]{2,1,0:T(8,128)(2,1)S(1)}, bf16[4,16,1152]{2,1,0:T(8,128)(2,1)S(1)}, u32[]{:S(2)}, u32[]{:S(2)}) %collective-permute-start.34) | collective-permute-done | bytes 147488 | tf_op jit(solution)/shard_map/ppermute | solution.py:252
  129.6 4.6 %restore.1 = bf16[4,128,1152]{2,1,0:T(8,128)(2,1)} custom-call(s32[2]{0:T(128)S(1)} %pad_add_fusion.index_ref, bf16[4,128,1152]{2,1,0:T(8,128)(2,1)S(1)} %copy-done.1, f32[4,3,1152]{2,1,0:T(4,128)S(1)} %copy.6.modulation_ref, bf16[4,16,1152]{2,1,0:T(8,128)(2,1)S(1)} %get-tuple-element.99.refs_0_, bf16[4,16,1152]{2,1,0:T(8,128)(2,1)S(1)} %collective-permute-done.28.refs_1_, ...), custom_call_target="tpu_custom_call" | custom-call | tf_op jit(solution)/shard_map/restore/pallas_call | solution.py:406
  (32 shorter events, 0.2 us)
Async XLA Ops:
  0.9 1.3 copy-start
  2.2 2.4 %copy-start.2 = (bf16[1152,432]{0,1:T(8,128)(2,1)S(1)}, bf16[1152,432]{0,1:T(8,128)(2,1)}, u32[]{:S(2)}) copy-start(bf16[1152,432]{0,1:T(8,128)(2,1)} %param.6) | copy-start | bytes 2985988
  2.2 5.2 %copy-start.3 = (bf16[1152,144]{0,1:T(8,128)(2,1)S(1)}, bf16[1152,144]{0,1:T(8,128)(2,1)}, u32[]{:S(2)}) copy-start(bf16[1152,144]{0,1:T(8,128)(2,1)} %param.7) | copy-start | bytes 995332
  3.8 3.8 %collective-permute-start.1 = (bf16[4,4,16,1152]{3,2,1,0:T(8,128)(2,1)S(1)}, bf16[4,4,16,1152]{3,2,1,0:T(8,128)(2,1)S(1)}, u32[]{:S(2)}, u32[]{:S(2)}) collective-permute-start(bf16[4,4,16,1152]{3,2,1,0:T(8,128)(2,1)S(1)} %get-tuple-element.60), channel_id=1, source_target_pairs={{0,1},{1,0},{2,3},{3,2},{4,5},{5,4},{6,7},{7,6},{8,9},{9,8},{10,11... | collective-permute-start | bytes 1769480 | tf_op jit(solution)/shard_map/ppermute | solution.py:252
  4.7 13.8 %collective-permute-start = (bf16[112,1152]{1,0:T(8,128)(2,1)S(1)}, bf16[112,1152]{1,0:T(8,128)(2,1)S(1)}, u32[]{:S(2)}, u32[]{:S(2)}) collective-permute-start(bf16[112,1152]{1,0:T(8,128)(2,1)S(1)} %dynamic-slice_bitcast_fusion), channel_id=1, source_target_pairs={{0,4},{1,5},{2,6},{3,7},{4,0},{5,1},{6,2},{7,3},{8,12},{9,13},{10,... | collective-permute-start | bytes 774152 | tf_op jit(solution)/shard_map/ppermute | solution.py:252
  7.0 12.9 %collective-permute-start.2 = (bf16[432,1152]{1,0:T(8,128)(2,1)S(1)}, bf16[432,1152]{1,0:T(8,128)(2,1)S(1)}, u32[]{:S(2)}, u32[]{:S(2)}) collective-permute-start(bf16[432,1152]{1,0:T(8,128)(2,1)S(1)} %bitcast.13), channel_id=1, source_target_pairs={{0,1},{1,0},{2,3},{3,2},{4,5},{5,4},{6,7},{7,6},{8,9},{9,8},{10,11... | collective-permute-start | bytes 2985992 | tf_op jit(solution)/shard_map/ppermute | solution.py:252
  7.4 11.1 %collective-permute-start.3 = (bf16[144,1152]{1,0:T(8,128)(2,1)S(1)}, bf16[144,1152]{1,0:T(8,128)(2,1)S(1)}, u32[]{:S(2)}, u32[]{:S(2)}) collective-permute-start(bf16[144,1152]{1,0:T(8,128)(2,1)S(1)} %bitcast.15), channel_id=1, source_target_pairs={{0,1},{1,0},{2,3},{3,2},{4,5},{5,4},{6,7},{7,6},{8,9},{9,8},{10,11... | collective-permute-start | bytes 995336 | tf_op jit(solution)/shard_map/ppermute | solution.py:252
  7.7 12.2 %collective-permute-start.4 = (bf16[2,4,16,1152]{3,2,1,0:T(8,128)(2,1)S(1)}, bf16[2,4,16,1152]{3,2,1,0:T(8,128)(2,1)S(1)}, u32[]{:S(2)}, u32[]{:S(2)}) collective-permute-start(bf16[2,4,16,1152]{3,2,1,0:T(8,128)(2,1)S(1)} %pad_maximum_fusion.4), channel_id=1, source_target_pairs={{0,2},{1,3},{2,0},{3,1},{4,6},{5,7},{6,4},{7,5},{8,10},{9,11},{10,... | collective-permute-start | bytes 884744 | tf_op jit(solution)/shard_map/ppermute | solution.py:252
  20.0 20.8 %collective-permute-start.9 = (bf16[2,2,4,16,1152]{4,3,2,1,0:T(8,128)(2,1)S(1)}, bf16[2,2,4,16,1152]{4,3,2,1,0:T(8,128)(2,1)S(1)}, u32[]{:S(2)}, u32[]{:S(2)}) collective-permute-start(bf16[2,2,4,16,1152]{4,3,2,1,0:T(8,128)(2,1)S(1)} %pad_maximum_fusion.1), channel_id=1, source_target_pairs={{0,24},{1,25},{2,26},{3,27},{4,12},{5,13},{6,14},{7,15},{8,0},{9,1... | collective-permute-start | bytes 1769480 | tf_op jit(solution)/shard_map/ppermute | solution.py:279
  22.3 18.5 %collective-permute-start.7 = (bf16[2,112,1152]{2,1,0:T(8,128)(2,1)S(1)}, bf16[2,112,1152]{2,1,0:T(8,128)(2,1)S(1)}, u32[]{:S(2)}, u32[]{:S(2)}) collective-permute-start(bf16[2,112,1152]{2,1,0:T(8,128)(2,1)S(1)} %pad_maximum_fusion.2), channel_id=1, source_target_pairs={{0,2},{1,3},{2,0},{3,1},{4,6},{5,7},{6,4},{7,5},{8,10},{9,11},{10,... | collective-permute-start | bytes 1548296 | tf_op jit(solution)/shard_map/ppermute | solution.py:252
  23.1 17.7 %collective-permute-start.8 = (bf16[2,4,16,1152]{3,2,1,0:T(8,128)(2,1)S(1)}, bf16[2,4,16,1152]{3,2,1,0:T(8,128)(2,1)S(1)}, u32[]{:S(2)}, u32[]{:S(2)}) collective-permute-start(bf16[2,4,16,1152]{3,2,1,0:T(8,128)(2,1)S(1)} %get-tuple-element.63), channel_id=1, source_target_pairs={{0,4},{1,5},{2,6},{3,7},{4,0},{5,1},{6,2},{7,3},{8,12},{9,13},{10,... | collective-permute-start | bytes 884744 | tf_op jit(solution)/shard_map/ppermute | solution.py:252
  23.9 15.7 %collective-permute-start.5 = (bf16[112,1152]{1,0:T(8,128)(2,1)S(1)}, bf16[112,1152]{1,0:T(8,128)(2,1)S(1)}, u32[]{:S(2)}, u32[]{:S(2)}) collective-permute-start(bf16[112,1152]{1,0:T(8,128)(2,1)S(1)} %collective-permute-done.refs_2_), channel_id=1, source_target_pairs={{0,8},{1,9},{2,10},{3,11},{4,12},{5,13},{6,14},{7,15},{8,0},{9,1},... | collective-permute-start | bytes 774152 | tf_op jit(solution)/shard_map/ppermute | solution.py:252
  25.1 14.5 %collective-permute-start.6 = (bf16[112,1152]{1,0:T(8,128)(2,1)S(1)}, bf16[112,1152]{1,0:T(8,128)(2,1)S(1)}, u32[]{:S(2)}, u32[]{:S(2)}) collective-permute-start(bf16[112,1152]{1,0:T(8,128)(2,1)S(1)} %collective-permute-done.refs_2_), channel_id=1, source_target_pairs={{0,16},{1,17},{2,18},{3,19},{4,20},{5,21},{6,22},{7,23},{8,24},{9,... | collective-permute-start | bytes 774152 | tf_op jit(solution)/shard_map/ppermute | solution.py:252
  40.8 19.0 %collective-permute-start.10 = (bf16[2,112,1152]{2,1,0:T(8,128)(2,1)S(1)}, bf16[2,112,1152]{2,1,0:T(8,128)(2,1)S(1)}, u32[]{:S(2)}, u32[]{:S(2)}) collective-permute-start(bf16[2,112,1152]{2,1,0:T(8,128)(2,1)S(1)} %collective-permute-done.7.refs_8_), channel_id=1, source_target_pairs={{0,8},{1,9},{2,10},{3,11},{4,12},{5,13},{6,14},{7,15},{8,0},{9,1},... | collective-permute-start | bytes 1548296 | tf_op jit(solution)/shard_map/ppermute | solution.py:252
  43.0 16.8 %collective-permute-start.11 = (bf16[2,112,1152]{2,1,0:T(8,128)(2,1)S(1)}, bf16[2,112,1152]{2,1,0:T(8,128)(2,1)S(1)}, u32[]{:S(2)}, u32[]{:S(2)}) collective-permute-start(bf16[2,112,1152]{2,1,0:T(8,128)(2,1)S(1)} %collective-permute-done.7.refs_8_), channel_id=1, source_target_pairs={{0,16},{1,17},{2,18},{3,19},{4,20},{5,21},{6,22},{7,23},{8,24},{9,... | collective-permute-start | bytes 1548296 | tf_op jit(solution)/shard_map/ppermute | solution.py:252
  44.2 15.1 %collective-permute-start.12 = (bf16[144,1152]{1,0:T(8,128)(2,1)S(1)}, bf16[144,1152]{1,0:T(8,128)(2,1)S(1)}, u32[]{:S(2)}, u32[]{:S(2)}) collective-permute-start(bf16[144,1152]{1,0:T(8,128)(2,1)S(1)} %bitcast.16), channel_id=1, source_target_pairs={{0,4},{1,5},{2,6},{3,7},{4,0},{5,1},{6,2},{7,3},{8,12},{9,13},{10,... | collective-permute-start | bytes 995336 | tf_op jit(solution)/shard_map/ppermute | solution.py:252
  45.6 15.8 %collective-permute-start.17 = (bf16[2,112,1152]{2,1,0:T(8,128)(2,1)S(1)}, bf16[2,112,1152]{2,1,0:T(8,128)(2,1)S(1)}, u32[]{:S(2)}, u32[]{:S(2)}) collective-permute-start(bf16[2,112,1152]{2,1,0:T(8,128)(2,1)S(1)} %collective-permute-done.7.refs_8_), channel_id=1, source_target_pairs={{0,1},{1,0},{2,3},{3,2},{4,5},{5,4},{6,7},{7,6},{8,9},{9,8},{10,11... | collective-permute-start | bytes 1548296 | tf_op jit(solution)/shard_map/ppermute | solution.py:252
  47.2 13.2 %collective-permute-start.14 = (bf16[112,1152]{1,0:T(8,128)(2,1)S(1)}, bf16[112,1152]{1,0:T(8,128)(2,1)S(1)}, u32[]{:S(2)}, u32[]{:S(2)}) collective-permute-start(bf16[112,1152]{1,0:T(8,128)(2,1)S(1)} %collective-permute-done.refs_2_), channel_id=1, source_target_pairs={{0,1},{1,0},{2,3},{3,2},{4,5},{5,4},{6,7},{7,6},{8,9},{9,8},{10,11... | collective-permute-start | bytes 774152 | tf_op jit(solution)/shard_map/ppermute | solution.py:252
  59.3 1.6 %collective-permute-start.15 = (bf16[112,1152]{1,0:T(8,128)(2,1)S(1)}, bf16[112,1152]{1,0:T(8,128)(2,1)S(1)}, u32[]{:S(2)}, u32[]{:S(2)}) collective-permute-start(bf16[112,1152]{1,0:T(8,128)(2,1)S(1)} %collective-permute-done.5.refs_4_), channel_id=1, source_target_pairs={{0,1},{1,0},{2,3},{3,2},{4,5},{5,4},{6,7},{7,6},{8,9},{9,8},{10,11... | collective-permute-start | bytes 774152 | tf_op jit(solution)/shard_map/ppermute | solution.py:252
  59.8 4.1 %collective-permute-start.18 = (bf16[2,112,1152]{2,1,0:T(8,128)(2,1)S(1)}, bf16[2,112,1152]{2,1,0:T(8,128)(2,1)S(1)}, u32[]{:S(2)}, u32[]{:S(2)}) collective-permute-start(bf16[2,112,1152]{2,1,0:T(8,128)(2,1)S(1)} %collective-permute-done.10.refs_10_), channel_id=1, source_target_pairs={{0,1},{1,0},{2,3},{3,2},{4,5},{5,4},{6,7},{7,6},{8,9},{9,8},{10,11... | collective-permute-start | bytes 1548296 | tf_op jit(solution)/shard_map/ppermute | solution.py:252
  59.9 4.1 %collective-permute-start.19 = (bf16[2,112,1152]{2,1,0:T(8,128)(2,1)S(1)}, bf16[2,112,1152]{2,1,0:T(8,128)(2,1)S(1)}, u32[]{:S(2)}, u32[]{:S(2)}) collective-permute-start(bf16[2,112,1152]{2,1,0:T(8,128)(2,1)S(1)} %collective-permute-done.11.refs_12_), channel_id=1, source_target_pairs={{0,1},{1,0},{2,3},{3,2},{4,5},{5,4},{6,7},{7,6},{8,9},{9,8},{10,11... | collective-permute-start | bytes 1548296 | tf_op jit(solution)/shard_map/ppermute | solution.py:252
  60.3 15.8 %collective-permute-start.13 = (bf16[2,112,1152]{2,1,0:T(8,128)(2,1)S(1)}, bf16[2,112,1152]{2,1,0:T(8,128)(2,1)S(1)}, u32[]{:S(2)}, u32[]{:S(2)}) collective-permute-start(bf16[2,112,1152]{2,1,0:T(8,128)(2,1)S(1)} %collective-permute-done.10.refs_10_), channel_id=1, source_target_pairs={{0,16},{1,17},{2,18},{3,19},{4,20},{5,21},{6,22},{7,23},{8,24},{9,... | collective-permute-start | bytes 1548296 | tf_op jit(solution)/shard_map/ppermute | solution.py:252
  61.0 1.9 %collective-permute-start.16 = (bf16[112,1152]{1,0:T(8,128)(2,1)S(1)}, bf16[112,1152]{1,0:T(8,128)(2,1)S(1)}, u32[]{:S(2)}, u32[]{:S(2)}) collective-permute-start(bf16[112,1152]{1,0:T(8,128)(2,1)S(1)} %collective-permute-done.6.refs_6_), channel_id=1, source_target_pairs={{0,1},{1,0},{2,3},{3,2},{4,5},{5,4},{6,7},{7,6},{8,9},{9,8},{10,11... | collective-permute-start | bytes 774152 | tf_op jit(solution)/shard_map/ppermute | solution.py:252
  61.3 14.8 %collective-permute-start.20 = (bf16[2,4,16,1152]{3,2,1,0:T(8,128)(2,1)S(1)}, bf16[2,4,16,1152]{3,2,1,0:T(8,128)(2,1)S(1)}, u32[]{:S(2)}, u32[]{:S(2)}) collective-permute-start(bf16[2,4,16,1152]{3,2,1,0:T(8,128)(2,1)S(1)} %get-tuple-element.74), channel_id=1, source_target_pairs={{0,6},{1,7},{2,4},{3,5},{4,2},{5,3},{6,0},{7,1},{8,14},{9,15},{10,... | collective-permute-start | bytes 884744 | tf_op jit(solution)/shard_map/ppermute | solution.py:252
  62.8 14.3 %collective-permute-start.22 = (bf16[112,1152]{1,0:T(8,128)(2,1)S(1)}, bf16[112,1152]{1,0:T(8,128)(2,1)S(1)}, u32[]{:S(2)}, u32[]{:S(2)}) collective-permute-start(bf16[112,1152]{1,0:T(8,128)(2,1)S(1)} %collective-permute-done.6.refs_6_), channel_id=1, source_target_pairs={{0,8},{1,9},{2,10},{3,11},{4,12},{5,13},{6,14},{7,15},{8,0},{9,1},... | collective-permute-start | bytes 774152 | tf_op jit(solution)/shard_map/ppermute | solution.py:252
  76.1 2.9 %collective-permute-start.24 = (bf16[2,112,1152]{2,1,0:T(8,128)(2,1)S(1)}, bf16[2,112,1152]{2,1,0:T(8,128)(2,1)S(1)}, u32[]{:S(2)}, u32[]{:S(2)}) collective-permute-start(bf16[2,112,1152]{2,1,0:T(8,128)(2,1)S(1)} %collective-permute-done.13.refs_7_.refs_8_), channel_id=1, source_target_pairs={{0,1},{1,0},{2,3},{3,2},{4,5},{5,4},{6,7},{7,6},{8,9},{9,8},{10,11... | collective-permute-start | bytes 1548296 | tf_op jit(solution)/shard_map/ppermute | solution.py:252
  77.1 1.9 %collective-permute-start.23 = (bf16[112,1152]{1,0:T(8,128)(2,1)S(1)}, bf16[112,1152]{1,0:T(8,128)(2,1)S(1)}, u32[]{:S(2)}, u32[]{:S(2)}) collective-permute-start(bf16[112,1152]{1,0:T(8,128)(2,1)S(1)} %collective-permute-done.22.refs_5_.refs_6_), channel_id=1, source_target_pairs={{0,1},{1,0},{2,3},{3,2},{4,5},{5,4},{6,7},{7,6},{8,9},{9,8},{10,11... | collective-permute-start | bytes 774152 | tf_op jit(solution)/shard_map/ppermute | solution.py:252
  77.2 16.4 %collective-permute-start.21 = (bf16[2,144,1152]{2,1,0:T(8,128)(2,1)S(1)}, bf16[2,144,1152]{2,1,0:T(8,128)(2,1)S(1)}, u32[]{:S(2)}, u32[]{:S(2)}) collective-permute-start(bf16[2,144,1152]{2,1,0:T(8,128)(2,1)S(1)} %pad_maximum_fusion), channel_id=1, source_target_pairs={{0,2},{1,3},{2,0},{3,1},{4,6},{5,7},{6,4},{7,5},{8,10},{9,11},{10,... | collective-permute-start | bytes 1990664 | tf_op jit(solution)/shard_map/ppermute | solution.py:252
  85.9 9.9 %collective-permute-start.25 = (bf16[4,4,16,640]{3,2,1,0:T(8,128)(2,1)S(1)}, bf16[4,4,16,640]{3,2,1,0:T(8,128)(2,1)S(1)}, u32[]{:S(2)}, u32[]{:S(2)}) collective-permute-start(bf16[4,4,16,640]{3,2,1,0:T(8,128)(2,1)S(1)} %get-tuple-element.84), channel_id=1, source_target_pairs={{0,8},{1,9},{2,10},{3,11},{4,28},{5,29},{6,30},{7,31},{8,16},{9,17... | collective-permute-start | bytes 983048 | tf_op jit(solution)/shard_map/ppermute | solution.py:279
  93.6 36.0 %copy-start.1 = (bf16[4,128,1152]{2,1,0:T(8,128)(2,1)S(1)}, bf16[4,128,1152]{2,1,0:T(8,128)(2,1)}, u32[]{:S(2)}) copy-start(bf16[4,128,1152]{2,1,0:T(8,128)(2,1)} %tokens_ref.3) | copy-start | bytes 3538948
  95.8 3.4 %collective-permute-start.27 = (bf16[2,144,1152]{2,1,0:T(8,128)(2,1)S(1)}, bf16[2,144,1152]{2,1,0:T(8,128)(2,1)S(1)}, u32[]{:S(2)}, u32[]{:S(2)}) collective-permute-start(bf16[2,144,1152]{2,1,0:T(8,128)(2,1)S(1)} %collective-permute-done.21.refs_12_), channel_id=1, source_target_pairs={{0,1},{1,0},{2,3},{3,2},{4,5},{5,4},{6,7},{7,6},{8,9},{9,8},{10,11... | collective-permute-start | bytes 1990664 | tf_op jit(solution)/shard_map/ppermute | solution.py:252
  97.0 2.2 %collective-permute-start.26 = (bf16[144,1152]{1,0:T(8,128)(2,1)S(1)}, bf16[144,1152]{1,0:T(8,128)(2,1)S(1)}, u32[]{:S(2)}, u32[]{:S(2)}) collective-permute-start(bf16[144,1152]{1,0:T(8,128)(2,1)S(1)} %collective-permute-done.12.refs_10_), channel_id=1, source_target_pairs={{0,1},{1,0},{2,3},{3,2},{4,5},{5,4},{6,7},{7,6},{8,9},{9,8},{10,11... | collective-permute-start | bytes 995336 | tf_op jit(solution)/shard_map/ppermute | solution.py:252
  99.2 4.8 %collective-permute-start.28 = (bf16[4,16,1152]{2,1,0:T(8,128)(2,1)S(1)}, bf16[4,16,1152]{2,1,0:T(8,128)(2,1)S(1)}, u32[]{:S(2)}, u32[]{:S(2)}) collective-permute-start(bf16[4,16,1152]{2,1,0:T(8,128)(2,1)S(1)} %get-tuple-element.100), channel_id=1, source_target_pairs={{0,1},{1,0},{2,3},{3,2},{4,5},{5,4},{6,7},{7,6},{8,9},{9,8},{10,11... | collective-permute-start | bytes 442376 | tf_op jit(solution)/shard_map/ppermute | solution.py:252
  99.6 5.3 %collective-permute-start.29 = (bf16[4,16,1152]{2,1,0:T(8,128)(2,1)S(1)}, bf16[4,16,1152]{2,1,0:T(8,128)(2,1)S(1)}, u32[]{:S(2)}, u32[]{:S(2)}) collective-permute-start(bf16[4,16,1152]{2,1,0:T(8,128)(2,1)S(1)} %get-tuple-element.101), channel_id=1, source_target_pairs={{0,2},{1,3},{2,0},{3,1},{4,6},{5,7},{6,4},{7,5},{8,10},{9,11},{10,... | collective-permute-start | bytes 442376 | tf_op jit(solution)/shard_map/ppermute | solution.py:252
  100.4 9.9 %collective-permute-start.30 = (bf16[4,16,1152]{2,1,0:T(8,128)(2,1)S(1)}, bf16[4,16,1152]{2,1,0:T(8,128)(2,1)S(1)}, u32[]{:S(2)}, u32[]{:S(2)}) collective-permute-start(bf16[4,16,1152]{2,1,0:T(8,128)(2,1)S(1)} %get-tuple-element.102), channel_id=1, source_target_pairs={{0,3},{1,2},{2,1},{3,0},{4,7},{5,6},{6,5},{7,4},{8,11},{9,10},{10,... | collective-permute-start | bytes 442376 | tf_op jit(solution)/shard_map/ppermute | solution.py:252
  101.4 9.5 %collective-permute-start.31 = (bf16[4,16,1152]{2,1,0:T(8,128)(2,1)S(1)}, bf16[4,16,1152]{2,1,0:T(8,128)(2,1)S(1)}, u32[]{:S(2)}, u32[]{:S(2)}) collective-permute-start(bf16[4,16,1152]{2,1,0:T(8,128)(2,1)S(1)} %get-tuple-element.103), channel_id=1, source_target_pairs={{0,4},{1,5},{2,6},{3,7},{4,0},{5,1},{6,2},{7,3},{8,12},{9,13},{10,... | collective-permute-start | bytes 442376 | tf_op jit(solution)/shard_map/ppermute | solution.py:252
  101.4 13.5 %collective-permute-start.32 = (bf16[4,16,1152]{2,1,0:T(8,128)(2,1)S(1)}, bf16[4,16,1152]{2,1,0:T(8,128)(2,1)S(1)}, u32[]{:S(2)}, u32[]{:S(2)}) collective-permute-start(bf16[4,16,1152]{2,1,0:T(8,128)(2,1)S(1)} %get-tuple-element.104), channel_id=1, source_target_pairs={{0,5},{1,4},{2,7},{3,6},{4,1},{5,0},{6,3},{7,2},{8,13},{9,12},{10,... | collective-permute-start | bytes 442376 | tf_op jit(solution)/shard_map/ppermute | solution.py:252
  104.0 22.3 %collective-permute-start.33 = (bf16[4,16,1152]{2,1,0:T(8,128)(2,1)S(1)}, bf16[4,16,1152]{2,1,0:T(8,128)(2,1)S(1)}, u32[]{:S(2)}, u32[]{:S(2)}) collective-permute-start(bf16[4,16,1152]{2,1,0:T(8,128)(2,1)S(1)} %get-tuple-element.105), channel_id=1, source_target_pairs={{0,6},{1,7},{2,4},{3,5},{4,2},{5,3},{6,0},{7,1},{8,14},{9,15},{10,... | collective-permute-start | bytes 442376 | tf_op jit(solution)/shard_map/ppermute | solution.py:252
  104.9 24.7 %collective-permute-start.34 = (bf16[4,16,1152]{2,1,0:T(8,128)(2,1)S(1)}, bf16[4,16,1152]{2,1,0:T(8,128)(2,1)S(1)}, u32[]{:S(2)}, u32[]{:S(2)}) collective-permute-start(bf16[4,16,1152]{2,1,0:T(8,128)(2,1)S(1)} %get-tuple-element.106), channel_id=1, source_target_pairs={{0,7},{1,6},{2,5},{3,4},{4,3},{5,2},{6,1},{7,0},{8,15},{9,14},{10,... | collective-permute-start | bytes 442376 | tf_op jit(solution)/shard_map/ppermute | solution.py:252

commit v5 on v4

--- a/solution.py
+++ b/solution.py
@@ -34,7 +34,7 @@
             centered = values - average
             variance = jnp.mean(centered * centered, axis=-1, keepdims=True)
             normed = centered * lax.rsqrt(variance + EPSILON)
-            result = normed * (1.0 + modulation_ref[f, 1:2, :]) + modulation_ref[f, 0:1, :]
+            result = normed * (1.0 + modulation_ref[1, f : f + 1, :]) + modulation_ref[0, f : f + 1, :]
             for t in range(width // LANES):
                 mixed[t, pl.ds(f, positions, stride=frames), :] = result[:, t * LANES : (t + 1) * LANES]
         for t in range(width // LANES):
@@ -180,26 +180,27 @@
     lax.fori_loop(0, groups, one_group, 0, unroll=True)
 
 
-def merge_kernel(first_d, index_ref, first_ref, second_ref, *out_refs):
+def merge_kernel(first_z, index_ref, first_ref, second_ref, *out_refs):
     index = index_ref[0]
+    lanes = first_ref.shape[-1]
     for n, out_ref in enumerate(out_refs):
-        at = lax.rem(lax.bitwise_xor(index, first_d + n), len(out_refs))
-        first, second = first_ref[:, at], second_ref[:, at]
-        lanes = first.shape[-1]
         cut = 2 * lanes - out_ref.shape[-1]
-        if cut:
-            out_ref[..., : lanes - cut] = first[..., : lanes - cut]
-            out_ref[..., lanes - cut : lanes] = first[..., lanes - cut :] + second[..., :cut]
-            out_ref[..., lanes:] = second[..., cut:]
-        else:
-            out_ref[..., :lanes] = first
-            out_ref[..., lanes:] = second
+        for sibling in range(2):
+            at = lax.rem(lax.bitwise_xor(index, 2 * (first_z + n) + sibling), 2 * len(out_refs))
+            first, second = first_ref[:, at], second_ref[:, at]
+            if cut:
+                out_ref[sibling, ..., : lanes - cut] = first[..., : lanes - cut]
+                out_ref[sibling, ..., lanes - cut : lanes] = first[..., lanes - cut :] + second[..., :cut]
+                out_ref[sibling, ..., lanes:] = second[..., cut:]
+            else:
+                out_ref[sibling, ..., :lanes] = first
+                out_ref[sibling, ..., lanes:] = second
 
 
 def restore_kernel(plan, index_ref, tokens_ref, modulation_ref, *refs):
     count, moves = plan["count"], plan["moves"]
     refs = list(refs)
-    in_refs = [refs.pop(0) for _ in range(count)]
+    in_refs = [refs.pop(0).at[n % 2] for n in range(count)]
     w_refs = [refs.pop(0) for _ in range(plan["weights"])]
     out_ref, wall, mixed, sems = refs
     index = index_ref[0]
@@ -229,7 +230,7 @@
             values = tokens_ref[f, pl.ds(start, positions), :].astype(jnp.float32)
             rows_of = pl.ds(d * block_rows + f, positions, stride=frames)
             update = jnp.concatenate([mixed[t, rows_of, :] for t in range(width // LANES)], axis=1)
-            result = values + modulation_ref[f, 2:3, :] * update
+            result = values + modulation_ref[2, f : f + 1, :] * update
             out_ref[f, pl.ds(start, positions), :] = result.astype(out_ref.dtype)
 
 
@@ -242,6 +243,7 @@
     groups = block_rows // ROWS
     block = jax.ShapeDtypeStruct((groups, ROWS, width), jnp.bfloat16)
     own_index = jnp.stack([index, slab]).astype(jnp.int32)
+    kinds = jnp.transpose(modulation, (1, 0, 2))
     smem = pl.BlockSpec(memory_space=pltpu.SMEM)
     vmem = pl.BlockSpec(memory_space=pltpu.VMEM)
     anywhere = pl.BlockSpec(memory_space=pl.ANY)
@@ -269,7 +271,7 @@
         scratch_shapes=[pltpu.VMEM((width // LANES, block_rows, LANES), jnp.float32)],
         compiler_params=params,
         name="norm",
-    )(own_index, video_tokens, modulation)
+    )(own_index, video_tokens, kinds)
     swapped = hop(give, 1)
     pair = [jnp.stack([keep[z], swapped[z]]) for z in range(chips)]
 
@@ -380,28 +382,31 @@
         out_rest = hop(jnp.stack([narrow, out_far]), 2)
     second_near = to_neighbour(second_near, 1)
     first_near, first_far = attention(0, blocks)
-    if shared:
-        out_rest, first_near, first_far, second_near = tie((out_rest, first_near, first_far, second_near))
-        out_operands = [narrow, narrow_other, out_far, hop(out_far, 1), out_rest, hop(out_rest, 1)]
-        out_moves = [(0, (), (0,)), (1, (), (1,)), (2, (), (4,)), (3, (), (5,)), (4, (0,), (2,)), (5, (0,), (3,)),
-                     (4, (1,), (6,)), (5, (1,), (7,))]
-
-    def merged(first_d, first, second, flops):
+    def merged(first_z, first, second, flops):
         return pl.pallas_call(
-            functools.partial(merge_kernel, first_d),
-            out_shape=[block] * middle,
+            functools.partial(merge_kernel, first_z),
+            out_shape=[jax.ShapeDtypeStruct((2,) + block.shape, block.dtype)] * (chips // 2),
             in_specs=[smem] + [vmem] * 2,
-            out_specs=[vmem] * middle,
+            out_specs=[vmem] * (chips // 2),
             compiler_params=params,
             cost_estimate=pl.CostEstimate(flops=flops, bytes_accessed=4 * 1024 * 1024, transcendentals=0),
             name="merge",
         )(own_index, first, second)
 
-    sent_far = merged(middle, first_far, second_far, 0)
+    sent_far = merged(chips // 2, first_far, second_far, 0)
     sent_near = merged(0, first_near, second_near, 0)
-    sent_far, sent_near, out_operands = tie((sent_far, sent_near, out_operands))
-    returned = [sent_near[0]] + [hop(sent_near[d], d) for d in range(1, middle)]
-    returned += [hop(value, middle + n) for n, value in enumerate(sent_far)]
+    sent = sent_near + sent_far
+    arrived = [hop(sent[z], 2 * z) if z else sent[z] for z in range(chips)]
+    if shared:
+        out_rest, arrived = tie((out_rest, arrived))
+    returned = []
+    for value in arrived:
+        returned += [value, hop(value, 1)]
+    if shared:
+        out_operands = [narrow, narrow_other, out_far, hop(out_far, 1), out_rest, hop(out_rest, 1)]
+        out_moves = [(0, (), (0,)), (1, (), (1,)), (2, (), (4,)), (3, (), (5,)), (4, (0,), (2,)), (5, (0,), (3,)),
+                     (4, (1,), (6,)), (5, (1,), (7,))]
+
     plan = dict(count=count, weights=len(out_operands), moves=out_moves)
     return pl.pallas_call(
         functools.partial(restore_kernel, plan),
@@ -415,7 +420,7 @@
         ],
         compiler_params=params,
         name="restore",
-    )(own_index, video_tokens, modulation, *returned, *out_operands)
+    )(own_index, video_tokens, kinds, *returned, *out_operands)
 
 
 def solution(mesh):

time: 135 us -> 131 us (0.970)
  waiting for transfers between devices: 72.6 us -> 69.9 us
    ppermute x2, waiting for transfers between devices: 2.2 us -> 0.52 us  [to_neighbour(): return lax.ppermute(value, ('slab', 'seq'), pairs)]
  transfers between devices with their start and end apart: 35 -> 35, of which waited for: 16 -> 15; matrix products, arithmetic and copies ran while one was open for 0% -> 0% of each run, Pallas kernels for 17% -> 17%
where the time goes in v5:
time: 131 us
  waiting for transfers between devices  69.9 us (53%)
  starting transfers between devices  29.2 us (22%)
  Pallas kernels  28.8 us (22%)
  local copies, waits for them, and re-layouts  2.26 us (2%)
    ppermute x33, waiting for transfers between devices, hop(): return lax.ppermute(value, ('slab', 'seq'), pairs)  69.4 us
    ppermute x33, starting transfers between devices, hop(): return lax.ppermute(value, ('slab', 'seq'), pairs)  25.8 us
    pallas_call x2, Pallas kernels, attention(): pl.pallas_call(functools.partial(block_kernel, plan, frames), out_shape=[...  13.4 us
    pallas_call x1, Pallas kernels, per_device(): pl.pallas_call(functools.partial(gather_kernel, plan), out_shape=jax.Shap...  7.9 us
    pallas_call x1, Pallas kernels, per_device(): pl.pallas_call(functools.partial(restore_kernel, plan), out_shape=jax.Sha...  4.62 us
    ppermute x2, starting transfers between devices, to_neighbour(): return lax.ppermute(value, ('slab', 'seq'), pairs)  3.4 us
  transfers between devices with their start and end apart: 35, of which 15 were waited for; matrix products, arithmetic and copies ran while one was open for 0% of the time, Pallas kernels for 17%

profile of v5, /device:TPU:9, one launch (start us, length us, event | category | flops | bytes accessed | tf_op | source)
XLA Modules:
  0.0 130.9 jit_solution(5445624323012392884)
XLA Ops:
  0.0 0.1 pad_add_fusion.index_ref
  0.1 1.3 copy-done
  1.3 0.8 copy-done.4
  2.2 1.7 %norm.1 = (bf16[4,4,16,1152]{3,2,1,0:T(8,128)(2,1)S(1)}, bf16[4,4,16,1152]{3,2,1,0:T(8,128)(2,1)S(1)}) custom-call(s32[2]{0:T(128)S(1)} %pad_add_fusion.index_ref, bf16[4,128,1152]{2,1,0:T(8,128)(2,1)S(1)} %copy-done, f32[3,4,1152]{2,1,0:T(4,128)S(1)} %bitcast.23), custom_call_target="tpu_custom_call" | custom-call | tf_op jit(solution)/shard_map/norm/pallas_call | solution.py:266
  3.8 0.7 collective-permute-start.1
  4.6 0.1 dynamic-slice_bitcast_fusion
  4.7 2.4 %collective-permute-start = (bf16[112,1152]{1,0:T(8,128)(2,1)S(1)}, bf16[112,1152]{1,0:T(8,128)(2,1)S(1)}, u32[]{:S(2)}, u32[]{:S(2)}) collective-permute-start(bf16[112,1152]{1,0:T(8,128)(2,1)S(1)} %dynamic-slice_bitcast_fusion), channel_id=1, source_target_pairs={{0,4},{1,5},{2,6},{3,7},{4,0},{5,1},{6,2},{7,3},{8,12},{9,13},{10,... | collective-permute-start | bytes 774152 | tf_op jit(solution)/shard_map/ppermute | solution.py:254
  7.0 0.3 collective-permute-start.2
  7.3 0.2 collective-permute-start.3
  7.7 0.2 collective-permute-start.4
  8.0 0.1 pad_maximum_fusion.5
  8.1 10.4 %collective-permute-done.refs_2_ = bf16[112,1152]{1,0:T(8,128)(2,1)S(1)} collective-permute-done((bf16[112,1152]{1,0:T(8,128)(2,1)S(1)}, bf16[112,1152]{1,0:T(8,128)(2,1)S(1)}, u32[]{:S(2)}, u32[]{:S(2)}) %collective-permute-start) | collective-permute-done | bytes 258080 | tf_op jit(solution)/shard_map/ppermute | solution.py:254
  18.5 1.4 %collective-permute-done.4.refs_1_ = bf16[2,4,16,1152]{3,2,1,0:T(8,128)(2,1)S(1)} collective-permute-done((bf16[2,4,16,1152]{3,2,1,0:T(8,128)(2,1)S(1)}, bf16[2,4,16,1152]{3,2,1,0:T(8,128)(2,1)S(1)}, u32[]{:S(2)}, u32[]{:S(2)}) %collective-permute-start.4) | collective-permute-done | bytes 294944 | tf_op jit(solution)/shard_map/ppermute | solution.py:254
  19.9 0.1 pad_maximum_fusion.1
  20.0 2.2 %collective-permute-start.9 = (bf16[2,2,4,16,1152]{4,3,2,1,0:T(8,128)(2,1)S(1)}, bf16[2,2,4,16,1152]{4,3,2,1,0:T(8,128)(2,1)S(1)}, u32[]{:S(2)}, u32[]{:S(2)}) collective-permute-start(bf16[2,2,4,16,1152]{4,3,2,1,0:T(8,128)(2,1)S(1)} %pad_maximum_fusion.1), channel_id=1, source_target_pairs={{0,24},{1,25},{2,26},{3,27},{4,12},{5,13},{6,14},{7,15},{8,0},{9,1... | collective-permute-start | bytes 1769480 | tf_op jit(solution)/shard_map/ppermute | solution.py:281
  22.2 0.1 pad_maximum_fusion.2
  22.3 0.8 collective-permute-start.7
  23.0 0.9 collective-permute-start.8
  23.9 1.2 collective-permute-start.5
  25.1 0.2 collective-permute-start.6
  25.4 14.2 %collective-permute-done.5.refs_4_ = bf16[112,1152]{1,0:T(8,128)(2,1)S(1)} collective-permute-done((bf16[112,1152]{1,0:T(8,128)(2,1)S(1)}, bf16[112,1152]{1,0:T(8,128)(2,1)S(1)}, u32[]{:S(2)}, u32[]{:S(2)}) %collective-permute-start.5) | collective-permute-done | bytes 258080 | tf_op jit(solution)/shard_map/ppermute | solution.py:254
  39.6 1.2 collective-permute-done.8.refs_2_
  40.8 2.2 %collective-permute-start.10 = (bf16[2,112,1152]{2,1,0:T(8,128)(2,1)S(1)}, bf16[2,112,1152]{2,1,0:T(8,128)(2,1)S(1)}, u32[]{:S(2)}, u32[]{:S(2)}) collective-permute-start(bf16[2,112,1152]{2,1,0:T(8,128)(2,1)S(1)} %collective-permute-done.7.refs_8_), channel_id=1, source_target_pairs={{0,8},{1,9},{2,10},{3,11},{4,12},{5,13},{6,14},{7,15},{8,0},{9,1},... | collective-permute-start | bytes 1548296 | tf_op jit(solution)/shard_map/ppermute | solution.py:254
  43.0 1.2 collective-permute-start.11
  44.2 1.3 %collective-permute-start.12 = (bf16[144,1152]{1,0:T(8,128)(2,1)S(1)}, bf16[144,1152]{1,0:T(8,128)(2,1)S(1)}, u32[]{:S(2)}, u32[]{:S(2)}) collective-permute-start(bf16[144,1152]{1,0:T(8,128)(2,1)S(1)} %bitcast.17), channel_id=1, source_target_pairs={{0,4},{1,5},{2,6},{3,7},{4,0},{5,1},{6,2},{7,3},{8,12},{9,13},{10,... | collective-permute-start | bytes 995336 | tf_op jit(solution)/shard_map/ppermute | solution.py:254
  45.6 1.6 %collective-permute-start.17 = (bf16[2,112,1152]{2,1,0:T(8,128)(2,1)S(1)}, bf16[2,112,1152]{2,1,0:T(8,128)(2,1)S(1)}, u32[]{:S(2)}, u32[]{:S(2)}) collective-permute-start(bf16[2,112,1152]{2,1,0:T(8,128)(2,1)S(1)} %collective-permute-done.7.refs_8_), channel_id=1, source_target_pairs={{0,1},{1,0},{2,3},{3,2},{4,5},{5,4},{6,7},{7,6},{8,9},{9,8},{10,11... | collective-permute-start | bytes 1548296 | tf_op jit(solution)/shard_map/ppermute | solution.py:254
  47.2 12.1 %collective-permute-done.12.refs_10_ = bf16[144,1152]{1,0:T(8,128)(2,1)S(1)} collective-permute-done((bf16[144,1152]{1,0:T(8,128)(2,1)S(1)}, bf16[144,1152]{1,0:T(8,128)(2,1)S(1)}, u32[]{:S(2)}, u32[]{:S(2)}) %collective-permute-start.12) | collective-permute-done | bytes 331808 | tf_op jit(solution)/shard_map/ppermute | solution.py:254
  59.3 0.5 collective-permute-start.15
  59.8 0.1 collective-permute-start.18
  59.9 0.4 collective-permute-start.19
  60.3 0.2 collective-permute-start.13
  60.6 0.4 collective-permute-done.15.refs_5_
  61.0 0.4 collective-permute-start.16
  61.3 1.5 %collective-permute-start.20 = (bf16[2,4,16,1152]{3,2,1,0:T(8,128)(2,1)S(1)}, bf16[2,4,16,1152]{3,2,1,0:T(8,128)(2,1)S(1)}, u32[]{:S(2)}, u32[]{:S(2)}) collective-permute-start(bf16[2,4,16,1152]{3,2,1,0:T(8,128)(2,1)S(1)} %get-tuple-element.57), channel_id=1, source_target_pairs={{0,6},{1,7},{2,4},{3,5},{4,2},{5,3},{6,0},{7,1},{8,14},{9,15},{10,... | collective-permute-start | bytes 884744 | tf_op jit(solution)/shard_map/ppermute | solution.py:254
  62.8 0.0 collective-permute-done.16.refs_7_
  62.8 1.1 collective-permute-start.22
  64.0 7.9 %gather.1.refs_4_.refs_5_ = bf16[3584,1152]{1,0:T(8,128)(2,1)S(1)} custom-call(s32[2]{0:T(128)S(1)} %pad_add_fusion.index_ref, bf16[432,1152]{1,0:T(8,128)(2,1)S(1)} %bitcast.15, bf16[432,1152]{1,0:T(8,128)(2,1)S(1)} %collective-permute-done.2.refs_1_, bf16[112,1152]{1,0:T(8,128)(2,1)S(1)} %collective-permute-done.refs_2_, ...), custom_call_target="tpu_custom_call" | custom-call | flops 2000000000 | bytes 8388608 | tf_op jit(solution)/shard_map/gather/pallas_call | solution.py:325
  71.9 4.3 %collective-permute-done.20.refs_3_ = bf16[2,4,16,1152]{3,2,1,0:T(8,128)(2,1)S(1)} collective-permute-done((bf16[2,4,16,1152]{3,2,1,0:T(8,128)(2,1)S(1)}, bf16[2,4,16,1152]{3,2,1,0:T(8,128)(2,1)S(1)}, u32[]{:S(2)}, u32[]{:S(2)}) %collective-permute-start.20) | collective-permute-done | bytes 294944 | tf_op jit(solution)/shard_map/ppermute | solution.py:254
  76.1 1.0 collective-permute-start.24
  77.1 0.1 collective-permute-start.23
  77.2 0.1 pad_maximum_fusion
  77.2 0.8 collective-permute-start.21
  78.0 1.0 collective-permute-done.23.refs_6_.refs_7_
  79.0 6.9 %shifted.1 = (bf16[4,4,16,640]{3,2,1,0:T(8,128)(2,1)S(1)}, bf16[4,4,16,640]{3,2,1,0:T(8,128)(2,1)S(1)}) custom-call(s32[2]{0:T(128)S(1)} %pad_add_fusion.index_ref, bf16[2,4,16,1152]{3,2,1,0:T(8,128)(2,1)S(1)} %get-tuple-element.88.refs_0_, bf16[2,4,16,1152]{3,2,1,0:T(8,128)(2,1)S(1)} %collective-permute-done.4.refs_1_, ...), custom_call_target="tpu_custom_call" | custom-call | flops 40000000000 | bytes 8388608 | tf_op jit(solution)/shard_map/shifted/pallas_call | solution.py:359
  85.9 1.2 collective-permute-start.25
  87.1 6.5 %windowed.1 = (bf16[4,4,16,640]{3,2,1,0:T(8,128)(2,1)S(1)}, bf16[4,4,16,640]{3,2,1,0:T(8,128)(2,1)S(1)}) custom-call(s32[2]{0:T(128)S(1)} %pad_add_fusion.index_ref, bf16[2,4,16,1152]{3,2,1,0:T(8,128)(2,1)S(1)} %get-tuple-element.88.refs_0_, bf16[2,4,16,1152]{3,2,1,0:T(8,128)(2,1)S(1)} %collective-permute-done.4.refs_1_, ...), custom_call_target="tpu_custom_call" | custom-call | flops 40000000000 | bytes 8388608 | tf_op jit(solution)/shard_map/windowed/pallas_call | solution.py:359
  93.6 0.6 merge.3
  94.2 0.5 collective-permute-start.27
  94.7 0.6 collective-permute-start.28
  95.3 0.5 collective-permute-done.25.second_ref
  95.8 0.6 merge.2
  96.4 2.1 %collective-permute-start.26 = (bf16[2,4,16,1152]{3,2,1,0:T(8,128)(2,1)S(1)}, bf16[2,4,16,1152]{3,2,1,0:T(8,128)(2,1)S(1)}, u32[]{:S(2)}, u32[]{:S(2)}) collective-permute-start(bf16[2,4,16,1152]{3,2,1,0:T(8,128)(2,1)S(1)} %get-tuple-element.68), channel_id=1, source_target_pairs={{0,2},{1,3},{2,0},{3,1},{4,6},{5,7},{6,4},{7,5},{8,10},{9,11},{10,... | collective-permute-start | bytes 884744 | tf_op jit(solution)/shard_map/ppermute | solution.py:254
  98.5 14.2 %collective-permute-done.27.refs_4_ = bf16[2,4,16,1152]{3,2,1,0:T(8,128)(2,1)S(1)} collective-permute-done((bf16[2,4,16,1152]{3,2,1,0:T(8,128)(2,1)S(1)}, bf16[2,4,16,1152]{3,2,1,0:T(8,128)(2,1)S(1)}, u32[]{:S(2)}, u32[]{:S(2)}) %collective-permute-start.27) | collective-permute-done | bytes 294944 | tf_op jit(solution)/shard_map/ppermute | solution.py:254
  112.7 7.6 %collective-permute-done.28.refs_6_ = bf16[2,4,16,1152]{3,2,1,0:T(8,128)(2,1)S(1)} collective-permute-done((bf16[2,4,16,1152]{3,2,1,0:T(8,128)(2,1)S(1)}, bf16[2,4,16,1152]{3,2,1,0:T(8,128)(2,1)S(1)}, u32[]{:S(2)}, u32[]{:S(2)}) %collective-permute-start.28) | collective-permute-done | bytes 294944 | tf_op jit(solution)/shard_map/ppermute | solution.py:254
  120.3 1.9 %collective-permute-start.34 = (bf16[2,144,1152]{2,1,0:T(8,128)(2,1)S(1)}, bf16[2,144,1152]{2,1,0:T(8,128)(2,1)S(1)}, u32[]{:S(2)}, u32[]{:S(2)}) collective-permute-start(bf16[2,144,1152]{2,1,0:T(8,128)(2,1)S(1)} %collective-permute-done.21.refs_12_), channel_id=1, source_target_pairs={{0,1},{1,0},{2,3},{3,2},{4,5},{5,4},{6,7},{7,6},{8,9},{9,8},{10,11... | collective-permute-start | bytes 1990664 | tf_op jit(solution)/shard_map/ppermute | solution.py:254
  122.2 0.5 collective-permute-start.29
  122.7 0.5 collective-permute-start.31
  123.2 1.2 collective-permute-done.33.refs_11_
  124.4 0.4 collective-permute-start.32
  124.8 0.0 collective-permute-done.29.refs_1_
  124.9 0.4 collective-permute-done.30.refs_3_
  125.3 0.4 collective-permute-done.31.refs_5_
  125.7 0.4 collective-permute-done.32.refs_7_
  126.1 4.6 %restore.1 = bf16[4,128,1152]{2,1,0:T(8,128)(2,1)} custom-call(s32[2]{0:T(128)S(1)} %pad_add_fusion.index_ref, bf16[4,128,1152]{2,1,0:T(8,128)(2,1)S(1)} %copy-done.1, f32[3,4,1152]{2,1,0:T(4,128)S(1)} %bitcast.24, bf16[2,4,16,1152]{3,2,1,0:T(8,128)(2,1)S(1)} %get-tuple-element.73.refs_0_, bf16[2,4,16,1152]{3,2,1,0:T(8,128)(2,1)S(1)} %collective-permute-done.29.refs_1_, ...), custom_call_target="tpu_custom_call" | custom-call | tf_op jit(solution)/shard_map/restore/pallas_call | solution.py:411
  (35 shorter events, 0.3 us)
Async XLA Ops:
  0.1 1.3 copy-start
  1.3 0.8 copy-start.4
  2.2 2.4 %copy-start.2 = (bf16[1152,432]{0,1:T(8,128)(2,1)S(1)}, bf16[1152,432]{0,1:T(8,128)(2,1)}, u32[]{:S(2)}) copy-start(bf16[1152,432]{0,1:T(8,128)(2,1)} %param.6) | copy-start | bytes 2985988
  2.2 5.2 %copy-start.3 = (bf16[1152,144]{0,1:T(8,128)(2,1)S(1)}, bf16[1152,144]{0,1:T(8,128)(2,1)}, u32[]{:S(2)}) copy-start(bf16[1152,144]{0,1:T(8,128)(2,1)} %param.7) | copy-start | bytes 995332
  3.8 3.8 %collective-permute-start.1 = (bf16[4,4,16,1152]{3,2,1,0:T(8,128)(2,1)S(1)}, bf16[4,4,16,1152]{3,2,1,0:T(8,128)(2,1)S(1)}, u32[]{:S(2)}, u32[]{:S(2)}) collective-permute-start(bf16[4,4,16,1152]{3,2,1,0:T(8,128)(2,1)S(1)} %get-tuple-element.43), channel_id=1, source_target_pairs={{0,1},{1,0},{2,3},{3,2},{4,5},{5,4},{6,7},{7,6},{8,9},{9,8},{10,11... | collective-permute-start | bytes 1769480 | tf_op jit(solution)/shard_map/ppermute | solution.py:254
  4.7 13.8 %collective-permute-start = (bf16[112,1152]{1,0:T(8,128)(2,1)S(1)}, bf16[112,1152]{1,0:T(8,128)(2,1)S(1)}, u32[]{:S(2)}, u32[]{:S(2)}) collective-permute-start(bf16[112,1152]{1,0:T(8,128)(2,1)S(1)} %dynamic-slice_bitcast_fusion), channel_id=1, source_target_pairs={{0,4},{1,5},{2,6},{3,7},{4,0},{5,1},{6,2},{7,3},{8,12},{9,13},{10,... | collective-permute-start | bytes 774152 | tf_op jit(solution)/shard_map/ppermute | solution.py:254
  7.0 12.9 %collective-permute-start.2 = (bf16[432,1152]{1,0:T(8,128)(2,1)S(1)}, bf16[432,1152]{1,0:T(8,128)(2,1)S(1)}, u32[]{:S(2)}, u32[]{:S(2)}) collective-permute-start(bf16[432,1152]{1,0:T(8,128)(2,1)S(1)} %bitcast.14), channel_id=1, source_target_pairs={{0,1},{1,0},{2,3},{3,2},{4,5},{5,4},{6,7},{7,6},{8,9},{9,8},{10,11... | collective-permute-start | bytes 2985992 | tf_op jit(solution)/shard_map/ppermute | solution.py:254
  7.3 11.1 %collective-permute-start.3 = (bf16[144,1152]{1,0:T(8,128)(2,1)S(1)}, bf16[144,1152]{1,0:T(8,128)(2,1)S(1)}, u32[]{:S(2)}, u32[]{:S(2)}) collective-permute-start(bf16[144,1152]{1,0:T(8,128)(2,1)S(1)} %bitcast.16), channel_id=1, source_target_pairs={{0,1},{1,0},{2,3},{3,2},{4,5},{5,4},{6,7},{7,6},{8,9},{9,8},{10,11... | collective-permute-start | bytes 995336 | tf_op jit(solution)/shard_map/ppermute | solution.py:254
  7.7 12.2 %collective-permute-start.4 = (bf16[2,4,16,1152]{3,2,1,0:T(8,128)(2,1)S(1)}, bf16[2,4,16,1152]{3,2,1,0:T(8,128)(2,1)S(1)}, u32[]{:S(2)}, u32[]{:S(2)}) collective-permute-start(bf16[2,4,16,1152]{3,2,1,0:T(8,128)(2,1)S(1)} %pad_maximum_fusion.4), channel_id=1, source_target_pairs={{0,2},{1,3},{2,0},{3,1},{4,6},{5,7},{6,4},{7,5},{8,10},{9,11},{10,... | collective-permute-start | bytes 884744 | tf_op jit(solution)/shard_map/ppermute | solution.py:254
  20.0 20.8 %collective-permute-start.9 = (bf16[2,2,4,16,1152]{4,3,2,1,0:T(8,128)(2,1)S(1)}, bf16[2,2,4,16,1152]{4,3,2,1,0:T(8,128)(2,1)S(1)}, u32[]{:S(2)}, u32[]{:S(2)}) collective-permute-start(bf16[2,2,4,16,1152]{4,3,2,1,0:T(8,128)(2,1)S(1)} %pad_maximum_fusion.1), channel_id=1, source_target_pairs={{0,24},{1,25},{2,26},{3,27},{4,12},{5,13},{6,14},{7,15},{8,0},{9,1... | collective-permute-start | bytes 1769480 | tf_op jit(solution)/shard_map/ppermute | solution.py:281
  22.3 18.5 %collective-permute-start.7 = (bf16[2,112,1152]{2,1,0:T(8,128)(2,1)S(1)}, bf16[2,112,1152]{2,1,0:T(8,128)(2,1)S(1)}, u32[]{:S(2)}, u32[]{:S(2)}) collective-permute-start(bf16[2,112,1152]{2,1,0:T(8,128)(2,1)S(1)} %pad_maximum_fusion.2), channel_id=1, source_target_pairs={{0,2},{1,3},{2,0},{3,1},{4,6},{5,7},{6,4},{7,5},{8,10},{9,11},{10,... | collective-permute-start | bytes 1548296 | tf_op jit(solution)/shard_map/ppermute | solution.py:254
  23.0 17.7 %collective-permute-start.8 = (bf16[2,4,16,1152]{3,2,1,0:T(8,128)(2,1)S(1)}, bf16[2,4,16,1152]{3,2,1,0:T(8,128)(2,1)S(1)}, u32[]{:S(2)}, u32[]{:S(2)}) collective-permute-start(bf16[2,4,16,1152]{3,2,1,0:T(8,128)(2,1)S(1)} %get-tuple-element.46), channel_id=1, source_target_pairs={{0,4},{1,5},{2,6},{3,7},{4,0},{5,1},{6,2},{7,3},{8,12},{9,13},{10,... | collective-permute-start | bytes 884744 | tf_op jit(solution)/shard_map/ppermute | solution.py:254
  23.9 15.7 %collective-permute-start.5 = (bf16[112,1152]{1,0:T(8,128)(2,1)S(1)}, bf16[112,1152]{1,0:T(8,128)(2,1)S(1)}, u32[]{:S(2)}, u32[]{:S(2)}) collective-permute-start(bf16[112,1152]{1,0:T(8,128)(2,1)S(1)} %collective-permute-done.refs_2_), channel_id=1, source_target_pairs={{0,8},{1,9},{2,10},{3,11},{4,12},{5,13},{6,14},{7,15},{8,0},{9,1},... | collective-permute-start | bytes 774152 | tf_op jit(solution)/shard_map/ppermute | solution.py:254
  25.1 14.5 %collective-permute-start.6 = (bf16[112,1152]{1,0:T(8,128)(2,1)S(1)}, bf16[112,1152]{1,0:T(8,128)(2,1)S(1)}, u32[]{:S(2)}, u32[]{:S(2)}) collective-permute-start(bf16[112,1152]{1,0:T(8,128)(2,1)S(1)} %collective-permute-done.refs_2_), channel_id=1, source_target_pairs={{0,16},{1,17},{2,18},{3,19},{4,20},{5,21},{6,22},{7,23},{8,24},{9,... | collective-permute-start | bytes 774152 | tf_op jit(solution)/shard_map/ppermute | solution.py:254
  40.8 19.0 %collective-permute-start.10 = (bf16[2,112,1152]{2,1,0:T(8,128)(2,1)S(1)}, bf16[2,112,1152]{2,1,0:T(8,128)(2,1)S(1)}, u32[]{:S(2)}, u32[]{:S(2)}) collective-permute-start(bf16[2,112,1152]{2,1,0:T(8,128)(2,1)S(1)} %collective-permute-done.7.refs_8_), channel_id=1, source_target_pairs={{0,8},{1,9},{2,10},{3,11},{4,12},{5,13},{6,14},{7,15},{8,0},{9,1},... | collective-permute-start | bytes 1548296 | tf_op jit(solution)/shard_map/ppermute | solution.py:254
  43.0 16.8 %collective-permute-start.11 = (bf16[2,112,1152]{2,1,0:T(8,128)(2,1)S(1)}, bf16[2,112,1152]{2,1,0:T(8,128)(2,1)S(1)}, u32[]{:S(2)}, u32[]{:S(2)}) collective-permute-start(bf16[2,112,1152]{2,1,0:T(8,128)(2,1)S(1)} %collective-permute-done.7.refs_8_), channel_id=1, source_target_pairs={{0,16},{1,17},{2,18},{3,19},{4,20},{5,21},{6,22},{7,23},{8,24},{9,... | collective-permute-start | bytes 1548296 | tf_op jit(solution)/shard_map/ppermute | solution.py:254
  44.2 15.1 %collective-permute-start.12 = (bf16[144,1152]{1,0:T(8,128)(2,1)S(1)}, bf16[144,1152]{1,0:T(8,128)(2,1)S(1)}, u32[]{:S(2)}, u32[]{:S(2)}) collective-permute-start(bf16[144,1152]{1,0:T(8,128)(2,1)S(1)} %bitcast.17), channel_id=1, source_target_pairs={{0,4},{1,5},{2,6},{3,7},{4,0},{5,1},{6,2},{7,3},{8,12},{9,13},{10,... | collective-permute-start | bytes 995336 | tf_op jit(solution)/shard_map/ppermute | solution.py:254
  45.6 15.8 %collective-permute-start.17 = (bf16[2,112,1152]{2,1,0:T(8,128)(2,1)S(1)}, bf16[2,112,1152]{2,1,0:T(8,128)(2,1)S(1)}, u32[]{:S(2)}, u32[]{:S(2)}) collective-permute-start(bf16[2,112,1152]{2,1,0:T(8,128)(2,1)S(1)} %collective-permute-done.7.refs_8_), channel_id=1, source_target_pairs={{0,1},{1,0},{2,3},{3,2},{4,5},{5,4},{6,7},{7,6},{8,9},{9,8},{10,11... | collective-permute-start | bytes 1548296 | tf_op jit(solution)/shard_map/ppermute | solution.py:254
  47.2 13.2 %collective-permute-start.14 = (bf16[112,1152]{1,0:T(8,128)(2,1)S(1)}, bf16[112,1152]{1,0:T(8,128)(2,1)S(1)}, u32[]{:S(2)}, u32[]{:S(2)}) collective-permute-start(bf16[112,1152]{1,0:T(8,128)(2,1)S(1)} %collective-permute-done.refs_2_), channel_id=1, source_target_pairs={{0,1},{1,0},{2,3},{3,2},{4,5},{5,4},{6,7},{7,6},{8,9},{9,8},{10,11... | collective-permute-start | bytes 774152 | tf_op jit(solution)/shard_map/ppermute | solution.py:254
  59.3 1.6 %collective-permute-start.15 = (bf16[112,1152]{1,0:T(8,128)(2,1)S(1)}, bf16[112,1152]{1,0:T(8,128)(2,1)S(1)}, u32[]{:S(2)}, u32[]{:S(2)}) collective-permute-start(bf16[112,1152]{1,0:T(8,128)(2,1)S(1)} %collective-permute-done.5.refs_4_), channel_id=1, source_target_pairs={{0,1},{1,0},{2,3},{3,2},{4,5},{5,4},{6,7},{7,6},{8,9},{9,8},{10,11... | collective-permute-start | bytes 774152 | tf_op jit(solution)/shard_map/ppermute | solution.py:254
  59.8 4.1 %collective-permute-start.18 = (bf16[2,112,1152]{2,1,0:T(8,128)(2,1)S(1)}, bf16[2,112,1152]{2,1,0:T(8,128)(2,1)S(1)}, u32[]{:S(2)}, u32[]{:S(2)}) collective-permute-start(bf16[2,112,1152]{2,1,0:T(8,128)(2,1)S(1)} %collective-permute-done.10.refs_10_), channel_id=1, source_target_pairs={{0,1},{1,0},{2,3},{3,2},{4,5},{5,4},{6,7},{7,6},{8,9},{9,8},{10,11... | collective-permute-start | bytes 1548296 | tf_op jit(solution)/shard_map/ppermute | solution.py:254
  59.9 4.1 %collective-permute-start.19 = (bf16[2,112,1152]{2,1,0:T(8,128)(2,1)S(1)}, bf16[2,112,1152]{2,1,0:T(8,128)(2,1)S(1)}, u32[]{:S(2)}, u32[]{:S(2)}) collective-permute-start(bf16[2,112,1152]{2,1,0:T(8,128)(2,1)S(1)} %collective-permute-done.11.refs_12_), channel_id=1, source_target_pairs={{0,1},{1,0},{2,3},{3,2},{4,5},{5,4},{6,7},{7,6},{8,9},{9,8},{10,11... | collective-permute-start | bytes 1548296 | tf_op jit(solution)/shard_map/ppermute | solution.py:254
  60.3 15.8 %collective-permute-start.13 = (bf16[2,112,1152]{2,1,0:T(8,128)(2,1)S(1)}, bf16[2,112,1152]{2,1,0:T(8,128)(2,1)S(1)}, u32[]{:S(2)}, u32[]{:S(2)}) collective-permute-start(bf16[2,112,1152]{2,1,0:T(8,128)(2,1)S(1)} %collective-permute-done.10.refs_10_), channel_id=1, source_target_pairs={{0,16},{1,17},{2,18},{3,19},{4,20},{5,21},{6,22},{7,23},{8,24},{9,... | collective-permute-start | bytes 1548296 | tf_op jit(solution)/shard_map/ppermute | solution.py:254
  61.0 1.9 %collective-permute-start.16 = (bf16[112,1152]{1,0:T(8,128)(2,1)S(1)}, bf16[112,1152]{1,0:T(8,128)(2,1)S(1)}, u32[]{:S(2)}, u32[]{:S(2)}) collective-permute-start(bf16[112,1152]{1,0:T(8,128)(2,1)S(1)} %collective-permute-done.6.refs_6_), channel_id=1, source_target_pairs={{0,1},{1,0},{2,3},{3,2},{4,5},{5,4},{6,7},{7,6},{8,9},{9,8},{10,11... | collective-permute-start | bytes 774152 | tf_op jit(solution)/shard_map/ppermute | solution.py:254
  61.3 14.8 %collective-permute-start.20 = (bf16[2,4,16,1152]{3,2,1,0:T(8,128)(2,1)S(1)}, bf16[2,4,16,1152]{3,2,1,0:T(8,128)(2,1)S(1)}, u32[]{:S(2)}, u32[]{:S(2)}) collective-permute-start(bf16[2,4,16,1152]{3,2,1,0:T(8,128)(2,1)S(1)} %get-tuple-element.57), channel_id=1, source_target_pairs={{0,6},{1,7},{2,4},{3,5},{4,2},{5,3},{6,0},{7,1},{8,14},{9,15},{10,... | collective-permute-start | bytes 884744 | tf_op jit(solution)/shard_map/ppermute | solution.py:254
  62.8 14.3 %collective-permute-start.22 = (bf16[112,1152]{1,0:T(8,128)(2,1)S(1)}, bf16[112,1152]{1,0:T(8,128)(2,1)S(1)}, u32[]{:S(2)}, u32[]{:S(2)}) collective-permute-start(bf16[112,1152]{1,0:T(8,128)(2,1)S(1)} %collective-permute-done.6.refs_6_), channel_id=1, source_target_pairs={{0,8},{1,9},{2,10},{3,11},{4,12},{5,13},{6,14},{7,15},{8,0},{9,1},... | collective-permute-start | bytes 774152 | tf_op jit(solution)/shard_map/ppermute | solution.py:254
  76.1 2.9 %collective-permute-start.24 = (bf16[2,112,1152]{2,1,0:T(8,128)(2,1)S(1)}, bf16[2,112,1152]{2,1,0:T(8,128)(2,1)S(1)}, u32[]{:S(2)}, u32[]{:S(2)}) collective-permute-start(bf16[2,112,1152]{2,1,0:T(8,128)(2,1)S(1)} %collective-permute-done.13.refs_7_.refs_8_), channel_id=1, source_target_pairs={{0,1},{1,0},{2,3},{3,2},{4,5},{5,4},{6,7},{7,6},{8,9},{9,8},{10,11... | collective-permute-start | bytes 1548296 | tf_op jit(solution)/shard_map/ppermute | solution.py:254
  77.1 1.9 %collective-permute-start.23 = (bf16[112,1152]{1,0:T(8,128)(2,1)S(1)}, bf16[112,1152]{1,0:T(8,128)(2,1)S(1)}, u32[]{:S(2)}, u32[]{:S(2)}) collective-permute-start(bf16[112,1152]{1,0:T(8,128)(2,1)S(1)} %collective-permute-done.22.refs_5_.refs_6_), channel_id=1, source_target_pairs={{0,1},{1,0},{2,3},{3,2},{4,5},{5,4},{6,7},{7,6},{8,9},{9,8},{10,11... | collective-permute-start | bytes 774152 | tf_op jit(solution)/shard_map/ppermute | solution.py:254
  77.2 21.3 %collective-permute-start.21 = (bf16[2,144,1152]{2,1,0:T(8,128)(2,1)S(1)}, bf16[2,144,1152]{2,1,0:T(8,128)(2,1)S(1)}, u32[]{:S(2)}, u32[]{:S(2)}) collective-permute-start(bf16[2,144,1152]{2,1,0:T(8,128)(2,1)S(1)} %pad_maximum_fusion), channel_id=1, source_target_pairs={{0,2},{1,3},{2,0},{3,1},{4,6},{5,7},{6,4},{7,5},{8,10},{9,11},{10,... | collective-permute-start | bytes 1990664 | tf_op jit(solution)/shard_map/ppermute | solution.py:254
  85.9 9.9 %collective-permute-start.25 = (bf16[4,4,16,640]{3,2,1,0:T(8,128)(2,1)S(1)}, bf16[4,4,16,640]{3,2,1,0:T(8,128)(2,1)S(1)}, u32[]{:S(2)}, u32[]{:S(2)}) collective-permute-start(bf16[4,4,16,640]{3,2,1,0:T(8,128)(2,1)S(1)} %get-tuple-element.66), channel_id=1, source_target_pairs={{0,8},{1,9},{2,10},{3,11},{4,28},{5,29},{6,30},{7,31},{8,16},{9,17... | collective-permute-start | bytes 983048 | tf_op jit(solution)/shard_map/ppermute | solution.py:281
  93.6 32.5 %copy-start.1 = (bf16[4,128,1152]{2,1,0:T(8,128)(2,1)S(1)}, bf16[4,128,1152]{2,1,0:T(8,128)(2,1)}, u32[]{:S(2)}) copy-start(bf16[4,128,1152]{2,1,0:T(8,128)(2,1)} %tokens_ref.3) | copy-start | bytes 3538948
  93.6 32.5 %copy-start.5 = (f32[4,3,1152]{2,0,1:T(4,128)S(1)}, f32[4,3,1152]{2,0,1:T(4,128)}, u32[]{:S(2)}) copy-start(f32[4,3,1152]{2,0,1:T(4,128)} %param.5) | copy-start | bytes 165892
  94.2 18.5 %collective-permute-start.27 = (bf16[2,4,16,1152]{3,2,1,0:T(8,128)(2,1)S(1)}, bf16[2,4,16,1152]{3,2,1,0:T(8,128)(2,1)S(1)}, u32[]{:S(2)}, u32[]{:S(2)}) collective-permute-start(bf16[2,4,16,1152]{3,2,1,0:T(8,128)(2,1)S(1)} %get-tuple-element.71), channel_id=1, source_target_pairs={{0,4},{1,5},{2,6},{3,7},{4,0},{5,1},{6,2},{7,3},{8,12},{9,13},{10,... | collective-permute-start | bytes 884744 | tf_op jit(solution)/shard_map/ppermute | solution.py:254
  94.7 25.6 %collective-permute-start.28 = (bf16[2,4,16,1152]{3,2,1,0:T(8,128)(2,1)S(1)}, bf16[2,4,16,1152]{3,2,1,0:T(8,128)(2,1)S(1)}, u32[]{:S(2)}, u32[]{:S(2)}) collective-permute-start(bf16[2,4,16,1152]{3,2,1,0:T(8,128)(2,1)S(1)} %get-tuple-element.72), channel_id=1, source_target_pairs={{0,6},{1,7},{2,4},{3,5},{4,2},{5,3},{6,0},{7,1},{8,14},{9,15},{10,... | collective-permute-start | bytes 884744 | tf_op jit(solution)/shard_map/ppermute | solution.py:254
  96.4 23.9 %collective-permute-start.26 = (bf16[2,4,16,1152]{3,2,1,0:T(8,128)(2,1)S(1)}, bf16[2,4,16,1152]{3,2,1,0:T(8,128)(2,1)S(1)}, u32[]{:S(2)}, u32[]{:S(2)}) collective-permute-start(bf16[2,4,16,1152]{3,2,1,0:T(8,128)(2,1)S(1)} %get-tuple-element.68), channel_id=1, source_target_pairs={{0,2},{1,3},{2,0},{3,1},{4,6},{5,7},{6,4},{7,5},{8,10},{9,11},{10,... | collective-permute-start | bytes 884744 | tf_op jit(solution)/shard_map/ppermute | solution.py:254
  120.3 5.8 %collective-permute-start.34 = (bf16[2,144,1152]{2,1,0:T(8,128)(2,1)S(1)}, bf16[2,144,1152]{2,1,0:T(8,128)(2,1)S(1)}, u32[]{:S(2)}, u32[]{:S(2)}) collective-permute-start(bf16[2,144,1152]{2,1,0:T(8,128)(2,1)S(1)} %collective-permute-done.21.refs_12_), channel_id=1, source_target_pairs={{0,1},{1,0},{2,3},{3,2},{4,5},{5,4},{6,7},{7,6},{8,9},{9,8},{10,11... | collective-permute-start | bytes 1990664 | tf_op jit(solution)/shard_map/ppermute | solution.py:254
  122.2 2.2 %collective-permute-start.33 = (bf16[144,1152]{1,0:T(8,128)(2,1)S(1)}, bf16[144,1152]{1,0:T(8,128)(2,1)S(1)}, u32[]{:S(2)}, u32[]{:S(2)}) collective-permute-start(bf16[144,1152]{1,0:T(8,128)(2,1)S(1)} %collective-permute-done.12.refs_10_), channel_id=1, source_target_pairs={{0,1},{1,0},{2,3},{3,2},{4,5},{5,4},{6,7},{7,6},{8,9},{9,8},{10,11... | collective-permute-start | bytes 995336 | tf_op jit(solution)/shard_map/ppermute | solution.py:254
  122.2 2.6 %collective-permute-start.29 = (bf16[2,4,16,1152]{3,2,1,0:T(8,128)(2,1)S(1)}, bf16[2,4,16,1152]{3,2,1,0:T(8,128)(2,1)S(1)}, u32[]{:S(2)}, u32[]{:S(2)}) collective-permute-start(bf16[2,4,16,1152]{3,2,1,0:T(8,128)(2,1)S(1)} %get-tuple-element.73.refs_0_), channel_id=1, source_target_pairs={{0,1},{1,0},{2,3},{3,2},{4,5},{5,4},{6,7},{7,6},{8,9},{9,8},{10,11... | collective-permute-start | bytes 884744 | tf_op jit(solution)/shard_map/ppermute | solution.py:254
  122.7 2.5 %collective-permute-start.30 = (bf16[2,4,16,1152]{3,2,1,0:T(8,128)(2,1)S(1)}, bf16[2,4,16,1152]{3,2,1,0:T(8,128)(2,1)S(1)}, u32[]{:S(2)}, u32[]{:S(2)}) collective-permute-start(bf16[2,4,16,1152]{3,2,1,0:T(8,128)(2,1)S(1)} %collective-permute-done.26.refs_2_), channel_id=1, source_target_pairs={{0,1},{1,0},{2,3},{3,2},{4,5},{5,4},{6,7},{7,6},{8,9},{9,8},{10,11... | collective-permute-start | bytes 884744 | tf_op jit(solution)/shard_map/ppermute | solution.py:254
  122.7 3.0 %collective-permute-start.31 = (bf16[2,4,16,1152]{3,2,1,0:T(8,128)(2,1)S(1)}, bf16[2,4,16,1152]{3,2,1,0:T(8,128)(2,1)S(1)}, u32[]{:S(2)}, u32[]{:S(2)}) collective-permute-start(bf16[2,4,16,1152]{3,2,1,0:T(8,128)(2,1)S(1)} %collective-permute-done.27.refs_4_), channel_id=1, source_target_pairs={{0,1},{1,0},{2,3},{3,2},{4,5},{5,4},{6,7},{7,6},{8,9},{9,8},{10,11... | collective-permute-start | bytes 884744 | tf_op jit(solution)/shard_map/ppermute | solution.py:254
  124.4 1.7 %collective-permute-start.32 = (bf16[2,4,16,1152]{3,2,1,0:T(8,128)(2,1)S(1)}, bf16[2,4,16,1152]{3,2,1,0:T(8,128)(2,1)S(1)}, u32[]{:S(2)}, u32[]{:S(2)}) collective-permute-start(bf16[2,4,16,1152]{3,2,1,0:T(8,128)(2,1)S(1)} %collective-permute-done.28.refs_6_), channel_id=1, source_target_pairs={{0,1},{1,0},{2,3},{3,2},{4,5},{5,4},{6,7},{7,6},{8,9},{9,8},{10,11... | collective-permute-start | bytes 884744 | tf_op jit(solution)/shard_map/ppermute | solution.py:254

commit v6 on v5

--- a/solution.py
+++ b/solution.py
@@ -120,7 +120,8 @@
     sources = []
     for d in range(count):
         owner = lax.bitwise_xor(index, d)
-        source = x_refs[-1].at[d // 2, d % 2] if kind == 1 and d < count // 2 else x_refs[d // 2].at[d % 2]
+        near = kind == 1 and d < count // 2
+        source = (x_refs[-1] if near else x_refs[d // 2]).at[pl.ds((d if near else d % 2) * groups, groups)]
         sources.append(pltpu.make_async_copy(source, xs.at[:, owner], sems.at[d]))
     for copy in sources:
         copy.start()
@@ -200,7 +201,8 @@
 def restore_kernel(plan, index_ref, tokens_ref, modulation_ref, *refs):
     count, moves = plan["count"], plan["moves"]
     refs = list(refs)
-    in_refs = [refs.pop(0).at[n % 2] for n in range(count)]
+    in_refs = [refs.pop(0) for _ in range(count)]
+    in_refs = [ref.at[n % ref.shape[0]] for n, ref in enumerate(in_refs)]
     w_refs = [refs.pop(0) for _ in range(plan["weights"])]
     out_ref, wall, mixed, sems = refs
     index = index_ref[0]
@@ -306,15 +308,16 @@
         rest = hop(jnp.stack([mine, far]), 2)
         blocks[2] = hop(pair[2], 4)
         following = following_of(blocks[:2])
-        ax, ay, rest, blocks[2], following, narrow = tie((ax, ay, rest, blocks[2], following, narrow))
+        ax, ay, rest, blocks[2], following, pair[3] = tie((ax, ay, rest, blocks[2], following, pair[3]))
         bx, by = hop(rest, 0, x), hop(rest, 0, y)
-        out_far = hop(narrow, 4)
-        ay, bx, by, pair[3], out_far = tie((ay, bx, by, pair[3], out_far))
-        blocks[3] = hop(pair[3], 6)
+        both = jnp.concatenate([pair[3].reshape(-1, ROWS, width), narrow.reshape(-1, ROWS, width)], axis=0)
+        blocks[3] = hop(both, 6)
+        early = [hop(far, 1), hop(rest, 1)]
+        ay, bx, by, early, ax = tie((ay, bx, by, early, ax))
         axy = hop(ay, 0, x)
-        bxy = hop(bx, 0, y)
-        swaps = [hop(value, 1) for value in (far, ax, ay)]
-        swaps += [None] + [hop(value, 1) for value in (rest, bx, by)]
+        bxy = jnp.stack([hop(bx[0], 0, y), hop(by[1], 0, x)])
+        swaps = [early[0], hop(ax, 1), hop(ay, 1), None]
+        swaps += [early[1], hop(bx, 1), hop(by, 1)]
         with_sibling(wide, [((), columns, 0, None)], wide_other)
         for e, value in enumerate((far, ax, ay)):
             with_sibling(value, [((), size, 2, e)], swaps[e])
@@ -329,12 +332,13 @@
             out_specs=anywhere,
             scratch_shapes=[pltpu.SemaphoreType.DMA((2 * len(moves),))],
             compiler_params=params,
-            cost_estimate=pl.CostEstimate(flops=2 * 10**9, bytes_accessed=8 * 1024 * 1024, transcendentals=0),
+            cost_estimate=pl.CostEstimate(flops=0, bytes_accessed=0, transcendentals=0),
             name="gather",
         )(own_index, *operands)
         operands.clear()
         moves.clear()
-        bxy, swaps, out_far, blocks[3], full = tie((bxy, swaps, out_far, blocks[3], full))
+        bxy, swaps, blocks[3], full = tie((bxy, swaps, blocks[3], full))
+        out_far = blocks[3][2 * groups :].reshape(narrow.shape)
         swaps.append(hop(bxy, 1))
         swaps[3] = hop(axy, 1)
         with_sibling(axy, [((), size, 2, 3)], swaps[3])
@@ -353,6 +357,7 @@
     tokens = count * block_rows
 
     def attention(kind, inputs):
+        inputs = [value.reshape((-1,) + block.shape[1:]) for value in inputs]
         plan = dict(kind=kind, weights=len(operands), inputs=len(inputs), half=half, moves=by_kind[kind],
                     columns=columns, over=over, pieces=slabs)
         copies = max([1] + [2 * len(entries) for _, entries in by_kind[kind]])
@@ -394,18 +399,22 @@
         )(own_index, first, second)
 
     sent_far = merged(chips // 2, first_far, second_far, 0)
+    if shared:
+        out_rest, second_near = tie((out_rest, second_near))
     sent_near = merged(0, first_near, second_near, 0)
     sent = sent_near + sent_far
-    arrived = [hop(sent[z], 2 * z) if z else sent[z] for z in range(chips)]
+    arrived = [hop(sent[z], 2 * z) if z else sent[z] for z in range(chips // 2)]
+    singles = [hop(sent[z][n], 2 * z + n)[None] for z in range(chips // 2, chips) for n in range(2)]
     if shared:
-        out_rest, arrived = tie((out_rest, arrived))
+        out_rest, arrived, singles = tie((out_rest, arrived, singles))
     returned = []
     for value in arrived:
         returned += [value, hop(value, 1)]
+    returned += singles
     if shared:
         out_operands = [narrow, narrow_other, out_far, hop(out_far, 1), out_rest, hop(out_rest, 1)]
-        out_moves = [(0, (), (0,)), (1, (), (1,)), (2, (), (4,)), (3, (), (5,)), (4, (0,), (2,)), (5, (0,), (3,)),
-                     (4, (1,), (6,)), (5, (1,), (7,))]
+        out_moves = [(0, (), (0,)), (1, (), (1,)), (2, (), (6,)), (3, (), (7,)), (4, (0,), (2,)), (5, (0,), (3,)),
+                     (4, (1,), (4,)), (5, (1,), (5,))]
 
     plan = dict(count=count, weights=len(out_operands), moves=out_moves)
     return pl.pallas_call(

time: 131 us -> 129 us (0.985)
  waiting for transfers between devices: 69.9 us -> 65.2 us
  starting transfers between devices: 29.2 us -> 30.7 us
    ppermute x33, waiting for transfers between devices: 69.4 us -> 65.2 us  [hop(): return lax.ppermute(value, ('slab', 'seq'), pairs)]
    ppermute x33, starting transfers between devices: 25.8 us -> 28.2 us  [hop(): return lax.ppermute(value, ('slab', 'seq'), pairs)]
  transfers between devices with their start and end apart: 35 -> 35, of which waited for: 15 -> 17; matrix products, arithmetic and copies ran while one was open for 0% -> 1% of each run, Pallas kernels for 17% -> 17%
where the time goes in v6:
time: 129 us
  waiting for transfers between devices  65.2 us (51%)
  starting transfers between devices  30.7 us (24%)
  Pallas kernels  28.8 us (22%)
  local copies, waits for them, and re-layouts  3.33 us (3%)
    ppermute x33, waiting for transfers between devices, hop(): return lax.ppermute(value, ('slab', 'seq'), pairs)  65.2 us
    ppermute x33, starting transfers between devices, hop(): return lax.ppermute(value, ('slab', 'seq'), pairs)  28.2 us
    pallas_call x2, Pallas kernels, attention(): pl.pallas_call(functools.partial(block_kernel, plan, frames), out_shape=[...  13.4 us
    pallas_call x1, Pallas kernels, per_device(): pl.pallas_call(functools.partial(gather_kernel, plan), out_shape=jax.Shap...  7.9 us
    pallas_call x1, Pallas kernels, per_device(): pl.pallas_call(functools.partial(restore_kernel, plan), out_shape=jax.Sha...  4.64 us
  transfers between devices with their start and end apart: 35, of which 17 were waited for; matrix products, arithmetic and copies ran while one was open for 1% of the time, Pallas kernels for 17%

profile of v6, /device:TPU:9, one launch (start us, length us, event | category | flops | bytes accessed | tf_op | source)
XLA Modules:
  0.0 129.0 jit_solution(1675473548861165865)
XLA Ops:
  0.0 0.1 pad_add_fusion.index_ref
  0.1 1.3 copy-done
  1.3 0.8 copy-done.4
  2.2 1.7 %norm.1 = (bf16[4,4,16,1152]{3,2,1,0:T(8,128)(2,1)S(1)}, bf16[4,4,16,1152]{3,2,1,0:T(8,128)(2,1)S(1)}) custom-call(s32[2]{0:T(128)S(1)} %pad_add_fusion.index_ref, bf16[4,128,1152]{2,1,0:T(8,128)(2,1)S(1)} %copy-done, f32[3,4,1152]{2,1,0:T(4,128)S(1)} %bitcast.56), custom_call_target="tpu_custom_call" | custom-call | tf_op jit(solution)/shard_map/norm/pallas_call | solution.py:268
  3.8 0.7 collective-permute-start.1
  4.6 1.0 dynamic-slice_bitcast_fusion
  5.6 2.4 %collective-permute-start = (bf16[112,1152]{1,0:T(8,128)(2,1)S(1)}, bf16[112,1152]{1,0:T(8,128)(2,1)S(1)}, u32[]{:S(2)}, u32[]{:S(2)}) collective-permute-start(bf16[112,1152]{1,0:T(8,128)(2,1)S(1)} %dynamic-slice_bitcast_fusion), channel_id=1, source_target_pairs={{0,4},{1,5},{2,6},{3,7},{4,0},{5,1},{6,2},{7,3},{8,12},{9,13},{10,... | collective-permute-start | bytes 774152 | tf_op jit(solution)/shard_map/ppermute | solution.py:256
  8.0 0.3 collective-permute-start.2
  8.3 0.2 collective-permute-start.3
  8.7 0.2 collective-permute-start.4
  8.9 0.1 pad_maximum_fusion.7
  9.0 10.4 %collective-permute-done.refs_2_ = bf16[112,1152]{1,0:T(8,128)(2,1)S(1)} collective-permute-done((bf16[112,1152]{1,0:T(8,128)(2,1)S(1)}, bf16[112,1152]{1,0:T(8,128)(2,1)S(1)}, u32[]{:S(2)}, u32[]{:S(2)}) %collective-permute-start) | collective-permute-done | bytes 258080 | tf_op jit(solution)/shard_map/ppermute | solution.py:256
  19.4 1.4 %collective-permute-done.4 = bf16[2,4,16,1152]{3,2,1,0:T(8,128)(2,1)S(1)} collective-permute-done((bf16[2,4,16,1152]{3,2,1,0:T(8,128)(2,1)S(1)}, bf16[2,4,16,1152]{3,2,1,0:T(8,128)(2,1)S(1)}, u32[]{:S(2)}, u32[]{:S(2)}) %collective-permute-start.4) | collective-permute-done | bytes 294944 | tf_op jit(solution)/shard_map/ppermute | solution.py:256
  20.9 0.1 pad_maximum_fusion.2
  20.9 2.2 %collective-permute-start.9 = (bf16[2,2,4,16,1152]{4,3,2,1,0:T(8,128)(2,1)S(1)}, bf16[2,2,4,16,1152]{4,3,2,1,0:T(8,128)(2,1)S(1)}, u32[]{:S(2)}, u32[]{:S(2)}) collective-permute-start(bf16[2,2,4,16,1152]{4,3,2,1,0:T(8,128)(2,1)S(1)} %pad_maximum_fusion.2), channel_id=1, source_target_pairs={{0,24},{1,25},{2,26},{3,27},{4,12},{5,13},{6,14},{7,15},{8,0},{9,1... | collective-permute-start | bytes 1769480 | tf_op jit(solution)/shard_map/ppermute | solution.py:283
  23.1 0.1 pad_maximum_fusion.3
  23.2 0.8 collective-permute-start.7
  24.0 0.3 collective-permute-start.8
  24.3 1.2 collective-permute-start.5
  25.5 0.2 collective-permute-start.6
  25.7 14.8 %collective-permute-done.5.refs_4_ = bf16[112,1152]{1,0:T(8,128)(2,1)S(1)} collective-permute-done((bf16[112,1152]{1,0:T(8,128)(2,1)S(1)}, bf16[112,1152]{1,0:T(8,128)(2,1)S(1)}, u32[]{:S(2)}, u32[]{:S(2)}) %collective-permute-start.5) | collective-permute-done | bytes 258080 | tf_op jit(solution)/shard_map/ppermute | solution.py:256
  40.6 0.7 collective-permute-done.8
  41.3 2.7 %collective-permute-start.10 = (bf16[2,112,1152]{2,1,0:T(8,128)(2,1)S(1)}, bf16[2,112,1152]{2,1,0:T(8,128)(2,1)S(1)}, u32[]{:S(2)}, u32[]{:S(2)}) collective-permute-start(bf16[2,112,1152]{2,1,0:T(8,128)(2,1)S(1)} %collective-permute-done.7.refs_8_), channel_id=1, source_target_pairs={{0,8},{1,9},{2,10},{3,11},{4,12},{5,13},{6,14},{7,15},{8,0},{9,1},... | collective-permute-start | bytes 1548296 | tf_op jit(solution)/shard_map/ppermute | solution.py:256
  44.0 1.2 collective-permute-start.11
  45.2 1.1 collective-permute-start.13
  46.2 0.1 pad_maximum_fusion.1
  46.3 0.1 collective-permute-start.20
  46.4 1.7 %collective-permute-done.12.refs_3_ = bf16[112,1152]{1,0:T(8,128)(2,1)S(1)} collective-permute-done((bf16[112,1152]{1,0:T(8,128)(2,1)S(1)}, bf16[112,1152]{1,0:T(8,128)(2,1)S(1)}, u32[]{:S(2)}, u32[]{:S(2)}) %collective-permute-start.12) | collective-permute-done | bytes 258080 | tf_op jit(solution)/shard_map/ppermute | solution.py:256
  48.1 6.9 %collective-permute-done.10.refs_10_ = bf16[2,112,1152]{2,1,0:T(8,128)(2,1)S(1)} collective-permute-done((bf16[2,112,1152]{2,1,0:T(8,128)(2,1)S(1)}, bf16[2,112,1152]{2,1,0:T(8,128)(2,1)S(1)}, u32[]{:S(2)}, u32[]{:S(2)}) %collective-permute-start.10) | collective-permute-done | bytes 516128 | tf_op jit(solution)/shard_map/ppermute | solution.py:256
  55.1 1.3 collective-permute-done.11.refs_12_
  56.4 1.4 %collective-permute-start.14 = (bf16[112,1152]{1,0:T(8,128)(2,1)S(1)}, bf16[112,1152]{1,0:T(8,128)(2,1)S(1)}, u32[]{:S(2)}, u32[]{:S(2)}) collective-permute-start(bf16[112,1152]{1,0:T(8,128)(2,1)S(1)} %slice_bitcast_fusion.1), channel_id=1, source_target_pairs={{0,16},{1,17},{2,18},{3,19},{4,20},{5,21},{6,22},{7,23},{8,24},{9,... | collective-permute-start | bytes 774152 | tf_op jit(solution)/shard_map/ppermute | solution.py:256
  57.8 0.4 collective-permute-start.15
  58.2 2.0 %collective-permute-start.18 = (bf16[2,112,1152]{2,1,0:T(8,128)(2,1)S(1)}, bf16[2,112,1152]{2,1,0:T(8,128)(2,1)S(1)}, u32[]{:S(2)}, u32[]{:S(2)}) collective-permute-start(bf16[2,112,1152]{2,1,0:T(8,128)(2,1)S(1)} %collective-permute-done.10.refs_10_), channel_id=1, source_target_pairs={{0,1},{1,0},{2,3},{3,2},{4,5},{5,4},{6,7},{7,6},{8,9},{9,8},{10,11... | collective-permute-start | bytes 1548296 | tf_op jit(solution)/shard_map/ppermute | solution.py:256
  60.2 2.2 %collective-permute-done.14 = bf16[112,1152]{1,0:T(8,128)(2,1)S(1)} collective-permute-done((bf16[112,1152]{1,0:T(8,128)(2,1)S(1)}, bf16[112,1152]{1,0:T(8,128)(2,1)S(1)}, u32[]{:S(2)}, u32[]{:S(2)}) %collective-permute-start.14) | collective-permute-done | bytes 258080 | tf_op jit(solution)/shard_map/ppermute | solution.py:256
  62.4 2.7 %collective-permute-start.16 = (bf16[112,1152]{1,0:T(8,128)(2,1)S(1)}, bf16[112,1152]{1,0:T(8,128)(2,1)S(1)}, u32[]{:S(2)}, u32[]{:S(2)}) collective-permute-start(bf16[112,1152]{1,0:T(8,128)(2,1)S(1)} %collective-permute-done.5.refs_4_), channel_id=1, source_target_pairs={{0,1},{1,0},{2,3},{3,2},{4,5},{5,4},{6,7},{7,6},{8,9},{9,8},{10,11... | collective-permute-start | bytes 774152 | tf_op jit(solution)/shard_map/ppermute | solution.py:256
  65.1 1.4 %collective-permute-start.17 = (bf16[112,1152]{1,0:T(8,128)(2,1)S(1)}, bf16[112,1152]{1,0:T(8,128)(2,1)S(1)}, u32[]{:S(2)}, u32[]{:S(2)}) collective-permute-start(bf16[112,1152]{1,0:T(8,128)(2,1)S(1)} %collective-permute-done.6.refs_6_), channel_id=1, source_target_pairs={{0,1},{1,0},{2,3},{3,2},{4,5},{5,4},{6,7},{7,6},{8,9},{9,8},{10,11... | collective-permute-start | bytes 774152 | tf_op jit(solution)/shard_map/ppermute | solution.py:256
  66.5 0.1 pad_maximum_fusion.4.refs_8_.refs_7_
  66.6 0.4 collective-permute-start.22
  67.0 0.7 collective-permute-done.17.refs_7_
  67.7 7.9 %gather.1.refs_5_.refs_4_ = bf16[3584,1152]{1,0:T(8,128)(2,1)S(1)} custom-call(s32[2]{0:T(128)S(1)} %pad_add_fusion.index_ref, bf16[432,1152]{1,0:T(8,128)(2,1)S(1)} %bitcast.49, bf16[432,1152]{1,0:T(8,128)(2,1)S(1)} %collective-permute-done.2.refs_1_, bf16[112,1152]{1,0:T(8,128)(2,1)S(1)} %collective-permute-done.refs_2_, ...), custom_call_target="tpu_custom_call" | custom-call | tf_op jit(solution)/shard_map/gather/pallas_call | solution.py:328
  75.6 0.8 collective-permute-start.24
  76.4 0.1 pad_maximum_fusion
  76.5 0.6 collective-permute-start.21
  77.1 1.2 collective-permute-done.23.refs_7_.refs_6_
  78.2 6.9 %shifted.1 = (bf16[4,4,16,640]{3,2,1,0:T(8,128)(2,1)S(1)}, bf16[4,4,16,640]{3,2,1,0:T(8,128)(2,1)S(1)}) custom-call(s32[2]{0:T(128)S(1)} %pad_add_fusion.index_ref, bf16[8,16,1152]{2,1,0:T(8,128)(2,1)S(1)} %bitcast.51, bf16[8,16,1152]{2,1,0:T(8,128)(2,1)S(1)} %bitcast.54, bf16[8,16,1152]{2,1,0:T(8,128)(2,1)S(1)} %bitcast.63, ...), custom_call_target="tpu_custom_call" | custom-call | flops 40000000000 | bytes 8388608 | tf_op jit(solution)/shard_map/shifted/pallas_call | solution.py:364
  85.2 0.3 collective-permute-start.25
  85.4 6.5 %windowed.1 = (bf16[4,4,16,640]{3,2,1,0:T(8,128)(2,1)S(1)}, bf16[4,4,16,640]{3,2,1,0:T(8,128)(2,1)S(1)}) custom-call(s32[2]{0:T(128)S(1)} %pad_add_fusion.index_ref, bf16[8,16,1152]{2,1,0:T(8,128)(2,1)S(1)} %bitcast.52, bf16[8,16,1152]{2,1,0:T(8,128)(2,1)S(1)} %bitcast.55, bf16[8,16,1152]{2,1,0:T(8,128)(2,1)S(1)} %bitcast.64, ...), custom_call_target="tpu_custom_call" | custom-call | flops 40000000000 | bytes 8388608 | tf_op jit(solution)/shard_map/windowed/pallas_call | solution.py:364
  91.9 0.6 merge.3
  92.6 1.9 %collective-permute-start.27 = (bf16[4,16,1152]{2,1,0:T(8,128)(2,1)S(1)}, bf16[4,16,1152]{2,1,0:T(8,128)(2,1)S(1)}, u32[]{:S(2)}, u32[]{:S(2)}) collective-permute-start(bf16[4,16,1152]{2,1,0:T(8,128)(2,1)S(1)} %get-tuple-element.98), channel_id=1, source_target_pairs={{0,4},{1,5},{2,6},{3,7},{4,0},{5,1},{6,2},{7,3},{8,12},{9,13},{10,... | collective-permute-start | bytes 442376 | tf_op jit(solution)/shard_map/ppermute | solution.py:256
  94.5 1.4 %collective-permute-start.28 = (bf16[4,16,1152]{2,1,0:T(8,128)(2,1)S(1)}, bf16[4,16,1152]{2,1,0:T(8,128)(2,1)S(1)}, u32[]{:S(2)}, u32[]{:S(2)}) collective-permute-start(bf16[4,16,1152]{2,1,0:T(8,128)(2,1)S(1)} %get-tuple-element.97), channel_id=1, source_target_pairs={{0,5},{1,4},{2,7},{3,6},{4,1},{5,0},{6,3},{7,2},{8,13},{9,12},{10,... | collective-permute-start | bytes 442376 | tf_op jit(solution)/shard_map/ppermute | solution.py:256
  95.9 0.6 merge.2
  96.5 0.6 collective-permute-start.26
  97.1 1.6 %collective-permute-start.29 = (bf16[4,16,1152]{2,1,0:T(8,128)(2,1)S(1)}, bf16[4,16,1152]{2,1,0:T(8,128)(2,1)S(1)}, u32[]{:S(2)}, u32[]{:S(2)}) collective-permute-start(bf16[4,16,1152]{2,1,0:T(8,128)(2,1)S(1)} %get-tuple-element.96), channel_id=1, source_target_pairs={{0,6},{1,7},{2,4},{3,5},{4,2},{5,3},{6,0},{7,1},{8,14},{9,15},{10,... | collective-permute-start | bytes 442376 | tf_op jit(solution)/shard_map/ppermute | solution.py:256
  98.7 0.6 collective-permute-start.30
  99.3 4.1 %collective-permute-done.27 = bf16[4,16,1152]{2,1,0:T(8,128)(2,1)S(1)} collective-permute-done((bf16[4,16,1152]{2,1,0:T(8,128)(2,1)S(1)}, bf16[4,16,1152]{2,1,0:T(8,128)(2,1)S(1)}, u32[]{:S(2)}, u32[]{:S(2)}) %collective-permute-start.27) | collective-permute-done | bytes 147488 | tf_op jit(solution)/shard_map/ppermute | solution.py:256
  103.4 3.3 %collective-permute-done.28 = bf16[4,16,1152]{2,1,0:T(8,128)(2,1)S(1)} collective-permute-done((bf16[4,16,1152]{2,1,0:T(8,128)(2,1)S(1)}, bf16[4,16,1152]{2,1,0:T(8,128)(2,1)S(1)}, u32[]{:S(2)}, u32[]{:S(2)}) %collective-permute-start.28) | collective-permute-done | bytes 147488 | tf_op jit(solution)/shard_map/ppermute | solution.py:256
  106.8 10.5 %collective-permute-done.29 = bf16[4,16,1152]{2,1,0:T(8,128)(2,1)S(1)} collective-permute-done((bf16[4,16,1152]{2,1,0:T(8,128)(2,1)S(1)}, bf16[4,16,1152]{2,1,0:T(8,128)(2,1)S(1)}, u32[]{:S(2)}, u32[]{:S(2)}) %collective-permute-start.29) | collective-permute-done | bytes 147488 | tf_op jit(solution)/shard_map/ppermute | solution.py:256
  117.2 3.5 %collective-permute-done.30 = bf16[4,16,1152]{2,1,0:T(8,128)(2,1)S(1)} collective-permute-done((bf16[4,16,1152]{2,1,0:T(8,128)(2,1)S(1)}, bf16[4,16,1152]{2,1,0:T(8,128)(2,1)S(1)}, u32[]{:S(2)}, u32[]{:S(2)}) %collective-permute-start.30) | collective-permute-done | bytes 147488 | tf_op jit(solution)/shard_map/ppermute | solution.py:256
  120.8 0.5 collective-permute-start.33
  121.3 0.5 collective-permute-start.32
  121.8 1.6 %collective-permute-done.33.refs_11_ = bf16[144,1152]{1,0:T(8,128)(2,1)S(1)} collective-permute-done((bf16[144,1152]{1,0:T(8,128)(2,1)S(1)}, bf16[144,1152]{1,0:T(8,128)(2,1)S(1)}, u32[]{:S(2)}, u32[]{:S(2)}) %collective-permute-start.33) | collective-permute-done | bytes 331808 | tf_op jit(solution)/shard_map/ppermute | solution.py:256
  123.3 0.4 collective-permute-done.31.refs_1_
  123.8 0.4 collective-permute-done.32.refs_3_
  124.2 4.6 %restore.1 = bf16[4,128,1152]{2,1,0:T(8,128)(2,1)} custom-call(s32[2]{0:T(128)S(1)} %pad_add_fusion.index_ref, bf16[4,128,1152]{2,1,0:T(8,128)(2,1)S(1)} %copy-done.1, f32[3,4,1152]{2,1,0:T(4,128)S(1)} %bitcast.57, bf16[2,4,16,1152]{3,2,1,0:T(8,128)(2,1)S(1)} %get-tuple-element.79.refs_0_, bf16[2,4,16,1152]{3,2,1,0:T(8,128)(2,1)S(1)} %collective-permute-done.31.refs_1_, ...), custom_call_target="tpu_custom_call" | custom-call | tf_op jit(solution)/shard_map/restore/pallas_call | solution.py:420
  (42 shorter events, 0.4 us)
Async XLA Ops:
  0.1 1.3 copy-start
  1.3 0.8 copy-start.4
  2.2 5.8 %copy-start.3 = (bf16[1152,432]{0,1:T(8,128)(2,1)S(1)}, bf16[1152,432]{0,1:T(8,128)(2,1)}, u32[]{:S(2)}) copy-start(bf16[1152,432]{0,1:T(8,128)(2,1)} %param.6) | copy-start | bytes 2985988
  2.2 6.1 %copy-start.2 = (bf16[1152,144]{0,1:T(8,128)(2,1)S(1)}, bf16[1152,144]{0,1:T(8,128)(2,1)}, u32[]{:S(2)}) copy-start(bf16[1152,144]{0,1:T(8,128)(2,1)} %param.7) | copy-start | bytes 995332
  3.8 4.7 %collective-permute-start.1 = (bf16[4,4,16,1152]{3,2,1,0:T(8,128)(2,1)S(1)}, bf16[4,4,16,1152]{3,2,1,0:T(8,128)(2,1)S(1)}, u32[]{:S(2)}, u32[]{:S(2)}) collective-permute-start(bf16[4,4,16,1152]{3,2,1,0:T(8,128)(2,1)S(1)} %get-tuple-element.47), channel_id=1, source_target_pairs={{0,1},{1,0},{2,3},{3,2},{4,5},{5,4},{6,7},{7,6},{8,9},{9,8},{10,11... | collective-permute-start | bytes 1769480 | tf_op jit(solution)/shard_map/ppermute | solution.py:256
  5.6 13.8 %collective-permute-start = (bf16[112,1152]{1,0:T(8,128)(2,1)S(1)}, bf16[112,1152]{1,0:T(8,128)(2,1)S(1)}, u32[]{:S(2)}, u32[]{:S(2)}) collective-permute-start(bf16[112,1152]{1,0:T(8,128)(2,1)S(1)} %dynamic-slice_bitcast_fusion), channel_id=1, source_target_pairs={{0,4},{1,5},{2,6},{3,7},{4,0},{5,1},{6,2},{7,3},{8,12},{9,13},{10,... | collective-permute-start | bytes 774152 | tf_op jit(solution)/shard_map/ppermute | solution.py:256
  8.0 12.9 %collective-permute-start.2 = (bf16[432,1152]{1,0:T(8,128)(2,1)S(1)}, bf16[432,1152]{1,0:T(8,128)(2,1)S(1)}, u32[]{:S(2)}, u32[]{:S(2)}) collective-permute-start(bf16[432,1152]{1,0:T(8,128)(2,1)S(1)} %bitcast.48), channel_id=1, source_target_pairs={{0,1},{1,0},{2,3},{3,2},{4,5},{5,4},{6,7},{7,6},{8,9},{9,8},{10,11... | collective-permute-start | bytes 2985992 | tf_op jit(solution)/shard_map/ppermute | solution.py:256
  8.3 11.1 %collective-permute-start.3 = (bf16[144,1152]{1,0:T(8,128)(2,1)S(1)}, bf16[144,1152]{1,0:T(8,128)(2,1)S(1)}, u32[]{:S(2)}, u32[]{:S(2)}) collective-permute-start(bf16[144,1152]{1,0:T(8,128)(2,1)S(1)} %bitcast.41), channel_id=1, source_target_pairs={{0,1},{1,0},{2,3},{3,2},{4,5},{5,4},{6,7},{7,6},{8,9},{9,8},{10,11... | collective-permute-start | bytes 995336 | tf_op jit(solution)/shard_map/ppermute | solution.py:256
  8.7 12.2 %collective-permute-start.4 = (bf16[2,4,16,1152]{3,2,1,0:T(8,128)(2,1)S(1)}, bf16[2,4,16,1152]{3,2,1,0:T(8,128)(2,1)S(1)}, u32[]{:S(2)}, u32[]{:S(2)}) collective-permute-start(bf16[2,4,16,1152]{3,2,1,0:T(8,128)(2,1)S(1)} %pad_maximum_fusion.6), channel_id=1, source_target_pairs={{0,2},{1,3},{2,0},{3,1},{4,6},{5,7},{6,4},{7,5},{8,10},{9,11},{10,... | collective-permute-start | bytes 884744 | tf_op jit(solution)/shard_map/ppermute | solution.py:256
  20.9 20.3 %collective-permute-start.9 = (bf16[2,2,4,16,1152]{4,3,2,1,0:T(8,128)(2,1)S(1)}, bf16[2,2,4,16,1152]{4,3,2,1,0:T(8,128)(2,1)S(1)}, u32[]{:S(2)}, u32[]{:S(2)}) collective-permute-start(bf16[2,2,4,16,1152]{4,3,2,1,0:T(8,128)(2,1)S(1)} %pad_maximum_fusion.2), channel_id=1, source_target_pairs={{0,24},{1,25},{2,26},{3,27},{4,12},{5,13},{6,14},{7,15},{8,0},{9,1... | collective-permute-start | bytes 1769480 | tf_op jit(solution)/shard_map/ppermute | solution.py:283
  23.2 18.1 %collective-permute-start.7 = (bf16[2,112,1152]{2,1,0:T(8,128)(2,1)S(1)}, bf16[2,112,1152]{2,1,0:T(8,128)(2,1)S(1)}, u32[]{:S(2)}, u32[]{:S(2)}) collective-permute-start(bf16[2,112,1152]{2,1,0:T(8,128)(2,1)S(1)} %pad_maximum_fusion.3), channel_id=1, source_target_pairs={{0,2},{1,3},{2,0},{3,1},{4,6},{5,7},{6,4},{7,5},{8,10},{9,11},{10,... | collective-permute-start | bytes 1548296 | tf_op jit(solution)/shard_map/ppermute | solution.py:256
  24.0 17.3 %collective-permute-start.8 = (bf16[2,4,16,1152]{3,2,1,0:T(8,128)(2,1)S(1)}, bf16[2,4,16,1152]{3,2,1,0:T(8,128)(2,1)S(1)}, u32[]{:S(2)}, u32[]{:S(2)}) collective-permute-start(bf16[2,4,16,1152]{3,2,1,0:T(8,128)(2,1)S(1)} %get-tuple-element.50), channel_id=1, source_target_pairs={{0,4},{1,5},{2,6},{3,7},{4,0},{5,1},{6,2},{7,3},{8,12},{9,13},{10,... | collective-permute-start | bytes 884744 | tf_op jit(solution)/shard_map/ppermute | solution.py:256
  24.3 16.3 %collective-permute-start.5 = (bf16[112,1152]{1,0:T(8,128)(2,1)S(1)}, bf16[112,1152]{1,0:T(8,128)(2,1)S(1)}, u32[]{:S(2)}, u32[]{:S(2)}) collective-permute-start(bf16[112,1152]{1,0:T(8,128)(2,1)S(1)} %collective-permute-done.refs_2_), channel_id=1, source_target_pairs={{0,8},{1,9},{2,10},{3,11},{4,12},{5,13},{6,14},{7,15},{8,0},{9,1},... | collective-permute-start | bytes 774152 | tf_op jit(solution)/shard_map/ppermute | solution.py:256
  25.5 15.1 %collective-permute-start.6 = (bf16[112,1152]{1,0:T(8,128)(2,1)S(1)}, bf16[112,1152]{1,0:T(8,128)(2,1)S(1)}, u32[]{:S(2)}, u32[]{:S(2)}) collective-permute-start(bf16[112,1152]{1,0:T(8,128)(2,1)S(1)} %collective-permute-done.refs_2_), channel_id=1, source_target_pairs={{0,16},{1,17},{2,18},{3,19},{4,20},{5,21},{6,22},{7,23},{8,24},{9,... | collective-permute-start | bytes 774152 | tf_op jit(solution)/shard_map/ppermute | solution.py:256
  41.3 13.8 %collective-permute-start.10 = (bf16[2,112,1152]{2,1,0:T(8,128)(2,1)S(1)}, bf16[2,112,1152]{2,1,0:T(8,128)(2,1)S(1)}, u32[]{:S(2)}, u32[]{:S(2)}) collective-permute-start(bf16[2,112,1152]{2,1,0:T(8,128)(2,1)S(1)} %collective-permute-done.7.refs_8_), channel_id=1, source_target_pairs={{0,8},{1,9},{2,10},{3,11},{4,12},{5,13},{6,14},{7,15},{8,0},{9,1},... | collective-permute-start | bytes 1548296 | tf_op jit(solution)/shard_map/ppermute | solution.py:256
  44.0 12.4 %collective-permute-start.11 = (bf16[2,112,1152]{2,1,0:T(8,128)(2,1)S(1)}, bf16[2,112,1152]{2,1,0:T(8,128)(2,1)S(1)}, u32[]{:S(2)}, u32[]{:S(2)}) collective-permute-start(bf16[2,112,1152]{2,1,0:T(8,128)(2,1)S(1)} %collective-permute-done.7.refs_8_), channel_id=1, source_target_pairs={{0,16},{1,17},{2,18},{3,19},{4,20},{5,21},{6,22},{7,23},{8,24},{9,... | collective-permute-start | bytes 1548296 | tf_op jit(solution)/shard_map/ppermute | solution.py:256
  45.2 11.2 %collective-permute-start.13 = (bf16[2,112,1152]{2,1,0:T(8,128)(2,1)S(1)}, bf16[2,112,1152]{2,1,0:T(8,128)(2,1)S(1)}, u32[]{:S(2)}, u32[]{:S(2)}) collective-permute-start(bf16[2,112,1152]{2,1,0:T(8,128)(2,1)S(1)} %collective-permute-done.7.refs_8_), channel_id=1, source_target_pairs={{0,1},{1,0},{2,3},{3,2},{4,5},{5,4},{6,7},{7,6},{8,9},{9,8},{10,11... | collective-permute-start | bytes 1548296 | tf_op jit(solution)/shard_map/ppermute | solution.py:256
  46.2 1.9 %collective-permute-start.12 = (bf16[112,1152]{1,0:T(8,128)(2,1)S(1)}, bf16[112,1152]{1,0:T(8,128)(2,1)S(1)}, u32[]{:S(2)}, u32[]{:S(2)}) collective-permute-start(bf16[112,1152]{1,0:T(8,128)(2,1)S(1)} %collective-permute-done.refs_2_), channel_id=1, source_target_pairs={{0,1},{1,0},{2,3},{3,2},{4,5},{5,4},{6,7},{7,6},{8,9},{9,8},{10,11... | collective-permute-start | bytes 774152 | tf_op jit(solution)/shard_map/ppermute | solution.py:256
  46.3 29.3 %collective-permute-start.20 = (bf16[17,16,1152]{2,1,0:T(8,128)(2,1)S(1)}, bf16[17,16,1152]{2,1,0:T(8,128)(2,1)S(1)}, u32[]{:S(2)}, u32[]{:S(2)}) collective-permute-start(bf16[17,16,1152]{2,1,0:T(8,128)(2,1)S(1)} %pad_maximum_fusion.1), channel_id=1, source_target_pairs={{0,6},{1,7},{2,4},{3,5},{4,2},{5,3},{6,0},{7,1},{8,14},{9,15},{10,... | collective-permute-start | bytes 1880072 | tf_op jit(solution)/shard_map/ppermute | solution.py:256
  56.4 6.0 %collective-permute-start.14 = (bf16[112,1152]{1,0:T(8,128)(2,1)S(1)}, bf16[112,1152]{1,0:T(8,128)(2,1)S(1)}, u32[]{:S(2)}, u32[]{:S(2)}) collective-permute-start(bf16[112,1152]{1,0:T(8,128)(2,1)S(1)} %slice_bitcast_fusion.1), channel_id=1, source_target_pairs={{0,16},{1,17},{2,18},{3,19},{4,20},{5,21},{6,22},{7,23},{8,24},{9,... | collective-permute-start | bytes 774152 | tf_op jit(solution)/shard_map/ppermute | solution.py:256
  57.8 7.3 %collective-permute-start.15 = (bf16[112,1152]{1,0:T(8,128)(2,1)S(1)}, bf16[112,1152]{1,0:T(8,128)(2,1)S(1)}, u32[]{:S(2)}, u32[]{:S(2)}) collective-permute-start(bf16[112,1152]{1,0:T(8,128)(2,1)S(1)} %slice_bitcast_fusion), channel_id=1, source_target_pairs={{0,8},{1,9},{2,10},{3,11},{4,12},{5,13},{6,14},{7,15},{8,0},{9,1},... | collective-permute-start | bytes 774152 | tf_op jit(solution)/shard_map/ppermute | solution.py:256
  58.2 9.5 %collective-permute-start.18 = (bf16[2,112,1152]{2,1,0:T(8,128)(2,1)S(1)}, bf16[2,112,1152]{2,1,0:T(8,128)(2,1)S(1)}, u32[]{:S(2)}, u32[]{:S(2)}) collective-permute-start(bf16[2,112,1152]{2,1,0:T(8,128)(2,1)S(1)} %collective-permute-done.10.refs_10_), channel_id=1, source_target_pairs={{0,1},{1,0},{2,3},{3,2},{4,5},{5,4},{6,7},{7,6},{8,9},{9,8},{10,11... | collective-permute-start | bytes 1548296 | tf_op jit(solution)/shard_map/ppermute | solution.py:256
  60.2 7.5 %collective-permute-start.19 = (bf16[2,112,1152]{2,1,0:T(8,128)(2,1)S(1)}, bf16[2,112,1152]{2,1,0:T(8,128)(2,1)S(1)}, u32[]{:S(2)}, u32[]{:S(2)}) collective-permute-start(bf16[2,112,1152]{2,1,0:T(8,128)(2,1)S(1)} %collective-permute-done.11.refs_12_), channel_id=1, source_target_pairs={{0,1},{1,0},{2,3},{3,2},{4,5},{5,4},{6,7},{7,6},{8,9},{9,8},{10,11... | collective-permute-start | bytes 1548296 | tf_op jit(solution)/shard_map/ppermute | solution.py:256
  62.4 4.2 %collective-permute-start.16 = (bf16[112,1152]{1,0:T(8,128)(2,1)S(1)}, bf16[112,1152]{1,0:T(8,128)(2,1)S(1)}, u32[]{:S(2)}, u32[]{:S(2)}) collective-permute-start(bf16[112,1152]{1,0:T(8,128)(2,1)S(1)} %collective-permute-done.5.refs_4_), channel_id=1, source_target_pairs={{0,1},{1,0},{2,3},{3,2},{4,5},{5,4},{6,7},{7,6},{8,9},{9,8},{10,11... | collective-permute-start | bytes 774152 | tf_op jit(solution)/shard_map/ppermute | solution.py:256
  65.1 2.6 %collective-permute-start.17 = (bf16[112,1152]{1,0:T(8,128)(2,1)S(1)}, bf16[112,1152]{1,0:T(8,128)(2,1)S(1)}, u32[]{:S(2)}, u32[]{:S(2)}) collective-permute-start(bf16[112,1152]{1,0:T(8,128)(2,1)S(1)} %collective-permute-done.6.refs_6_), channel_id=1, source_target_pairs={{0,1},{1,0},{2,3},{3,2},{4,5},{5,4},{6,7},{7,6},{8,9},{9,8},{10,11... | collective-permute-start | bytes 774152 | tf_op jit(solution)/shard_map/ppermute | solution.py:256
  66.6 9.8 %collective-permute-start.22 = (bf16[112,1152]{1,0:T(8,128)(2,1)S(1)}, bf16[112,1152]{1,0:T(8,128)(2,1)S(1)}, u32[]{:S(2)}, u32[]{:S(2)}) collective-permute-start(bf16[112,1152]{1,0:T(8,128)(2,1)S(1)} %collective-permute-done.6.refs_6_), channel_id=1, source_target_pairs={{0,8},{1,9},{2,10},{3,11},{4,12},{5,13},{6,14},{7,15},{8,0},{9,1},... | collective-permute-start | bytes 774152 | tf_op jit(solution)/shard_map/ppermute | solution.py:256
  75.6 2.7 %collective-permute-start.24 = (bf16[2,112,1152]{2,1,0:T(8,128)(2,1)S(1)}, bf16[2,112,1152]{2,1,0:T(8,128)(2,1)S(1)}, u32[]{:S(2)}, u32[]{:S(2)}) collective-permute-start(bf16[2,112,1152]{2,1,0:T(8,128)(2,1)S(1)} %pad_maximum_fusion.4.refs_8_.refs_7_), channel_id=1, source_target_pairs={{0,1},{1,0},{2,3},{3,2},{4,5},{5,4},{6,7},{7,6},{8,9},{9,8},{10,11... | collective-permute-start | bytes 1548296 | tf_op jit(solution)/shard_map/ppermute | solution.py:256
  76.3 1.9 %collective-permute-start.23 = (bf16[112,1152]{1,0:T(8,128)(2,1)S(1)}, bf16[112,1152]{1,0:T(8,128)(2,1)S(1)}, u32[]{:S(2)}, u32[]{:S(2)}) collective-permute-start(bf16[112,1152]{1,0:T(8,128)(2,1)S(1)} %collective-permute-done.22.refs_6_.refs_5_), channel_id=1, source_target_pairs={{0,1},{1,0},{2,3},{3,2},{4,5},{5,4},{6,7},{7,6},{8,9},{9,8},{10,11... | collective-permute-start | bytes 774152 | tf_op jit(solution)/shard_map/ppermute | solution.py:256
  76.5 19.4 %collective-permute-start.21 = (bf16[2,144,1152]{2,1,0:T(8,128)(2,1)S(1)}, bf16[2,144,1152]{2,1,0:T(8,128)(2,1)S(1)}, u32[]{:S(2)}, u32[]{:S(2)}) collective-permute-start(bf16[2,144,1152]{2,1,0:T(8,128)(2,1)S(1)} %pad_maximum_fusion), channel_id=1, source_target_pairs={{0,2},{1,3},{2,0},{3,1},{4,6},{5,7},{6,4},{7,5},{8,10},{9,11},{10,... | collective-permute-start | bytes 1990664 | tf_op jit(solution)/shard_map/ppermute | solution.py:256
  85.2 10.7 %collective-permute-start.25 = (bf16[4,4,16,640]{3,2,1,0:T(8,128)(2,1)S(1)}, bf16[4,4,16,640]{3,2,1,0:T(8,128)(2,1)S(1)}, u32[]{:S(2)}, u32[]{:S(2)}) collective-permute-start(bf16[4,4,16,640]{3,2,1,0:T(8,128)(2,1)S(1)} %get-tuple-element.69), channel_id=1, source_target_pairs={{0,8},{1,9},{2,10},{3,11},{4,28},{5,29},{6,30},{7,31},{8,16},{9,17... | collective-permute-start | bytes 983048 | tf_op jit(solution)/shard_map/ppermute | solution.py:283
  91.9 32.3 %copy-start.1 = (bf16[4,128,1152]{2,1,0:T(8,128)(2,1)S(1)}, bf16[4,128,1152]{2,1,0:T(8,128)(2,1)}, u32[]{:S(2)}) copy-start(bf16[4,128,1152]{2,1,0:T(8,128)(2,1)} %tokens_ref.3) | copy-start | bytes 3538948
  91.9 32.3 %copy-start.5 = (f32[4,3,1152]{2,0,1:T(4,128)S(1)}, f32[4,3,1152]{2,0,1:T(4,128)}, u32[]{:S(2)}) copy-start(f32[4,3,1152]{2,0,1:T(4,128)} %param.5) | copy-start | bytes 165892
  92.6 10.8 %collective-permute-start.27 = (bf16[4,16,1152]{2,1,0:T(8,128)(2,1)S(1)}, bf16[4,16,1152]{2,1,0:T(8,128)(2,1)S(1)}, u32[]{:S(2)}, u32[]{:S(2)}) collective-permute-start(bf16[4,16,1152]{2,1,0:T(8,128)(2,1)S(1)} %get-tuple-element.98), channel_id=1, source_target_pairs={{0,4},{1,5},{2,6},{3,7},{4,0},{5,1},{6,2},{7,3},{8,12},{9,13},{10,... | collective-permute-start | bytes 442376 | tf_op jit(solution)/shard_map/ppermute | solution.py:256
  94.5 12.3 %collective-permute-start.28 = (bf16[4,16,1152]{2,1,0:T(8,128)(2,1)S(1)}, bf16[4,16,1152]{2,1,0:T(8,128)(2,1)S(1)}, u32[]{:S(2)}, u32[]{:S(2)}) collective-permute-start(bf16[4,16,1152]{2,1,0:T(8,128)(2,1)S(1)} %get-tuple-element.97), channel_id=1, source_target_pairs={{0,5},{1,4},{2,7},{3,6},{4,1},{5,0},{6,3},{7,2},{8,13},{9,12},{10,... | collective-permute-start | bytes 442376 | tf_op jit(solution)/shard_map/ppermute | solution.py:256
  96.5 24.3 %collective-permute-start.26 = (bf16[2,4,16,1152]{3,2,1,0:T(8,128)(2,1)S(1)}, bf16[2,4,16,1152]{3,2,1,0:T(8,128)(2,1)S(1)}, u32[]{:S(2)}, u32[]{:S(2)}) collective-permute-start(bf16[2,4,16,1152]{3,2,1,0:T(8,128)(2,1)S(1)} %get-tuple-element.74), channel_id=1, source_target_pairs={{0,2},{1,3},{2,0},{3,1},{4,6},{5,7},{6,4},{7,5},{8,10},{9,11},{10,... | collective-permute-start | bytes 884744 | tf_op jit(solution)/shard_map/ppermute | solution.py:256
  97.1 20.1 %collective-permute-start.29 = (bf16[4,16,1152]{2,1,0:T(8,128)(2,1)S(1)}, bf16[4,16,1152]{2,1,0:T(8,128)(2,1)S(1)}, u32[]{:S(2)}, u32[]{:S(2)}) collective-permute-start(bf16[4,16,1152]{2,1,0:T(8,128)(2,1)S(1)} %get-tuple-element.96), channel_id=1, source_target_pairs={{0,6},{1,7},{2,4},{3,5},{4,2},{5,3},{6,0},{7,1},{8,14},{9,15},{10,... | collective-permute-start | bytes 442376 | tf_op jit(solution)/shard_map/ppermute | solution.py:256
  98.7 22.0 %collective-permute-start.30 = (bf16[4,16,1152]{2,1,0:T(8,128)(2,1)S(1)}, bf16[4,16,1152]{2,1,0:T(8,128)(2,1)S(1)}, u32[]{:S(2)}, u32[]{:S(2)}) collective-permute-start(bf16[4,16,1152]{2,1,0:T(8,128)(2,1)S(1)} %get-tuple-element.95), channel_id=1, source_target_pairs={{0,7},{1,6},{2,5},{3,4},{4,3},{5,2},{6,1},{7,0},{8,15},{9,14},{10,... | collective-permute-start | bytes 442376 | tf_op jit(solution)/shard_map/ppermute | solution.py:256
  120.8 3.4 %collective-permute-start.34 = (bf16[2,144,1152]{2,1,0:T(8,128)(2,1)S(1)}, bf16[2,144,1152]{2,1,0:T(8,128)(2,1)S(1)}, u32[]{:S(2)}, u32[]{:S(2)}) collective-permute-start(bf16[2,144,1152]{2,1,0:T(8,128)(2,1)S(1)} %collective-permute-done.21.refs_12_), channel_id=1, source_target_pairs={{0,1},{1,0},{2,3},{3,2},{4,5},{5,4},{6,7},{7,6},{8,9},{9,8},{10,11... | collective-permute-start | bytes 1990664 | tf_op jit(solution)/shard_map/ppermute | solution.py:256
  120.8 2.5 %collective-permute-start.33 = (bf16[144,1152]{1,0:T(8,128)(2,1)S(1)}, bf16[144,1152]{1,0:T(8,128)(2,1)S(1)}, u32[]{:S(2)}, u32[]{:S(2)}) collective-permute-start(bf16[144,1152]{1,0:T(8,128)(2,1)S(1)} %bitcast.46), channel_id=1, source_target_pairs={{0,1},{1,0},{2,3},{3,2},{4,5},{5,4},{6,7},{7,6},{8,9},{9,8},{10,11... | collective-permute-start | bytes 995336 | tf_op jit(solution)/shard_map/ppermute | solution.py:256
  121.3 2.5 %collective-permute-start.31 = (bf16[2,4,16,1152]{3,2,1,0:T(8,128)(2,1)S(1)}, bf16[2,4,16,1152]{3,2,1,0:T(8,128)(2,1)S(1)}, u32[]{:S(2)}, u32[]{:S(2)}) collective-permute-start(bf16[2,4,16,1152]{3,2,1,0:T(8,128)(2,1)S(1)} %get-tuple-element.79.refs_0_), channel_id=1, source_target_pairs={{0,1},{1,0},{2,3},{3,2},{4,5},{5,4},{6,7},{7,6},{8,9},{9,8},{10,11... | collective-permute-start | bytes 884744 | tf_op jit(solution)/shard_map/ppermute | solution.py:256
  121.3 2.9 %collective-permute-start.32 = (bf16[2,4,16,1152]{3,2,1,0:T(8,128)(2,1)S(1)}, bf16[2,4,16,1152]{3,2,1,0:T(8,128)(2,1)S(1)}, u32[]{:S(2)}, u32[]{:S(2)}) collective-permute-start(bf16[2,4,16,1152]{3,2,1,0:T(8,128)(2,1)S(1)} %collective-permute-done.26.refs_2_), channel_id=1, source_target_pairs={{0,1},{1,0},{2,3},{3,2},{4,5},{5,4},{6,7},{7,6},{8,9},{9,8},{10,11... | collective-permute-start | bytes 884744 | tf_op jit(solution)/shard_map/ppermute | solution.py:256

commit v7 on v6

--- a/solution.py
+++ b/solution.py
@@ -121,7 +121,7 @@
     for d in range(count):
         owner = lax.bitwise_xor(index, d)
         near = kind == 1 and d < count // 2
-        source = (x_refs[-1] if near else x_refs[d // 2]).at[pl.ds((d if near else d % 2) * groups, groups)]
+        source = x_refs[count // 2 + d // 2 if near else d // 2].at[pl.ds(d % 2 * groups, groups)]
         sources.append(pltpu.make_async_copy(source, xs.at[:, owner], sems.at[d]))
     for copy in sources:
         copy.start()
@@ -282,8 +282,8 @@
                  for s in range(slabs) for i in range(count)]
         return lax.ppermute(value, ("slab", "seq"), pairs)
 
-    def following_of(values):
-        return to_neighbour(jnp.stack(values), -1)
+    def following_of(value):
+        return to_neighbour(value, -1)
 
     wide, narrow = qkv_weight.T, out_weight.T
     out_operands, out_moves = [], []
@@ -303,11 +303,14 @@
         far = hop(mine, 4)
         wide_other, narrow_other = hop(wide, 1), hop(narrow, 1)
         blocks[1] = hop(pair[1], 2)
-        far, mine, pair, wide_other, narrow_other, blocks[1] = tie((far, mine, pair, wide_other, narrow_other, blocks[1]))
+        following = [following_of(pair[0])]
+        near_and_far = jnp.stack([mine, far])
+        blocks[1], far, near_and_far, pair, wide_other, narrow_other, following = tie(
+            (blocks[1], far, near_and_far, pair, wide_other, narrow_other, following))
         ax, ay = hop(far, 0, x), hop(far, 0, y)
-        rest = hop(jnp.stack([mine, far]), 2)
+        rest = hop(near_and_far, 2)
         blocks[2] = hop(pair[2], 4)
-        following = following_of(blocks[:2])
+        following.append(following_of(blocks[1]))
         ax, ay, rest, blocks[2], following, pair[3] = tie((ax, ay, rest, blocks[2], following, pair[3]))
         bx, by = hop(rest, 0, x), hop(rest, 0, y)
         both = jnp.concatenate([pair[3].reshape(-1, ROWS, width), narrow.reshape(-1, ROWS, width)], axis=0)
@@ -352,7 +355,7 @@
         out_operands = [lax.all_gather(narrow, "seq", axis=0, tiled=True)]
         out_moves = [(0, (), 0)]
         blocks = [hop(pair[z], 2 * z) if z else pair[z] for z in range(chips)]
-        following = following_of(blocks[: chips // 2])
+        following = [following_of(value) for value in blocks[: chips // 2]]
 
     tokens = count * block_rows
 
@@ -382,7 +385,7 @@
             name=("windowed", "shifted")[kind],
         )(own_index, *inputs, full, *operands)
 
-    second_near, second_far = attention(1, blocks + [following])
+    second_near, second_far = attention(1, blocks + following)
     if shared:
         out_rest = hop(jnp.stack([narrow, out_far]), 2)
     second_near = to_neighbour(second_near, 1)
@@ -406,7 +409,7 @@
     arrived = [hop(sent[z], 2 * z) if z else sent[z] for z in range(chips // 2)]
     singles = [hop(sent[z][n], 2 * z + n)[None] for z in range(chips // 2, chips) for n in range(2)]
     if shared:
-        out_rest, arrived, singles = tie((out_rest, arrived, singles))
+        arrived, singles = tie((arrived, singles))
     returned = []
     for value in arrived:
         returned += [value, hop(value, 1)]

time: 129 us -> 126 us (0.977)
  waiting for transfers between devices: 65.2 us -> 47.5 us
  starting transfers between devices: 30.7 us -> 45.7 us
    ppermute x33, waiting for transfers between devices: 65.2 us -> 47.5 us  [hop(): return lax.ppermute(value, ('slab', 'seq'), pairs)]
    ppermute x33, starting transfers between devices: 28.2 us -> 42.1 us  [hop(): return lax.ppermute(value, ('slab', 'seq'), pairs)]
    ppermute x2 -> x3, starting transfers between devices: 2.49 us -> 3.6 us  [to_neighbour(): return lax.ppermute(value, ('slab', 'seq'), pairs)]
  transfers between devices with their start and end apart: 35 -> 36, of which waited for: 17 -> 17; matrix products, arithmetic and copies ran while one was open for 1% -> 1% of each run, Pallas kernels for 17% -> 18%
where the time goes in v7:
time: 126 us
  waiting for transfers between devices  47.5 us (38%)
  starting transfers between devices  45.7 us (36%)
  Pallas kernels  28.8 us (23%)
  local copies, waits for them, and re-layouts  3.33 us (3%)
    ppermute x33, waiting for transfers between devices, hop(): return lax.ppermute(value, ('slab', 'seq'), pairs)  47.5 us
    ppermute x33, starting transfers between devices, hop(): return lax.ppermute(value, ('slab', 'seq'), pairs)  42.1 us
    pallas_call x2, Pallas kernels, attention(): pl.pallas_call(functools.partial(block_kernel, plan, frames), out_shape=[...  13.4 us
    pallas_call x1, Pallas kernels, per_device(): pl.pallas_call(functools.partial(gather_kernel, plan), out_shape=jax.Shap...  7.9 us
    pallas_call x1, Pallas kernels, per_device(): pl.pallas_call(functools.partial(restore_kernel, plan), out_shape=jax.Sha...  4.65 us
    ppermute x3, starting transfers between devices, to_neighbour(): return lax.ppermute(value, ('slab', 'seq'), pairs)  3.6 us
  transfers between devices with their start and end apart: 36, of which 17 were waited for; matrix products, arithmetic and copies ran while one was open for 1% of the time, Pallas kernels for 18%

profile of v7, /device:TPU:9, one launch (start us, length us, event | category | flops | bytes accessed | tf_op | source)
XLA Modules:
  0.0 126.2 jit_solution(16793591573951787713)
XLA Ops:
  0.0 0.1 pad_add_fusion.index_ref
  0.1 1.3 %copy-done = bf16[4,128,1152]{2,1,0:T(8,128)(2,1)S(1)} copy-done((bf16[4,128,1152]{2,1,0:T(8,128)(2,1)S(1)}, bf16[4,128,1152]{2,1,0:T(8,128)(2,1)}, u32[]{:S(2)}) %copy-start) | copy-done | bytes 1179672
  1.3 0.8 copy-done.4
  2.2 1.7 %norm.1 = (bf16[4,4,16,1152]{3,2,1,0:T(8,128)(2,1)S(1)}, bf16[4,4,16,1152]{3,2,1,0:T(8,128)(2,1)S(1)}) custom-call(s32[2]{0:T(128)S(1)} %pad_add_fusion.index_ref, bf16[4,128,1152]{2,1,0:T(8,128)(2,1)S(1)} %copy-done, f32[3,4,1152]{2,1,0:T(4,128)S(1)} %bitcast.53), custom_call_target="tpu_custom_call" | custom-call | tf_op jit(solution)/shard_map/norm/pallas_call | solution.py:268
  3.8 0.7 collective-permute-start
  4.6 1.0 dynamic-slice_bitcast_fusion
  5.6 2.4 %collective-permute-start.2 = (bf16[112,1152]{1,0:T(8,128)(2,1)S(1)}, bf16[112,1152]{1,0:T(8,128)(2,1)S(1)}, u32[]{:S(2)}, u32[]{:S(2)}) collective-permute-start(bf16[112,1152]{1,0:T(8,128)(2,1)S(1)} %get-tuple-element.90), channel_id=1, source_target_pairs={{0,4},{1,5},{2,6},{3,7},{4,0},{5,1},{6,2},{7,3},{8,12},{9,13},{10,... | collective-permute-start | bytes 774152 | tf_op jit(solution)/shard_map/ppermute | solution.py:256
  8.0 0.3 collective-permute-start.3
  8.3 0.2 collective-permute-start.4
  8.7 2.2 %collective-permute-start.5 = (bf16[2,4,16,1152]{3,2,1,0:T(8,128)(2,1)S(1)}, bf16[2,4,16,1152]{3,2,1,0:T(8,128)(2,1)S(1)}, u32[]{:S(2)}, u32[]{:S(2)}) collective-permute-start(bf16[2,4,16,1152]{3,2,1,0:T(8,128)(2,1)S(1)} %pad_maximum_fusion.4), channel_id=1, source_target_pairs={{0,24},{1,25},{2,26},{3,27},{4,12},{5,13},{6,14},{7,15},{8,0},{9,1... | collective-permute-start | bytes 884744 | tf_op jit(solution)/shard_map/ppermute | solution.py:283
  10.9 0.2 collective-permute-start.1
  11.1 8.3 %collective-permute-done.2.refs_2_ = bf16[112,1152]{1,0:T(8,128)(2,1)S(1)} collective-permute-done((bf16[112,1152]{1,0:T(8,128)(2,1)S(1)}, bf16[112,1152]{1,0:T(8,128)(2,1)S(1)}, u32[]{:S(2)}, u32[]{:S(2)}) %collective-permute-start.2) | collective-permute-done | bytes 258080 | tf_op jit(solution)/shard_map/ppermute | solution.py:256
  19.4 0.1 pad_maximum_fusion.2
  19.5 0.1 pad_maximum_fusion.6
  19.6 1.7 %collective-permute-done.1 = bf16[2,4,16,1152]{3,2,1,0:T(8,128)(2,1)S(1)} collective-permute-done((bf16[2,4,16,1152]{3,2,1,0:T(8,128)(2,1)S(1)}, bf16[2,4,16,1152]{3,2,1,0:T(8,128)(2,1)S(1)}, u32[]{:S(2)}, u32[]{:S(2)}) %collective-permute-start.1) | collective-permute-done | bytes 294944 | tf_op jit(solution)/shard_map/ppermute | solution.py:256
  21.3 2.2 %collective-permute-start.8 = (bf16[2,112,1152]{2,1,0:T(8,128)(2,1)S(1)}, bf16[2,112,1152]{2,1,0:T(8,128)(2,1)S(1)}, u32[]{:S(2)}, u32[]{:S(2)}) collective-permute-start(bf16[2,112,1152]{2,1,0:T(8,128)(2,1)S(1)} %pad_maximum_fusion.2), channel_id=1, source_target_pairs={{0,2},{1,3},{2,0},{3,1},{4,6},{5,7},{6,4},{7,5},{8,10},{9,11},{10,... | collective-permute-start | bytes 1548296 | tf_op jit(solution)/shard_map/ppermute | solution.py:256
  23.5 0.3 collective-permute-start.10
  23.8 1.0 collective-permute-start.9
  24.8 1.2 collective-permute-start.6
  26.0 0.2 collective-permute-start.7
  26.2 9.6 %collective-permute-done.6.refs_4_ = bf16[112,1152]{1,0:T(8,128)(2,1)S(1)} collective-permute-done((bf16[112,1152]{1,0:T(8,128)(2,1)S(1)}, bf16[112,1152]{1,0:T(8,128)(2,1)S(1)}, u32[]{:S(2)}, u32[]{:S(2)}) %collective-permute-start.6) | collective-permute-done | bytes 258080 | tf_op jit(solution)/shard_map/ppermute | solution.py:256
  35.8 4.7 %collective-permute-done.9 = bf16[2,4,16,1152]{3,2,1,0:T(8,128)(2,1)S(1)} collective-permute-done((bf16[2,4,16,1152]{3,2,1,0:T(8,128)(2,1)S(1)}, bf16[2,4,16,1152]{3,2,1,0:T(8,128)(2,1)S(1)}, u32[]{:S(2)}, u32[]{:S(2)}) %collective-permute-start.9) | collective-permute-done | bytes 294944 | tf_op jit(solution)/shard_map/ppermute | solution.py:256
  40.5 1.2 collective-permute-start.11
  41.7 0.6 collective-permute-start.12
  42.4 2.5 %collective-permute-start.14 = (bf16[2,112,1152]{2,1,0:T(8,128)(2,1)S(1)}, bf16[2,112,1152]{2,1,0:T(8,128)(2,1)S(1)}, u32[]{:S(2)}, u32[]{:S(2)}) collective-permute-start(bf16[2,112,1152]{2,1,0:T(8,128)(2,1)S(1)} %collective-permute-done.8.refs_8_), channel_id=1, source_target_pairs={{0,1},{1,0},{2,3},{3,2},{4,5},{5,4},{6,7},{7,6},{8,9},{9,8},{10,11... | collective-permute-start | bytes 1548296 | tf_op jit(solution)/shard_map/ppermute | solution.py:256
  44.8 0.1 pad_maximum_fusion.1
  44.9 0.8 collective-permute-start.21
  45.7 1.0 collective-permute-done.13.refs_3_
  46.7 5.0 %collective-permute-done.11.refs_10_ = bf16[2,112,1152]{2,1,0:T(8,128)(2,1)S(1)} collective-permute-done((bf16[2,112,1152]{2,1,0:T(8,128)(2,1)S(1)}, bf16[2,112,1152]{2,1,0:T(8,128)(2,1)S(1)}, u32[]{:S(2)}, u32[]{:S(2)}) %collective-permute-start.11) | collective-permute-done | bytes 516128 | tf_op jit(solution)/shard_map/ppermute | solution.py:256
  51.7 0.9 collective-permute-done.12.refs_12_
  52.7 0.8 collective-permute-start.15
  53.5 0.8 collective-permute-start.16
  54.3 3.8 %collective-permute-start.19 = (bf16[2,112,1152]{2,1,0:T(8,128)(2,1)S(1)}, bf16[2,112,1152]{2,1,0:T(8,128)(2,1)S(1)}, u32[]{:S(2)}, u32[]{:S(2)}) collective-permute-start(bf16[2,112,1152]{2,1,0:T(8,128)(2,1)S(1)} %collective-permute-done.11.refs_10_), channel_id=1, source_target_pairs={{0,1},{1,0},{2,3},{3,2},{4,5},{5,4},{6,7},{7,6},{8,9},{9,8},{10,11... | collective-permute-start | bytes 1548296 | tf_op jit(solution)/shard_map/ppermute | solution.py:256
  58.1 0.1 collective-permute-done.15
  58.3 4.1 %collective-permute-start.17 = (bf16[112,1152]{1,0:T(8,128)(2,1)S(1)}, bf16[112,1152]{1,0:T(8,128)(2,1)S(1)}, u32[]{:S(2)}, u32[]{:S(2)}) collective-permute-start(bf16[112,1152]{1,0:T(8,128)(2,1)S(1)} %collective-permute-done.6.refs_4_), channel_id=1, source_target_pairs={{0,1},{1,0},{2,3},{3,2},{4,5},{5,4},{6,7},{7,6},{8,9},{9,8},{10,11... | collective-permute-start | bytes 774152 | tf_op jit(solution)/shard_map/ppermute | solution.py:256
  62.3 1.0 collective-permute-start.18
  63.4 0.1 collective-permute-done.17.refs_5_
  63.5 0.8 collective-permute-start.22
  64.3 0.2 collective-permute-done.18.refs_7_
  64.5 7.9 %gather.1.refs_4_.refs_6_ = bf16[3584,1152]{1,0:T(8,128)(2,1)S(1)} custom-call(s32[2]{0:T(128)S(1)} %pad_add_fusion.index_ref, bf16[432,1152]{1,0:T(8,128)(2,1)S(1)} %bitcast.49, bf16[432,1152]{1,0:T(8,128)(2,1)S(1)} %collective-permute-done.3.refs_1_, bf16[112,1152]{1,0:T(8,128)(2,1)S(1)} %collective-permute-done.2.refs_2_, ...), custom_call_target="tpu_custom_call" | custom-call | tf_op jit(solution)/shard_map/gather/pallas_call | solution.py:331
  72.4 1.2 collective-permute-done.21.refs_3_
  73.6 1.3 %collective-permute-start.24 = (bf16[2,112,1152]{2,1,0:T(8,128)(2,1)S(1)}, bf16[2,112,1152]{2,1,0:T(8,128)(2,1)S(1)}, u32[]{:S(2)}, u32[]{:S(2)}) collective-permute-start(bf16[2,112,1152]{2,1,0:T(8,128)(2,1)S(1)} %pad_maximum_fusion.3.refs_7_.refs_9_), channel_id=1, source_target_pairs={{0,1},{1,0},{2,3},{3,2},{4,5},{5,4},{6,7},{7,6},{8,9},{9,8},{10,11... | collective-permute-start | bytes 1548296 | tf_op jit(solution)/shard_map/ppermute | solution.py:256
  74.9 0.1 pad_maximum_fusion
  75.0 0.1 collective-permute-start.25
  75.1 1.7 %collective-permute-done.23.refs_6_.refs_8_ = bf16[112,1152]{1,0:T(8,128)(2,1)S(1)} collective-permute-done((bf16[112,1152]{1,0:T(8,128)(2,1)S(1)}, bf16[112,1152]{1,0:T(8,128)(2,1)S(1)}, u32[]{:S(2)}, u32[]{:S(2)}) %collective-permute-start.23) | collective-permute-done | bytes 258080 | tf_op jit(solution)/shard_map/ppermute | solution.py:256
  76.8 6.9 %shifted.1 = (bf16[4,4,16,640]{3,2,1,0:T(8,128)(2,1)S(1)}, bf16[4,4,16,640]{3,2,1,0:T(8,128)(2,1)S(1)}) custom-call(s32[2]{0:T(128)S(1)} %pad_add_fusion.index_ref, bf16[8,16,1152]{2,1,0:T(8,128)(2,1)S(1)} %bitcast.51, bf16[8,16,1152]{2,1,0:T(8,128)(2,1)S(1)} %bitcast.59, bf16[8,16,1152]{2,1,0:T(8,128)(2,1)S(1)} %bitcast.62, ...), custom_call_target="tpu_custom_call" | custom-call | flops 40000000000 | bytes 8388608 | tf_op jit(solution)/shard_map/shifted/pallas_call | solution.py:367
  83.7 1.1 collective-permute-start.26
  84.8 6.5 %windowed.1 = (bf16[4,4,16,640]{3,2,1,0:T(8,128)(2,1)S(1)}, bf16[4,4,16,640]{3,2,1,0:T(8,128)(2,1)S(1)}) custom-call(s32[2]{0:T(128)S(1)} %pad_add_fusion.index_ref, bf16[8,16,1152]{2,1,0:T(8,128)(2,1)S(1)} %bitcast.52, bf16[8,16,1152]{2,1,0:T(8,128)(2,1)S(1)} %bitcast.60, bf16[8,16,1152]{2,1,0:T(8,128)(2,1)S(1)} %bitcast.63, ...), custom_call_target="tpu_custom_call" | custom-call | flops 40000000000 | bytes 8388608 | tf_op jit(solution)/shard_map/windowed/pallas_call | solution.py:367
  91.3 0.6 merge.3
  92.0 0.6 collective-permute-start.28
  92.6 2.7 %collective-permute-start.29 = (bf16[4,16,1152]{2,1,0:T(8,128)(2,1)S(1)}, bf16[4,16,1152]{2,1,0:T(8,128)(2,1)S(1)}, u32[]{:S(2)}, u32[]{:S(2)}) collective-permute-start(bf16[4,16,1152]{2,1,0:T(8,128)(2,1)S(1)} %get-tuple-element.101), channel_id=1, source_target_pairs={{0,5},{1,4},{2,7},{3,6},{4,1},{5,0},{6,3},{7,2},{8,13},{9,12},{10,... | collective-permute-start | bytes 442376 | tf_op jit(solution)/shard_map/ppermute | solution.py:256
  95.2 0.6 merge.2
  95.9 0.2 collective-permute-start.27
  96.1 0.1 collective-permute-start.35
  96.2 1.0 collective-permute-start.30
  97.2 0.5 collective-permute-done.28
  97.7 7.1 %collective-permute-start.31 = (bf16[4,16,1152]{2,1,0:T(8,128)(2,1)S(1)}, bf16[4,16,1152]{2,1,0:T(8,128)(2,1)S(1)}, u32[]{:S(2)}, u32[]{:S(2)}) collective-permute-start(bf16[4,16,1152]{2,1,0:T(8,128)(2,1)S(1)} %get-tuple-element.99), channel_id=1, source_target_pairs={{0,7},{1,6},{2,5},{3,4},{4,3},{5,2},{6,1},{7,0},{8,15},{9,14},{10,... | collective-permute-start | bytes 442376 | tf_op jit(solution)/shard_map/ppermute | solution.py:256
  104.9 3.5 %collective-permute-start.34 = (bf16[144,1152]{1,0:T(8,128)(2,1)S(1)}, bf16[144,1152]{1,0:T(8,128)(2,1)S(1)}, u32[]{:S(2)}, u32[]{:S(2)}) collective-permute-start(bf16[144,1152]{1,0:T(8,128)(2,1)S(1)} %bitcast.46), channel_id=1, source_target_pairs={{0,1},{1,0},{2,3},{3,2},{4,5},{5,4},{6,7},{7,6},{8,9},{9,8},{10,11... | collective-permute-start | bytes 995336 | tf_op jit(solution)/shard_map/ppermute | solution.py:256
  108.4 6.6 %collective-permute-done.30 = bf16[4,16,1152]{2,1,0:T(8,128)(2,1)S(1)} collective-permute-done((bf16[4,16,1152]{2,1,0:T(8,128)(2,1)S(1)}, bf16[4,16,1152]{2,1,0:T(8,128)(2,1)S(1)}, u32[]{:S(2)}, u32[]{:S(2)}) %collective-permute-start.30) | collective-permute-done | bytes 147488 | tf_op jit(solution)/shard_map/ppermute | solution.py:256
  115.0 4.3 %collective-permute-done.31 = bf16[4,16,1152]{2,1,0:T(8,128)(2,1)S(1)} collective-permute-done((bf16[4,16,1152]{2,1,0:T(8,128)(2,1)S(1)}, bf16[4,16,1152]{2,1,0:T(8,128)(2,1)S(1)}, u32[]{:S(2)}, u32[]{:S(2)}) %collective-permute-start.31) | collective-permute-done | bytes 147488 | tf_op jit(solution)/shard_map/ppermute | solution.py:256
  119.4 0.5 collective-permute-start.33
  119.9 1.1 collective-permute-done.32.refs_1_
  120.9 0.4 collective-permute-done.33.refs_3_
  121.4 4.6 %restore.1 = bf16[4,128,1152]{2,1,0:T(8,128)(2,1)} custom-call(s32[2]{0:T(128)S(1)} %pad_add_fusion.index_ref, bf16[4,128,1152]{2,1,0:T(8,128)(2,1)S(1)} %copy-done.1, f32[3,4,1152]{2,1,0:T(4,128)S(1)} %bitcast.54, bf16[2,4,16,1152]{3,2,1,0:T(8,128)(2,1)S(1)} %get-tuple-element.81.refs_0_, bf16[2,4,16,1152]{3,2,1,0:T(8,128)(2,1)S(1)} %collective-permute-done.32.refs_1_, ...), custom_call_target="tpu_custom_call" | custom-call | tf_op jit(solution)/shard_map/restore/pallas_call | solution.py:423
  (43 shorter events, 0.4 us)
Async XLA Ops:
  0.1 1.3 %copy-start = (bf16[4,128,1152]{2,1,0:T(8,128)(2,1)S(1)}, bf16[4,128,1152]{2,1,0:T(8,128)(2,1)}, u32[]{:S(2)}) copy-start(bf16[4,128,1152]{2,1,0:T(8,128)(2,1)} %tokens_ref.3) | copy-start | bytes 3538948
  1.3 0.8 copy-start.4
  2.2 5.8 %copy-start.3 = (bf16[1152,432]{0,1:T(8,128)(2,1)S(1)}, bf16[1152,432]{0,1:T(8,128)(2,1)}, u32[]{:S(2)}) copy-start(bf16[1152,432]{0,1:T(8,128)(2,1)} %param.6) | copy-start | bytes 2985988
  2.2 6.1 %copy-start.2 = (bf16[1152,144]{0,1:T(8,128)(2,1)S(1)}, bf16[1152,144]{0,1:T(8,128)(2,1)}, u32[]{:S(2)}) copy-start(bf16[1152,144]{0,1:T(8,128)(2,1)} %param.7) | copy-start | bytes 995332
  3.8 4.7 %collective-permute-start = (bf16[4,4,16,1152]{3,2,1,0:T(8,128)(2,1)S(1)}, bf16[4,4,16,1152]{3,2,1,0:T(8,128)(2,1)S(1)}, u32[]{:S(2)}, u32[]{:S(2)}) collective-permute-start(bf16[4,4,16,1152]{3,2,1,0:T(8,128)(2,1)S(1)} %get-tuple-element.48), channel_id=1, source_target_pairs={{0,1},{1,0},{2,3},{3,2},{4,5},{5,4},{6,7},{7,6},{8,9},{9,8},{10,11... | collective-permute-start | bytes 1769480 | tf_op jit(solution)/shard_map/ppermute | solution.py:256
  5.6 13.8 %collective-permute-start.2 = (bf16[112,1152]{1,0:T(8,128)(2,1)S(1)}, bf16[112,1152]{1,0:T(8,128)(2,1)S(1)}, u32[]{:S(2)}, u32[]{:S(2)}) collective-permute-start(bf16[112,1152]{1,0:T(8,128)(2,1)S(1)} %get-tuple-element.90), channel_id=1, source_target_pairs={{0,4},{1,5},{2,6},{3,7},{4,0},{5,1},{6,2},{7,3},{8,12},{9,13},{10,... | collective-permute-start | bytes 774152 | tf_op jit(solution)/shard_map/ppermute | solution.py:256
  8.0 13.3 %collective-permute-start.3 = (bf16[432,1152]{1,0:T(8,128)(2,1)S(1)}, bf16[432,1152]{1,0:T(8,128)(2,1)S(1)}, u32[]{:S(2)}, u32[]{:S(2)}) collective-permute-start(bf16[432,1152]{1,0:T(8,128)(2,1)S(1)} %bitcast.48), channel_id=1, source_target_pairs={{0,1},{1,0},{2,3},{3,2},{4,5},{5,4},{6,7},{7,6},{8,9},{9,8},{10,11... | collective-permute-start | bytes 2985992 | tf_op jit(solution)/shard_map/ppermute | solution.py:256
  8.3 11.3 %collective-permute-start.4 = (bf16[144,1152]{1,0:T(8,128)(2,1)S(1)}, bf16[144,1152]{1,0:T(8,128)(2,1)S(1)}, u32[]{:S(2)}, u32[]{:S(2)}) collective-permute-start(bf16[144,1152]{1,0:T(8,128)(2,1)S(1)} %bitcast.41), channel_id=1, source_target_pairs={{0,1},{1,0},{2,3},{3,2},{4,5},{5,4},{6,7},{7,6},{8,9},{9,8},{10,11... | collective-permute-start | bytes 995336 | tf_op jit(solution)/shard_map/ppermute | solution.py:256
  8.7 10.9 %collective-permute-start.5 = (bf16[2,4,16,1152]{3,2,1,0:T(8,128)(2,1)S(1)}, bf16[2,4,16,1152]{3,2,1,0:T(8,128)(2,1)S(1)}, u32[]{:S(2)}, u32[]{:S(2)}) collective-permute-start(bf16[2,4,16,1152]{3,2,1,0:T(8,128)(2,1)S(1)} %pad_maximum_fusion.4), channel_id=1, source_target_pairs={{0,24},{1,25},{2,26},{3,27},{4,12},{5,13},{6,14},{7,15},{8,0},{9,1... | collective-permute-start | bytes 884744 | tf_op jit(solution)/shard_map/ppermute | solution.py:283
  10.9 10.4 %collective-permute-start.1 = (bf16[2,4,16,1152]{3,2,1,0:T(8,128)(2,1)S(1)}, bf16[2,4,16,1152]{3,2,1,0:T(8,128)(2,1)S(1)}, u32[]{:S(2)}, u32[]{:S(2)}) collective-permute-start(bf16[2,4,16,1152]{3,2,1,0:T(8,128)(2,1)S(1)} %pad_maximum_fusion.5), channel_id=1, source_target_pairs={{0,2},{1,3},{2,0},{3,1},{4,6},{5,7},{6,4},{7,5},{8,10},{9,11},{10,... | collective-permute-start | bytes 884744 | tf_op jit(solution)/shard_map/ppermute | solution.py:256
  21.3 19.2 %collective-permute-start.8 = (bf16[2,112,1152]{2,1,0:T(8,128)(2,1)S(1)}, bf16[2,112,1152]{2,1,0:T(8,128)(2,1)S(1)}, u32[]{:S(2)}, u32[]{:S(2)}) collective-permute-start(bf16[2,112,1152]{2,1,0:T(8,128)(2,1)S(1)} %pad_maximum_fusion.2), channel_id=1, source_target_pairs={{0,2},{1,3},{2,0},{3,1},{4,6},{5,7},{6,4},{7,5},{8,10},{9,11},{10,... | collective-permute-start | bytes 1548296 | tf_op jit(solution)/shard_map/ppermute | solution.py:256
  23.5 12.3 %collective-permute-start.10 = (bf16[2,4,16,1152]{3,2,1,0:T(8,128)(2,1)S(1)}, bf16[2,4,16,1152]{3,2,1,0:T(8,128)(2,1)S(1)}, u32[]{:S(2)}, u32[]{:S(2)}) collective-permute-start(bf16[2,4,16,1152]{3,2,1,0:T(8,128)(2,1)S(1)} %collective-permute-done.1), channel_id=1, source_target_pairs={{0,24},{1,25},{2,26},{3,27},{4,12},{5,13},{6,14},{7,15},{8,0},{9,1... | collective-permute-start | bytes 884744 | tf_op jit(solution)/shard_map/ppermute | solution.py:283
  23.8 16.7 %collective-permute-start.9 = (bf16[2,4,16,1152]{3,2,1,0:T(8,128)(2,1)S(1)}, bf16[2,4,16,1152]{3,2,1,0:T(8,128)(2,1)S(1)}, u32[]{:S(2)}, u32[]{:S(2)}) collective-permute-start(bf16[2,4,16,1152]{3,2,1,0:T(8,128)(2,1)S(1)} %get-tuple-element.52), channel_id=1, source_target_pairs={{0,4},{1,5},{2,6},{3,7},{4,0},{5,1},{6,2},{7,3},{8,12},{9,13},{10,... | collective-permute-start | bytes 884744 | tf_op jit(solution)/shard_map/ppermute | solution.py:256
  24.8 11.0 %collective-permute-start.6 = (bf16[112,1152]{1,0:T(8,128)(2,1)S(1)}, bf16[112,1152]{1,0:T(8,128)(2,1)S(1)}, u32[]{:S(2)}, u32[]{:S(2)}) collective-permute-start(bf16[112,1152]{1,0:T(8,128)(2,1)S(1)} %collective-permute-done.2.refs_2_), channel_id=1, source_target_pairs={{0,8},{1,9},{2,10},{3,11},{4,12},{5,13},{6,14},{7,15},{8,0},{9,1},... | collective-permute-start | bytes 774152 | tf_op jit(solution)/shard_map/ppermute | solution.py:256
  26.0 9.8 %collective-permute-start.7 = (bf16[112,1152]{1,0:T(8,128)(2,1)S(1)}, bf16[112,1152]{1,0:T(8,128)(2,1)S(1)}, u32[]{:S(2)}, u32[]{:S(2)}) collective-permute-start(bf16[112,1152]{1,0:T(8,128)(2,1)S(1)} %collective-permute-done.2.refs_2_), channel_id=1, source_target_pairs={{0,16},{1,17},{2,18},{3,19},{4,20},{5,21},{6,22},{7,23},{8,24},{9,... | collective-permute-start | bytes 774152 | tf_op jit(solution)/shard_map/ppermute | solution.py:256
  40.5 11.2 %collective-permute-start.11 = (bf16[2,112,1152]{2,1,0:T(8,128)(2,1)S(1)}, bf16[2,112,1152]{2,1,0:T(8,128)(2,1)S(1)}, u32[]{:S(2)}, u32[]{:S(2)}) collective-permute-start(bf16[2,112,1152]{2,1,0:T(8,128)(2,1)S(1)} %collective-permute-done.8.refs_8_), channel_id=1, source_target_pairs={{0,8},{1,9},{2,10},{3,11},{4,12},{5,13},{6,14},{7,15},{8,0},{9,1},... | collective-permute-start | bytes 1548296 | tf_op jit(solution)/shard_map/ppermute | solution.py:256
  41.7 10.9 %collective-permute-start.12 = (bf16[2,112,1152]{2,1,0:T(8,128)(2,1)S(1)}, bf16[2,112,1152]{2,1,0:T(8,128)(2,1)S(1)}, u32[]{:S(2)}, u32[]{:S(2)}) collective-permute-start(bf16[2,112,1152]{2,1,0:T(8,128)(2,1)S(1)} %collective-permute-done.8.refs_8_), channel_id=1, source_target_pairs={{0,16},{1,17},{2,18},{3,19},{4,20},{5,21},{6,22},{7,23},{8,24},{9,... | collective-permute-start | bytes 1548296 | tf_op jit(solution)/shard_map/ppermute | solution.py:256
  42.4 10.3 %collective-permute-start.14 = (bf16[2,112,1152]{2,1,0:T(8,128)(2,1)S(1)}, bf16[2,112,1152]{2,1,0:T(8,128)(2,1)S(1)}, u32[]{:S(2)}, u32[]{:S(2)}) collective-permute-start(bf16[2,112,1152]{2,1,0:T(8,128)(2,1)S(1)} %collective-permute-done.8.refs_8_), channel_id=1, source_target_pairs={{0,1},{1,0},{2,3},{3,2},{4,5},{5,4},{6,7},{7,6},{8,9},{9,8},{10,11... | collective-permute-start | bytes 1548296 | tf_op jit(solution)/shard_map/ppermute | solution.py:256
  44.8 1.9 %collective-permute-start.13 = (bf16[112,1152]{1,0:T(8,128)(2,1)S(1)}, bf16[112,1152]{1,0:T(8,128)(2,1)S(1)}, u32[]{:S(2)}, u32[]{:S(2)}) collective-permute-start(bf16[112,1152]{1,0:T(8,128)(2,1)S(1)} %collective-permute-done.2.refs_2_), channel_id=1, source_target_pairs={{0,1},{1,0},{2,3},{3,2},{4,5},{5,4},{6,7},{7,6},{8,9},{9,8},{10,11... | collective-permute-start | bytes 774152 | tf_op jit(solution)/shard_map/ppermute | solution.py:256
  44.9 28.7 %collective-permute-start.21 = (bf16[17,16,1152]{2,1,0:T(8,128)(2,1)S(1)}, bf16[17,16,1152]{2,1,0:T(8,128)(2,1)S(1)}, u32[]{:S(2)}, u32[]{:S(2)}) collective-permute-start(bf16[17,16,1152]{2,1,0:T(8,128)(2,1)S(1)} %pad_maximum_fusion.1), channel_id=1, source_target_pairs={{0,6},{1,7},{2,4},{3,5},{4,2},{5,3},{6,0},{7,1},{8,14},{9,15},{10,... | collective-permute-start | bytes 1880072 | tf_op jit(solution)/shard_map/ppermute | solution.py:256
  52.7 5.6 %collective-permute-start.15 = (bf16[112,1152]{1,0:T(8,128)(2,1)S(1)}, bf16[112,1152]{1,0:T(8,128)(2,1)S(1)}, u32[]{:S(2)}, u32[]{:S(2)}) collective-permute-start(bf16[112,1152]{1,0:T(8,128)(2,1)S(1)} %slice_bitcast_fusion.1), channel_id=1, source_target_pairs={{0,16},{1,17},{2,18},{3,19},{4,20},{5,21},{6,22},{7,23},{8,24},{9,... | collective-permute-start | bytes 774152 | tf_op jit(solution)/shard_map/ppermute | solution.py:256
  53.5 8.8 %collective-permute-start.16 = (bf16[112,1152]{1,0:T(8,128)(2,1)S(1)}, bf16[112,1152]{1,0:T(8,128)(2,1)S(1)}, u32[]{:S(2)}, u32[]{:S(2)}) collective-permute-start(bf16[112,1152]{1,0:T(8,128)(2,1)S(1)} %slice_bitcast_fusion), channel_id=1, source_target_pairs={{0,8},{1,9},{2,10},{3,11},{4,12},{5,13},{6,14},{7,15},{8,0},{9,1},... | collective-permute-start | bytes 774152 | tf_op jit(solution)/shard_map/ppermute | solution.py:256
  54.3 10.2 %collective-permute-start.19 = (bf16[2,112,1152]{2,1,0:T(8,128)(2,1)S(1)}, bf16[2,112,1152]{2,1,0:T(8,128)(2,1)S(1)}, u32[]{:S(2)}, u32[]{:S(2)}) collective-permute-start(bf16[2,112,1152]{2,1,0:T(8,128)(2,1)S(1)} %collective-permute-done.11.refs_10_), channel_id=1, source_target_pairs={{0,1},{1,0},{2,3},{3,2},{4,5},{5,4},{6,7},{7,6},{8,9},{9,8},{10,11... | collective-permute-start | bytes 1548296 | tf_op jit(solution)/shard_map/ppermute | solution.py:256
  58.1 6.3 %collective-permute-start.20 = (bf16[2,112,1152]{2,1,0:T(8,128)(2,1)S(1)}, bf16[2,112,1152]{2,1,0:T(8,128)(2,1)S(1)}, u32[]{:S(2)}, u32[]{:S(2)}) collective-permute-start(bf16[2,112,1152]{2,1,0:T(8,128)(2,1)S(1)} %collective-permute-done.12.refs_12_), channel_id=1, source_target_pairs={{0,1},{1,0},{2,3},{3,2},{4,5},{5,4},{6,7},{7,6},{8,9},{9,8},{10,11... | collective-permute-start | bytes 1548296 | tf_op jit(solution)/shard_map/ppermute | solution.py:256
  58.3 5.2 %collective-permute-start.17 = (bf16[112,1152]{1,0:T(8,128)(2,1)S(1)}, bf16[112,1152]{1,0:T(8,128)(2,1)S(1)}, u32[]{:S(2)}, u32[]{:S(2)}) collective-permute-start(bf16[112,1152]{1,0:T(8,128)(2,1)S(1)} %collective-permute-done.6.refs_4_), channel_id=1, source_target_pairs={{0,1},{1,0},{2,3},{3,2},{4,5},{5,4},{6,7},{7,6},{8,9},{9,8},{10,11... | collective-permute-start | bytes 774152 | tf_op jit(solution)/shard_map/ppermute | solution.py:256
  62.3 2.1 %collective-permute-start.18 = (bf16[112,1152]{1,0:T(8,128)(2,1)S(1)}, bf16[112,1152]{1,0:T(8,128)(2,1)S(1)}, u32[]{:S(2)}, u32[]{:S(2)}) collective-permute-start(bf16[112,1152]{1,0:T(8,128)(2,1)S(1)} %collective-permute-done.7.refs_6_), channel_id=1, source_target_pairs={{0,1},{1,0},{2,3},{3,2},{4,5},{5,4},{6,7},{7,6},{8,9},{9,8},{10,11... | collective-permute-start | bytes 774152 | tf_op jit(solution)/shard_map/ppermute | solution.py:256
  63.5 11.4 %collective-permute-start.22 = (bf16[112,1152]{1,0:T(8,128)(2,1)S(1)}, bf16[112,1152]{1,0:T(8,128)(2,1)S(1)}, u32[]{:S(2)}, u32[]{:S(2)}) collective-permute-start(bf16[112,1152]{1,0:T(8,128)(2,1)S(1)} %collective-permute-done.7.refs_6_), channel_id=1, source_target_pairs={{0,8},{1,9},{2,10},{3,11},{4,12},{5,13},{6,14},{7,15},{8,0},{9,1},... | collective-permute-start | bytes 774152 | tf_op jit(solution)/shard_map/ppermute | solution.py:256
  73.6 3.2 %collective-permute-start.24 = (bf16[2,112,1152]{2,1,0:T(8,128)(2,1)S(1)}, bf16[2,112,1152]{2,1,0:T(8,128)(2,1)S(1)}, u32[]{:S(2)}, u32[]{:S(2)}) collective-permute-start(bf16[2,112,1152]{2,1,0:T(8,128)(2,1)S(1)} %pad_maximum_fusion.3.refs_7_.refs_9_), channel_id=1, source_target_pairs={{0,1},{1,0},{2,3},{3,2},{4,5},{5,4},{6,7},{7,6},{8,9},{9,8},{10,11... | collective-permute-start | bytes 1548296 | tf_op jit(solution)/shard_map/ppermute | solution.py:256
  74.9 1.9 %collective-permute-start.23 = (bf16[112,1152]{1,0:T(8,128)(2,1)S(1)}, bf16[112,1152]{1,0:T(8,128)(2,1)S(1)}, u32[]{:S(2)}, u32[]{:S(2)}) collective-permute-start(bf16[112,1152]{1,0:T(8,128)(2,1)S(1)} %collective-permute-done.22.refs_5_.refs_7_), channel_id=1, source_target_pairs={{0,1},{1,0},{2,3},{3,2},{4,5},{5,4},{6,7},{7,6},{8,9},{9,8},{10,11... | collective-permute-start | bytes 774152 | tf_op jit(solution)/shard_map/ppermute | solution.py:256
  75.0 20.2 %collective-permute-start.25 = (bf16[2,144,1152]{2,1,0:T(8,128)(2,1)S(1)}, bf16[2,144,1152]{2,1,0:T(8,128)(2,1)S(1)}, u32[]{:S(2)}, u32[]{:S(2)}) collective-permute-start(bf16[2,144,1152]{2,1,0:T(8,128)(2,1)S(1)} %pad_maximum_fusion), channel_id=1, source_target_pairs={{0,2},{1,3},{2,0},{3,1},{4,6},{5,7},{6,4},{7,5},{8,10},{9,11},{10,... | collective-permute-start | bytes 1990664 | tf_op jit(solution)/shard_map/ppermute | solution.py:256
  83.7 11.5 %collective-permute-start.26 = (bf16[4,4,16,640]{3,2,1,0:T(8,128)(2,1)S(1)}, bf16[4,4,16,640]{3,2,1,0:T(8,128)(2,1)S(1)}, u32[]{:S(2)}, u32[]{:S(2)}) collective-permute-start(bf16[4,4,16,640]{3,2,1,0:T(8,128)(2,1)S(1)} %get-tuple-element.73), channel_id=1, source_target_pairs={{0,8},{1,9},{2,10},{3,11},{4,28},{5,29},{6,30},{7,31},{8,16},{9,17... | collective-permute-start | bytes 983048 | tf_op jit(solution)/shard_map/ppermute | solution.py:283
  91.3 30.1 %copy-start.1 = (bf16[4,128,1152]{2,1,0:T(8,128)(2,1)S(1)}, bf16[4,128,1152]{2,1,0:T(8,128)(2,1)}, u32[]{:S(2)}) copy-start(bf16[4,128,1152]{2,1,0:T(8,128)(2,1)} %tokens_ref.3) | copy-start | bytes 3538948
  91.3 30.1 %copy-start.5 = (f32[4,3,1152]{2,0,1:T(4,128)S(1)}, f32[4,3,1152]{2,0,1:T(4,128)}, u32[]{:S(2)}) copy-start(f32[4,3,1152]{2,0,1:T(4,128)} %param.5) | copy-start | bytes 165892
  92.0 5.8 %collective-permute-start.28 = (bf16[4,16,1152]{2,1,0:T(8,128)(2,1)S(1)}, bf16[4,16,1152]{2,1,0:T(8,128)(2,1)S(1)}, u32[]{:S(2)}, u32[]{:S(2)}) collective-permute-start(bf16[4,16,1152]{2,1,0:T(8,128)(2,1)S(1)} %get-tuple-element.102), channel_id=1, source_target_pairs={{0,4},{1,5},{2,6},{3,7},{4,0},{5,1},{6,2},{7,3},{8,12},{9,13},{10,... | collective-permute-start | bytes 442376 | tf_op jit(solution)/shard_map/ppermute | solution.py:256
  92.6 12.3 %collective-permute-start.29 = (bf16[4,16,1152]{2,1,0:T(8,128)(2,1)S(1)}, bf16[4,16,1152]{2,1,0:T(8,128)(2,1)S(1)}, u32[]{:S(2)}, u32[]{:S(2)}) collective-permute-start(bf16[4,16,1152]{2,1,0:T(8,128)(2,1)S(1)} %get-tuple-element.101), channel_id=1, source_target_pairs={{0,5},{1,4},{2,7},{3,6},{4,1},{5,0},{6,3},{7,2},{8,13},{9,12},{10,... | collective-permute-start | bytes 442376 | tf_op jit(solution)/shard_map/ppermute | solution.py:256
  95.9 23.5 %collective-permute-start.27 = (bf16[2,4,16,1152]{3,2,1,0:T(8,128)(2,1)S(1)}, bf16[2,4,16,1152]{3,2,1,0:T(8,128)(2,1)S(1)}, u32[]{:S(2)}, u32[]{:S(2)}) collective-permute-start(bf16[2,4,16,1152]{3,2,1,0:T(8,128)(2,1)S(1)} %get-tuple-element.76), channel_id=1, source_target_pairs={{0,2},{1,3},{2,0},{3,1},{4,6},{5,7},{6,4},{7,5},{8,10},{9,11},{10,... | collective-permute-start | bytes 884744 | tf_op jit(solution)/shard_map/ppermute | solution.py:256
  96.1 25.3 %collective-permute-start.35 = (bf16[2,144,1152]{2,1,0:T(8,128)(2,1)S(1)}, bf16[2,144,1152]{2,1,0:T(8,128)(2,1)S(1)}, u32[]{:S(2)}, u32[]{:S(2)}) collective-permute-start(bf16[2,144,1152]{2,1,0:T(8,128)(2,1)S(1)} %collective-permute-done.25.refs_12_), channel_id=1, source_target_pairs={{0,1},{1,0},{2,3},{3,2},{4,5},{5,4},{6,7},{7,6},{8,9},{9,8},{10,11... | collective-permute-start | bytes 1990664 | tf_op jit(solution)/shard_map/ppermute | solution.py:256
  96.2 18.9 %collective-permute-start.30 = (bf16[4,16,1152]{2,1,0:T(8,128)(2,1)S(1)}, bf16[4,16,1152]{2,1,0:T(8,128)(2,1)S(1)}, u32[]{:S(2)}, u32[]{:S(2)}) collective-permute-start(bf16[4,16,1152]{2,1,0:T(8,128)(2,1)S(1)} %get-tuple-element.100), channel_id=1, source_target_pairs={{0,6},{1,7},{2,4},{3,5},{4,2},{5,3},{6,0},{7,1},{8,14},{9,15},{10,... | collective-permute-start | bytes 442376 | tf_op jit(solution)/shard_map/ppermute | solution.py:256
  97.7 21.6 %collective-permute-start.31 = (bf16[4,16,1152]{2,1,0:T(8,128)(2,1)S(1)}, bf16[4,16,1152]{2,1,0:T(8,128)(2,1)S(1)}, u32[]{:S(2)}, u32[]{:S(2)}) collective-permute-start(bf16[4,16,1152]{2,1,0:T(8,128)(2,1)S(1)} %get-tuple-element.99), channel_id=1, source_target_pairs={{0,7},{1,6},{2,5},{3,4},{4,3},{5,2},{6,1},{7,0},{8,15},{9,14},{10,... | collective-permute-start | bytes 442376 | tf_op jit(solution)/shard_map/ppermute | solution.py:256
  104.9 15.0 %collective-permute-start.34 = (bf16[144,1152]{1,0:T(8,128)(2,1)S(1)}, bf16[144,1152]{1,0:T(8,128)(2,1)S(1)}, u32[]{:S(2)}, u32[]{:S(2)}) collective-permute-start(bf16[144,1152]{1,0:T(8,128)(2,1)S(1)} %bitcast.46), channel_id=1, source_target_pairs={{0,1},{1,0},{2,3},{3,2},{4,5},{5,4},{6,7},{7,6},{8,9},{9,8},{10,11... | collective-permute-start | bytes 995336 | tf_op jit(solution)/shard_map/ppermute | solution.py:256
  119.4 1.6 %collective-permute-start.32 = (bf16[2,4,16,1152]{3,2,1,0:T(8,128)(2,1)S(1)}, bf16[2,4,16,1152]{3,2,1,0:T(8,128)(2,1)S(1)}, u32[]{:S(2)}, u32[]{:S(2)}) collective-permute-start(bf16[2,4,16,1152]{3,2,1,0:T(8,128)(2,1)S(1)} %get-tuple-element.81.refs_0_), channel_id=1, source_target_pairs={{0,1},{1,0},{2,3},{3,2},{4,5},{5,4},{6,7},{7,6},{8,9},{9,8},{10,11... | collective-permute-start | bytes 884744 | tf_op jit(solution)/shard_map/ppermute | solution.py:256
  119.4 2.0 %collective-permute-start.33 = (bf16[2,4,16,1152]{3,2,1,0:T(8,128)(2,1)S(1)}, bf16[2,4,16,1152]{3,2,1,0:T(8,128)(2,1)S(1)}, u32[]{:S(2)}, u32[]{:S(2)}) collective-permute-start(bf16[2,4,16,1152]{3,2,1,0:T(8,128)(2,1)S(1)} %collective-permute-done.27.refs_2_), channel_id=1, source_target_pairs={{0,1},{1,0},{2,3},{3,2},{4,5},{5,4},{6,7},{7,6},{8,9},{9,8},{10,11... | collective-permute-start | bytes 884744 | tf_op jit(solution)/shard_map/ppermute | solution.py:256

commit v8 on v7

--- a/solution.py
+++ b/solution.py
@@ -198,26 +198,28 @@
                 out_ref[sibling, ..., lanes:] = second
 
 
-def restore_kernel(plan, index_ref, tokens_ref, modulation_ref, *refs):
-    count, moves = plan["count"], plan["moves"]
-    refs = list(refs)
-    in_refs = [refs.pop(0) for _ in range(count)]
-    in_refs = [ref.at[n % ref.shape[0]] for n, ref in enumerate(in_refs)]
-    w_refs = [refs.pop(0) for _ in range(plan["weights"])]
-    out_ref, wall, mixed, sems = refs
-    index = index_ref[0]
+def gather_out_kernel(moves, index_ref, *refs):
+    w_refs, wall, sems = refs[:-2], refs[-2], refs[-1]
     copies = []
     for n, (operand, at, owner) in enumerate(moves):
         source = w_refs[operand]
         for step in at:
             source = source.at[step]
         size = source.shape[0]
-        row = pl.multiple_of(lax.bitwise_xor(index, owner[0]) * size, ROWS) if isinstance(owner, tuple) else owner * size
-        copies.append(pltpu.make_async_copy(source, wall.at[pl.ds(row, size)], sems.at[n]))
+        row = lax.bitwise_xor(index_ref[0], owner[0]) * size if isinstance(owner, tuple) else owner * size
+        copies.append(pltpu.make_async_copy(source, wall.at[pl.ds(pl.multiple_of(row, ROWS), size)], sems.at[n]))
     for copy in copies:
         copy.start()
     for copy in copies:
         copy.wait()
+
+
+def restore_kernel(count, index_ref, tokens_ref, modulation_ref, wall, *refs):
+    refs = list(refs)
+    in_refs = [refs.pop(0) for _ in range(count)]
+    in_refs = [ref.at[n % ref.shape[0]] for n, ref in enumerate(in_refs)]
+    out_ref, mixed = refs
+    index = index_ref[0]
     frames = tokens_ref.shape[0]
     groups, rows, width = in_refs[0].shape
     block_rows = groups * rows
@@ -409,30 +411,33 @@
     arrived = [hop(sent[z], 2 * z) if z else sent[z] for z in range(chips // 2)]
     singles = [hop(sent[z][n], 2 * z + n)[None] for z in range(chips // 2, chips) for n in range(2)]
     if shared:
+        out_operands = [narrow, narrow_other, out_far, hop(out_far, 1), out_rest, hop(out_rest, 1)]
+        out_moves = [(0, (), (0,)), (1, (), (1,)), (2, (), (6,)), (3, (), (7,)), (4, (0,), (2,)), (5, (0,), (3,)),
+                     (4, (1,), (4,)), (5, (1,), (5,))]
+    out_full = pl.pallas_call(
+        functools.partial(gather_out_kernel, out_moves),
+        out_shape=jax.ShapeDtypeStruct((width, width), jnp.bfloat16),
+        in_specs=[smem] + [anywhere] * len(out_operands),
+        out_specs=anywhere,
+        scratch_shapes=[pltpu.SemaphoreType.DMA((len(out_moves),))],
+        compiler_params=params,
+        name="gather_out",
+    )(own_index, *out_operands)
+    if shared:
         arrived, singles = tie((arrived, singles))
     returned = []
     for value in arrived:
         returned += [value, hop(value, 1)]
     returned += singles
-    if shared:
-        out_operands = [narrow, narrow_other, out_far, hop(out_far, 1), out_rest, hop(out_rest, 1)]
-        out_moves = [(0, (), (0,)), (1, (), (1,)), (2, (), (6,)), (3, (), (7,)), (4, (0,), (2,)), (5, (0,), (3,)),
-                     (4, (1,), (4,)), (5, (1,), (5,))]
-
-    plan = dict(count=count, weights=len(out_operands), moves=out_moves)
     return pl.pallas_call(
-        functools.partial(restore_kernel, plan),
+        functools.partial(restore_kernel, count),
         out_shape=jax.ShapeDtypeStruct(video_tokens.shape, video_tokens.dtype),
-        in_specs=[smem, vmem, vmem] + [vmem] * count + [anywhere] * len(out_operands),
+        in_specs=[smem] + [vmem] * (3 + count),
         out_specs=vmem,
-        scratch_shapes=[
-            pltpu.VMEM((width, width), jnp.bfloat16),
-            pltpu.VMEM((width // LANES, tokens, LANES), jnp.float32),
-            pltpu.SemaphoreType.DMA((len(out_moves),)),
-        ],
+        scratch_shapes=[pltpu.VMEM((width // LANES, tokens, LANES), jnp.float32)],
         compiler_params=params,
         name="restore",
-    )(own_index, video_tokens, kinds, *returned, *out_operands)
+    )(own_index, video_tokens, kinds, out_full, *returned)
 
 
 def solution(mesh):

time: 126 us -> 125 us (level)
  waiting for transfers between devices: 47.5 us -> 46.2 us
    ppermute x33, waiting for transfers between devices: 47.5 us -> 46.2 us  [hop(): return lax.ppermute(value, ('slab', 'seq'), pairs)]
    pallas_call x1 -> x2, Pallas kernels: 4.65 us -> 5.17 us  [the longest x1 3.66 us: per_device(): pl.pallas_call(functools.partial(restore_kernel, count), out_shape=jax.Sh...]
  transfers between devices with their start and end apart: 36 -> 36, of which waited for: 17 -> 14; matrix products, arithmetic and copies ran while one was open for 1% -> 1% of each run, Pallas kernels for 18% -> 19%
where the time goes in v8:
time: 125 us
  waiting for transfers between devices  46.2 us (37%)
  starting transfers between devices  45.6 us (36%)
  Pallas kernels  29.3 us (23%)
  local copies, waits for them, and re-layouts  3.33 us (3%)
    ppermute x33, waiting for transfers between devices, hop(): return lax.ppermute(value, ('slab', 'seq'), pairs)  46.2 us
    ppermute x33, starting transfers between devices, hop(): return lax.ppermute(value, ('slab', 'seq'), pairs)  42 us
    pallas_call x2, Pallas kernels, attention(): pl.pallas_call(functools.partial(block_kernel, plan, frames), out_shape=[...  13.4 us
    pallas_call x1, Pallas kernels, per_device(): pl.pallas_call(functools.partial(gather_kernel, plan), out_shape=jax.Shap...  7.91 us
    pallas_call x1, Pallas kernels, per_device(): pl.pallas_call(functools.partial(restore_kernel, count), out_shape=jax.Sh...  3.66 us
    ppermute x3, starting transfers between devices, to_neighbour(): return lax.ppermute(value, ('slab', 'seq'), pairs)  3.58 us
  transfers between devices with their start and end apart: 36, of which 14 were waited for; matrix products, arithmetic and copies ran while one was open for 1% of the time, Pallas kernels for 19%

profile of v8, /device:TPU:9, one launch (start us, length us, event | category | flops | bytes accessed | tf_op | source)
XLA Modules:
  0.0 125.1 jit_solution(14040581407934482986)
XLA Ops:
  0.0 0.1 pad_add_fusion.index_ref
  0.1 1.3 %copy-done = bf16[4,128,1152]{2,1,0:T(8,128)(2,1)S(1)} copy-done((bf16[4,128,1152]{2,1,0:T(8,128)(2,1)S(1)}, bf16[4,128,1152]{2,1,0:T(8,128)(2,1)}, u32[]{:S(2)}) %copy-start) | copy-done | bytes 1179672
  1.3 0.8 copy-done.4
  2.2 1.7 %norm.1 = (bf16[4,4,16,1152]{3,2,1,0:T(8,128)(2,1)S(1)}, bf16[4,4,16,1152]{3,2,1,0:T(8,128)(2,1)S(1)}) custom-call(s32[2]{0:T(128)S(1)} %pad_add_fusion.index_ref, bf16[4,128,1152]{2,1,0:T(8,128)(2,1)S(1)} %copy-done, f32[3,4,1152]{2,1,0:T(4,128)S(1)} %bitcast.53), custom_call_target="tpu_custom_call" | custom-call | tf_op jit(solution)/shard_map/norm/pallas_call | solution.py:270
  3.8 0.7 collective-permute-start
  4.6 1.0 dynamic-slice_bitcast_fusion
  5.6 2.4 %collective-permute-start.2 = (bf16[112,1152]{1,0:T(8,128)(2,1)S(1)}, bf16[112,1152]{1,0:T(8,128)(2,1)S(1)}, u32[]{:S(2)}, u32[]{:S(2)}) collective-permute-start(bf16[112,1152]{1,0:T(8,128)(2,1)S(1)} %get-tuple-element.90), channel_id=1, source_target_pairs={{0,4},{1,5},{2,6},{3,7},{4,0},{5,1},{6,2},{7,3},{8,12},{9,13},{10,... | collective-permute-start | bytes 774152 | tf_op jit(solution)/shard_map/ppermute | solution.py:258
  8.0 0.3 collective-permute-start.3
  8.3 0.2 collective-permute-start.4
  8.6 2.2 %collective-permute-start.5 = (bf16[2,4,16,1152]{3,2,1,0:T(8,128)(2,1)S(1)}, bf16[2,4,16,1152]{3,2,1,0:T(8,128)(2,1)S(1)}, u32[]{:S(2)}, u32[]{:S(2)}) collective-permute-start(bf16[2,4,16,1152]{3,2,1,0:T(8,128)(2,1)S(1)} %pad_maximum_fusion.5), channel_id=1, source_target_pairs={{0,24},{1,25},{2,26},{3,27},{4,12},{5,13},{6,14},{7,15},{8,0},{9,1... | collective-permute-start | bytes 884744 | tf_op jit(solution)/shard_map/ppermute | solution.py:285
  10.9 0.2 collective-permute-start.1
  11.1 8.3 %collective-permute-done.2.refs_2_ = bf16[112,1152]{1,0:T(8,128)(2,1)S(1)} collective-permute-done((bf16[112,1152]{1,0:T(8,128)(2,1)S(1)}, bf16[112,1152]{1,0:T(8,128)(2,1)S(1)}, u32[]{:S(2)}, u32[]{:S(2)}) %collective-permute-start.2) | collective-permute-done | bytes 258080 | tf_op jit(solution)/shard_map/ppermute | solution.py:258
  19.4 0.1 pad_maximum_fusion.2
  19.5 0.1 pad_maximum_fusion.6
  19.6 1.7 %collective-permute-done.1 = bf16[2,4,16,1152]{3,2,1,0:T(8,128)(2,1)S(1)} collective-permute-done((bf16[2,4,16,1152]{3,2,1,0:T(8,128)(2,1)S(1)}, bf16[2,4,16,1152]{3,2,1,0:T(8,128)(2,1)S(1)}, u32[]{:S(2)}, u32[]{:S(2)}) %collective-permute-start.1) | collective-permute-done | bytes 294944 | tf_op jit(solution)/shard_map/ppermute | solution.py:258
  21.3 2.2 %collective-permute-start.8 = (bf16[2,112,1152]{2,1,0:T(8,128)(2,1)S(1)}, bf16[2,112,1152]{2,1,0:T(8,128)(2,1)S(1)}, u32[]{:S(2)}, u32[]{:S(2)}) collective-permute-start(bf16[2,112,1152]{2,1,0:T(8,128)(2,1)S(1)} %pad_maximum_fusion.2), channel_id=1, source_target_pairs={{0,2},{1,3},{2,0},{3,1},{4,6},{5,7},{6,4},{7,5},{8,10},{9,11},{10,... | collective-permute-start | bytes 1548296 | tf_op jit(solution)/shard_map/ppermute | solution.py:258
  23.5 0.3 collective-permute-start.10
  23.8 1.0 collective-permute-start.9
  24.7 1.2 collective-permute-start.6
  25.9 0.2 collective-permute-start.7
  26.2 9.6 %collective-permute-done.6.refs_4_ = bf16[112,1152]{1,0:T(8,128)(2,1)S(1)} collective-permute-done((bf16[112,1152]{1,0:T(8,128)(2,1)S(1)}, bf16[112,1152]{1,0:T(8,128)(2,1)S(1)}, u32[]{:S(2)}, u32[]{:S(2)}) %collective-permute-start.6) | collective-permute-done | bytes 258080 | tf_op jit(solution)/shard_map/ppermute | solution.py:258
  35.8 4.7 %collective-permute-done.9 = bf16[2,4,16,1152]{3,2,1,0:T(8,128)(2,1)S(1)} collective-permute-done((bf16[2,4,16,1152]{3,2,1,0:T(8,128)(2,1)S(1)}, bf16[2,4,16,1152]{3,2,1,0:T(8,128)(2,1)S(1)}, u32[]{:S(2)}, u32[]{:S(2)}) %collective-permute-start.9) | collective-permute-done | bytes 294944 | tf_op jit(solution)/shard_map/ppermute | solution.py:258
  40.5 1.2 collective-permute-start.11
  41.7 0.7 collective-permute-start.12
  42.4 2.4 %collective-permute-start.14 = (bf16[2,112,1152]{2,1,0:T(8,128)(2,1)S(1)}, bf16[2,112,1152]{2,1,0:T(8,128)(2,1)S(1)}, u32[]{:S(2)}, u32[]{:S(2)}) collective-permute-start(bf16[2,112,1152]{2,1,0:T(8,128)(2,1)S(1)} %collective-permute-done.8.refs_8_), channel_id=1, source_target_pairs={{0,1},{1,0},{2,3},{3,2},{4,5},{5,4},{6,7},{7,6},{8,9},{9,8},{10,11... | collective-permute-start | bytes 1548296 | tf_op jit(solution)/shard_map/ppermute | solution.py:258
  44.8 0.1 pad_maximum_fusion.1
  44.9 0.8 collective-permute-start.21
  45.7 1.0 collective-permute-done.13.refs_3_
  46.7 5.0 %collective-permute-done.11.refs_10_ = bf16[2,112,1152]{2,1,0:T(8,128)(2,1)S(1)} collective-permute-done((bf16[2,112,1152]{2,1,0:T(8,128)(2,1)S(1)}, bf16[2,112,1152]{2,1,0:T(8,128)(2,1)S(1)}, u32[]{:S(2)}, u32[]{:S(2)}) %collective-permute-start.11) | collective-permute-done | bytes 516128 | tf_op jit(solution)/shard_map/ppermute | solution.py:258
  51.7 0.9 collective-permute-done.12.refs_12_
  52.6 0.3 collective-permute-start.16
  53.0 1.3 %collective-permute-start.15 = (bf16[112,1152]{1,0:T(8,128)(2,1)S(1)}, bf16[112,1152]{1,0:T(8,128)(2,1)S(1)}, u32[]{:S(2)}, u32[]{:S(2)}) collective-permute-start(bf16[112,1152]{1,0:T(8,128)(2,1)S(1)} %slice_bitcast_fusion.1), channel_id=1, source_target_pairs={{0,16},{1,17},{2,18},{3,19},{4,20},{5,21},{6,22},{7,23},{8,24},{9,... | collective-permute-start | bytes 774152 | tf_op jit(solution)/shard_map/ppermute | solution.py:258
  54.3 3.8 %collective-permute-start.19 = (bf16[2,112,1152]{2,1,0:T(8,128)(2,1)S(1)}, bf16[2,112,1152]{2,1,0:T(8,128)(2,1)S(1)}, u32[]{:S(2)}, u32[]{:S(2)}) collective-permute-start(bf16[2,112,1152]{2,1,0:T(8,128)(2,1)S(1)} %collective-permute-done.11.refs_10_), channel_id=1, source_target_pairs={{0,1},{1,0},{2,3},{3,2},{4,5},{5,4},{6,7},{7,6},{8,9},{9,8},{10,11... | collective-permute-start | bytes 1548296 | tf_op jit(solution)/shard_map/ppermute | solution.py:258
  58.1 0.1 collective-permute-done.16
  58.2 4.1 %collective-permute-start.17 = (bf16[112,1152]{1,0:T(8,128)(2,1)S(1)}, bf16[112,1152]{1,0:T(8,128)(2,1)S(1)}, u32[]{:S(2)}, u32[]{:S(2)}) collective-permute-start(bf16[112,1152]{1,0:T(8,128)(2,1)S(1)} %collective-permute-done.6.refs_4_), channel_id=1, source_target_pairs={{0,1},{1,0},{2,3},{3,2},{4,5},{5,4},{6,7},{7,6},{8,9},{9,8},{10,11... | collective-permute-start | bytes 774152 | tf_op jit(solution)/shard_map/ppermute | solution.py:258
  62.3 0.6 collective-permute-start.18
  62.9 0.1 pad_maximum_fusion.3.refs_9_.refs_7_
  63.0 0.5 collective-permute-done.17.refs_5_
  63.4 0.8 collective-permute-start.24
  64.3 7.9 %gather.1.refs_6_.refs_4_ = bf16[3584,1152]{1,0:T(8,128)(2,1)S(1)} custom-call(s32[2]{0:T(128)S(1)} %pad_add_fusion.index_ref, bf16[432,1152]{1,0:T(8,128)(2,1)S(1)} %bitcast.49, bf16[432,1152]{1,0:T(8,128)(2,1)S(1)} %collective-permute-done.3.refs_1_, bf16[112,1152]{1,0:T(8,128)(2,1)S(1)} %collective-permute-done.2.refs_2_, ...), custom_call_target="tpu_custom_call" | custom-call | tf_op jit(solution)/shard_map/gather/pallas_call | solution.py:333
  72.2 1.4 %collective-permute-done.21.refs_3_ = bf16[17,16,1152]{2,1,0:T(8,128)(2,1)S(1)} collective-permute-done((bf16[17,16,1152]{2,1,0:T(8,128)(2,1)S(1)}, bf16[17,16,1152]{2,1,0:T(8,128)(2,1)S(1)}, u32[]{:S(2)}, u32[]{:S(2)}) %collective-permute-start.21) | collective-permute-done | bytes 626720 | tf_op jit(solution)/shard_map/ppermute | solution.py:258
  73.6 1.3 %collective-permute-start.26 = (bf16[2,112,1152]{2,1,0:T(8,128)(2,1)S(1)}, bf16[2,112,1152]{2,1,0:T(8,128)(2,1)S(1)}, u32[]{:S(2)}, u32[]{:S(2)}) collective-permute-start(bf16[2,112,1152]{2,1,0:T(8,128)(2,1)S(1)} %pad_maximum_fusion.3.refs_9_.refs_7_), channel_id=1, source_target_pairs={{0,1},{1,0},{2,3},{3,2},{4,5},{5,4},{6,7},{7,6},{8,9},{9,8},{10,11... | collective-permute-start | bytes 1548296 | tf_op jit(solution)/shard_map/ppermute | solution.py:258
  75.0 0.1 pad_maximum_fusion
  75.0 0.1 collective-permute-start.23
  75.1 1.7 %collective-permute-done.25.refs_8_.refs_6_ = bf16[112,1152]{1,0:T(8,128)(2,1)S(1)} collective-permute-done((bf16[112,1152]{1,0:T(8,128)(2,1)S(1)}, bf16[112,1152]{1,0:T(8,128)(2,1)S(1)}, u32[]{:S(2)}, u32[]{:S(2)}) %collective-permute-start.25) | collective-permute-done | bytes 258080 | tf_op jit(solution)/shard_map/ppermute | solution.py:258
  76.8 6.9 %shifted.1 = (bf16[4,4,16,640]{3,2,1,0:T(8,128)(2,1)S(1)}, bf16[4,4,16,640]{3,2,1,0:T(8,128)(2,1)S(1)}) custom-call(s32[2]{0:T(128)S(1)} %pad_add_fusion.index_ref, bf16[8,16,1152]{2,1,0:T(8,128)(2,1)S(1)} %bitcast.51, bf16[8,16,1152]{2,1,0:T(8,128)(2,1)S(1)} %bitcast.59, bf16[8,16,1152]{2,1,0:T(8,128)(2,1)S(1)} %bitcast.62, ...), custom_call_target="tpu_custom_call" | custom-call | flops 40000000000 | bytes 8388608 | tf_op jit(solution)/shard_map/shifted/pallas_call | solution.py:369
  83.7 1.1 collective-permute-start.27
  84.8 6.5 %windowed.1 = (bf16[4,4,16,640]{3,2,1,0:T(8,128)(2,1)S(1)}, bf16[4,4,16,640]{3,2,1,0:T(8,128)(2,1)S(1)}) custom-call(s32[2]{0:T(128)S(1)} %pad_add_fusion.index_ref, bf16[8,16,1152]{2,1,0:T(8,128)(2,1)S(1)} %bitcast.52, bf16[8,16,1152]{2,1,0:T(8,128)(2,1)S(1)} %bitcast.60, bf16[8,16,1152]{2,1,0:T(8,128)(2,1)S(1)} %bitcast.63, ...), custom_call_target="tpu_custom_call" | custom-call | flops 40000000000 | bytes 8388608 | tf_op jit(solution)/shard_map/windowed/pallas_call | solution.py:369
  91.3 0.6 merge.3
  91.9 0.6 collective-permute-start.30
  92.5 2.7 %collective-permute-start.31 = (bf16[4,16,1152]{2,1,0:T(8,128)(2,1)S(1)}, bf16[4,16,1152]{2,1,0:T(8,128)(2,1)S(1)}, u32[]{:S(2)}, u32[]{:S(2)}) collective-permute-start(bf16[4,16,1152]{2,1,0:T(8,128)(2,1)S(1)} %get-tuple-element.101), channel_id=1, source_target_pairs={{0,5},{1,4},{2,7},{3,6},{4,1},{5,0},{6,3},{7,2},{8,13},{9,12},{10,... | collective-permute-start | bytes 442376 | tf_op jit(solution)/shard_map/ppermute | solution.py:258
  95.2 0.6 merge.2
  95.8 0.2 collective-permute-start.29
  96.0 0.1 collective-permute-start.28
  96.1 1.0 collective-permute-start.32
  97.2 0.4 collective-permute-done.30
  97.6 7.2 %collective-permute-start.33 = (bf16[4,16,1152]{2,1,0:T(8,128)(2,1)S(1)}, bf16[4,16,1152]{2,1,0:T(8,128)(2,1)S(1)}, u32[]{:S(2)}, u32[]{:S(2)}) collective-permute-start(bf16[4,16,1152]{2,1,0:T(8,128)(2,1)S(1)} %get-tuple-element.99), channel_id=1, source_target_pairs={{0,7},{1,6},{2,5},{3,4},{4,3},{5,2},{6,1},{7,0},{8,15},{9,14},{10,... | collective-permute-start | bytes 442376 | tf_op jit(solution)/shard_map/ppermute | solution.py:258
  104.8 3.6 %collective-permute-start.22 = (bf16[144,1152]{1,0:T(8,128)(2,1)S(1)}, bf16[144,1152]{1,0:T(8,128)(2,1)S(1)}, u32[]{:S(2)}, u32[]{:S(2)}) collective-permute-start(bf16[144,1152]{1,0:T(8,128)(2,1)S(1)} %bitcast.46), channel_id=1, source_target_pairs={{0,1},{1,0},{2,3},{3,2},{4,5},{5,4},{6,7},{7,6},{8,9},{9,8},{10,11... | collective-permute-start | bytes 995336 | tf_op jit(solution)/shard_map/ppermute | solution.py:258
  108.4 6.6 %collective-permute-done.32 = bf16[4,16,1152]{2,1,0:T(8,128)(2,1)S(1)} collective-permute-done((bf16[4,16,1152]{2,1,0:T(8,128)(2,1)S(1)}, bf16[4,16,1152]{2,1,0:T(8,128)(2,1)S(1)}, u32[]{:S(2)}, u32[]{:S(2)}) %collective-permute-start.32) | collective-permute-done | bytes 147488 | tf_op jit(solution)/shard_map/ppermute | solution.py:258
  115.0 4.3 %collective-permute-done.33 = bf16[4,16,1152]{2,1,0:T(8,128)(2,1)S(1)} collective-permute-done((bf16[4,16,1152]{2,1,0:T(8,128)(2,1)S(1)}, bf16[4,16,1152]{2,1,0:T(8,128)(2,1)S(1)}, u32[]{:S(2)}, u32[]{:S(2)}) %collective-permute-start.33) | collective-permute-done | bytes 147488 | tf_op jit(solution)/shard_map/ppermute | solution.py:258
  119.3 0.1 collective-permute-start.34
  119.4 0.5 collective-permute-start.35
  119.9 1.5 %gather_out.1.wall = bf16[1152,1152]{1,0:T(8,128)(2,1)S(1)} custom-call(s32[2]{0:T(128)S(1)} %pad_add_fusion.index_ref, bf16[144,1152]{1,0:T(8,128)(2,1)S(1)} %bitcast.44, bf16[144,1152]{1,0:T(8,128)(2,1)S(1)} %collective-permute-done.4.refs_1_, bf16[144,1152]{1,0:T(8,128)(2,1)S(1)} %bitcast.47, bf16[144,1152]{1,0:T(8,128)(2,1)S(1)} %collective-permute-done.22.refs_3_, ...), custom_call_target="tpu_custom_call" | custom-call | tf_op jit(solution)/shard_map/gather_out/pallas_call | solution.py:417
  121.5 3.7 %restore.1 = bf16[4,128,1152]{2,1,0:T(8,128)(2,1)} custom-call(s32[2]{0:T(128)S(1)} %pad_add_fusion.index_ref, bf16[4,128,1152]{2,1,0:T(8,128)(2,1)S(1)} %copy-done.1, f32[3,4,1152]{2,1,0:T(4,128)S(1)} %bitcast.54, bf16[1152,1152]{1,0:T(8,128)(2,1)S(1)} %gather_out.1.wall, bf16[2,4,16,1152]{3,2,1,0:T(8,128)(2,1)S(1)} %get-tuple-element.83.refs_0_, ...), custom_call_target="tpu_custom_call" | custom-call | tf_op jit(solution)/shard_map/restore/pallas_call | solution.py:432
  (44 shorter events, 0.4 us)
Async XLA Ops:
  0.1 1.3 %copy-start = (bf16[4,128,1152]{2,1,0:T(8,128)(2,1)S(1)}, bf16[4,128,1152]{2,1,0:T(8,128)(2,1)}, u32[]{:S(2)}) copy-start(bf16[4,128,1152]{2,1,0:T(8,128)(2,1)} %tokens_ref.3) | copy-start | bytes 3538948
  1.3 0.8 copy-start.4
  3.8 4.7 %collective-permute-start = (bf16[4,4,16,1152]{3,2,1,0:T(8,128)(2,1)S(1)}, bf16[4,4,16,1152]{3,2,1,0:T(8,128)(2,1)S(1)}, u32[]{:S(2)}, u32[]{:S(2)}) collective-permute-start(bf16[4,4,16,1152]{3,2,1,0:T(8,128)(2,1)S(1)} %get-tuple-element.48), channel_id=1, source_target_pairs={{0,1},{1,0},{2,3},{3,2},{4,5},{5,4},{6,7},{7,6},{8,9},{9,8},{10,11... | collective-permute-start | bytes 1769480 | tf_op jit(solution)/shard_map/ppermute | solution.py:258
  5.6 13.8 %collective-permute-start.2 = (bf16[112,1152]{1,0:T(8,128)(2,1)S(1)}, bf16[112,1152]{1,0:T(8,128)(2,1)S(1)}, u32[]{:S(2)}, u32[]{:S(2)}) collective-permute-start(bf16[112,1152]{1,0:T(8,128)(2,1)S(1)} %get-tuple-element.90), channel_id=1, source_target_pairs={{0,4},{1,5},{2,6},{3,7},{4,0},{5,1},{6,2},{7,3},{8,12},{9,13},{10,... | collective-permute-start | bytes 774152 | tf_op jit(solution)/shard_map/ppermute | solution.py:258
  8.0 13.3 %collective-permute-start.3 = (bf16[432,1152]{1,0:T(8,128)(2,1)}, bf16[432,1152]{1,0:T(8,128)(2,1)S(1)}, u32[]{:S(2)}, u32[]{:S(2)}) collective-permute-start(bf16[432,1152]{1,0:T(8,128)(2,1)} %bitcast.48), channel_id=1, source_target_pairs={{0,1},{1,0},{2,3},{3,2},{4,5},{5,4},{6,7},{7,6},{8,9},{9,8},{10,11... | collective-permute-start | bytes 2985992 | tf_op jit(solution)/shard_map/ppermute | solution.py:258
  8.3 11.3 %collective-permute-start.4 = (bf16[144,1152]{1,0:T(8,128)(2,1)}, bf16[144,1152]{1,0:T(8,128)(2,1)S(1)}, u32[]{:S(2)}, u32[]{:S(2)}) collective-permute-start(bf16[144,1152]{1,0:T(8,128)(2,1)} %bitcast.41), channel_id=1, source_target_pairs={{0,1},{1,0},{2,3},{3,2},{4,5},{5,4},{6,7},{7,6},{8,9},{9,8},{10,11... | collective-permute-start | bytes 995336 | tf_op jit(solution)/shard_map/ppermute | solution.py:258
  8.5 36.3 %copy-start.2 = (bf16[1152,144]{0,1:T(8,128)(2,1)S(1)}, bf16[1152,144]{0,1:T(8,128)(2,1)}, u32[]{:S(2)}) copy-start(bf16[1152,144]{0,1:T(8,128)(2,1)} %param.7) | copy-start | bytes 995332
  8.6 10.9 %collective-permute-start.5 = (bf16[2,4,16,1152]{3,2,1,0:T(8,128)(2,1)S(1)}, bf16[2,4,16,1152]{3,2,1,0:T(8,128)(2,1)S(1)}, u32[]{:S(2)}, u32[]{:S(2)}) collective-permute-start(bf16[2,4,16,1152]{3,2,1,0:T(8,128)(2,1)S(1)} %pad_maximum_fusion.5), channel_id=1, source_target_pairs={{0,24},{1,25},{2,26},{3,27},{4,12},{5,13},{6,14},{7,15},{8,0},{9,1... | collective-permute-start | bytes 884744 | tf_op jit(solution)/shard_map/ppermute | solution.py:285
  10.9 10.4 %collective-permute-start.1 = (bf16[2,4,16,1152]{3,2,1,0:T(8,128)(2,1)S(1)}, bf16[2,4,16,1152]{3,2,1,0:T(8,128)(2,1)S(1)}, u32[]{:S(2)}, u32[]{:S(2)}) collective-permute-start(bf16[2,4,16,1152]{3,2,1,0:T(8,128)(2,1)S(1)} %pad_maximum_fusion.4), channel_id=1, source_target_pairs={{0,2},{1,3},{2,0},{3,1},{4,6},{5,7},{6,4},{7,5},{8,10},{9,11},{10,... | collective-permute-start | bytes 884744 | tf_op jit(solution)/shard_map/ppermute | solution.py:258
  19.4 44.8 %copy-start.3 = (bf16[1152,432]{0,1:T(8,128)(2,1)S(1)}, bf16[1152,432]{0,1:T(8,128)(2,1)}, u32[]{:S(2)}) copy-start(bf16[1152,432]{0,1:T(8,128)(2,1)} %param.6) | copy-start | bytes 2985988
  21.3 19.2 %collective-permute-start.8 = (bf16[2,112,1152]{2,1,0:T(8,128)(2,1)S(1)}, bf16[2,112,1152]{2,1,0:T(8,128)(2,1)S(1)}, u32[]{:S(2)}, u32[]{:S(2)}) collective-permute-start(bf16[2,112,1152]{2,1,0:T(8,128)(2,1)S(1)} %pad_maximum_fusion.2), channel_id=1, source_target_pairs={{0,2},{1,3},{2,0},{3,1},{4,6},{5,7},{6,4},{7,5},{8,10},{9,11},{10,... | collective-permute-start | bytes 1548296 | tf_op jit(solution)/shard_map/ppermute | solution.py:258
  23.5 12.3 %collective-permute-start.10 = (bf16[2,4,16,1152]{3,2,1,0:T(8,128)(2,1)S(1)}, bf16[2,4,16,1152]{3,2,1,0:T(8,128)(2,1)S(1)}, u32[]{:S(2)}, u32[]{:S(2)}) collective-permute-start(bf16[2,4,16,1152]{3,2,1,0:T(8,128)(2,1)S(1)} %collective-permute-done.1), channel_id=1, source_target_pairs={{0,24},{1,25},{2,26},{3,27},{4,12},{5,13},{6,14},{7,15},{8,0},{9,1... | collective-permute-start | bytes 884744 | tf_op jit(solution)/shard_map/ppermute | solution.py:285
  23.8 16.7 %collective-permute-start.9 = (bf16[2,4,16,1152]{3,2,1,0:T(8,128)(2,1)S(1)}, bf16[2,4,16,1152]{3,2,1,0:T(8,128)(2,1)S(1)}, u32[]{:S(2)}, u32[]{:S(2)}) collective-permute-start(bf16[2,4,16,1152]{3,2,1,0:T(8,128)(2,1)S(1)} %get-tuple-element.52), channel_id=1, source_target_pairs={{0,4},{1,5},{2,6},{3,7},{4,0},{5,1},{6,2},{7,3},{8,12},{9,13},{10,... | collective-permute-start | bytes 884744 | tf_op jit(solution)/shard_map/ppermute | solution.py:258
  24.7 11.0 %collective-permute-start.6 = (bf16[112,1152]{1,0:T(8,128)(2,1)S(1)}, bf16[112,1152]{1,0:T(8,128)(2,1)S(1)}, u32[]{:S(2)}, u32[]{:S(2)}) collective-permute-start(bf16[112,1152]{1,0:T(8,128)(2,1)S(1)} %collective-permute-done.2.refs_2_), channel_id=1, source_target_pairs={{0,8},{1,9},{2,10},{3,11},{4,12},{5,13},{6,14},{7,15},{8,0},{9,1},... | collective-permute-start | bytes 774152 | tf_op jit(solution)/shard_map/ppermute | solution.py:258
  25.9 9.8 %collective-permute-start.7 = (bf16[112,1152]{1,0:T(8,128)(2,1)S(1)}, bf16[112,1152]{1,0:T(8,128)(2,1)S(1)}, u32[]{:S(2)}, u32[]{:S(2)}) collective-permute-start(bf16[112,1152]{1,0:T(8,128)(2,1)S(1)} %collective-permute-done.2.refs_2_), channel_id=1, source_target_pairs={{0,16},{1,17},{2,18},{3,19},{4,20},{5,21},{6,22},{7,23},{8,24},{9,... | collective-permute-start | bytes 774152 | tf_op jit(solution)/shard_map/ppermute | solution.py:258
  40.5 11.2 %collective-permute-start.11 = (bf16[2,112,1152]{2,1,0:T(8,128)(2,1)S(1)}, bf16[2,112,1152]{2,1,0:T(8,128)(2,1)S(1)}, u32[]{:S(2)}, u32[]{:S(2)}) collective-permute-start(bf16[2,112,1152]{2,1,0:T(8,128)(2,1)S(1)} %collective-permute-done.8.refs_8_), channel_id=1, source_target_pairs={{0,8},{1,9},{2,10},{3,11},{4,12},{5,13},{6,14},{7,15},{8,0},{9,1},... | collective-permute-start | bytes 1548296 | tf_op jit(solution)/shard_map/ppermute | solution.py:258
  41.7 10.9 %collective-permute-start.12 = (bf16[2,112,1152]{2,1,0:T(8,128)(2,1)S(1)}, bf16[2,112,1152]{2,1,0:T(8,128)(2,1)S(1)}, u32[]{:S(2)}, u32[]{:S(2)}) collective-permute-start(bf16[2,112,1152]{2,1,0:T(8,128)(2,1)S(1)} %collective-permute-done.8.refs_8_), channel_id=1, source_target_pairs={{0,16},{1,17},{2,18},{3,19},{4,20},{5,21},{6,22},{7,23},{8,24},{9,... | collective-permute-start | bytes 1548296 | tf_op jit(solution)/shard_map/ppermute | solution.py:258
  42.4 10.2 %collective-permute-start.14 = (bf16[2,112,1152]{2,1,0:T(8,128)(2,1)S(1)}, bf16[2,112,1152]{2,1,0:T(8,128)(2,1)S(1)}, u32[]{:S(2)}, u32[]{:S(2)}) collective-permute-start(bf16[2,112,1152]{2,1,0:T(8,128)(2,1)S(1)} %collective-permute-done.8.refs_8_), channel_id=1, source_target_pairs={{0,1},{1,0},{2,3},{3,2},{4,5},{5,4},{6,7},{7,6},{8,9},{9,8},{10,11... | collective-permute-start | bytes 1548296 | tf_op jit(solution)/shard_map/ppermute | solution.py:258
  44.8 1.9 %collective-permute-start.13 = (bf16[112,1152]{1,0:T(8,128)(2,1)S(1)}, bf16[112,1152]{1,0:T(8,128)(2,1)S(1)}, u32[]{:S(2)}, u32[]{:S(2)}) collective-permute-start(bf16[112,1152]{1,0:T(8,128)(2,1)S(1)} %collective-permute-done.2.refs_2_), channel_id=1, source_target_pairs={{0,1},{1,0},{2,3},{3,2},{4,5},{5,4},{6,7},{7,6},{8,9},{9,8},{10,11... | collective-permute-start | bytes 774152 | tf_op jit(solution)/shard_map/ppermute | solution.py:258
  44.9 28.7 %collective-permute-start.21 = (bf16[17,16,1152]{2,1,0:T(8,128)(2,1)S(1)}, bf16[17,16,1152]{2,1,0:T(8,128)(2,1)S(1)}, u32[]{:S(2)}, u32[]{:S(2)}) collective-permute-start(bf16[17,16,1152]{2,1,0:T(8,128)(2,1)S(1)} %pad_maximum_fusion.1), channel_id=1, source_target_pairs={{0,6},{1,7},{2,4},{3,5},{4,2},{5,3},{6,0},{7,1},{8,14},{9,15},{10,... | collective-permute-start | bytes 1880072 | tf_op jit(solution)/shard_map/ppermute | solution.py:258
  52.6 5.5 %collective-permute-start.16 = (bf16[112,1152]{1,0:T(8,128)(2,1)S(1)}, bf16[112,1152]{1,0:T(8,128)(2,1)S(1)}, u32[]{:S(2)}, u32[]{:S(2)}) collective-permute-start(bf16[112,1152]{1,0:T(8,128)(2,1)S(1)} %slice_bitcast_fusion), channel_id=1, source_target_pairs={{0,8},{1,9},{2,10},{3,11},{4,12},{5,13},{6,14},{7,15},{8,0},{9,1},... | collective-permute-start | bytes 774152 | tf_op jit(solution)/shard_map/ppermute | solution.py:258
  53.0 9.3 %collective-permute-start.15 = (bf16[112,1152]{1,0:T(8,128)(2,1)S(1)}, bf16[112,1152]{1,0:T(8,128)(2,1)S(1)}, u32[]{:S(2)}, u32[]{:S(2)}) collective-permute-start(bf16[112,1152]{1,0:T(8,128)(2,1)S(1)} %slice_bitcast_fusion.1), channel_id=1, source_target_pairs={{0,16},{1,17},{2,18},{3,19},{4,20},{5,21},{6,22},{7,23},{8,24},{9,... | collective-permute-start | bytes 774152 | tf_op jit(solution)/shard_map/ppermute | solution.py:258
  54.3 10.0 %collective-permute-start.19 = (bf16[2,112,1152]{2,1,0:T(8,128)(2,1)S(1)}, bf16[2,112,1152]{2,1,0:T(8,128)(2,1)S(1)}, u32[]{:S(2)}, u32[]{:S(2)}) collective-permute-start(bf16[2,112,1152]{2,1,0:T(8,128)(2,1)S(1)} %collective-permute-done.11.refs_10_), channel_id=1, source_target_pairs={{0,1},{1,0},{2,3},{3,2},{4,5},{5,4},{6,7},{7,6},{8,9},{9,8},{10,11... | collective-permute-start | bytes 1548296 | tf_op jit(solution)/shard_map/ppermute | solution.py:258
  58.1 6.2 %collective-permute-start.20 = (bf16[2,112,1152]{2,1,0:T(8,128)(2,1)S(1)}, bf16[2,112,1152]{2,1,0:T(8,128)(2,1)S(1)}, u32[]{:S(2)}, u32[]{:S(2)}) collective-permute-start(bf16[2,112,1152]{2,1,0:T(8,128)(2,1)S(1)} %collective-permute-done.12.refs_12_), channel_id=1, source_target_pairs={{0,1},{1,0},{2,3},{3,2},{4,5},{5,4},{6,7},{7,6},{8,9},{9,8},{10,11... | collective-permute-start | bytes 1548296 | tf_op jit(solution)/shard_map/ppermute | solution.py:258
  58.2 5.3 %collective-permute-start.17 = (bf16[112,1152]{1,0:T(8,128)(2,1)S(1)}, bf16[112,1152]{1,0:T(8,128)(2,1)S(1)}, u32[]{:S(2)}, u32[]{:S(2)}) collective-permute-start(bf16[112,1152]{1,0:T(8,128)(2,1)S(1)} %collective-permute-done.6.refs_4_), channel_id=1, source_target_pairs={{0,1},{1,0},{2,3},{3,2},{4,5},{5,4},{6,7},{7,6},{8,9},{9,8},{10,11... | collective-permute-start | bytes 774152 | tf_op jit(solution)/shard_map/ppermute | solution.py:258
  62.3 2.0 %collective-permute-start.18 = (bf16[112,1152]{1,0:T(8,128)(2,1)S(1)}, bf16[112,1152]{1,0:T(8,128)(2,1)S(1)}, u32[]{:S(2)}, u32[]{:S(2)}) collective-permute-start(bf16[112,1152]{1,0:T(8,128)(2,1)S(1)} %collective-permute-done.7.refs_6_), channel_id=1, source_target_pairs={{0,1},{1,0},{2,3},{3,2},{4,5},{5,4},{6,7},{7,6},{8,9},{9,8},{10,11... | collective-permute-start | bytes 774152 | tf_op jit(solution)/shard_map/ppermute | solution.py:258
  63.4 11.5 %collective-permute-start.24 = (bf16[112,1152]{1,0:T(8,128)(2,1)S(1)}, bf16[112,1152]{1,0:T(8,128)(2,1)S(1)}, u32[]{:S(2)}, u32[]{:S(2)}) collective-permute-start(bf16[112,1152]{1,0:T(8,128)(2,1)S(1)} %collective-permute-done.7.refs_6_), channel_id=1, source_target_pairs={{0,8},{1,9},{2,10},{3,11},{4,12},{5,13},{6,14},{7,15},{8,0},{9,1},... | collective-permute-start | bytes 774152 | tf_op jit(solution)/shard_map/ppermute | solution.py:258
  73.6 3.2 %collective-permute-start.26 = (bf16[2,112,1152]{2,1,0:T(8,128)(2,1)S(1)}, bf16[2,112,1152]{2,1,0:T(8,128)(2,1)S(1)}, u32[]{:S(2)}, u32[]{:S(2)}) collective-permute-start(bf16[2,112,1152]{2,1,0:T(8,128)(2,1)S(1)} %pad_maximum_fusion.3.refs_9_.refs_7_), channel_id=1, source_target_pairs={{0,1},{1,0},{2,3},{3,2},{4,5},{5,4},{6,7},{7,6},{8,9},{9,8},{10,11... | collective-permute-start | bytes 1548296 | tf_op jit(solution)/shard_map/ppermute | solution.py:258
  74.9 1.9 %collective-permute-start.25 = (bf16[112,1152]{1,0:T(8,128)(2,1)S(1)}, bf16[112,1152]{1,0:T(8,128)(2,1)S(1)}, u32[]{:S(2)}, u32[]{:S(2)}) collective-permute-start(bf16[112,1152]{1,0:T(8,128)(2,1)S(1)} %collective-permute-done.24.refs_7_.refs_5_), channel_id=1, source_target_pairs={{0,1},{1,0},{2,3},{3,2},{4,5},{5,4},{6,7},{7,6},{8,9},{9,8},{10,11... | collective-permute-start | bytes 774152 | tf_op jit(solution)/shard_map/ppermute | solution.py:258
  75.0 20.2 %collective-permute-start.23 = (bf16[2,144,1152]{2,1,0:T(8,128)(2,1)S(1)}, bf16[2,144,1152]{2,1,0:T(8,128)(2,1)S(1)}, u32[]{:S(2)}, u32[]{:S(2)}) collective-permute-start(bf16[2,144,1152]{2,1,0:T(8,128)(2,1)S(1)} %pad_maximum_fusion), channel_id=1, source_target_pairs={{0,2},{1,3},{2,0},{3,1},{4,6},{5,7},{6,4},{7,5},{8,10},{9,11},{10,... | collective-permute-start | bytes 1990664 | tf_op jit(solution)/shard_map/ppermute | solution.py:258
  83.7 11.5 %collective-permute-start.27 = (bf16[4,4,16,640]{3,2,1,0:T(8,128)(2,1)S(1)}, bf16[4,4,16,640]{3,2,1,0:T(8,128)(2,1)S(1)}, u32[]{:S(2)}, u32[]{:S(2)}) collective-permute-start(bf16[4,4,16,640]{3,2,1,0:T(8,128)(2,1)S(1)} %get-tuple-element.73), channel_id=1, source_target_pairs={{0,8},{1,9},{2,10},{3,11},{4,28},{5,29},{6,30},{7,31},{8,16},{9,17... | collective-permute-start | bytes 983048 | tf_op jit(solution)/shard_map/ppermute | solution.py:285
  91.9 5.7 %collective-permute-start.30 = (bf16[4,16,1152]{2,1,0:T(8,128)(2,1)S(1)}, bf16[4,16,1152]{2,1,0:T(8,128)(2,1)S(1)}, u32[]{:S(2)}, u32[]{:S(2)}) collective-permute-start(bf16[4,16,1152]{2,1,0:T(8,128)(2,1)S(1)} %get-tuple-element.102), channel_id=1, source_target_pairs={{0,4},{1,5},{2,6},{3,7},{4,0},{5,1},{6,2},{7,3},{8,12},{9,13},{10,... | collective-permute-start | bytes 442376 | tf_op jit(solution)/shard_map/ppermute | solution.py:258
  92.5 12.3 %collective-permute-start.31 = (bf16[4,16,1152]{2,1,0:T(8,128)(2,1)S(1)}, bf16[4,16,1152]{2,1,0:T(8,128)(2,1)S(1)}, u32[]{:S(2)}, u32[]{:S(2)}) collective-permute-start(bf16[4,16,1152]{2,1,0:T(8,128)(2,1)S(1)} %get-tuple-element.101), channel_id=1, source_target_pairs={{0,5},{1,4},{2,7},{3,6},{4,1},{5,0},{6,3},{7,2},{8,13},{9,12},{10,... | collective-permute-start | bytes 442376 | tf_op jit(solution)/shard_map/ppermute | solution.py:258
  95.8 23.5 %collective-permute-start.29 = (bf16[2,4,16,1152]{3,2,1,0:T(8,128)(2,1)S(1)}, bf16[2,4,16,1152]{3,2,1,0:T(8,128)(2,1)S(1)}, u32[]{:S(2)}, u32[]{:S(2)}) collective-permute-start(bf16[2,4,16,1152]{3,2,1,0:T(8,128)(2,1)S(1)} %get-tuple-element.78), channel_id=1, source_target_pairs={{0,2},{1,3},{2,0},{3,1},{4,6},{5,7},{6,4},{7,5},{8,10},{9,11},{10,... | collective-permute-start | bytes 884744 | tf_op jit(solution)/shard_map/ppermute | solution.py:258
  96.0 23.9 %collective-permute-start.28 = (bf16[2,144,1152]{2,1,0:T(8,128)(2,1)S(1)}, bf16[2,144,1152]{2,1,0:T(8,128)(2,1)S(1)}, u32[]{:S(2)}, u32[]{:S(2)}) collective-permute-start(bf16[2,144,1152]{2,1,0:T(8,128)(2,1)S(1)} %collective-permute-done.23.refs_4_), channel_id=1, source_target_pairs={{0,1},{1,0},{2,3},{3,2},{4,5},{5,4},{6,7},{7,6},{8,9},{9,8},{10,11... | collective-permute-start | bytes 1990664 | tf_op jit(solution)/shard_map/ppermute | solution.py:258
  96.1 18.9 %collective-permute-start.32 = (bf16[4,16,1152]{2,1,0:T(8,128)(2,1)S(1)}, bf16[4,16,1152]{2,1,0:T(8,128)(2,1)S(1)}, u32[]{:S(2)}, u32[]{:S(2)}) collective-permute-start(bf16[4,16,1152]{2,1,0:T(8,128)(2,1)S(1)} %get-tuple-element.100), channel_id=1, source_target_pairs={{0,6},{1,7},{2,4},{3,5},{4,2},{5,3},{6,0},{7,1},{8,14},{9,15},{10,... | collective-permute-start | bytes 442376 | tf_op jit(solution)/shard_map/ppermute | solution.py:258
  97.6 21.7 %collective-permute-start.33 = (bf16[4,16,1152]{2,1,0:T(8,128)(2,1)S(1)}, bf16[4,16,1152]{2,1,0:T(8,128)(2,1)S(1)}, u32[]{:S(2)}, u32[]{:S(2)}) collective-permute-start(bf16[4,16,1152]{2,1,0:T(8,128)(2,1)S(1)} %get-tuple-element.99), channel_id=1, source_target_pairs={{0,7},{1,6},{2,5},{3,4},{4,3},{5,2},{6,1},{7,0},{8,15},{9,14},{10,... | collective-permute-start | bytes 442376 | tf_op jit(solution)/shard_map/ppermute | solution.py:258
  104.8 15.1 %collective-permute-start.22 = (bf16[144,1152]{1,0:T(8,128)(2,1)S(1)}, bf16[144,1152]{1,0:T(8,128)(2,1)S(1)}, u32[]{:S(2)}, u32[]{:S(2)}) collective-permute-start(bf16[144,1152]{1,0:T(8,128)(2,1)S(1)} %bitcast.46), channel_id=1, source_target_pairs={{0,1},{1,0},{2,3},{3,2},{4,5},{5,4},{6,7},{7,6},{8,9},{9,8},{10,11... | collective-permute-start | bytes 995336 | tf_op jit(solution)/shard_map/ppermute | solution.py:258
  119.3 2.1 %copy-start.1 = (bf16[4,128,1152]{2,1,0:T(8,128)(2,1)S(1)}, bf16[4,128,1152]{2,1,0:T(8,128)(2,1)}, u32[]{:S(2)}) copy-start(bf16[4,128,1152]{2,1,0:T(8,128)(2,1)} %tokens_ref.3) | copy-start | bytes 3538948
  119.3 2.1 %copy-start.5 = (f32[4,3,1152]{2,0,1:T(4,128)S(1)}, f32[4,3,1152]{2,0,1:T(4,128)}, u32[]{:S(2)}) copy-start(f32[4,3,1152]{2,0,1:T(4,128)} %param.5) | copy-start | bytes 165892
  119.3 2.1 %collective-permute-start.34 = (bf16[2,4,16,1152]{3,2,1,0:T(8,128)(2,1)S(1)}, bf16[2,4,16,1152]{3,2,1,0:T(8,128)(2,1)S(1)}, u32[]{:S(2)}, u32[]{:S(2)}) collective-permute-start(bf16[2,4,16,1152]{3,2,1,0:T(8,128)(2,1)S(1)} %get-tuple-element.83.refs_0_), channel_id=1, source_target_pairs={{0,1},{1,0},{2,3},{3,2},{4,5},{5,4},{6,7},{7,6},{8,9},{9,8},{10,11... | collective-permute-start | bytes 884744 | tf_op jit(solution)/shard_map/ppermute | solution.py:258
  119.4 2.0 %collective-permute-start.35 = (bf16[2,4,16,1152]{3,2,1,0:T(8,128)(2,1)S(1)}, bf16[2,4,16,1152]{3,2,1,0:T(8,128)(2,1)S(1)}, u32[]{:S(2)}, u32[]{:S(2)}) collective-permute-start(bf16[2,4,16,1152]{3,2,1,0:T(8,128)(2,1)S(1)} %collective-permute-done.29.refs_2_), channel_id=1, source_target_pairs={{0,1},{1,0},{2,3},{3,2},{4,5},{5,4},{6,7},{7,6},{8,9},{9,8},{10,11... | collective-permute-start | bytes 884744 | tf_op jit(solution)/shard_map/ppermute | solution.py:258

commit v9 on v8

--- a/solution.py
+++ b/solution.py
@@ -303,12 +303,12 @@
         x, y = 1, 2
         blocks = [pair[0], None, None, None]
         far = hop(mine, 4)
-        wide_other, narrow_other = hop(wide, 1), hop(narrow, 1)
+        wide_other = hop(wide, 1)
         blocks[1] = hop(pair[1], 2)
         following = [following_of(pair[0])]
         near_and_far = jnp.stack([mine, far])
-        blocks[1], far, near_and_far, pair, wide_other, narrow_other, following = tie(
-            (blocks[1], far, near_and_far, pair, wide_other, narrow_other, following))
+        blocks[1], far, near_and_far, pair, wide_other, following, narrow = tie(
+            (blocks[1], far, near_and_far, pair, wide_other, following, narrow))
         ax, ay = hop(far, 0, x), hop(far, 0, y)
         rest = hop(near_and_far, 2)
         blocks[2] = hop(pair[2], 4)
@@ -318,6 +318,7 @@
         both = jnp.concatenate([pair[3].reshape(-1, ROWS, width), narrow.reshape(-1, ROWS, width)], axis=0)
         blocks[3] = hop(both, 6)
         early = [hop(far, 1), hop(rest, 1)]
+        narrow_other = hop(narrow, 1)
         ay, bx, by, early, ax = tie((ay, bx, by, early, ax))
         axy = hop(ay, 0, x)
         bxy = jnp.stack([hop(bx[0], 0, y), hop(by[1], 0, x)])

time: 125 us -> 125 us (level)
  waiting for transfers between devices: 46.2 us -> 43.1 us
  starting transfers between devices: 45.6 us -> 48.6 us
    ppermute x33, starting transfers between devices: 42 us -> 45.2 us  [hop(): return lax.ppermute(value, ('slab', 'seq'), pairs)]
    ppermute x33, waiting for transfers between devices: 46.2 us -> 43.1 us  [hop(): return lax.ppermute(value, ('slab', 'seq'), pairs)]
  transfers between devices with their start and end apart: 36 -> 36, of which waited for: 14 -> 13; matrix products, arithmetic and copies ran while one was open for 1% -> 1% of each run, Pallas kernels for 19% -> 19%
where the time goes in v9:
time: 125 us
  starting transfers between devices  48.6 us (39%)
  waiting for transfers between devices  43.1 us (34%)
  Pallas kernels  29.3 us (23%)
  local copies, waits for them, and re-layouts  3.33 us (3%)
    ppermute x33, starting transfers between devices, hop(): return lax.ppermute(value, ('slab', 'seq'), pairs)  45.2 us
    ppermute x33, waiting for transfers between devices, hop(): return lax.ppermute(value, ('slab', 'seq'), pairs)  43.1 us
    pallas_call x2, Pallas kernels, attention(): pl.pallas_call(functools.partial(block_kernel, plan, frames), out_shape=[...  13.4 us
    pallas_call x1, Pallas kernels, per_device(): pl.pallas_call(functools.partial(gather_kernel, plan), out_shape=jax.Shap...  7.91 us
    pallas_call x1, Pallas kernels, per_device(): pl.pallas_call(functools.partial(restore_kernel, count), out_shape=jax.Sh...  3.64 us
    ppermute x3, starting transfers between devices, to_neighbour(): return lax.ppermute(value, ('slab', 'seq'), pairs)  3.4 us
  transfers between devices with their start and end apart: 36, of which 13 were waited for; matrix products, arithmetic and copies ran while one was open for 1% of the time, Pallas kernels for 19%

profile of v9, /device:TPU:9, one launch (start us, length us, event | category | flops | bytes accessed | tf_op | source)
XLA Modules:
  0.0 125.0 jit_solution(10885319880824926998)
XLA Ops:
  0.0 0.1 pad_add_fusion.index_ref
  0.1 1.3 %copy-done = bf16[4,128,1152]{2,1,0:T(8,128)(2,1)S(1)} copy-done((bf16[4,128,1152]{2,1,0:T(8,128)(2,1)S(1)}, bf16[4,128,1152]{2,1,0:T(8,128)(2,1)}, u32[]{:S(2)}) %copy-start) | copy-done | bytes 1179672
  1.3 0.8 copy-done.4
  2.2 1.7 %norm.1 = (bf16[4,4,16,1152]{3,2,1,0:T(8,128)(2,1)S(1)}, bf16[4,4,16,1152]{3,2,1,0:T(8,128)(2,1)S(1)}) custom-call(s32[2]{0:T(128)S(1)} %pad_add_fusion.index_ref, bf16[4,128,1152]{2,1,0:T(8,128)(2,1)S(1)} %copy-done, f32[3,4,1152]{2,1,0:T(4,128)S(1)} %bitcast.51), custom_call_target="tpu_custom_call" | custom-call | tf_op jit(solution)/shard_map/norm/pallas_call | solution.py:270
  3.8 0.7 collective-permute-start
  4.6 1.0 dynamic-slice_bitcast_fusion
  5.6 2.4 %collective-permute-start.2 = (bf16[112,1152]{1,0:T(8,128)(2,1)S(1)}, bf16[112,1152]{1,0:T(8,128)(2,1)S(1)}, u32[]{:S(2)}, u32[]{:S(2)}) collective-permute-start(bf16[112,1152]{1,0:T(8,128)(2,1)S(1)} %get-tuple-element.90), channel_id=1, source_target_pairs={{0,4},{1,5},{2,6},{3,7},{4,0},{5,1},{6,2},{7,3},{8,12},{9,13},{10,... | collective-permute-start | bytes 774152 | tf_op jit(solution)/shard_map/ppermute | solution.py:258
  8.0 0.3 collective-permute-start.3
  8.4 2.2 %collective-permute-start.4 = (bf16[2,4,16,1152]{3,2,1,0:T(8,128)(2,1)S(1)}, bf16[2,4,16,1152]{3,2,1,0:T(8,128)(2,1)S(1)}, u32[]{:S(2)}, u32[]{:S(2)}) collective-permute-start(bf16[2,4,16,1152]{3,2,1,0:T(8,128)(2,1)S(1)} %pad_maximum_fusion.5), channel_id=1, source_target_pairs={{0,24},{1,25},{2,26},{3,27},{4,12},{5,13},{6,14},{7,15},{8,0},{9,1... | collective-permute-start | bytes 884744 | tf_op jit(solution)/shard_map/ppermute | solution.py:285
  10.7 0.2 collective-permute-start.1
  10.9 8.5 %collective-permute-done.2.refs_2_ = bf16[112,1152]{1,0:T(8,128)(2,1)S(1)} collective-permute-done((bf16[112,1152]{1,0:T(8,128)(2,1)S(1)}, bf16[112,1152]{1,0:T(8,128)(2,1)S(1)}, u32[]{:S(2)}, u32[]{:S(2)}) %collective-permute-start.2) | collective-permute-done | bytes 258080 | tf_op jit(solution)/shard_map/ppermute | solution.py:258
  19.4 0.1 pad_maximum_fusion.2
  19.5 0.1 pad_maximum_fusion.6
  19.6 1.6 %collective-permute-done.1 = bf16[2,4,16,1152]{3,2,1,0:T(8,128)(2,1)S(1)} collective-permute-done((bf16[2,4,16,1152]{3,2,1,0:T(8,128)(2,1)S(1)}, bf16[2,4,16,1152]{3,2,1,0:T(8,128)(2,1)S(1)}, u32[]{:S(2)}, u32[]{:S(2)}) %collective-permute-start.1) | collective-permute-done | bytes 294944 | tf_op jit(solution)/shard_map/ppermute | solution.py:258
  21.2 2.2 %collective-permute-start.8 = (bf16[2,112,1152]{2,1,0:T(8,128)(2,1)S(1)}, bf16[2,112,1152]{2,1,0:T(8,128)(2,1)S(1)}, u32[]{:S(2)}, u32[]{:S(2)}) collective-permute-start(bf16[2,112,1152]{2,1,0:T(8,128)(2,1)S(1)} %pad_maximum_fusion.2), channel_id=1, source_target_pairs={{0,2},{1,3},{2,0},{3,1},{4,6},{5,7},{6,4},{7,5},{8,10},{9,11},{10,... | collective-permute-start | bytes 1548296 | tf_op jit(solution)/shard_map/ppermute | solution.py:258
  23.4 0.3 collective-permute-start.10
  23.7 0.8 collective-permute-start.9
  24.5 1.2 collective-permute-start.6
  25.7 0.2 collective-permute-start.7
  26.0 9.9 %collective-permute-done.6.refs_4_ = bf16[112,1152]{1,0:T(8,128)(2,1)S(1)} collective-permute-done((bf16[112,1152]{1,0:T(8,128)(2,1)S(1)}, bf16[112,1152]{1,0:T(8,128)(2,1)S(1)}, u32[]{:S(2)}, u32[]{:S(2)}) %collective-permute-start.6) | collective-permute-done | bytes 258080 | tf_op jit(solution)/shard_map/ppermute | solution.py:258
  35.8 4.3 %collective-permute-done.9 = bf16[2,4,16,1152]{3,2,1,0:T(8,128)(2,1)S(1)} collective-permute-done((bf16[2,4,16,1152]{3,2,1,0:T(8,128)(2,1)S(1)}, bf16[2,4,16,1152]{3,2,1,0:T(8,128)(2,1)S(1)}, u32[]{:S(2)}, u32[]{:S(2)}) %collective-permute-start.9) | collective-permute-done | bytes 294944 | tf_op jit(solution)/shard_map/ppermute | solution.py:258
  40.2 1.2 collective-permute-start.11
  41.4 1.1 collective-permute-start.12
  42.5 2.3 %collective-permute-start.14 = (bf16[2,112,1152]{2,1,0:T(8,128)(2,1)S(1)}, bf16[2,112,1152]{2,1,0:T(8,128)(2,1)S(1)}, u32[]{:S(2)}, u32[]{:S(2)}) collective-permute-start(bf16[2,112,1152]{2,1,0:T(8,128)(2,1)S(1)} %collective-permute-done.8.refs_8_), channel_id=1, source_target_pairs={{0,1},{1,0},{2,3},{3,2},{4,5},{5,4},{6,7},{7,6},{8,9},{9,8},{10,11... | collective-permute-start | bytes 1548296 | tf_op jit(solution)/shard_map/ppermute | solution.py:258
  44.8 0.1 pad_maximum_fusion.1
  44.9 0.8 collective-permute-start.21
  45.7 1.0 collective-permute-done.13.refs_3_
  46.7 4.5 %collective-permute-done.11.refs_10_ = bf16[2,112,1152]{2,1,0:T(8,128)(2,1)S(1)} collective-permute-done((bf16[2,112,1152]{2,1,0:T(8,128)(2,1)S(1)}, bf16[2,112,1152]{2,1,0:T(8,128)(2,1)S(1)}, u32[]{:S(2)}, u32[]{:S(2)}) %collective-permute-start.11) | collective-permute-done | bytes 516128 | tf_op jit(solution)/shard_map/ppermute | solution.py:258
  51.2 0.9 collective-permute-done.12.refs_12_
  52.2 0.3 collective-permute-start.16
  52.6 1.5 %collective-permute-start.15 = (bf16[112,1152]{1,0:T(8,128)(2,1)S(1)}, bf16[112,1152]{1,0:T(8,128)(2,1)S(1)}, u32[]{:S(2)}, u32[]{:S(2)}) collective-permute-start(bf16[112,1152]{1,0:T(8,128)(2,1)S(1)} %slice_bitcast_fusion.1), channel_id=1, source_target_pairs={{0,16},{1,17},{2,18},{3,19},{4,20},{5,21},{6,22},{7,23},{8,24},{9,... | collective-permute-start | bytes 774152 | tf_op jit(solution)/shard_map/ppermute | solution.py:258
  54.1 3.7 %collective-permute-start.19 = (bf16[2,112,1152]{2,1,0:T(8,128)(2,1)S(1)}, bf16[2,112,1152]{2,1,0:T(8,128)(2,1)S(1)}, u32[]{:S(2)}, u32[]{:S(2)}) collective-permute-start(bf16[2,112,1152]{2,1,0:T(8,128)(2,1)S(1)} %collective-permute-done.11.refs_10_), channel_id=1, source_target_pairs={{0,1},{1,0},{2,3},{3,2},{4,5},{5,4},{6,7},{7,6},{8,9},{9,8},{10,11... | collective-permute-start | bytes 1548296 | tf_op jit(solution)/shard_map/ppermute | solution.py:258
  57.8 4.2 %collective-permute-start.17 = (bf16[112,1152]{1,0:T(8,128)(2,1)S(1)}, bf16[112,1152]{1,0:T(8,128)(2,1)S(1)}, u32[]{:S(2)}, u32[]{:S(2)}) collective-permute-start(bf16[112,1152]{1,0:T(8,128)(2,1)S(1)} %collective-permute-done.6.refs_4_), channel_id=1, source_target_pairs={{0,1},{1,0},{2,3},{3,2},{4,5},{5,4},{6,7},{7,6},{8,9},{9,8},{10,11... | collective-permute-start | bytes 774152 | tf_op jit(solution)/shard_map/ppermute | solution.py:258
  62.0 0.6 collective-permute-start.18
  62.6 0.1 pad_maximum_fusion.3.refs_9_.refs_7_
  62.6 0.5 collective-permute-done.17.refs_5_
  63.1 0.8 collective-permute-start.24
  64.0 7.9 %gather.1.refs_6_.refs_4_ = bf16[3584,1152]{1,0:T(8,128)(2,1)S(1)} custom-call(s32[2]{0:T(128)S(1)} %pad_add_fusion.index_ref, bf16[432,1152]{1,0:T(8,128)(2,1)S(1)} %bitcast.47, bf16[432,1152]{1,0:T(8,128)(2,1)S(1)} %collective-permute-done.3.refs_1_, bf16[112,1152]{1,0:T(8,128)(2,1)S(1)} %collective-permute-done.2.refs_2_, ...), custom_call_target="tpu_custom_call" | custom-call | tf_op jit(solution)/shard_map/gather/pallas_call | solution.py:334
  71.9 1.7 %collective-permute-done.21.refs_3_ = bf16[17,16,1152]{2,1,0:T(8,128)(2,1)S(1)} collective-permute-done((bf16[17,16,1152]{2,1,0:T(8,128)(2,1)S(1)}, bf16[17,16,1152]{2,1,0:T(8,128)(2,1)S(1)}, u32[]{:S(2)}, u32[]{:S(2)}) %collective-permute-start.21) | collective-permute-done | bytes 626720 | tf_op jit(solution)/shard_map/ppermute | solution.py:258
  73.6 1.3 %collective-permute-start.26 = (bf16[2,112,1152]{2,1,0:T(8,128)(2,1)S(1)}, bf16[2,112,1152]{2,1,0:T(8,128)(2,1)S(1)}, u32[]{:S(2)}, u32[]{:S(2)}) collective-permute-start(bf16[2,112,1152]{2,1,0:T(8,128)(2,1)S(1)} %pad_maximum_fusion.3.refs_9_.refs_7_), channel_id=1, source_target_pairs={{0,1},{1,0},{2,3},{3,2},{4,5},{5,4},{6,7},{7,6},{8,9},{9,8},{10,11... | collective-permute-start | bytes 1548296 | tf_op jit(solution)/shard_map/ppermute | solution.py:258
  74.9 0.0 collective-permute-start.25
  74.9 0.1 pad_maximum_fusion
  75.0 0.1 collective-permute-start.23
  75.1 1.7 %collective-permute-done.25.refs_8_.refs_6_ = bf16[112,1152]{1,0:T(8,128)(2,1)S(1)} collective-permute-done((bf16[112,1152]{1,0:T(8,128)(2,1)S(1)}, bf16[112,1152]{1,0:T(8,128)(2,1)S(1)}, u32[]{:S(2)}, u32[]{:S(2)}) %collective-permute-start.25) | collective-permute-done | bytes 258080 | tf_op jit(solution)/shard_map/ppermute | solution.py:258
  76.8 6.9 %shifted.1 = (bf16[4,4,16,640]{3,2,1,0:T(8,128)(2,1)S(1)}, bf16[4,4,16,640]{3,2,1,0:T(8,128)(2,1)S(1)}) custom-call(s32[2]{0:T(128)S(1)} %pad_add_fusion.index_ref, bf16[8,16,1152]{2,1,0:T(8,128)(2,1)S(1)} %bitcast.49, bf16[8,16,1152]{2,1,0:T(8,128)(2,1)S(1)} %bitcast.57, bf16[8,16,1152]{2,1,0:T(8,128)(2,1)S(1)} %bitcast.60, ...), custom_call_target="tpu_custom_call" | custom-call | flops 40000000000 | bytes 8388608 | tf_op jit(solution)/shard_map/shifted/pallas_call | solution.py:370
  83.7 0.9 collective-permute-start.27
  84.6 6.5 %windowed.1 = (bf16[4,4,16,640]{3,2,1,0:T(8,128)(2,1)S(1)}, bf16[4,4,16,640]{3,2,1,0:T(8,128)(2,1)S(1)}) custom-call(s32[2]{0:T(128)S(1)} %pad_add_fusion.index_ref, bf16[8,16,1152]{2,1,0:T(8,128)(2,1)S(1)} %bitcast.50, bf16[8,16,1152]{2,1,0:T(8,128)(2,1)S(1)} %bitcast.58, bf16[8,16,1152]{2,1,0:T(8,128)(2,1)S(1)} %bitcast.61, ...), custom_call_target="tpu_custom_call" | custom-call | flops 40000000000 | bytes 8388608 | tf_op jit(solution)/shard_map/windowed/pallas_call | solution.py:370
  91.1 0.6 merge.3
  91.7 0.7 collective-permute-start.30
  92.4 2.5 %collective-permute-start.31 = (bf16[4,16,1152]{2,1,0:T(8,128)(2,1)S(1)}, bf16[4,16,1152]{2,1,0:T(8,128)(2,1)S(1)}, u32[]{:S(2)}, u32[]{:S(2)}) collective-permute-start(bf16[4,16,1152]{2,1,0:T(8,128)(2,1)S(1)} %get-tuple-element.101), channel_id=1, source_target_pairs={{0,5},{1,4},{2,7},{3,6},{4,1},{5,0},{6,3},{7,2},{8,13},{9,12},{10,... | collective-permute-start | bytes 442376 | tf_op jit(solution)/shard_map/ppermute | solution.py:258
  95.0 0.6 merge.2
  95.6 0.2 collective-permute-start.29
  95.8 0.3 collective-permute-start.28
  96.1 1.0 collective-permute-start.32
  97.1 0.4 collective-permute-done.30
  97.5 7.0 %collective-permute-start.33 = (bf16[4,16,1152]{2,1,0:T(8,128)(2,1)S(1)}, bf16[4,16,1152]{2,1,0:T(8,128)(2,1)S(1)}, u32[]{:S(2)}, u32[]{:S(2)}) collective-permute-start(bf16[4,16,1152]{2,1,0:T(8,128)(2,1)S(1)} %get-tuple-element.99), channel_id=1, source_target_pairs={{0,7},{1,6},{2,5},{3,4},{4,3},{5,2},{6,1},{7,0},{8,15},{9,14},{10,... | collective-permute-start | bytes 442376 | tf_op jit(solution)/shard_map/ppermute | solution.py:258
  104.5 3.8 %collective-permute-start.5 = (bf16[144,1152]{1,0:T(8,128)(2,1)S(1)}, bf16[144,1152]{1,0:T(8,128)(2,1)S(1)}, u32[]{:S(2)}, u32[]{:S(2)}) collective-permute-start(bf16[144,1152]{1,0:T(8,128)(2,1)S(1)} %bitcast.41), channel_id=1, source_target_pairs={{0,1},{1,0},{2,3},{3,2},{4,5},{5,4},{6,7},{7,6},{8,9},{9,8},{10,11... | collective-permute-start | bytes 995336 | tf_op jit(solution)/shard_map/ppermute | solution.py:258
  108.4 6.7 %collective-permute-done.32 = bf16[4,16,1152]{2,1,0:T(8,128)(2,1)S(1)} collective-permute-done((bf16[4,16,1152]{2,1,0:T(8,128)(2,1)S(1)}, bf16[4,16,1152]{2,1,0:T(8,128)(2,1)S(1)}, u32[]{:S(2)}, u32[]{:S(2)}) %collective-permute-start.32) | collective-permute-done | bytes 147488 | tf_op jit(solution)/shard_map/ppermute | solution.py:258
  115.1 2.9 %collective-permute-start.22 = (bf16[144,1152]{1,0:T(8,128)(2,1)S(1)}, bf16[144,1152]{1,0:T(8,128)(2,1)S(1)}, u32[]{:S(2)}, u32[]{:S(2)}) collective-permute-start(bf16[144,1152]{1,0:T(8,128)(2,1)S(1)} %bitcast.44), channel_id=1, source_target_pairs={{0,1},{1,0},{2,3},{3,2},{4,5},{5,4},{6,7},{7,6},{8,9},{9,8},{10,11... | collective-permute-start | bytes 995336 | tf_op jit(solution)/shard_map/ppermute | solution.py:258
  118.0 1.2 collective-permute-done.33
  119.2 0.1 collective-permute-start.34
  119.3 0.5 collective-permute-start.35
  119.8 1.5 %gather_out.1.wall = bf16[1152,1152]{1,0:T(8,128)(2,1)S(1)} custom-call(s32[2]{0:T(128)S(1)} %pad_add_fusion.index_ref, bf16[144,1152]{1,0:T(8,128)(2,1)S(1)} %bitcast.42, bf16[144,1152]{1,0:T(8,128)(2,1)S(1)} %collective-permute-done.5.refs_1_, bf16[144,1152]{1,0:T(8,128)(2,1)S(1)} %bitcast.45, bf16[144,1152]{1,0:T(8,128)(2,1)S(1)} %collective-permute-done.22.refs_3_, ...), custom_call_target="tpu_custom_call" | custom-call | tf_op jit(solution)/shard_map/gather_out/pallas_call | solution.py:418
  121.4 3.6 %restore.1 = bf16[4,128,1152]{2,1,0:T(8,128)(2,1)} custom-call(s32[2]{0:T(128)S(1)} %pad_add_fusion.index_ref, bf16[4,128,1152]{2,1,0:T(8,128)(2,1)S(1)} %copy-done.1, f32[3,4,1152]{2,1,0:T(4,128)S(1)} %bitcast.52, bf16[1152,1152]{1,0:T(8,128)(2,1)S(1)} %gather_out.1.wall, bf16[2,4,16,1152]{3,2,1,0:T(8,128)(2,1)S(1)} %get-tuple-element.83.refs_0_, ...), custom_call_target="tpu_custom_call" | custom-call | tf_op jit(solution)/shard_map/restore/pallas_call | solution.py:433
  (44 shorter events, 0.4 us)
Async XLA Ops:
  0.1 1.3 %copy-start = (bf16[4,128,1152]{2,1,0:T(8,128)(2,1)S(1)}, bf16[4,128,1152]{2,1,0:T(8,128)(2,1)}, u32[]{:S(2)}) copy-start(bf16[4,128,1152]{2,1,0:T(8,128)(2,1)} %tokens_ref.3) | copy-start | bytes 3538948
  1.3 0.8 copy-start.4
  3.8 4.5 %collective-permute-start = (bf16[4,4,16,1152]{3,2,1,0:T(8,128)(2,1)S(1)}, bf16[4,4,16,1152]{3,2,1,0:T(8,128)(2,1)S(1)}, u32[]{:S(2)}, u32[]{:S(2)}) collective-permute-start(bf16[4,4,16,1152]{3,2,1,0:T(8,128)(2,1)S(1)} %get-tuple-element.48), channel_id=1, source_target_pairs={{0,1},{1,0},{2,3},{3,2},{4,5},{5,4},{6,7},{7,6},{8,9},{9,8},{10,11... | collective-permute-start | bytes 1769480 | tf_op jit(solution)/shard_map/ppermute | solution.py:258
  5.6 13.8 %collective-permute-start.2 = (bf16[112,1152]{1,0:T(8,128)(2,1)S(1)}, bf16[112,1152]{1,0:T(8,128)(2,1)S(1)}, u32[]{:S(2)}, u32[]{:S(2)}) collective-permute-start(bf16[112,1152]{1,0:T(8,128)(2,1)S(1)} %get-tuple-element.90), channel_id=1, source_target_pairs={{0,4},{1,5},{2,6},{3,7},{4,0},{5,1},{6,2},{7,3},{8,12},{9,13},{10,... | collective-permute-start | bytes 774152 | tf_op jit(solution)/shard_map/ppermute | solution.py:258
  8.0 13.2 %collective-permute-start.3 = (bf16[432,1152]{1,0:T(8,128)(2,1)}, bf16[432,1152]{1,0:T(8,128)(2,1)S(1)}, u32[]{:S(2)}, u32[]{:S(2)}) collective-permute-start(bf16[432,1152]{1,0:T(8,128)(2,1)} %bitcast.46), channel_id=1, source_target_pairs={{0,1},{1,0},{2,3},{3,2},{4,5},{5,4},{6,7},{7,6},{8,9},{9,8},{10,11... | collective-permute-start | bytes 2985992 | tf_op jit(solution)/shard_map/ppermute | solution.py:258
  8.3 36.5 %copy-start.2 = (bf16[1152,144]{0,1:T(8,128)(2,1)S(1)}, bf16[1152,144]{0,1:T(8,128)(2,1)}, u32[]{:S(2)}) copy-start(bf16[1152,144]{0,1:T(8,128)(2,1)} %param.7) | copy-start | bytes 995332
  8.4 11.1 %collective-permute-start.4 = (bf16[2,4,16,1152]{3,2,1,0:T(8,128)(2,1)S(1)}, bf16[2,4,16,1152]{3,2,1,0:T(8,128)(2,1)S(1)}, u32[]{:S(2)}, u32[]{:S(2)}) collective-permute-start(bf16[2,4,16,1152]{3,2,1,0:T(8,128)(2,1)S(1)} %pad_maximum_fusion.5), channel_id=1, source_target_pairs={{0,24},{1,25},{2,26},{3,27},{4,12},{5,13},{6,14},{7,15},{8,0},{9,1... | collective-permute-start | bytes 884744 | tf_op jit(solution)/shard_map/ppermute | solution.py:285
  10.7 10.5 %collective-permute-start.1 = (bf16[2,4,16,1152]{3,2,1,0:T(8,128)(2,1)S(1)}, bf16[2,4,16,1152]{3,2,1,0:T(8,128)(2,1)S(1)}, u32[]{:S(2)}, u32[]{:S(2)}) collective-permute-start(bf16[2,4,16,1152]{3,2,1,0:T(8,128)(2,1)S(1)} %pad_maximum_fusion.4), channel_id=1, source_target_pairs={{0,2},{1,3},{2,0},{3,1},{4,6},{5,7},{6,4},{7,5},{8,10},{9,11},{10,... | collective-permute-start | bytes 884744 | tf_op jit(solution)/shard_map/ppermute | solution.py:258
  19.4 44.5 %copy-start.3 = (bf16[1152,432]{0,1:T(8,128)(2,1)S(1)}, bf16[1152,432]{0,1:T(8,128)(2,1)}, u32[]{:S(2)}) copy-start(bf16[1152,432]{0,1:T(8,128)(2,1)} %param.6) | copy-start | bytes 2985988
  21.2 19.0 %collective-permute-start.8 = (bf16[2,112,1152]{2,1,0:T(8,128)(2,1)S(1)}, bf16[2,112,1152]{2,1,0:T(8,128)(2,1)S(1)}, u32[]{:S(2)}, u32[]{:S(2)}) collective-permute-start(bf16[2,112,1152]{2,1,0:T(8,128)(2,1)S(1)} %pad_maximum_fusion.2), channel_id=1, source_target_pairs={{0,2},{1,3},{2,0},{3,1},{4,6},{5,7},{6,4},{7,5},{8,10},{9,11},{10,... | collective-permute-start | bytes 1548296 | tf_op jit(solution)/shard_map/ppermute | solution.py:258
  23.4 12.4 %collective-permute-start.10 = (bf16[2,4,16,1152]{3,2,1,0:T(8,128)(2,1)S(1)}, bf16[2,4,16,1152]{3,2,1,0:T(8,128)(2,1)S(1)}, u32[]{:S(2)}, u32[]{:S(2)}) collective-permute-start(bf16[2,4,16,1152]{3,2,1,0:T(8,128)(2,1)S(1)} %collective-permute-done.1), channel_id=1, source_target_pairs={{0,24},{1,25},{2,26},{3,27},{4,12},{5,13},{6,14},{7,15},{8,0},{9,1... | collective-permute-start | bytes 884744 | tf_op jit(solution)/shard_map/ppermute | solution.py:285
  23.7 16.5 %collective-permute-start.9 = (bf16[2,4,16,1152]{3,2,1,0:T(8,128)(2,1)S(1)}, bf16[2,4,16,1152]{3,2,1,0:T(8,128)(2,1)S(1)}, u32[]{:S(2)}, u32[]{:S(2)}) collective-permute-start(bf16[2,4,16,1152]{3,2,1,0:T(8,128)(2,1)S(1)} %get-tuple-element.52), channel_id=1, source_target_pairs={{0,4},{1,5},{2,6},{3,7},{4,0},{5,1},{6,2},{7,3},{8,12},{9,13},{10,... | collective-permute-start | bytes 884744 | tf_op jit(solution)/shard_map/ppermute | solution.py:258
  24.5 11.3 %collective-permute-start.6 = (bf16[112,1152]{1,0:T(8,128)(2,1)S(1)}, bf16[112,1152]{1,0:T(8,128)(2,1)S(1)}, u32[]{:S(2)}, u32[]{:S(2)}) collective-permute-start(bf16[112,1152]{1,0:T(8,128)(2,1)S(1)} %collective-permute-done.2.refs_2_), channel_id=1, source_target_pairs={{0,8},{1,9},{2,10},{3,11},{4,12},{5,13},{6,14},{7,15},{8,0},{9,1},... | collective-permute-start | bytes 774152 | tf_op jit(solution)/shard_map/ppermute | solution.py:258
  25.7 10.1 %collective-permute-start.7 = (bf16[112,1152]{1,0:T(8,128)(2,1)S(1)}, bf16[112,1152]{1,0:T(8,128)(2,1)S(1)}, u32[]{:S(2)}, u32[]{:S(2)}) collective-permute-start(bf16[112,1152]{1,0:T(8,128)(2,1)S(1)} %collective-permute-done.2.refs_2_), channel_id=1, source_target_pairs={{0,16},{1,17},{2,18},{3,19},{4,20},{5,21},{6,22},{7,23},{8,24},{9,... | collective-permute-start | bytes 774152 | tf_op jit(solution)/shard_map/ppermute | solution.py:258
  40.2 11.1 %collective-permute-start.11 = (bf16[2,112,1152]{2,1,0:T(8,128)(2,1)S(1)}, bf16[2,112,1152]{2,1,0:T(8,128)(2,1)S(1)}, u32[]{:S(2)}, u32[]{:S(2)}) collective-permute-start(bf16[2,112,1152]{2,1,0:T(8,128)(2,1)S(1)} %collective-permute-done.8.refs_8_), channel_id=1, source_target_pairs={{0,8},{1,9},{2,10},{3,11},{4,12},{5,13},{6,14},{7,15},{8,0},{9,1},... | collective-permute-start | bytes 1548296 | tf_op jit(solution)/shard_map/ppermute | solution.py:258
  41.4 10.8 %collective-permute-start.12 = (bf16[2,112,1152]{2,1,0:T(8,128)(2,1)S(1)}, bf16[2,112,1152]{2,1,0:T(8,128)(2,1)S(1)}, u32[]{:S(2)}, u32[]{:S(2)}) collective-permute-start(bf16[2,112,1152]{2,1,0:T(8,128)(2,1)S(1)} %collective-permute-done.8.refs_8_), channel_id=1, source_target_pairs={{0,16},{1,17},{2,18},{3,19},{4,20},{5,21},{6,22},{7,23},{8,24},{9,... | collective-permute-start | bytes 1548296 | tf_op jit(solution)/shard_map/ppermute | solution.py:258
  42.5 9.7 %collective-permute-start.14 = (bf16[2,112,1152]{2,1,0:T(8,128)(2,1)S(1)}, bf16[2,112,1152]{2,1,0:T(8,128)(2,1)S(1)}, u32[]{:S(2)}, u32[]{:S(2)}) collective-permute-start(bf16[2,112,1152]{2,1,0:T(8,128)(2,1)S(1)} %collective-permute-done.8.refs_8_), channel_id=1, source_target_pairs={{0,1},{1,0},{2,3},{3,2},{4,5},{5,4},{6,7},{7,6},{8,9},{9,8},{10,11... | collective-permute-start | bytes 1548296 | tf_op jit(solution)/shard_map/ppermute | solution.py:258
  44.8 1.9 %collective-permute-start.13 = (bf16[112,1152]{1,0:T(8,128)(2,1)S(1)}, bf16[112,1152]{1,0:T(8,128)(2,1)S(1)}, u32[]{:S(2)}, u32[]{:S(2)}) collective-permute-start(bf16[112,1152]{1,0:T(8,128)(2,1)S(1)} %collective-permute-done.2.refs_2_), channel_id=1, source_target_pairs={{0,1},{1,0},{2,3},{3,2},{4,5},{5,4},{6,7},{7,6},{8,9},{9,8},{10,11... | collective-permute-start | bytes 774152 | tf_op jit(solution)/shard_map/ppermute | solution.py:258
  44.9 28.7 %collective-permute-start.21 = (bf16[17,16,1152]{2,1,0:T(8,128)(2,1)S(1)}, bf16[17,16,1152]{2,1,0:T(8,128)(2,1)S(1)}, u32[]{:S(2)}, u32[]{:S(2)}) collective-permute-start(bf16[17,16,1152]{2,1,0:T(8,128)(2,1)S(1)} %pad_maximum_fusion.1), channel_id=1, source_target_pairs={{0,6},{1,7},{2,4},{3,5},{4,2},{5,3},{6,0},{7,1},{8,14},{9,15},{10,... | collective-permute-start | bytes 1880072 | tf_op jit(solution)/shard_map/ppermute | solution.py:258
  52.2 5.6 %collective-permute-start.16 = (bf16[112,1152]{1,0:T(8,128)(2,1)S(1)}, bf16[112,1152]{1,0:T(8,128)(2,1)S(1)}, u32[]{:S(2)}, u32[]{:S(2)}) collective-permute-start(bf16[112,1152]{1,0:T(8,128)(2,1)S(1)} %slice_bitcast_fusion), channel_id=1, source_target_pairs={{0,8},{1,9},{2,10},{3,11},{4,12},{5,13},{6,14},{7,15},{8,0},{9,1},... | collective-permute-start | bytes 774152 | tf_op jit(solution)/shard_map/ppermute | solution.py:258
  52.6 9.4 %collective-permute-start.15 = (bf16[112,1152]{1,0:T(8,128)(2,1)S(1)}, bf16[112,1152]{1,0:T(8,128)(2,1)S(1)}, u32[]{:S(2)}, u32[]{:S(2)}) collective-permute-start(bf16[112,1152]{1,0:T(8,128)(2,1)S(1)} %slice_bitcast_fusion.1), channel_id=1, source_target_pairs={{0,16},{1,17},{2,18},{3,19},{4,20},{5,21},{6,22},{7,23},{8,24},{9,... | collective-permute-start | bytes 774152 | tf_op jit(solution)/shard_map/ppermute | solution.py:258
  54.1 9.8 %collective-permute-start.19 = (bf16[2,112,1152]{2,1,0:T(8,128)(2,1)S(1)}, bf16[2,112,1152]{2,1,0:T(8,128)(2,1)S(1)}, u32[]{:S(2)}, u32[]{:S(2)}) collective-permute-start(bf16[2,112,1152]{2,1,0:T(8,128)(2,1)S(1)} %collective-permute-done.11.refs_10_), channel_id=1, source_target_pairs={{0,1},{1,0},{2,3},{3,2},{4,5},{5,4},{6,7},{7,6},{8,9},{9,8},{10,11... | collective-permute-start | bytes 1548296 | tf_op jit(solution)/shard_map/ppermute | solution.py:258
  57.8 6.2 %collective-permute-start.20 = (bf16[2,112,1152]{2,1,0:T(8,128)(2,1)S(1)}, bf16[2,112,1152]{2,1,0:T(8,128)(2,1)S(1)}, u32[]{:S(2)}, u32[]{:S(2)}) collective-permute-start(bf16[2,112,1152]{2,1,0:T(8,128)(2,1)S(1)} %collective-permute-done.12.refs_12_), channel_id=1, source_target_pairs={{0,1},{1,0},{2,3},{3,2},{4,5},{5,4},{6,7},{7,6},{8,9},{9,8},{10,11... | collective-permute-start | bytes 1548296 | tf_op jit(solution)/shard_map/ppermute | solution.py:258
  57.8 5.3 %collective-permute-start.17 = (bf16[112,1152]{1,0:T(8,128)(2,1)S(1)}, bf16[112,1152]{1,0:T(8,128)(2,1)S(1)}, u32[]{:S(2)}, u32[]{:S(2)}) collective-permute-start(bf16[112,1152]{1,0:T(8,128)(2,1)S(1)} %collective-permute-done.6.refs_4_), channel_id=1, source_target_pairs={{0,1},{1,0},{2,3},{3,2},{4,5},{5,4},{6,7},{7,6},{8,9},{9,8},{10,11... | collective-permute-start | bytes 774152 | tf_op jit(solution)/shard_map/ppermute | solution.py:258
  62.0 2.0 %collective-permute-start.18 = (bf16[112,1152]{1,0:T(8,128)(2,1)S(1)}, bf16[112,1152]{1,0:T(8,128)(2,1)S(1)}, u32[]{:S(2)}, u32[]{:S(2)}) collective-permute-start(bf16[112,1152]{1,0:T(8,128)(2,1)S(1)} %collective-permute-done.7.refs_6_), channel_id=1, source_target_pairs={{0,1},{1,0},{2,3},{3,2},{4,5},{5,4},{6,7},{7,6},{8,9},{9,8},{10,11... | collective-permute-start | bytes 774152 | tf_op jit(solution)/shard_map/ppermute | solution.py:258
  63.1 11.8 %collective-permute-start.24 = (bf16[112,1152]{1,0:T(8,128)(2,1)S(1)}, bf16[112,1152]{1,0:T(8,128)(2,1)S(1)}, u32[]{:S(2)}, u32[]{:S(2)}) collective-permute-start(bf16[112,1152]{1,0:T(8,128)(2,1)S(1)} %collective-permute-done.7.refs_6_), channel_id=1, source_target_pairs={{0,8},{1,9},{2,10},{3,11},{4,12},{5,13},{6,14},{7,15},{8,0},{9,1},... | collective-permute-start | bytes 774152 | tf_op jit(solution)/shard_map/ppermute | solution.py:258
  73.6 3.2 %collective-permute-start.26 = (bf16[2,112,1152]{2,1,0:T(8,128)(2,1)S(1)}, bf16[2,112,1152]{2,1,0:T(8,128)(2,1)S(1)}, u32[]{:S(2)}, u32[]{:S(2)}) collective-permute-start(bf16[2,112,1152]{2,1,0:T(8,128)(2,1)S(1)} %pad_maximum_fusion.3.refs_9_.refs_7_), channel_id=1, source_target_pairs={{0,1},{1,0},{2,3},{3,2},{4,5},{5,4},{6,7},{7,6},{8,9},{9,8},{10,11... | collective-permute-start | bytes 1548296 | tf_op jit(solution)/shard_map/ppermute | solution.py:258
  74.9 1.9 %collective-permute-start.25 = (bf16[112,1152]{1,0:T(8,128)(2,1)S(1)}, bf16[112,1152]{1,0:T(8,128)(2,1)S(1)}, u32[]{:S(2)}, u32[]{:S(2)}) collective-permute-start(bf16[112,1152]{1,0:T(8,128)(2,1)S(1)} %collective-permute-done.24.refs_7_.refs_5_), channel_id=1, source_target_pairs={{0,1},{1,0},{2,3},{3,2},{4,5},{5,4},{6,7},{7,6},{8,9},{9,8},{10,11... | collective-permute-start | bytes 774152 | tf_op jit(solution)/shard_map/ppermute | solution.py:258
  75.0 19.9 %collective-permute-start.23 = (bf16[2,144,1152]{2,1,0:T(8,128)(2,1)S(1)}, bf16[2,144,1152]{2,1,0:T(8,128)(2,1)S(1)}, u32[]{:S(2)}, u32[]{:S(2)}) collective-permute-start(bf16[2,144,1152]{2,1,0:T(8,128)(2,1)S(1)} %pad_maximum_fusion), channel_id=1, source_target_pairs={{0,2},{1,3},{2,0},{3,1},{4,6},{5,7},{6,4},{7,5},{8,10},{9,11},{10,... | collective-permute-start | bytes 1990664 | tf_op jit(solution)/shard_map/ppermute | solution.py:258
  83.7 11.2 %collective-permute-start.27 = (bf16[4,4,16,640]{3,2,1,0:T(8,128)(2,1)S(1)}, bf16[4,4,16,640]{3,2,1,0:T(8,128)(2,1)S(1)}, u32[]{:S(2)}, u32[]{:S(2)}) collective-permute-start(bf16[4,4,16,640]{3,2,1,0:T(8,128)(2,1)S(1)} %get-tuple-element.73), channel_id=1, source_target_pairs={{0,8},{1,9},{2,10},{3,11},{4,28},{5,29},{6,30},{7,31},{8,16},{9,17... | collective-permute-start | bytes 983048 | tf_op jit(solution)/shard_map/ppermute | solution.py:285
  91.7 5.8 %collective-permute-start.30 = (bf16[4,16,1152]{2,1,0:T(8,128)(2,1)S(1)}, bf16[4,16,1152]{2,1,0:T(8,128)(2,1)S(1)}, u32[]{:S(2)}, u32[]{:S(2)}) collective-permute-start(bf16[4,16,1152]{2,1,0:T(8,128)(2,1)S(1)} %get-tuple-element.102), channel_id=1, source_target_pairs={{0,4},{1,5},{2,6},{3,7},{4,0},{5,1},{6,2},{7,3},{8,12},{9,13},{10,... | collective-permute-start | bytes 442376 | tf_op jit(solution)/shard_map/ppermute | solution.py:258
  92.4 12.1 %collective-permute-start.31 = (bf16[4,16,1152]{2,1,0:T(8,128)(2,1)S(1)}, bf16[4,16,1152]{2,1,0:T(8,128)(2,1)S(1)}, u32[]{:S(2)}, u32[]{:S(2)}) collective-permute-start(bf16[4,16,1152]{2,1,0:T(8,128)(2,1)S(1)} %get-tuple-element.101), channel_id=1, source_target_pairs={{0,5},{1,4},{2,7},{3,6},{4,1},{5,0},{6,3},{7,2},{8,13},{9,12},{10,... | collective-permute-start | bytes 442376 | tf_op jit(solution)/shard_map/ppermute | solution.py:258
  95.6 23.7 %collective-permute-start.29 = (bf16[2,4,16,1152]{3,2,1,0:T(8,128)(2,1)S(1)}, bf16[2,4,16,1152]{3,2,1,0:T(8,128)(2,1)S(1)}, u32[]{:S(2)}, u32[]{:S(2)}) collective-permute-start(bf16[2,4,16,1152]{3,2,1,0:T(8,128)(2,1)S(1)} %get-tuple-element.78), channel_id=1, source_target_pairs={{0,2},{1,3},{2,0},{3,1},{4,6},{5,7},{6,4},{7,5},{8,10},{9,11},{10,... | collective-permute-start | bytes 884744 | tf_op jit(solution)/shard_map/ppermute | solution.py:258
  95.8 24.0 %collective-permute-start.28 = (bf16[2,144,1152]{2,1,0:T(8,128)(2,1)S(1)}, bf16[2,144,1152]{2,1,0:T(8,128)(2,1)S(1)}, u32[]{:S(2)}, u32[]{:S(2)}) collective-permute-start(bf16[2,144,1152]{2,1,0:T(8,128)(2,1)S(1)} %collective-permute-done.23.refs_4_), channel_id=1, source_target_pairs={{0,1},{1,0},{2,3},{3,2},{4,5},{5,4},{6,7},{7,6},{8,9},{9,8},{10,11... | collective-permute-start | bytes 1990664 | tf_op jit(solution)/shard_map/ppermute | solution.py:258
  96.1 19.0 %collective-permute-start.32 = (bf16[4,16,1152]{2,1,0:T(8,128)(2,1)S(1)}, bf16[4,16,1152]{2,1,0:T(8,128)(2,1)S(1)}, u32[]{:S(2)}, u32[]{:S(2)}) collective-permute-start(bf16[4,16,1152]{2,1,0:T(8,128)(2,1)S(1)} %get-tuple-element.100), channel_id=1, source_target_pairs={{0,6},{1,7},{2,4},{3,5},{4,2},{5,3},{6,0},{7,1},{8,14},{9,15},{10,... | collective-permute-start | bytes 442376 | tf_op jit(solution)/shard_map/ppermute | solution.py:258
  97.5 21.7 %collective-permute-start.33 = (bf16[4,16,1152]{2,1,0:T(8,128)(2,1)S(1)}, bf16[4,16,1152]{2,1,0:T(8,128)(2,1)S(1)}, u32[]{:S(2)}, u32[]{:S(2)}) collective-permute-start(bf16[4,16,1152]{2,1,0:T(8,128)(2,1)S(1)} %get-tuple-element.99), channel_id=1, source_target_pairs={{0,7},{1,6},{2,5},{3,4},{4,3},{5,2},{6,1},{7,0},{8,15},{9,14},{10,... | collective-permute-start | bytes 442376 | tf_op jit(solution)/shard_map/ppermute | solution.py:258
  104.5 15.3 %collective-permute-start.5 = (bf16[144,1152]{1,0:T(8,128)(2,1)S(1)}, bf16[144,1152]{1,0:T(8,128)(2,1)S(1)}, u32[]{:S(2)}, u32[]{:S(2)}) collective-permute-start(bf16[144,1152]{1,0:T(8,128)(2,1)S(1)} %bitcast.41), channel_id=1, source_target_pairs={{0,1},{1,0},{2,3},{3,2},{4,5},{5,4},{6,7},{7,6},{8,9},{9,8},{10,11... | collective-permute-start | bytes 995336 | tf_op jit(solution)/shard_map/ppermute | solution.py:258
  115.1 4.7 %collective-permute-start.22 = (bf16[144,1152]{1,0:T(8,128)(2,1)S(1)}, bf16[144,1152]{1,0:T(8,128)(2,1)S(1)}, u32[]{:S(2)}, u32[]{:S(2)}) collective-permute-start(bf16[144,1152]{1,0:T(8,128)(2,1)S(1)} %bitcast.44), channel_id=1, source_target_pairs={{0,1},{1,0},{2,3},{3,2},{4,5},{5,4},{6,7},{7,6},{8,9},{9,8},{10,11... | collective-permute-start | bytes 995336 | tf_op jit(solution)/shard_map/ppermute | solution.py:258
  119.2 2.1 %copy-start.1 = (bf16[4,128,1152]{2,1,0:T(8,128)(2,1)S(1)}, bf16[4,128,1152]{2,1,0:T(8,128)(2,1)}, u32[]{:S(2)}) copy-start(bf16[4,128,1152]{2,1,0:T(8,128)(2,1)} %tokens_ref.3) | copy-start | bytes 3538948
  119.2 2.1 %copy-start.5 = (f32[4,3,1152]{2,0,1:T(4,128)S(1)}, f32[4,3,1152]{2,0,1:T(4,128)}, u32[]{:S(2)}) copy-start(f32[4,3,1152]{2,0,1:T(4,128)} %param.5) | copy-start | bytes 165892
  119.2 2.1 %collective-permute-start.34 = (bf16[2,4,16,1152]{3,2,1,0:T(8,128)(2,1)S(1)}, bf16[2,4,16,1152]{3,2,1,0:T(8,128)(2,1)S(1)}, u32[]{:S(2)}, u32[]{:S(2)}) collective-permute-start(bf16[2,4,16,1152]{3,2,1,0:T(8,128)(2,1)S(1)} %get-tuple-element.83.refs_0_), channel_id=1, source_target_pairs={{0,1},{1,0},{2,3},{3,2},{4,5},{5,4},{6,7},{7,6},{8,9},{9,8},{10,11... | collective-permute-start | bytes 884744 | tf_op jit(solution)/shard_map/ppermute | solution.py:258
  119.3 2.0 %collective-permute-start.35 = (bf16[2,4,16,1152]{3,2,1,0:T(8,128)(2,1)S(1)}, bf16[2,4,16,1152]{3,2,1,0:T(8,128)(2,1)S(1)}, u32[]{:S(2)}, u32[]{:S(2)}) collective-permute-start(bf16[2,4,16,1152]{3,2,1,0:T(8,128)(2,1)S(1)} %collective-permute-done.29.refs_2_), channel_id=1, source_target_pairs={{0,1},{1,0},{2,3},{3,2},{4,5},{5,4},{6,7},{7,6},{8,9},{9,8},{10,11... | collective-permute-start | bytes 884744 | tf_op jit(solution)/shard_map/ppermute | solution.py:258

commit v10 on v9

--- a/solution.py
+++ b/solution.py
@@ -66,46 +66,52 @@
     return exponent * (1.0 / total)
 
 
-def piece_moves(plan, index, slab, entries, w_refs, wall, first_row, rows):
+def piece_moves(plan, index, slab, entries, w_refs, wall, first_row, sems):
     moves = []
-    for operand, at, size, owner, part in entries:
+    for n, (operand, at, size, owner, part) in enumerate(entries):
         source = w_refs[operand]
         for step in at:
             source = source.at[step]
         base = lax.bitwise_xor(index, owner) * plan["columns"] - first_row
         if part is None:
-            moves.append((source, wall.at[pl.ds(pl.multiple_of(base, ROWS), size)]))
+            moves.append((None, pltpu.make_async_copy(source, wall.at[pl.ds(pl.multiple_of(base, ROWS), size)], sems.at[n])))
             continue
-        piece, over, spare = lax.bitwise_xor(slab, part[0]), plan["over"], part[1]
+        piece, over = lax.bitwise_xor(slab, part), plan["over"]
+        row = pl.multiple_of(base + piece * size, ROWS)
+        whole = pltpu.make_async_copy(source, wall.at[pl.ds(row, size)], sems.at[n])
+        if not over:
+            moves.append((None, whole))
+            continue
         ends = piece == plan["pieces"] - 1
-        row = base + piece * size
-        skip = jnp.where(ends, over, 0)
-        moves.append((source.at[pl.ds(pl.multiple_of(skip, ROWS), size - over)],
-                      wall.at[pl.ds(pl.multiple_of(row, ROWS), size - over)]))
-        if over:
-            row = jnp.where(ends, rows + spare * over, row + size - over)
-            moves.append((source.at[pl.ds(size - over, over)], wall.at[pl.ds(pl.multiple_of(row, ROWS), over)]))
+        rest = pltpu.make_async_copy(source.at[pl.ds(over, size - over)], wall.at[pl.ds(row, size - over)], sems.at[n])
+        moves += [(jnp.logical_not(ends), whole), (ends, rest)]
     return moves
+
+
+def on_moves(moves, act):
+    for condition, copy in moves:
+        if condition is None:
+            act(copy)
+        else:
+            pl.when(condition)(functools.partial(act, copy))
 
 
 def gather_kernel(plan, index_ref, *refs):
     w_refs, wall, sems = refs[:-2], refs[-2], refs[-1]
-    moves = piece_moves(plan, index_ref[0], index_ref[1], plan["moves"], w_refs, wall, 0, 6 * plan["half"])
-    moves = [pltpu.make_async_copy(a, b, sems.at[n]) for n, (a, b) in enumerate(moves)]
-    for move in moves:
-        move.start()
-    for move in moves:
-        move.wait()
+    moves = piece_moves(plan, index_ref[0], index_ref[1], plan["moves"], w_refs, wall, 0, sems)
+    on_moves(moves, lambda copy: copy.start())
+    on_moves(moves, lambda copy: copy.wait())
 
 
 def block_kernel(plan, frames, index_ref, *refs):
     kind, weights, half = plan["kind"], plan["weights"], plan["half"]
     refs = list(refs)
     x_refs = [refs.pop(0) for _ in range(plan["inputs"])]
-    full_ref = refs.pop(0)
+    refs.pop(0)
     w_refs = [refs.pop(0) for _ in range(weights)]
     out_refs = [refs.pop(0) for _ in range(2)]
-    xs, wall, qt, kn, vt, sems, full_sem, wsems = refs
+    wall = refs.pop(0)
+    xs, qt, kn, vt, sems, wsems = refs
     groups, count, rows, width = xs.shape
     lanes = qt.shape[0]
     heads_half = H // 2
@@ -114,9 +120,6 @@
     slot = count * rows
     index, slab = index_ref[0], index_ref[1]
     upper = index >= count // 2
-    full = pltpu.make_async_copy(full_ref.at[pl.ds(3 * kind * half, 3 * half)], wall.at[pl.ds(0, 3 * half)], full_sem.at[0])
-    full.start()
-
     sources = []
     for d in range(count):
         owner = lax.bitwise_xor(index, d)
@@ -125,18 +128,13 @@
         sources.append(pltpu.make_async_copy(source, xs.at[:, owner], sems.at[d]))
     for copy in sources:
         copy.start()
-    full.wait()
     choices = []
     for chosen, entries in plan["moves"]:
-        moves = piece_moves(plan, index, slab, entries, w_refs, wall, 3 * kind * half, 3 * half)
-        choices.append((chosen, [pltpu.make_async_copy(a, b, wsems.at[n]) for n, (a, b) in enumerate(moves)]))
+        choices.append((chosen, piece_moves(plan, index, slab, entries, w_refs, wall, 0, wsems)))
 
     def on_choice(act):
         for chosen, moves in choices:
-            @pl.when(upper == chosen)
-            def _():
-                for copy in moves:
-                    act(copy)
+            pl.when(upper == chosen)(functools.partial(on_moves, moves, act))
 
     on_choice(lambda copy: copy.start())
     gap = lanes - half
@@ -149,7 +147,7 @@
 
     tokens = groups * slot
     own = xs[...].reshape(tokens, width)
-    parts = [wall[n * half : (n + 1) * half, :] for n in range(3)]
+    parts = [wall[(3 * kind + n) * half : (3 * kind + n + 1) * half, :] for n in range(3)]
     qt[:half, :] = nt_dot(parts[0], own).astype(qt.dtype)
     kn[:, :half] = nt_dot(own, parts[1]).astype(kn.dtype)
     vt[...] = nt_dot(parts[2], own).astype(vt.dtype)
@@ -297,7 +295,6 @@
             for sibling in range(2):
                 operands.append(other if sibling else value)
                 for at, length, z, part in entries:
-                    part = part if part is None else (part, 2 * z + sibling)
                     moves.append((len(operands) - 1, at, length, (2 * z) ^ sibling, part))
 
         x, y = 1, 2
@@ -329,14 +326,14 @@
             with_sibling(value, [((), size, 2, e)], swaps[e])
         for e, value in enumerate((rest, bx, by)):
             with_sibling(value, [((n,), size, z, e) for n, z in enumerate((1, 3))], swaps[4 + e])
-        full_rows = 6 * half + count * over
+        full_rows = 6 * half
         plan = dict(half=half, columns=columns, over=over, pieces=slabs, moves=moves)
         full = pl.pallas_call(
             functools.partial(gather_kernel, plan),
             out_shape=jax.ShapeDtypeStruct((full_rows, width), jnp.bfloat16),
             in_specs=[smem] + [anywhere] * len(operands),
             out_specs=anywhere,
-            scratch_shapes=[pltpu.SemaphoreType.DMA((2 * len(moves),))],
+            scratch_shapes=[pltpu.SemaphoreType.DMA((len(moves),))],
             compiler_params=params,
             cost_estimate=pl.CostEstimate(flops=0, bytes_accessed=0, transcendentals=0),
             name="gather",
@@ -362,24 +359,24 @@
 
     tokens = count * block_rows
 
-    def attention(kind, inputs):
+    def attention(kind, inputs, full):
         inputs = [value.reshape((-1,) + block.shape[1:]) for value in inputs]
         plan = dict(kind=kind, weights=len(operands), inputs=len(inputs), half=half, moves=by_kind[kind],
                     columns=columns, over=over, pieces=slabs)
-        copies = max([1] + [2 * len(entries) for _, entries in by_kind[kind]])
+        copies = max([1] + [len(entries) for _, entries in by_kind[kind]])
         return pl.pallas_call(
             functools.partial(block_kernel, plan, frames),
-            out_shape=[jax.ShapeDtypeStruct((groups, middle, ROWS, lanes), jnp.bfloat16)] * 2,
-            in_specs=[smem] + [anywhere] * (len(inputs) + 1 + len(operands)),
-            out_specs=[vmem] * 2,
+            out_shape=[jax.ShapeDtypeStruct((groups, middle, ROWS, lanes), jnp.bfloat16)] * 2
+            + [jax.ShapeDtypeStruct(full.shape, full.dtype)],
+            in_specs=[smem] + [anywhere] * len(inputs) + [vmem] + [anywhere] * len(operands),
+            out_specs=[vmem] * 3,
+            input_output_aliases={1 + len(inputs): 2},
             scratch_shapes=[
                 pltpu.VMEM((groups, count, ROWS, width), jnp.bfloat16),
-                pltpu.VMEM((3 * half + count * over, width), jnp.bfloat16),
                 pltpu.VMEM((lanes, tokens), jnp.bfloat16),
                 pltpu.VMEM((tokens, lanes), jnp.bfloat16),
                 pltpu.VMEM((half, tokens), jnp.bfloat16),
                 pltpu.SemaphoreType.DMA((count,)),
-                pltpu.SemaphoreType.DMA((1,)),
                 pltpu.SemaphoreType.DMA((copies,)),
             ],
             compiler_params=params,
@@ -388,11 +385,11 @@
             name=("windowed", "shifted")[kind],
         )(own_index, *inputs, full, *operands)
 
-    second_near, second_far = attention(1, blocks + following)
+    second_near, second_far, full = attention(1, blocks + following, full)
     if shared:
         out_rest = hop(jnp.stack([narrow, out_far]), 2)
     second_near = to_neighbour(second_near, 1)
-    first_near, first_far = attention(0, blocks)
+    first_near, first_far, full = attention(0, blocks, full)
     def merged(first_z, first, second, flops):
         return pl.pallas_call(
             functools.partial(merge_kernel, first_z),

time: 125 us -> 124 us (level)
  no operation moved by 1% of the time
where the time goes in v10:
time: 124 us
  starting transfers between devices  48.8 us (39%)
  waiting for transfers between devices  42.3 us (34%)
  Pallas kernels  28.9 us (23%)
  local copies, waits for them, and re-layouts  3.33 us (3%)
    ppermute x33, starting transfers between devices, hop(): return lax.ppermute(value, ('slab', 'seq'), pairs)  45.2 us
    ppermute x33, waiting for transfers between devices, hop(): return lax.ppermute(value, ('slab', 'seq'), pairs)  42.3 us
    pallas_call x2, Pallas kernels, attention(): pl.pallas_call(functools.partial(block_kernel, plan, frames), out_shape=[...  12.3 us
    pallas_call x1, Pallas kernels, per_device(): pl.pallas_call(functools.partial(gather_kernel, plan), out_shape=jax.Shap...  8.55 us
    pallas_call x1, Pallas kernels, per_device(): pl.pallas_call(functools.partial(restore_kernel, count), out_shape=jax.Sh...  3.65 us
    ppermute x3, starting transfers between devices, to_neighbour(): return lax.ppermute(value, ('slab', 'seq'), pairs)  3.57 us
  transfers between devices with their start and end apart: 36, of which 13 were waited for; matrix products, arithmetic and copies ran while one was open for 1% of the time, Pallas kernels for 19%

profile of v10, /device:TPU:9, one launch (start us, length us, event | category | flops | bytes accessed | tf_op | source)
XLA Modules:
  0.0 124.0 jit_solution(5137600170578227895)
XLA Ops:
  0.0 0.1 pad_add_fusion.index_ref
  0.1 1.3 %copy-done = bf16[4,128,1152]{2,1,0:T(8,128)(2,1)S(1)} copy-done((bf16[4,128,1152]{2,1,0:T(8,128)(2,1)S(1)}, bf16[4,128,1152]{2,1,0:T(8,128)(2,1)}, u32[]{:S(2)}) %copy-start) | copy-done | bytes 1179672
  1.3 0.8 copy-done.4
  2.2 1.7 %norm.1 = (bf16[4,4,16,1152]{3,2,1,0:T(8,128)(2,1)S(1)}, bf16[4,4,16,1152]{3,2,1,0:T(8,128)(2,1)S(1)}) custom-call(s32[2]{0:T(128)S(1)} %pad_add_fusion.index_ref, bf16[4,128,1152]{2,1,0:T(8,128)(2,1)S(1)} %copy-done, f32[3,4,1152]{2,1,0:T(4,128)S(1)} %bitcast.51), custom_call_target="tpu_custom_call" | custom-call | tf_op jit(solution)/shard_map/norm/pallas_call | solution.py:268
  3.8 0.7 collective-permute-start
  4.6 1.0 dynamic-slice_bitcast_fusion
  5.6 2.4 %collective-permute-start.2 = (bf16[112,1152]{1,0:T(8,128)(2,1)S(1)}, bf16[112,1152]{1,0:T(8,128)(2,1)S(1)}, u32[]{:S(2)}, u32[]{:S(2)}) collective-permute-start(bf16[112,1152]{1,0:T(8,128)(2,1)S(1)} %get-tuple-element.92), channel_id=1, source_target_pairs={{0,4},{1,5},{2,6},{3,7},{4,0},{5,1},{6,2},{7,3},{8,12},{9,13},{10,... | collective-permute-start | bytes 774152 | tf_op jit(solution)/shard_map/ppermute | solution.py:256
  8.0 0.3 collective-permute-start.3
  8.4 2.2 %collective-permute-start.4 = (bf16[2,4,16,1152]{3,2,1,0:T(8,128)(2,1)S(1)}, bf16[2,4,16,1152]{3,2,1,0:T(8,128)(2,1)S(1)}, u32[]{:S(2)}, u32[]{:S(2)}) collective-permute-start(bf16[2,4,16,1152]{3,2,1,0:T(8,128)(2,1)S(1)} %pad_maximum_fusion.5), channel_id=1, source_target_pairs={{0,24},{1,25},{2,26},{3,27},{4,12},{5,13},{6,14},{7,15},{8,0},{9,1... | collective-permute-start | bytes 884744 | tf_op jit(solution)/shard_map/ppermute | solution.py:283
  10.7 0.2 collective-permute-start.1
  10.9 8.5 %collective-permute-done.2.refs_2_ = bf16[112,1152]{1,0:T(8,128)(2,1)S(1)} collective-permute-done((bf16[112,1152]{1,0:T(8,128)(2,1)S(1)}, bf16[112,1152]{1,0:T(8,128)(2,1)S(1)}, u32[]{:S(2)}, u32[]{:S(2)}) %collective-permute-start.2) | collective-permute-done | bytes 258080 | tf_op jit(solution)/shard_map/ppermute | solution.py:256
  19.4 0.1 pad_maximum_fusion.2
  19.5 0.1 pad_maximum_fusion.6
  19.6 1.6 %collective-permute-done.1 = bf16[2,4,16,1152]{3,2,1,0:T(8,128)(2,1)S(1)} collective-permute-done((bf16[2,4,16,1152]{3,2,1,0:T(8,128)(2,1)S(1)}, bf16[2,4,16,1152]{3,2,1,0:T(8,128)(2,1)S(1)}, u32[]{:S(2)}, u32[]{:S(2)}) %collective-permute-start.1) | collective-permute-done | bytes 294944 | tf_op jit(solution)/shard_map/ppermute | solution.py:256
  21.2 2.2 %collective-permute-start.8 = (bf16[2,112,1152]{2,1,0:T(8,128)(2,1)S(1)}, bf16[2,112,1152]{2,1,0:T(8,128)(2,1)S(1)}, u32[]{:S(2)}, u32[]{:S(2)}) collective-permute-start(bf16[2,112,1152]{2,1,0:T(8,128)(2,1)S(1)} %pad_maximum_fusion.2), channel_id=1, source_target_pairs={{0,2},{1,3},{2,0},{3,1},{4,6},{5,7},{6,4},{7,5},{8,10},{9,11},{10,... | collective-permute-start | bytes 1548296 | tf_op jit(solution)/shard_map/ppermute | solution.py:256
  23.4 0.3 collective-permute-start.10
  23.7 0.8 collective-permute-start.9
  24.5 1.2 collective-permute-start.6
  25.7 0.2 collective-permute-start.7
  26.0 9.9 %collective-permute-done.6.refs_4_ = bf16[112,1152]{1,0:T(8,128)(2,1)S(1)} collective-permute-done((bf16[112,1152]{1,0:T(8,128)(2,1)S(1)}, bf16[112,1152]{1,0:T(8,128)(2,1)S(1)}, u32[]{:S(2)}, u32[]{:S(2)}) %collective-permute-start.6) | collective-permute-done | bytes 258080 | tf_op jit(solution)/shard_map/ppermute | solution.py:256
  35.8 4.3 %collective-permute-done.9 = bf16[2,4,16,1152]{3,2,1,0:T(8,128)(2,1)S(1)} collective-permute-done((bf16[2,4,16,1152]{3,2,1,0:T(8,128)(2,1)S(1)}, bf16[2,4,16,1152]{3,2,1,0:T(8,128)(2,1)S(1)}, u32[]{:S(2)}, u32[]{:S(2)}) %collective-permute-start.9) | collective-permute-done | bytes 294944 | tf_op jit(solution)/shard_map/ppermute | solution.py:256
  40.2 1.2 collective-permute-start.11
  41.4 1.1 collective-permute-start.12
  42.5 2.3 %collective-permute-start.14 = (bf16[2,112,1152]{2,1,0:T(8,128)(2,1)S(1)}, bf16[2,112,1152]{2,1,0:T(8,128)(2,1)S(1)}, u32[]{:S(2)}, u32[]{:S(2)}) collective-permute-start(bf16[2,112,1152]{2,1,0:T(8,128)(2,1)S(1)} %collective-permute-done.8.refs_8_), channel_id=1, source_target_pairs={{0,1},{1,0},{2,3},{3,2},{4,5},{5,4},{6,7},{7,6},{8,9},{9,8},{10,11... | collective-permute-start | bytes 1548296 | tf_op jit(solution)/shard_map/ppermute | solution.py:256
  44.8 0.1 pad_maximum_fusion.1
  44.9 0.8 collective-permute-start.21
  45.7 1.0 collective-permute-done.13.refs_3_
  46.7 4.6 %collective-permute-done.11.refs_10_ = bf16[2,112,1152]{2,1,0:T(8,128)(2,1)S(1)} collective-permute-done((bf16[2,112,1152]{2,1,0:T(8,128)(2,1)S(1)}, bf16[2,112,1152]{2,1,0:T(8,128)(2,1)S(1)}, u32[]{:S(2)}, u32[]{:S(2)}) %collective-permute-start.11) | collective-permute-done | bytes 516128 | tf_op jit(solution)/shard_map/ppermute | solution.py:256
  51.2 0.9 collective-permute-done.12.refs_12_
  52.2 0.3 collective-permute-start.16
  52.6 1.5 %collective-permute-start.15 = (bf16[112,1152]{1,0:T(8,128)(2,1)S(1)}, bf16[112,1152]{1,0:T(8,128)(2,1)S(1)}, u32[]{:S(2)}, u32[]{:S(2)}) collective-permute-start(bf16[112,1152]{1,0:T(8,128)(2,1)S(1)} %slice_bitcast_fusion.1), channel_id=1, source_target_pairs={{0,16},{1,17},{2,18},{3,19},{4,20},{5,21},{6,22},{7,23},{8,24},{9,... | collective-permute-start | bytes 774152 | tf_op jit(solution)/shard_map/ppermute | solution.py:256
  54.1 3.7 %collective-permute-start.19 = (bf16[2,112,1152]{2,1,0:T(8,128)(2,1)S(1)}, bf16[2,112,1152]{2,1,0:T(8,128)(2,1)S(1)}, u32[]{:S(2)}, u32[]{:S(2)}) collective-permute-start(bf16[2,112,1152]{2,1,0:T(8,128)(2,1)S(1)} %collective-permute-done.11.refs_10_), channel_id=1, source_target_pairs={{0,1},{1,0},{2,3},{3,2},{4,5},{5,4},{6,7},{7,6},{8,9},{9,8},{10,11... | collective-permute-start | bytes 1548296 | tf_op jit(solution)/shard_map/ppermute | solution.py:256
  57.8 4.2 %collective-permute-start.17 = (bf16[112,1152]{1,0:T(8,128)(2,1)S(1)}, bf16[112,1152]{1,0:T(8,128)(2,1)S(1)}, u32[]{:S(2)}, u32[]{:S(2)}) collective-permute-start(bf16[112,1152]{1,0:T(8,128)(2,1)S(1)} %collective-permute-done.6.refs_4_), channel_id=1, source_target_pairs={{0,1},{1,0},{2,3},{3,2},{4,5},{5,4},{6,7},{7,6},{8,9},{9,8},{10,11... | collective-permute-start | bytes 774152 | tf_op jit(solution)/shard_map/ppermute | solution.py:256
  62.0 0.6 collective-permute-start.18
  62.6 0.1 pad_maximum_fusion.3.refs_9_.refs_7_
  62.7 0.5 collective-permute-done.17.refs_5_
  63.1 0.8 collective-permute-start.24
  64.0 8.6 %gather.1.refs_6_ = bf16[3456,1152]{1,0:T(8,128)(2,1)S(1)} custom-call(s32[2]{0:T(128)S(1)} %pad_add_fusion.index_ref, bf16[432,1152]{1,0:T(8,128)(2,1)S(1)} %bitcast.47, bf16[432,1152]{1,0:T(8,128)(2,1)S(1)} %collective-permute-done.3.refs_1_, bf16[112,1152]{1,0:T(8,128)(2,1)S(1)} %collective-permute-done.2.refs_2_, ...), custom_call_target="tpu_custom_call" | custom-call | tf_op jit(solution)/shard_map/gather/pallas_call | solution.py:331
  72.5 1.0 collective-permute-done.21.refs_3_
  73.6 1.3 %collective-permute-start.26 = (bf16[2,112,1152]{2,1,0:T(8,128)(2,1)S(1)}, bf16[2,112,1152]{2,1,0:T(8,128)(2,1)S(1)}, u32[]{:S(2)}, u32[]{:S(2)}) collective-permute-start(bf16[2,112,1152]{2,1,0:T(8,128)(2,1)S(1)} %pad_maximum_fusion.3.refs_9_.refs_7_), channel_id=1, source_target_pairs={{0,1},{1,0},{2,3},{3,2},{4,5},{5,4},{6,7},{7,6},{8,9},{9,8},{10,11... | collective-permute-start | bytes 1548296 | tf_op jit(solution)/shard_map/ppermute | solution.py:256
  74.9 0.0 collective-permute-start.25
  74.9 0.1 pad_maximum_fusion
  75.0 0.1 collective-permute-start.23
  75.1 1.7 %collective-permute-done.25.refs_8_.refs_6_ = bf16[112,1152]{1,0:T(8,128)(2,1)S(1)} collective-permute-done((bf16[112,1152]{1,0:T(8,128)(2,1)S(1)}, bf16[112,1152]{1,0:T(8,128)(2,1)S(1)}, u32[]{:S(2)}, u32[]{:S(2)}) %collective-permute-start.25) | collective-permute-done | bytes 258080 | tf_op jit(solution)/shard_map/ppermute | solution.py:256
  76.8 6.3 %shifted.1 = (bf16[4,4,16,640]{3,2,1,0:T(8,128)(2,1)S(1)}, bf16[4,4,16,640]{3,2,1,0:T(8,128)(2,1)S(1)}, bf16[3456,1152]{1,0:T(8,128)(2,1)S(1)}) custom-call(s32[2]{0:T(128)S(1)} %pad_add_fusion.index_ref, bf16[8,16,1152]{2,1,0:T(8,128)(2,1)S(1)} %bitcast.49, bf16[8,16,1152]{2,1,0:T(8,128)(2,1)S(1)} %bitcast.57, ...), custom_call_target="tpu_custom_call", output_to_operand_aliasing={{2}: (7, {})} | custom-call | flops 40000000000 | bytes 8388608 | tf_op jit(solution)/shard_map/shifted/pallas_call | solution.py:367
  83.1 1.0 collective-permute-start.27
  84.2 6.0 %windowed.1 = (bf16[4,4,16,640]{3,2,1,0:T(8,128)(2,1)S(1)}, bf16[4,4,16,640]{3,2,1,0:T(8,128)(2,1)S(1)}, bf16[3456,1152]{1,0:T(8,128)(2,1)S(1)}) custom-call(s32[2]{0:T(128)S(1)} %pad_add_fusion.index_ref, bf16[8,16,1152]{2,1,0:T(8,128)(2,1)S(1)} %bitcast.50, bf16[8,16,1152]{2,1,0:T(8,128)(2,1)S(1)} %bitcast.58, ...), custom_call_target="tpu_custom_call", output_to_operand_aliasing={{2}: (5, {})} | custom-call | flops 40000000000 | bytes 8388608 | tf_op jit(solution)/shard_map/windowed/pallas_call | solution.py:367
  90.2 0.0 copy-start.1
  90.2 0.6 merge.3
  90.9 0.7 collective-permute-start.30
  91.5 2.6 %collective-permute-start.31 = (bf16[4,16,1152]{2,1,0:T(8,128)(2,1)S(1)}, bf16[4,16,1152]{2,1,0:T(8,128)(2,1)S(1)}, u32[]{:S(2)}, u32[]{:S(2)}) collective-permute-start(bf16[4,16,1152]{2,1,0:T(8,128)(2,1)S(1)} %get-tuple-element.103), channel_id=1, source_target_pairs={{0,5},{1,4},{2,7},{3,6},{4,1},{5,0},{6,3},{7,2},{8,13},{9,12},{10,... | collective-permute-start | bytes 442376 | tf_op jit(solution)/shard_map/ppermute | solution.py:256
  94.1 0.6 merge.2
  94.7 0.2 collective-permute-start.29
  95.0 0.2 collective-permute-start.28
  95.2 1.0 collective-permute-start.32
  96.2 0.5 collective-permute-done.30
  96.7 7.0 %collective-permute-start.33 = (bf16[4,16,1152]{2,1,0:T(8,128)(2,1)S(1)}, bf16[4,16,1152]{2,1,0:T(8,128)(2,1)S(1)}, u32[]{:S(2)}, u32[]{:S(2)}) collective-permute-start(bf16[4,16,1152]{2,1,0:T(8,128)(2,1)S(1)} %get-tuple-element.101), channel_id=1, source_target_pairs={{0,7},{1,6},{2,5},{3,4},{4,3},{5,2},{6,1},{7,0},{8,15},{9,14},{10,... | collective-permute-start | bytes 442376 | tf_op jit(solution)/shard_map/ppermute | solution.py:256
  103.7 3.7 %collective-permute-start.5 = (bf16[144,1152]{1,0:T(8,128)(2,1)S(1)}, bf16[144,1152]{1,0:T(8,128)(2,1)S(1)}, u32[]{:S(2)}, u32[]{:S(2)}) collective-permute-start(bf16[144,1152]{1,0:T(8,128)(2,1)S(1)} %bitcast.41), channel_id=1, source_target_pairs={{0,1},{1,0},{2,3},{3,2},{4,5},{5,4},{6,7},{7,6},{8,9},{9,8},{10,11... | collective-permute-start | bytes 995336 | tf_op jit(solution)/shard_map/ppermute | solution.py:256
  107.4 6.6 %collective-permute-done.32 = bf16[4,16,1152]{2,1,0:T(8,128)(2,1)S(1)} collective-permute-done((bf16[4,16,1152]{2,1,0:T(8,128)(2,1)S(1)}, bf16[4,16,1152]{2,1,0:T(8,128)(2,1)S(1)}, u32[]{:S(2)}, u32[]{:S(2)}) %collective-permute-start.32) | collective-permute-done | bytes 147488 | tf_op jit(solution)/shard_map/ppermute | solution.py:256
  114.0 3.2 %collective-permute-start.22 = (bf16[144,1152]{1,0:T(8,128)(2,1)S(1)}, bf16[144,1152]{1,0:T(8,128)(2,1)S(1)}, u32[]{:S(2)}, u32[]{:S(2)}) collective-permute-start(bf16[144,1152]{1,0:T(8,128)(2,1)S(1)} %bitcast.44), channel_id=1, source_target_pairs={{0,1},{1,0},{2,3},{3,2},{4,5},{5,4},{6,7},{7,6},{8,9},{9,8},{10,11... | collective-permute-start | bytes 995336 | tf_op jit(solution)/shard_map/ppermute | solution.py:256
  117.2 1.1 collective-permute-done.33
  118.3 0.5 collective-permute-start.35
  118.8 1.5 %gather_out.1.wall = bf16[1152,1152]{1,0:T(8,128)(2,1)S(1)} custom-call(s32[2]{0:T(128)S(1)} %pad_add_fusion.index_ref, bf16[144,1152]{1,0:T(8,128)(2,1)S(1)} %bitcast.42, bf16[144,1152]{1,0:T(8,128)(2,1)S(1)} %collective-permute-done.5.refs_1_, bf16[144,1152]{1,0:T(8,128)(2,1)S(1)} %bitcast.45, bf16[144,1152]{1,0:T(8,128)(2,1)S(1)} %collective-permute-done.22.refs_3_, ...), custom_call_target="tpu_custom_call" | custom-call | tf_op jit(solution)/shard_map/gather_out/pallas_call | solution.py:415
  120.4 3.6 %restore.1 = bf16[4,128,1152]{2,1,0:T(8,128)(2,1)} custom-call(s32[2]{0:T(128)S(1)} %pad_add_fusion.index_ref, bf16[4,128,1152]{2,1,0:T(8,128)(2,1)S(1)} %copy-done.1, f32[3,4,1152]{2,1,0:T(4,128)S(1)} %bitcast.52, bf16[1152,1152]{1,0:T(8,128)(2,1)S(1)} %gather_out.1.wall, bf16[2,4,16,1152]{3,2,1,0:T(8,128)(2,1)S(1)} %get-tuple-element.85.refs_0_, ...), custom_call_target="tpu_custom_call" | custom-call | tf_op jit(solution)/shard_map/restore/pallas_call | solution.py:430
  (44 shorter events, 0.4 us)
Async XLA Ops:
  0.1 1.3 %copy-start = (bf16[4,128,1152]{2,1,0:T(8,128)(2,1)S(1)}, bf16[4,128,1152]{2,1,0:T(8,128)(2,1)}, u32[]{:S(2)}) copy-start(bf16[4,128,1152]{2,1,0:T(8,128)(2,1)} %tokens_ref.3) | copy-start | bytes 3538948
  1.3 0.8 copy-start.4
  2.2 42.6 %copy-start.2 = (bf16[1152,144]{0,1:T(8,128)(2,1)S(1)}, bf16[1152,144]{0,1:T(8,128)(2,1)}, u32[]{:S(2)}) copy-start(bf16[1152,144]{0,1:T(8,128)(2,1)} %param.7) | copy-start | bytes 995332
  2.2 61.8 %copy-start.3 = (bf16[1152,432]{0,1:T(8,128)(2,1)S(1)}, bf16[1152,432]{0,1:T(8,128)(2,1)}, u32[]{:S(2)}) copy-start(bf16[1152,432]{0,1:T(8,128)(2,1)} %param.6) | copy-start | bytes 2985988
  3.8 4.5 %collective-permute-start = (bf16[4,4,16,1152]{3,2,1,0:T(8,128)(2,1)S(1)}, bf16[4,4,16,1152]{3,2,1,0:T(8,128)(2,1)S(1)}, u32[]{:S(2)}, u32[]{:S(2)}) collective-permute-start(bf16[4,4,16,1152]{3,2,1,0:T(8,128)(2,1)S(1)} %get-tuple-element.49), channel_id=1, source_target_pairs={{0,1},{1,0},{2,3},{3,2},{4,5},{5,4},{6,7},{7,6},{8,9},{9,8},{10,11... | collective-permute-start | bytes 1769480 | tf_op jit(solution)/shard_map/ppermute | solution.py:256
  5.6 13.8 %collective-permute-start.2 = (bf16[112,1152]{1,0:T(8,128)(2,1)S(1)}, bf16[112,1152]{1,0:T(8,128)(2,1)S(1)}, u32[]{:S(2)}, u32[]{:S(2)}) collective-permute-start(bf16[112,1152]{1,0:T(8,128)(2,1)S(1)} %get-tuple-element.92), channel_id=1, source_target_pairs={{0,4},{1,5},{2,6},{3,7},{4,0},{5,1},{6,2},{7,3},{8,12},{9,13},{10,... | collective-permute-start | bytes 774152 | tf_op jit(solution)/shard_map/ppermute | solution.py:256
  8.0 13.2 %collective-permute-start.3 = (bf16[432,1152]{1,0:T(8,128)(2,1)}, bf16[432,1152]{1,0:T(8,128)(2,1)S(1)}, u32[]{:S(2)}, u32[]{:S(2)}) collective-permute-start(bf16[432,1152]{1,0:T(8,128)(2,1)} %bitcast.46), channel_id=1, source_target_pairs={{0,1},{1,0},{2,3},{3,2},{4,5},{5,4},{6,7},{7,6},{8,9},{9,8},{10,11... | collective-permute-start | bytes 2985992 | tf_op jit(solution)/shard_map/ppermute | solution.py:256
  8.4 11.1 %collective-permute-start.4 = (bf16[2,4,16,1152]{3,2,1,0:T(8,128)(2,1)S(1)}, bf16[2,4,16,1152]{3,2,1,0:T(8,128)(2,1)S(1)}, u32[]{:S(2)}, u32[]{:S(2)}) collective-permute-start(bf16[2,4,16,1152]{3,2,1,0:T(8,128)(2,1)S(1)} %pad_maximum_fusion.5), channel_id=1, source_target_pairs={{0,24},{1,25},{2,26},{3,27},{4,12},{5,13},{6,14},{7,15},{8,0},{9,1... | collective-permute-start | bytes 884744 | tf_op jit(solution)/shard_map/ppermute | solution.py:283
  10.7 10.5 %collective-permute-start.1 = (bf16[2,4,16,1152]{3,2,1,0:T(8,128)(2,1)S(1)}, bf16[2,4,16,1152]{3,2,1,0:T(8,128)(2,1)S(1)}, u32[]{:S(2)}, u32[]{:S(2)}) collective-permute-start(bf16[2,4,16,1152]{3,2,1,0:T(8,128)(2,1)S(1)} %pad_maximum_fusion.4), channel_id=1, source_target_pairs={{0,2},{1,3},{2,0},{3,1},{4,6},{5,7},{6,4},{7,5},{8,10},{9,11},{10,... | collective-permute-start | bytes 884744 | tf_op jit(solution)/shard_map/ppermute | solution.py:256
  21.2 19.0 %collective-permute-start.8 = (bf16[2,112,1152]{2,1,0:T(8,128)(2,1)S(1)}, bf16[2,112,1152]{2,1,0:T(8,128)(2,1)S(1)}, u32[]{:S(2)}, u32[]{:S(2)}) collective-permute-start(bf16[2,112,1152]{2,1,0:T(8,128)(2,1)S(1)} %pad_maximum_fusion.2), channel_id=1, source_target_pairs={{0,2},{1,3},{2,0},{3,1},{4,6},{5,7},{6,4},{7,5},{8,10},{9,11},{10,... | collective-permute-start | bytes 1548296 | tf_op jit(solution)/shard_map/ppermute | solution.py:256
  23.4 12.4 %collective-permute-start.10 = (bf16[2,4,16,1152]{3,2,1,0:T(8,128)(2,1)S(1)}, bf16[2,4,16,1152]{3,2,1,0:T(8,128)(2,1)S(1)}, u32[]{:S(2)}, u32[]{:S(2)}) collective-permute-start(bf16[2,4,16,1152]{3,2,1,0:T(8,128)(2,1)S(1)} %collective-permute-done.1), channel_id=1, source_target_pairs={{0,24},{1,25},{2,26},{3,27},{4,12},{5,13},{6,14},{7,15},{8,0},{9,1... | collective-permute-start | bytes 884744 | tf_op jit(solution)/shard_map/ppermute | solution.py:283
  23.7 16.5 %collective-permute-start.9 = (bf16[2,4,16,1152]{3,2,1,0:T(8,128)(2,1)S(1)}, bf16[2,4,16,1152]{3,2,1,0:T(8,128)(2,1)S(1)}, u32[]{:S(2)}, u32[]{:S(2)}) collective-permute-start(bf16[2,4,16,1152]{3,2,1,0:T(8,128)(2,1)S(1)} %get-tuple-element.53), channel_id=1, source_target_pairs={{0,4},{1,5},{2,6},{3,7},{4,0},{5,1},{6,2},{7,3},{8,12},{9,13},{10,... | collective-permute-start | bytes 884744 | tf_op jit(solution)/shard_map/ppermute | solution.py:256
  24.5 11.3 %collective-permute-start.6 = (bf16[112,1152]{1,0:T(8,128)(2,1)S(1)}, bf16[112,1152]{1,0:T(8,128)(2,1)S(1)}, u32[]{:S(2)}, u32[]{:S(2)}) collective-permute-start(bf16[112,1152]{1,0:T(8,128)(2,1)S(1)} %collective-permute-done.2.refs_2_), channel_id=1, source_target_pairs={{0,8},{1,9},{2,10},{3,11},{4,12},{5,13},{6,14},{7,15},{8,0},{9,1},... | collective-permute-start | bytes 774152 | tf_op jit(solution)/shard_map/ppermute | solution.py:256
  25.7 10.1 %collective-permute-start.7 = (bf16[112,1152]{1,0:T(8,128)(2,1)S(1)}, bf16[112,1152]{1,0:T(8,128)(2,1)S(1)}, u32[]{:S(2)}, u32[]{:S(2)}) collective-permute-start(bf16[112,1152]{1,0:T(8,128)(2,1)S(1)} %collective-permute-done.2.refs_2_), channel_id=1, source_target_pairs={{0,16},{1,17},{2,18},{3,19},{4,20},{5,21},{6,22},{7,23},{8,24},{9,... | collective-permute-start | bytes 774152 | tf_op jit(solution)/shard_map/ppermute | solution.py:256
  40.2 11.1 %collective-permute-start.11 = (bf16[2,112,1152]{2,1,0:T(8,128)(2,1)S(1)}, bf16[2,112,1152]{2,1,0:T(8,128)(2,1)S(1)}, u32[]{:S(2)}, u32[]{:S(2)}) collective-permute-start(bf16[2,112,1152]{2,1,0:T(8,128)(2,1)S(1)} %collective-permute-done.8.refs_8_), channel_id=1, source_target_pairs={{0,8},{1,9},{2,10},{3,11},{4,12},{5,13},{6,14},{7,15},{8,0},{9,1},... | collective-permute-start | bytes 1548296 | tf_op jit(solution)/shard_map/ppermute | solution.py:256
  41.4 10.8 %collective-permute-start.12 = (bf16[2,112,1152]{2,1,0:T(8,128)(2,1)S(1)}, bf16[2,112,1152]{2,1,0:T(8,128)(2,1)S(1)}, u32[]{:S(2)}, u32[]{:S(2)}) collective-permute-start(bf16[2,112,1152]{2,1,0:T(8,128)(2,1)S(1)} %collective-permute-done.8.refs_8_), channel_id=1, source_target_pairs={{0,16},{1,17},{2,18},{3,19},{4,20},{5,21},{6,22},{7,23},{8,24},{9,... | collective-permute-start | bytes 1548296 | tf_op jit(solution)/shard_map/ppermute | solution.py:256
  42.5 9.7 %collective-permute-start.14 = (bf16[2,112,1152]{2,1,0:T(8,128)(2,1)S(1)}, bf16[2,112,1152]{2,1,0:T(8,128)(2,1)S(1)}, u32[]{:S(2)}, u32[]{:S(2)}) collective-permute-start(bf16[2,112,1152]{2,1,0:T(8,128)(2,1)S(1)} %collective-permute-done.8.refs_8_), channel_id=1, source_target_pairs={{0,1},{1,0},{2,3},{3,2},{4,5},{5,4},{6,7},{7,6},{8,9},{9,8},{10,11... | collective-permute-start | bytes 1548296 | tf_op jit(solution)/shard_map/ppermute | solution.py:256
  44.8 1.9 %collective-permute-start.13 = (bf16[112,1152]{1,0:T(8,128)(2,1)S(1)}, bf16[112,1152]{1,0:T(8,128)(2,1)S(1)}, u32[]{:S(2)}, u32[]{:S(2)}) collective-permute-start(bf16[112,1152]{1,0:T(8,128)(2,1)S(1)} %collective-permute-done.2.refs_2_), channel_id=1, source_target_pairs={{0,1},{1,0},{2,3},{3,2},{4,5},{5,4},{6,7},{7,6},{8,9},{9,8},{10,11... | collective-permute-start | bytes 774152 | tf_op jit(solution)/shard_map/ppermute | solution.py:256
  44.9 28.7 %collective-permute-start.21 = (bf16[17,16,1152]{2,1,0:T(8,128)(2,1)S(1)}, bf16[17,16,1152]{2,1,0:T(8,128)(2,1)S(1)}, u32[]{:S(2)}, u32[]{:S(2)}) collective-permute-start(bf16[17,16,1152]{2,1,0:T(8,128)(2,1)S(1)} %pad_maximum_fusion.1), channel_id=1, source_target_pairs={{0,6},{1,7},{2,4},{3,5},{4,2},{5,3},{6,0},{7,1},{8,14},{9,15},{10,... | collective-permute-start | bytes 1880072 | tf_op jit(solution)/shard_map/ppermute | solution.py:256
  52.2 5.6 %collective-permute-start.16 = (bf16[112,1152]{1,0:T(8,128)(2,1)S(1)}, bf16[112,1152]{1,0:T(8,128)(2,1)S(1)}, u32[]{:S(2)}, u32[]{:S(2)}) collective-permute-start(bf16[112,1152]{1,0:T(8,128)(2,1)S(1)} %slice_bitcast_fusion), channel_id=1, source_target_pairs={{0,8},{1,9},{2,10},{3,11},{4,12},{5,13},{6,14},{7,15},{8,0},{9,1},... | collective-permute-start | bytes 774152 | tf_op jit(solution)/shard_map/ppermute | solution.py:256
  52.6 9.4 %collective-permute-start.15 = (bf16[112,1152]{1,0:T(8,128)(2,1)S(1)}, bf16[112,1152]{1,0:T(8,128)(2,1)S(1)}, u32[]{:S(2)}, u32[]{:S(2)}) collective-permute-start(bf16[112,1152]{1,0:T(8,128)(2,1)S(1)} %slice_bitcast_fusion.1), channel_id=1, source_target_pairs={{0,16},{1,17},{2,18},{3,19},{4,20},{5,21},{6,22},{7,23},{8,24},{9,... | collective-permute-start | bytes 774152 | tf_op jit(solution)/shard_map/ppermute | solution.py:256
  54.1 9.8 %collective-permute-start.19 = (bf16[2,112,1152]{2,1,0:T(8,128)(2,1)S(1)}, bf16[2,112,1152]{2,1,0:T(8,128)(2,1)S(1)}, u32[]{:S(2)}, u32[]{:S(2)}) collective-permute-start(bf16[2,112,1152]{2,1,0:T(8,128)(2,1)S(1)} %collective-permute-done.11.refs_10_), channel_id=1, source_target_pairs={{0,1},{1,0},{2,3},{3,2},{4,5},{5,4},{6,7},{7,6},{8,9},{9,8},{10,11... | collective-permute-start | bytes 1548296 | tf_op jit(solution)/shard_map/ppermute | solution.py:256
  57.8 6.2 %collective-permute-start.20 = (bf16[2,112,1152]{2,1,0:T(8,128)(2,1)S(1)}, bf16[2,112,1152]{2,1,0:T(8,128)(2,1)S(1)}, u32[]{:S(2)}, u32[]{:S(2)}) collective-permute-start(bf16[2,112,1152]{2,1,0:T(8,128)(2,1)S(1)} %collective-permute-done.12.refs_12_), channel_id=1, source_target_pairs={{0,1},{1,0},{2,3},{3,2},{4,5},{5,4},{6,7},{7,6},{8,9},{9,8},{10,11... | collective-permute-start | bytes 1548296 | tf_op jit(solution)/shard_map/ppermute | solution.py:256
  57.8 5.3 %collective-permute-start.17 = (bf16[112,1152]{1,0:T(8,128)(2,1)S(1)}, bf16[112,1152]{1,0:T(8,128)(2,1)S(1)}, u32[]{:S(2)}, u32[]{:S(2)}) collective-permute-start(bf16[112,1152]{1,0:T(8,128)(2,1)S(1)} %collective-permute-done.6.refs_4_), channel_id=1, source_target_pairs={{0,1},{1,0},{2,3},{3,2},{4,5},{5,4},{6,7},{7,6},{8,9},{9,8},{10,11... | collective-permute-start | bytes 774152 | tf_op jit(solution)/shard_map/ppermute | solution.py:256
  62.0 2.0 %collective-permute-start.18 = (bf16[112,1152]{1,0:T(8,128)(2,1)S(1)}, bf16[112,1152]{1,0:T(8,128)(2,1)S(1)}, u32[]{:S(2)}, u32[]{:S(2)}) collective-permute-start(bf16[112,1152]{1,0:T(8,128)(2,1)S(1)} %collective-permute-done.7.refs_6_), channel_id=1, source_target_pairs={{0,1},{1,0},{2,3},{3,2},{4,5},{5,4},{6,7},{7,6},{8,9},{9,8},{10,11... | collective-permute-start | bytes 774152 | tf_op jit(solution)/shard_map/ppermute | solution.py:256
  63.1 11.8 %collective-permute-start.24 = (bf16[112,1152]{1,0:T(8,128)(2,1)S(1)}, bf16[112,1152]{1,0:T(8,128)(2,1)S(1)}, u32[]{:S(2)}, u32[]{:S(2)}) collective-permute-start(bf16[112,1152]{1,0:T(8,128)(2,1)S(1)} %collective-permute-done.7.refs_6_), channel_id=1, source_target_pairs={{0,8},{1,9},{2,10},{3,11},{4,12},{5,13},{6,14},{7,15},{8,0},{9,1},... | collective-permute-start | bytes 774152 | tf_op jit(solution)/shard_map/ppermute | solution.py:256
  73.6 3.2 %collective-permute-start.26 = (bf16[2,112,1152]{2,1,0:T(8,128)(2,1)S(1)}, bf16[2,112,1152]{2,1,0:T(8,128)(2,1)S(1)}, u32[]{:S(2)}, u32[]{:S(2)}) collective-permute-start(bf16[2,112,1152]{2,1,0:T(8,128)(2,1)S(1)} %pad_maximum_fusion.3.refs_9_.refs_7_), channel_id=1, source_target_pairs={{0,1},{1,0},{2,3},{3,2},{4,5},{5,4},{6,7},{7,6},{8,9},{9,8},{10,11... | collective-permute-start | bytes 1548296 | tf_op jit(solution)/shard_map/ppermute | solution.py:256
  74.9 1.9 %collective-permute-start.25 = (bf16[112,1152]{1,0:T(8,128)(2,1)S(1)}, bf16[112,1152]{1,0:T(8,128)(2,1)S(1)}, u32[]{:S(2)}, u32[]{:S(2)}) collective-permute-start(bf16[112,1152]{1,0:T(8,128)(2,1)S(1)} %collective-permute-done.24.refs_7_.refs_5_), channel_id=1, source_target_pairs={{0,1},{1,0},{2,3},{3,2},{4,5},{5,4},{6,7},{7,6},{8,9},{9,8},{10,11... | collective-permute-start | bytes 774152 | tf_op jit(solution)/shard_map/ppermute | solution.py:256
  75.0 19.1 %collective-permute-start.23 = (bf16[2,144,1152]{2,1,0:T(8,128)(2,1)S(1)}, bf16[2,144,1152]{2,1,0:T(8,128)(2,1)S(1)}, u32[]{:S(2)}, u32[]{:S(2)}) collective-permute-start(bf16[2,144,1152]{2,1,0:T(8,128)(2,1)S(1)} %pad_maximum_fusion), channel_id=1, source_target_pairs={{0,2},{1,3},{2,0},{3,1},{4,6},{5,7},{6,4},{7,5},{8,10},{9,11},{10,... | collective-permute-start | bytes 1990664 | tf_op jit(solution)/shard_map/ppermute | solution.py:256
  83.1 10.9 %collective-permute-start.27 = (bf16[4,4,16,640]{3,2,1,0:T(8,128)(2,1)S(1)}, bf16[4,4,16,640]{3,2,1,0:T(8,128)(2,1)S(1)}, u32[]{:S(2)}, u32[]{:S(2)}) collective-permute-start(bf16[4,4,16,640]{3,2,1,0:T(8,128)(2,1)S(1)} %get-tuple-element.74), channel_id=1, source_target_pairs={{0,8},{1,9},{2,10},{3,11},{4,28},{5,29},{6,30},{7,31},{8,16},{9,17... | collective-permute-start | bytes 983048 | tf_op jit(solution)/shard_map/ppermute | solution.py:283
  84.2 36.2 %copy-start.5 = (f32[4,3,1152]{2,0,1:T(4,128)S(1)}, f32[4,3,1152]{2,0,1:T(4,128)}, u32[]{:S(2)}) copy-start(f32[4,3,1152]{2,0,1:T(4,128)} %param.5) | copy-start | bytes 165892
  90.2 30.2 %copy-start.1 = (bf16[4,128,1152]{2,1,0:T(8,128)(2,1)S(1)}, bf16[4,128,1152]{2,1,0:T(8,128)(2,1)}, u32[]{:S(2)}) copy-start(bf16[4,128,1152]{2,1,0:T(8,128)(2,1)} %tokens_ref.3) | copy-start | bytes 3538948
  90.9 5.8 %collective-permute-start.30 = (bf16[4,16,1152]{2,1,0:T(8,128)(2,1)S(1)}, bf16[4,16,1152]{2,1,0:T(8,128)(2,1)S(1)}, u32[]{:S(2)}, u32[]{:S(2)}) collective-permute-start(bf16[4,16,1152]{2,1,0:T(8,128)(2,1)S(1)} %get-tuple-element.104), channel_id=1, source_target_pairs={{0,4},{1,5},{2,6},{3,7},{4,0},{5,1},{6,2},{7,3},{8,12},{9,13},{10,... | collective-permute-start | bytes 442376 | tf_op jit(solution)/shard_map/ppermute | solution.py:256
  91.5 12.2 %collective-permute-start.31 = (bf16[4,16,1152]{2,1,0:T(8,128)(2,1)S(1)}, bf16[4,16,1152]{2,1,0:T(8,128)(2,1)S(1)}, u32[]{:S(2)}, u32[]{:S(2)}) collective-permute-start(bf16[4,16,1152]{2,1,0:T(8,128)(2,1)S(1)} %get-tuple-element.103), channel_id=1, source_target_pairs={{0,5},{1,4},{2,7},{3,6},{4,1},{5,0},{6,3},{7,2},{8,13},{9,12},{10,... | collective-permute-start | bytes 442376 | tf_op jit(solution)/shard_map/ppermute | solution.py:256
  94.7 23.6 %collective-permute-start.29 = (bf16[2,4,16,1152]{3,2,1,0:T(8,128)(2,1)S(1)}, bf16[2,4,16,1152]{3,2,1,0:T(8,128)(2,1)S(1)}, u32[]{:S(2)}, u32[]{:S(2)}) collective-permute-start(bf16[2,4,16,1152]{3,2,1,0:T(8,128)(2,1)S(1)} %get-tuple-element.80), channel_id=1, source_target_pairs={{0,2},{1,3},{2,0},{3,1},{4,6},{5,7},{6,4},{7,5},{8,10},{9,11},{10,... | collective-permute-start | bytes 884744 | tf_op jit(solution)/shard_map/ppermute | solution.py:256
  95.0 23.9 %collective-permute-start.28 = (bf16[2,144,1152]{2,1,0:T(8,128)(2,1)S(1)}, bf16[2,144,1152]{2,1,0:T(8,128)(2,1)S(1)}, u32[]{:S(2)}, u32[]{:S(2)}) collective-permute-start(bf16[2,144,1152]{2,1,0:T(8,128)(2,1)S(1)} %collective-permute-done.23.refs_4_), channel_id=1, source_target_pairs={{0,1},{1,0},{2,3},{3,2},{4,5},{5,4},{6,7},{7,6},{8,9},{9,8},{10,11... | collective-permute-start | bytes 1990664 | tf_op jit(solution)/shard_map/ppermute | solution.py:256
  95.2 18.9 %collective-permute-start.32 = (bf16[4,16,1152]{2,1,0:T(8,128)(2,1)S(1)}, bf16[4,16,1152]{2,1,0:T(8,128)(2,1)S(1)}, u32[]{:S(2)}, u32[]{:S(2)}) collective-permute-start(bf16[4,16,1152]{2,1,0:T(8,128)(2,1)S(1)} %get-tuple-element.102), channel_id=1, source_target_pairs={{0,6},{1,7},{2,4},{3,5},{4,2},{5,3},{6,0},{7,1},{8,14},{9,15},{10,... | collective-permute-start | bytes 442376 | tf_op jit(solution)/shard_map/ppermute | solution.py:256
  96.7 21.6 %collective-permute-start.33 = (bf16[4,16,1152]{2,1,0:T(8,128)(2,1)S(1)}, bf16[4,16,1152]{2,1,0:T(8,128)(2,1)S(1)}, u32[]{:S(2)}, u32[]{:S(2)}) collective-permute-start(bf16[4,16,1152]{2,1,0:T(8,128)(2,1)S(1)} %get-tuple-element.101), channel_id=1, source_target_pairs={{0,7},{1,6},{2,5},{3,4},{4,3},{5,2},{6,1},{7,0},{8,15},{9,14},{10,... | collective-permute-start | bytes 442376 | tf_op jit(solution)/shard_map/ppermute | solution.py:256
  103.7 15.1 %collective-permute-start.5 = (bf16[144,1152]{1,0:T(8,128)(2,1)S(1)}, bf16[144,1152]{1,0:T(8,128)(2,1)S(1)}, u32[]{:S(2)}, u32[]{:S(2)}) collective-permute-start(bf16[144,1152]{1,0:T(8,128)(2,1)S(1)} %bitcast.41), channel_id=1, source_target_pairs={{0,1},{1,0},{2,3},{3,2},{4,5},{5,4},{6,7},{7,6},{8,9},{9,8},{10,11... | collective-permute-start | bytes 995336 | tf_op jit(solution)/shard_map/ppermute | solution.py:256
  114.0 4.8 %collective-permute-start.22 = (bf16[144,1152]{1,0:T(8,128)(2,1)S(1)}, bf16[144,1152]{1,0:T(8,128)(2,1)S(1)}, u32[]{:S(2)}, u32[]{:S(2)}) collective-permute-start(bf16[144,1152]{1,0:T(8,128)(2,1)S(1)} %bitcast.44), channel_id=1, source_target_pairs={{0,1},{1,0},{2,3},{3,2},{4,5},{5,4},{6,7},{7,6},{8,9},{9,8},{10,11... | collective-permute-start | bytes 995336 | tf_op jit(solution)/shard_map/ppermute | solution.py:256
  118.3 2.0 %collective-permute-start.34 = (bf16[2,4,16,1152]{3,2,1,0:T(8,128)(2,1)S(1)}, bf16[2,4,16,1152]{3,2,1,0:T(8,128)(2,1)S(1)}, u32[]{:S(2)}, u32[]{:S(2)}) collective-permute-start(bf16[2,4,16,1152]{3,2,1,0:T(8,128)(2,1)S(1)} %get-tuple-element.85.refs_0_), channel_id=1, source_target_pairs={{0,1},{1,0},{2,3},{3,2},{4,5},{5,4},{6,7},{7,6},{8,9},{9,8},{10,11... | collective-permute-start | bytes 884744 | tf_op jit(solution)/shard_map/ppermute | solution.py:256
  118.3 2.0 %collective-permute-start.35 = (bf16[2,4,16,1152]{3,2,1,0:T(8,128)(2,1)S(1)}, bf16[2,4,16,1152]{3,2,1,0:T(8,128)(2,1)S(1)}, u32[]{:S(2)}, u32[]{:S(2)}) collective-permute-start(bf16[2,4,16,1152]{3,2,1,0:T(8,128)(2,1)S(1)} %collective-permute-done.29.refs_2_), channel_id=1, source_target_pairs={{0,1},{1,0},{2,3},{3,2},{4,5},{5,4},{6,7},{7,6},{8,9},{9,8},{10,11... | collective-permute-start | bytes 884744 | tf_op jit(solution)/shard_map/ppermute | solution.py:256

commit v11 on v10

--- a/solution.py
+++ b/solution.py
@@ -317,7 +317,7 @@
         early = [hop(far, 1), hop(rest, 1)]
         narrow_other = hop(narrow, 1)
         ay, bx, by, early, ax = tie((ay, bx, by, early, ax))
-        axy = hop(ay, 0, x)
+        axy = hop(ax, 0, y)
         bxy = jnp.stack([hop(bx[0], 0, y), hop(by[1], 0, x)])
         swaps = [early[0], hop(ax, 1), hop(ay, 1), None]
         swaps += [early[1], hop(bx, 1), hop(by, 1)]

time: 124 us -> 124 us (level)
  no operation moved by 1% of the time
where the time goes in v11:
time: 124 us
  starting transfers between devices  49.1 us (40%)
  waiting for transfers between devices  42 us (34%)
  Pallas kernels  28.9 us (23%)
  local copies, waits for them, and re-layouts  3.33 us (3%)
    ppermute x33, starting transfers between devices, hop(): return lax.ppermute(value, ('slab', 'seq'), pairs)  45.5 us
    ppermute x33, waiting for transfers between devices, hop(): return lax.ppermute(value, ('slab', 'seq'), pairs)  42 us
    pallas_call x2, Pallas kernels, attention(): pl.pallas_call(functools.partial(block_kernel, plan, frames), out_shape=[...  12.3 us
    pallas_call x1, Pallas kernels, per_device(): pl.pallas_call(functools.partial(gather_kernel, plan), out_shape=jax.Shap...  8.55 us
    pallas_call x1, Pallas kernels, per_device(): pl.pallas_call(functools.partial(restore_kernel, count), out_shape=jax.Sh...  3.65 us
    ppermute x3, starting transfers between devices, to_neighbour(): return lax.ppermute(value, ('slab', 'seq'), pairs)  3.57 us
  transfers between devices with their start and end apart: 36, of which 13 were waited for; matrix products, arithmetic and copies ran while one was open for 1% of the time, Pallas kernels for 19%

profile of v11, /device:TPU:9, one launch (start us, length us, event | category | flops | bytes accessed | tf_op | source)
XLA Modules:
  0.0 124.0 jit_solution(4671960281599674681)
XLA Ops:
  0.0 0.1 pad_add_fusion.index_ref
  0.1 1.3 %copy-done = bf16[4,128,1152]{2,1,0:T(8,128)(2,1)S(1)} copy-done((bf16[4,128,1152]{2,1,0:T(8,128)(2,1)S(1)}, bf16[4,128,1152]{2,1,0:T(8,128)(2,1)}, u32[]{:S(2)}) %copy-start) | copy-done | bytes 1179672
  1.3 0.8 copy-done.4
  2.2 1.7 %norm.1 = (bf16[4,4,16,1152]{3,2,1,0:T(8,128)(2,1)S(1)}, bf16[4,4,16,1152]{3,2,1,0:T(8,128)(2,1)S(1)}) custom-call(s32[2]{0:T(128)S(1)} %pad_add_fusion.index_ref, bf16[4,128,1152]{2,1,0:T(8,128)(2,1)S(1)} %copy-done, f32[3,4,1152]{2,1,0:T(4,128)S(1)} %bitcast.51), custom_call_target="tpu_custom_call" | custom-call | tf_op jit(solution)/shard_map/norm/pallas_call | solution.py:268
  3.8 0.7 collective-permute-start
  4.6 1.0 dynamic-slice_bitcast_fusion
  5.6 2.4 %collective-permute-start.2 = (bf16[112,1152]{1,0:T(8,128)(2,1)S(1)}, bf16[112,1152]{1,0:T(8,128)(2,1)S(1)}, u32[]{:S(2)}, u32[]{:S(2)}) collective-permute-start(bf16[112,1152]{1,0:T(8,128)(2,1)S(1)} %get-tuple-element.92), channel_id=1, source_target_pairs={{0,4},{1,5},{2,6},{3,7},{4,0},{5,1},{6,2},{7,3},{8,12},{9,13},{10,... | collective-permute-start | bytes 774152 | tf_op jit(solution)/shard_map/ppermute | solution.py:256
  8.0 0.3 collective-permute-start.3
  8.4 2.2 %collective-permute-start.4 = (bf16[2,4,16,1152]{3,2,1,0:T(8,128)(2,1)S(1)}, bf16[2,4,16,1152]{3,2,1,0:T(8,128)(2,1)S(1)}, u32[]{:S(2)}, u32[]{:S(2)}) collective-permute-start(bf16[2,4,16,1152]{3,2,1,0:T(8,128)(2,1)S(1)} %pad_maximum_fusion.5), channel_id=1, source_target_pairs={{0,24},{1,25},{2,26},{3,27},{4,12},{5,13},{6,14},{7,15},{8,0},{9,1... | collective-permute-start | bytes 884744 | tf_op jit(solution)/shard_map/ppermute | solution.py:283
  10.7 0.2 collective-permute-start.1
  10.9 8.5 %collective-permute-done.2.refs_2_ = bf16[112,1152]{1,0:T(8,128)(2,1)S(1)} collective-permute-done((bf16[112,1152]{1,0:T(8,128)(2,1)S(1)}, bf16[112,1152]{1,0:T(8,128)(2,1)S(1)}, u32[]{:S(2)}, u32[]{:S(2)}) %collective-permute-start.2) | collective-permute-done | bytes 258080 | tf_op jit(solution)/shard_map/ppermute | solution.py:256
  19.4 0.1 pad_maximum_fusion.2
  19.5 0.1 pad_maximum_fusion.6
  19.6 1.6 %collective-permute-done.1 = bf16[2,4,16,1152]{3,2,1,0:T(8,128)(2,1)S(1)} collective-permute-done((bf16[2,4,16,1152]{3,2,1,0:T(8,128)(2,1)S(1)}, bf16[2,4,16,1152]{3,2,1,0:T(8,128)(2,1)S(1)}, u32[]{:S(2)}, u32[]{:S(2)}) %collective-permute-start.1) | collective-permute-done | bytes 294944 | tf_op jit(solution)/shard_map/ppermute | solution.py:256
  21.2 2.2 %collective-permute-start.8 = (bf16[2,112,1152]{2,1,0:T(8,128)(2,1)S(1)}, bf16[2,112,1152]{2,1,0:T(8,128)(2,1)S(1)}, u32[]{:S(2)}, u32[]{:S(2)}) collective-permute-start(bf16[2,112,1152]{2,1,0:T(8,128)(2,1)S(1)} %pad_maximum_fusion.2), channel_id=1, source_target_pairs={{0,2},{1,3},{2,0},{3,1},{4,6},{5,7},{6,4},{7,5},{8,10},{9,11},{10,... | collective-permute-start | bytes 1548296 | tf_op jit(solution)/shard_map/ppermute | solution.py:256
  23.4 0.3 collective-permute-start.10
  23.7 0.8 collective-permute-start.9
  24.5 1.2 collective-permute-start.6
  25.7 0.2 collective-permute-start.7
  26.0 9.9 %collective-permute-done.6.refs_4_ = bf16[112,1152]{1,0:T(8,128)(2,1)S(1)} collective-permute-done((bf16[112,1152]{1,0:T(8,128)(2,1)S(1)}, bf16[112,1152]{1,0:T(8,128)(2,1)S(1)}, u32[]{:S(2)}, u32[]{:S(2)}) %collective-permute-start.6) | collective-permute-done | bytes 258080 | tf_op jit(solution)/shard_map/ppermute | solution.py:256
  35.8 4.3 %collective-permute-done.9 = bf16[2,4,16,1152]{3,2,1,0:T(8,128)(2,1)S(1)} collective-permute-done((bf16[2,4,16,1152]{3,2,1,0:T(8,128)(2,1)S(1)}, bf16[2,4,16,1152]{3,2,1,0:T(8,128)(2,1)S(1)}, u32[]{:S(2)}, u32[]{:S(2)}) %collective-permute-start.9) | collective-permute-done | bytes 294944 | tf_op jit(solution)/shard_map/ppermute | solution.py:256
  40.2 1.2 collective-permute-start.11
  41.4 1.1 collective-permute-start.12
  42.5 2.3 %collective-permute-start.14 = (bf16[2,112,1152]{2,1,0:T(8,128)(2,1)S(1)}, bf16[2,112,1152]{2,1,0:T(8,128)(2,1)S(1)}, u32[]{:S(2)}, u32[]{:S(2)}) collective-permute-start(bf16[2,112,1152]{2,1,0:T(8,128)(2,1)S(1)} %collective-permute-done.8.refs_8_), channel_id=1, source_target_pairs={{0,1},{1,0},{2,3},{3,2},{4,5},{5,4},{6,7},{7,6},{8,9},{9,8},{10,11... | collective-permute-start | bytes 1548296 | tf_op jit(solution)/shard_map/ppermute | solution.py:256
  44.8 0.1 pad_maximum_fusion.1
  44.9 0.8 collective-permute-start.21
  45.7 1.0 collective-permute-done.13.refs_3_
  46.7 4.6 %collective-permute-done.11.refs_10_ = bf16[2,112,1152]{2,1,0:T(8,128)(2,1)S(1)} collective-permute-done((bf16[2,112,1152]{2,1,0:T(8,128)(2,1)S(1)}, bf16[2,112,1152]{2,1,0:T(8,128)(2,1)S(1)}, u32[]{:S(2)}, u32[]{:S(2)}) %collective-permute-start.11) | collective-permute-done | bytes 516128 | tf_op jit(solution)/shard_map/ppermute | solution.py:256
  51.2 0.9 collective-permute-done.12.refs_12_
  52.2 0.3 collective-permute-start.16
  52.6 1.5 %collective-permute-start.15 = (bf16[112,1152]{1,0:T(8,128)(2,1)S(1)}, bf16[112,1152]{1,0:T(8,128)(2,1)S(1)}, u32[]{:S(2)}, u32[]{:S(2)}) collective-permute-start(bf16[112,1152]{1,0:T(8,128)(2,1)S(1)} %slice_bitcast_fusion.1), channel_id=1, source_target_pairs={{0,16},{1,17},{2,18},{3,19},{4,20},{5,21},{6,22},{7,23},{8,24},{9,... | collective-permute-start | bytes 774152 | tf_op jit(solution)/shard_map/ppermute | solution.py:256
  54.1 3.7 %collective-permute-start.19 = (bf16[2,112,1152]{2,1,0:T(8,128)(2,1)S(1)}, bf16[2,112,1152]{2,1,0:T(8,128)(2,1)S(1)}, u32[]{:S(2)}, u32[]{:S(2)}) collective-permute-start(bf16[2,112,1152]{2,1,0:T(8,128)(2,1)S(1)} %collective-permute-done.11.refs_10_), channel_id=1, source_target_pairs={{0,1},{1,0},{2,3},{3,2},{4,5},{5,4},{6,7},{7,6},{8,9},{9,8},{10,11... | collective-permute-start | bytes 1548296 | tf_op jit(solution)/shard_map/ppermute | solution.py:256
  57.8 4.2 %collective-permute-start.17 = (bf16[112,1152]{1,0:T(8,128)(2,1)S(1)}, bf16[112,1152]{1,0:T(8,128)(2,1)S(1)}, u32[]{:S(2)}, u32[]{:S(2)}) collective-permute-start(bf16[112,1152]{1,0:T(8,128)(2,1)S(1)} %collective-permute-done.6.refs_4_), channel_id=1, source_target_pairs={{0,1},{1,0},{2,3},{3,2},{4,5},{5,4},{6,7},{7,6},{8,9},{9,8},{10,11... | collective-permute-start | bytes 774152 | tf_op jit(solution)/shard_map/ppermute | solution.py:256
  62.0 0.6 collective-permute-start.18
  62.6 0.1 pad_maximum_fusion.3.refs_9_.refs_7_
  62.7 0.5 collective-permute-done.17.refs_5_
  63.1 1.1 collective-permute-start.24
  64.2 8.6 %gather.1.refs_6_ = bf16[3456,1152]{1,0:T(8,128)(2,1)S(1)} custom-call(s32[2]{0:T(128)S(1)} %pad_add_fusion.index_ref, bf16[432,1152]{1,0:T(8,128)(2,1)S(1)} %bitcast.47, bf16[432,1152]{1,0:T(8,128)(2,1)S(1)} %collective-permute-done.3.refs_1_, bf16[112,1152]{1,0:T(8,128)(2,1)S(1)} %collective-permute-done.2.refs_2_, ...), custom_call_target="tpu_custom_call" | custom-call | tf_op jit(solution)/shard_map/gather/pallas_call | solution.py:331
  72.8 0.8 collective-permute-done.21.refs_3_
  73.6 1.3 %collective-permute-start.26 = (bf16[2,112,1152]{2,1,0:T(8,128)(2,1)S(1)}, bf16[2,112,1152]{2,1,0:T(8,128)(2,1)S(1)}, u32[]{:S(2)}, u32[]{:S(2)}) collective-permute-start(bf16[2,112,1152]{2,1,0:T(8,128)(2,1)S(1)} %pad_maximum_fusion.3.refs_9_.refs_7_), channel_id=1, source_target_pairs={{0,1},{1,0},{2,3},{3,2},{4,5},{5,4},{6,7},{7,6},{8,9},{9,8},{10,11... | collective-permute-start | bytes 1548296 | tf_op jit(solution)/shard_map/ppermute | solution.py:256
  74.9 0.0 collective-permute-start.25
  74.9 0.1 pad_maximum_fusion
  75.0 0.1 collective-permute-start.23
  75.1 1.7 %collective-permute-done.25.refs_8_.refs_6_ = bf16[112,1152]{1,0:T(8,128)(2,1)S(1)} collective-permute-done((bf16[112,1152]{1,0:T(8,128)(2,1)S(1)}, bf16[112,1152]{1,0:T(8,128)(2,1)S(1)}, u32[]{:S(2)}, u32[]{:S(2)}) %collective-permute-start.25) | collective-permute-done | bytes 258080 | tf_op jit(solution)/shard_map/ppermute | solution.py:256
  76.8 6.3 %shifted.1 = (bf16[4,4,16,640]{3,2,1,0:T(8,128)(2,1)S(1)}, bf16[4,4,16,640]{3,2,1,0:T(8,128)(2,1)S(1)}, bf16[3456,1152]{1,0:T(8,128)(2,1)S(1)}) custom-call(s32[2]{0:T(128)S(1)} %pad_add_fusion.index_ref, bf16[8,16,1152]{2,1,0:T(8,128)(2,1)S(1)} %bitcast.49, bf16[8,16,1152]{2,1,0:T(8,128)(2,1)S(1)} %bitcast.57, ...), custom_call_target="tpu_custom_call", output_to_operand_aliasing={{2}: (7, {})} | custom-call | flops 40000000000 | bytes 8388608 | tf_op jit(solution)/shard_map/shifted/pallas_call | solution.py:367
  83.1 1.0 collective-permute-start.27
  84.2 6.0 %windowed.1 = (bf16[4,4,16,640]{3,2,1,0:T(8,128)(2,1)S(1)}, bf16[4,4,16,640]{3,2,1,0:T(8,128)(2,1)S(1)}, bf16[3456,1152]{1,0:T(8,128)(2,1)S(1)}) custom-call(s32[2]{0:T(128)S(1)} %pad_add_fusion.index_ref, bf16[8,16,1152]{2,1,0:T(8,128)(2,1)S(1)} %bitcast.50, bf16[8,16,1152]{2,1,0:T(8,128)(2,1)S(1)} %bitcast.58, ...), custom_call_target="tpu_custom_call", output_to_operand_aliasing={{2}: (5, {})} | custom-call | flops 40000000000 | bytes 8388608 | tf_op jit(solution)/shard_map/windowed/pallas_call | solution.py:367
  90.2 0.0 copy-start.1
  90.2 0.6 merge.3
  90.9 0.7 collective-permute-start.30
  91.5 2.6 %collective-permute-start.31 = (bf16[4,16,1152]{2,1,0:T(8,128)(2,1)S(1)}, bf16[4,16,1152]{2,1,0:T(8,128)(2,1)S(1)}, u32[]{:S(2)}, u32[]{:S(2)}) collective-permute-start(bf16[4,16,1152]{2,1,0:T(8,128)(2,1)S(1)} %get-tuple-element.103), channel_id=1, source_target_pairs={{0,5},{1,4},{2,7},{3,6},{4,1},{5,0},{6,3},{7,2},{8,13},{9,12},{10,... | collective-permute-start | bytes 442376 | tf_op jit(solution)/shard_map/ppermute | solution.py:256
  94.1 0.6 merge.2
  94.7 0.2 collective-permute-start.29
  95.0 0.2 collective-permute-start.28
  95.2 1.0 collective-permute-start.32
  96.2 0.5 collective-permute-done.30
  96.7 7.0 %collective-permute-start.33 = (bf16[4,16,1152]{2,1,0:T(8,128)(2,1)S(1)}, bf16[4,16,1152]{2,1,0:T(8,128)(2,1)S(1)}, u32[]{:S(2)}, u32[]{:S(2)}) collective-permute-start(bf16[4,16,1152]{2,1,0:T(8,128)(2,1)S(1)} %get-tuple-element.101), channel_id=1, source_target_pairs={{0,7},{1,6},{2,5},{3,4},{4,3},{5,2},{6,1},{7,0},{8,15},{9,14},{10,... | collective-permute-start | bytes 442376 | tf_op jit(solution)/shard_map/ppermute | solution.py:256
  103.7 3.7 %collective-permute-start.5 = (bf16[144,1152]{1,0:T(8,128)(2,1)S(1)}, bf16[144,1152]{1,0:T(8,128)(2,1)S(1)}, u32[]{:S(2)}, u32[]{:S(2)}) collective-permute-start(bf16[144,1152]{1,0:T(8,128)(2,1)S(1)} %bitcast.41), channel_id=1, source_target_pairs={{0,1},{1,0},{2,3},{3,2},{4,5},{5,4},{6,7},{7,6},{8,9},{9,8},{10,11... | collective-permute-start | bytes 995336 | tf_op jit(solution)/shard_map/ppermute | solution.py:256
  107.4 6.6 %collective-permute-done.32 = bf16[4,16,1152]{2,1,0:T(8,128)(2,1)S(1)} collective-permute-done((bf16[4,16,1152]{2,1,0:T(8,128)(2,1)S(1)}, bf16[4,16,1152]{2,1,0:T(8,128)(2,1)S(1)}, u32[]{:S(2)}, u32[]{:S(2)}) %collective-permute-start.32) | collective-permute-done | bytes 147488 | tf_op jit(solution)/shard_map/ppermute | solution.py:256
  114.0 3.2 %collective-permute-start.22 = (bf16[144,1152]{1,0:T(8,128)(2,1)S(1)}, bf16[144,1152]{1,0:T(8,128)(2,1)S(1)}, u32[]{:S(2)}, u32[]{:S(2)}) collective-permute-start(bf16[144,1152]{1,0:T(8,128)(2,1)S(1)} %bitcast.44), channel_id=1, source_target_pairs={{0,1},{1,0},{2,3},{3,2},{4,5},{5,4},{6,7},{7,6},{8,9},{9,8},{10,11... | collective-permute-start | bytes 995336 | tf_op jit(solution)/shard_map/ppermute | solution.py:256
  117.2 1.1 collective-permute-done.33
  118.3 0.5 collective-permute-start.35
  118.8 1.5 %gather_out.1.wall = bf16[1152,1152]{1,0:T(8,128)(2,1)S(1)} custom-call(s32[2]{0:T(128)S(1)} %pad_add_fusion.index_ref, bf16[144,1152]{1,0:T(8,128)(2,1)S(1)} %bitcast.42, bf16[144,1152]{1,0:T(8,128)(2,1)S(1)} %collective-permute-done.5.refs_1_, bf16[144,1152]{1,0:T(8,128)(2,1)S(1)} %bitcast.45, bf16[144,1152]{1,0:T(8,128)(2,1)S(1)} %collective-permute-done.22.refs_3_, ...), custom_call_target="tpu_custom_call" | custom-call | tf_op jit(solution)/shard_map/gather_out/pallas_call | solution.py:415
  120.4 3.6 %restore.1 = bf16[4,128,1152]{2,1,0:T(8,128)(2,1)} custom-call(s32[2]{0:T(128)S(1)} %pad_add_fusion.index_ref, bf16[4,128,1152]{2,1,0:T(8,128)(2,1)S(1)} %copy-done.1, f32[3,4,1152]{2,1,0:T(4,128)S(1)} %bitcast.52, bf16[1152,1152]{1,0:T(8,128)(2,1)S(1)} %gather_out.1.wall, bf16[2,4,16,1152]{3,2,1,0:T(8,128)(2,1)S(1)} %get-tuple-element.85.refs_0_, ...), custom_call_target="tpu_custom_call" | custom-call | tf_op jit(solution)/shard_map/restore/pallas_call | solution.py:430
  (44 shorter events, 0.4 us)
Async XLA Ops:
  0.1 1.3 %copy-start = (bf16[4,128,1152]{2,1,0:T(8,128)(2,1)S(1)}, bf16[4,128,1152]{2,1,0:T(8,128)(2,1)}, u32[]{:S(2)}) copy-start(bf16[4,128,1152]{2,1,0:T(8,128)(2,1)} %tokens_ref.3) | copy-start | bytes 3538948
  1.3 0.8 copy-start.4
  2.2 42.6 %copy-start.2 = (bf16[1152,144]{0,1:T(8,128)(2,1)S(1)}, bf16[1152,144]{0,1:T(8,128)(2,1)}, u32[]{:S(2)}) copy-start(bf16[1152,144]{0,1:T(8,128)(2,1)} %param.7) | copy-start | bytes 995332
  2.2 62.1 %copy-start.3 = (bf16[1152,432]{0,1:T(8,128)(2,1)S(1)}, bf16[1152,432]{0,1:T(8,128)(2,1)}, u32[]{:S(2)}) copy-start(bf16[1152,432]{0,1:T(8,128)(2,1)} %param.6) | copy-start | bytes 2985988
  3.8 4.5 %collective-permute-start = (bf16[4,4,16,1152]{3,2,1,0:T(8,128)(2,1)S(1)}, bf16[4,4,16,1152]{3,2,1,0:T(8,128)(2,1)S(1)}, u32[]{:S(2)}, u32[]{:S(2)}) collective-permute-start(bf16[4,4,16,1152]{3,2,1,0:T(8,128)(2,1)S(1)} %get-tuple-element.49), channel_id=1, source_target_pairs={{0,1},{1,0},{2,3},{3,2},{4,5},{5,4},{6,7},{7,6},{8,9},{9,8},{10,11... | collective-permute-start | bytes 1769480 | tf_op jit(solution)/shard_map/ppermute | solution.py:256
  5.6 13.8 %collective-permute-start.2 = (bf16[112,1152]{1,0:T(8,128)(2,1)S(1)}, bf16[112,1152]{1,0:T(8,128)(2,1)S(1)}, u32[]{:S(2)}, u32[]{:S(2)}) collective-permute-start(bf16[112,1152]{1,0:T(8,128)(2,1)S(1)} %get-tuple-element.92), channel_id=1, source_target_pairs={{0,4},{1,5},{2,6},{3,7},{4,0},{5,1},{6,2},{7,3},{8,12},{9,13},{10,... | collective-permute-start | bytes 774152 | tf_op jit(solution)/shard_map/ppermute | solution.py:256
  8.0 13.2 %collective-permute-start.3 = (bf16[432,1152]{1,0:T(8,128)(2,1)}, bf16[432,1152]{1,0:T(8,128)(2,1)S(1)}, u32[]{:S(2)}, u32[]{:S(2)}) collective-permute-start(bf16[432,1152]{1,0:T(8,128)(2,1)} %bitcast.46), channel_id=1, source_target_pairs={{0,1},{1,0},{2,3},{3,2},{4,5},{5,4},{6,7},{7,6},{8,9},{9,8},{10,11... | collective-permute-start | bytes 2985992 | tf_op jit(solution)/shard_map/ppermute | solution.py:256
  8.4 11.1 %collective-permute-start.4 = (bf16[2,4,16,1152]{3,2,1,0:T(8,128)(2,1)S(1)}, bf16[2,4,16,1152]{3,2,1,0:T(8,128)(2,1)S(1)}, u32[]{:S(2)}, u32[]{:S(2)}) collective-permute-start(bf16[2,4,16,1152]{3,2,1,0:T(8,128)(2,1)S(1)} %pad_maximum_fusion.5), channel_id=1, source_target_pairs={{0,24},{1,25},{2,26},{3,27},{4,12},{5,13},{6,14},{7,15},{8,0},{9,1... | collective-permute-start | bytes 884744 | tf_op jit(solution)/shard_map/ppermute | solution.py:283
  10.7 10.5 %collective-permute-start.1 = (bf16[2,4,16,1152]{3,2,1,0:T(8,128)(2,1)S(1)}, bf16[2,4,16,1152]{3,2,1,0:T(8,128)(2,1)S(1)}, u32[]{:S(2)}, u32[]{:S(2)}) collective-permute-start(bf16[2,4,16,1152]{3,2,1,0:T(8,128)(2,1)S(1)} %pad_maximum_fusion.4), channel_id=1, source_target_pairs={{0,2},{1,3},{2,0},{3,1},{4,6},{5,7},{6,4},{7,5},{8,10},{9,11},{10,... | collective-permute-start | bytes 884744 | tf_op jit(solution)/shard_map/ppermute | solution.py:256
  21.2 19.0 %collective-permute-start.8 = (bf16[2,112,1152]{2,1,0:T(8,128)(2,1)S(1)}, bf16[2,112,1152]{2,1,0:T(8,128)(2,1)S(1)}, u32[]{:S(2)}, u32[]{:S(2)}) collective-permute-start(bf16[2,112,1152]{2,1,0:T(8,128)(2,1)S(1)} %pad_maximum_fusion.2), channel_id=1, source_target_pairs={{0,2},{1,3},{2,0},{3,1},{4,6},{5,7},{6,4},{7,5},{8,10},{9,11},{10,... | collective-permute-start | bytes 1548296 | tf_op jit(solution)/shard_map/ppermute | solution.py:256
  23.4 12.4 %collective-permute-start.10 = (bf16[2,4,16,1152]{3,2,1,0:T(8,128)(2,1)S(1)}, bf16[2,4,16,1152]{3,2,1,0:T(8,128)(2,1)S(1)}, u32[]{:S(2)}, u32[]{:S(2)}) collective-permute-start(bf16[2,4,16,1152]{3,2,1,0:T(8,128)(2,1)S(1)} %collective-permute-done.1), channel_id=1, source_target_pairs={{0,24},{1,25},{2,26},{3,27},{4,12},{5,13},{6,14},{7,15},{8,0},{9,1... | collective-permute-start | bytes 884744 | tf_op jit(solution)/shard_map/ppermute | solution.py:283
  23.7 16.5 %collective-permute-start.9 = (bf16[2,4,16,1152]{3,2,1,0:T(8,128)(2,1)S(1)}, bf16[2,4,16,1152]{3,2,1,0:T(8,128)(2,1)S(1)}, u32[]{:S(2)}, u32[]{:S(2)}) collective-permute-start(bf16[2,4,16,1152]{3,2,1,0:T(8,128)(2,1)S(1)} %get-tuple-element.53), channel_id=1, source_target_pairs={{0,4},{1,5},{2,6},{3,7},{4,0},{5,1},{6,2},{7,3},{8,12},{9,13},{10,... | collective-permute-start | bytes 884744 | tf_op jit(solution)/shard_map/ppermute | solution.py:256
  24.5 11.3 %collective-permute-start.6 = (bf16[112,1152]{1,0:T(8,128)(2,1)S(1)}, bf16[112,1152]{1,0:T(8,128)(2,1)S(1)}, u32[]{:S(2)}, u32[]{:S(2)}) collective-permute-start(bf16[112,1152]{1,0:T(8,128)(2,1)S(1)} %collective-permute-done.2.refs_2_), channel_id=1, source_target_pairs={{0,8},{1,9},{2,10},{3,11},{4,12},{5,13},{6,14},{7,15},{8,0},{9,1},... | collective-permute-start | bytes 774152 | tf_op jit(solution)/shard_map/ppermute | solution.py:256
  25.7 10.1 %collective-permute-start.7 = (bf16[112,1152]{1,0:T(8,128)(2,1)S(1)}, bf16[112,1152]{1,0:T(8,128)(2,1)S(1)}, u32[]{:S(2)}, u32[]{:S(2)}) collective-permute-start(bf16[112,1152]{1,0:T(8,128)(2,1)S(1)} %collective-permute-done.2.refs_2_), channel_id=1, source_target_pairs={{0,16},{1,17},{2,18},{3,19},{4,20},{5,21},{6,22},{7,23},{8,24},{9,... | collective-permute-start | bytes 774152 | tf_op jit(solution)/shard_map/ppermute | solution.py:256
  40.2 11.1 %collective-permute-start.11 = (bf16[2,112,1152]{2,1,0:T(8,128)(2,1)S(1)}, bf16[2,112,1152]{2,1,0:T(8,128)(2,1)S(1)}, u32[]{:S(2)}, u32[]{:S(2)}) collective-permute-start(bf16[2,112,1152]{2,1,0:T(8,128)(2,1)S(1)} %collective-permute-done.8.refs_8_), channel_id=1, source_target_pairs={{0,8},{1,9},{2,10},{3,11},{4,12},{5,13},{6,14},{7,15},{8,0},{9,1},... | collective-permute-start | bytes 1548296 | tf_op jit(solution)/shard_map/ppermute | solution.py:256
  41.4 10.8 %collective-permute-start.12 = (bf16[2,112,1152]{2,1,0:T(8,128)(2,1)S(1)}, bf16[2,112,1152]{2,1,0:T(8,128)(2,1)S(1)}, u32[]{:S(2)}, u32[]{:S(2)}) collective-permute-start(bf16[2,112,1152]{2,1,0:T(8,128)(2,1)S(1)} %collective-permute-done.8.refs_8_), channel_id=1, source_target_pairs={{0,16},{1,17},{2,18},{3,19},{4,20},{5,21},{6,22},{7,23},{8,24},{9,... | collective-permute-start | bytes 1548296 | tf_op jit(solution)/shard_map/ppermute | solution.py:256
  42.5 9.7 %collective-permute-start.14 = (bf16[2,112,1152]{2,1,0:T(8,128)(2,1)S(1)}, bf16[2,112,1152]{2,1,0:T(8,128)(2,1)S(1)}, u32[]{:S(2)}, u32[]{:S(2)}) collective-permute-start(bf16[2,112,1152]{2,1,0:T(8,128)(2,1)S(1)} %collective-permute-done.8.refs_8_), channel_id=1, source_target_pairs={{0,1},{1,0},{2,3},{3,2},{4,5},{5,4},{6,7},{7,6},{8,9},{9,8},{10,11... | collective-permute-start | bytes 1548296 | tf_op jit(solution)/shard_map/ppermute | solution.py:256
  44.8 1.9 %collective-permute-start.13 = (bf16[112,1152]{1,0:T(8,128)(2,1)S(1)}, bf16[112,1152]{1,0:T(8,128)(2,1)S(1)}, u32[]{:S(2)}, u32[]{:S(2)}) collective-permute-start(bf16[112,1152]{1,0:T(8,128)(2,1)S(1)} %collective-permute-done.2.refs_2_), channel_id=1, source_target_pairs={{0,1},{1,0},{2,3},{3,2},{4,5},{5,4},{6,7},{7,6},{8,9},{9,8},{10,11... | collective-permute-start | bytes 774152 | tf_op jit(solution)/shard_map/ppermute | solution.py:256
  44.9 28.7 %collective-permute-start.21 = (bf16[17,16,1152]{2,1,0:T(8,128)(2,1)S(1)}, bf16[17,16,1152]{2,1,0:T(8,128)(2,1)S(1)}, u32[]{:S(2)}, u32[]{:S(2)}) collective-permute-start(bf16[17,16,1152]{2,1,0:T(8,128)(2,1)S(1)} %pad_maximum_fusion.1), channel_id=1, source_target_pairs={{0,6},{1,7},{2,4},{3,5},{4,2},{5,3},{6,0},{7,1},{8,14},{9,15},{10,... | collective-permute-start | bytes 1880072 | tf_op jit(solution)/shard_map/ppermute | solution.py:256
  52.2 5.6 %collective-permute-start.16 = (bf16[112,1152]{1,0:T(8,128)(2,1)S(1)}, bf16[112,1152]{1,0:T(8,128)(2,1)S(1)}, u32[]{:S(2)}, u32[]{:S(2)}) collective-permute-start(bf16[112,1152]{1,0:T(8,128)(2,1)S(1)} %slice_bitcast_fusion), channel_id=1, source_target_pairs={{0,8},{1,9},{2,10},{3,11},{4,12},{5,13},{6,14},{7,15},{8,0},{9,1},... | collective-permute-start | bytes 774152 | tf_op jit(solution)/shard_map/ppermute | solution.py:256
  52.6 9.4 %collective-permute-start.15 = (bf16[112,1152]{1,0:T(8,128)(2,1)S(1)}, bf16[112,1152]{1,0:T(8,128)(2,1)S(1)}, u32[]{:S(2)}, u32[]{:S(2)}) collective-permute-start(bf16[112,1152]{1,0:T(8,128)(2,1)S(1)} %slice_bitcast_fusion.1), channel_id=1, source_target_pairs={{0,16},{1,17},{2,18},{3,19},{4,20},{5,21},{6,22},{7,23},{8,24},{9,... | collective-permute-start | bytes 774152 | tf_op jit(solution)/shard_map/ppermute | solution.py:256
  54.1 10.1 %collective-permute-start.19 = (bf16[2,112,1152]{2,1,0:T(8,128)(2,1)S(1)}, bf16[2,112,1152]{2,1,0:T(8,128)(2,1)S(1)}, u32[]{:S(2)}, u32[]{:S(2)}) collective-permute-start(bf16[2,112,1152]{2,1,0:T(8,128)(2,1)S(1)} %collective-permute-done.11.refs_10_), channel_id=1, source_target_pairs={{0,1},{1,0},{2,3},{3,2},{4,5},{5,4},{6,7},{7,6},{8,9},{9,8},{10,11... | collective-permute-start | bytes 1548296 | tf_op jit(solution)/shard_map/ppermute | solution.py:256
  57.8 6.4 %collective-permute-start.20 = (bf16[2,112,1152]{2,1,0:T(8,128)(2,1)S(1)}, bf16[2,112,1152]{2,1,0:T(8,128)(2,1)S(1)}, u32[]{:S(2)}, u32[]{:S(2)}) collective-permute-start(bf16[2,112,1152]{2,1,0:T(8,128)(2,1)S(1)} %collective-permute-done.12.refs_12_), channel_id=1, source_target_pairs={{0,1},{1,0},{2,3},{3,2},{4,5},{5,4},{6,7},{7,6},{8,9},{9,8},{10,11... | collective-permute-start | bytes 1548296 | tf_op jit(solution)/shard_map/ppermute | solution.py:256
  57.8 5.3 %collective-permute-start.17 = (bf16[112,1152]{1,0:T(8,128)(2,1)S(1)}, bf16[112,1152]{1,0:T(8,128)(2,1)S(1)}, u32[]{:S(2)}, u32[]{:S(2)}) collective-permute-start(bf16[112,1152]{1,0:T(8,128)(2,1)S(1)} %collective-permute-done.6.refs_4_), channel_id=1, source_target_pairs={{0,1},{1,0},{2,3},{3,2},{4,5},{5,4},{6,7},{7,6},{8,9},{9,8},{10,11... | collective-permute-start | bytes 774152 | tf_op jit(solution)/shard_map/ppermute | solution.py:256
  62.0 2.2 %collective-permute-start.18 = (bf16[112,1152]{1,0:T(8,128)(2,1)S(1)}, bf16[112,1152]{1,0:T(8,128)(2,1)S(1)}, u32[]{:S(2)}, u32[]{:S(2)}) collective-permute-start(bf16[112,1152]{1,0:T(8,128)(2,1)S(1)} %collective-permute-done.7.refs_6_), channel_id=1, source_target_pairs={{0,1},{1,0},{2,3},{3,2},{4,5},{5,4},{6,7},{7,6},{8,9},{9,8},{10,11... | collective-permute-start | bytes 774152 | tf_op jit(solution)/shard_map/ppermute | solution.py:256
  63.1 11.8 %collective-permute-start.24 = (bf16[112,1152]{1,0:T(8,128)(2,1)S(1)}, bf16[112,1152]{1,0:T(8,128)(2,1)S(1)}, u32[]{:S(2)}, u32[]{:S(2)}) collective-permute-start(bf16[112,1152]{1,0:T(8,128)(2,1)S(1)} %collective-permute-done.6.refs_4_), channel_id=1, source_target_pairs={{0,16},{1,17},{2,18},{3,19},{4,20},{5,21},{6,22},{7,23},{8,24},{9,... | collective-permute-start | bytes 774152 | tf_op jit(solution)/shard_map/ppermute | solution.py:256
  73.6 3.2 %collective-permute-start.26 = (bf16[2,112,1152]{2,1,0:T(8,128)(2,1)S(1)}, bf16[2,112,1152]{2,1,0:T(8,128)(2,1)S(1)}, u32[]{:S(2)}, u32[]{:S(2)}) collective-permute-start(bf16[2,112,1152]{2,1,0:T(8,128)(2,1)S(1)} %pad_maximum_fusion.3.refs_9_.refs_7_), channel_id=1, source_target_pairs={{0,1},{1,0},{2,3},{3,2},{4,5},{5,4},{6,7},{7,6},{8,9},{9,8},{10,11... | collective-permute-start | bytes 1548296 | tf_op jit(solution)/shard_map/ppermute | solution.py:256
  74.9 1.9 %collective-permute-start.25 = (bf16[112,1152]{1,0:T(8,128)(2,1)S(1)}, bf16[112,1152]{1,0:T(8,128)(2,1)S(1)}, u32[]{:S(2)}, u32[]{:S(2)}) collective-permute-start(bf16[112,1152]{1,0:T(8,128)(2,1)S(1)} %collective-permute-done.24.refs_7_.refs_5_), channel_id=1, source_target_pairs={{0,1},{1,0},{2,3},{3,2},{4,5},{5,4},{6,7},{7,6},{8,9},{9,8},{10,11... | collective-permute-start | bytes 774152 | tf_op jit(solution)/shard_map/ppermute | solution.py:256
  75.0 19.1 %collective-permute-start.23 = (bf16[2,144,1152]{2,1,0:T(8,128)(2,1)S(1)}, bf16[2,144,1152]{2,1,0:T(8,128)(2,1)S(1)}, u32[]{:S(2)}, u32[]{:S(2)}) collective-permute-start(bf16[2,144,1152]{2,1,0:T(8,128)(2,1)S(1)} %pad_maximum_fusion), channel_id=1, source_target_pairs={{0,2},{1,3},{2,0},{3,1},{4,6},{5,7},{6,4},{7,5},{8,10},{9,11},{10,... | collective-permute-start | bytes 1990664 | tf_op jit(solution)/shard_map/ppermute | solution.py:256
  83.1 10.9 %collective-permute-start.27 = (bf16[4,4,16,640]{3,2,1,0:T(8,128)(2,1)S(1)}, bf16[4,4,16,640]{3,2,1,0:T(8,128)(2,1)S(1)}, u32[]{:S(2)}, u32[]{:S(2)}) collective-permute-start(bf16[4,4,16,640]{3,2,1,0:T(8,128)(2,1)S(1)} %get-tuple-element.74), channel_id=1, source_target_pairs={{0,8},{1,9},{2,10},{3,11},{4,28},{5,29},{6,30},{7,31},{8,16},{9,17... | collective-permute-start | bytes 983048 | tf_op jit(solution)/shard_map/ppermute | solution.py:283
  84.2 36.2 %copy-start.5 = (f32[4,3,1152]{2,0,1:T(4,128)S(1)}, f32[4,3,1152]{2,0,1:T(4,128)}, u32[]{:S(2)}) copy-start(f32[4,3,1152]{2,0,1:T(4,128)} %param.5) | copy-start | bytes 165892
  90.2 30.2 %copy-start.1 = (bf16[4,128,1152]{2,1,0:T(8,128)(2,1)S(1)}, bf16[4,128,1152]{2,1,0:T(8,128)(2,1)}, u32[]{:S(2)}) copy-start(bf16[4,128,1152]{2,1,0:T(8,128)(2,1)} %tokens_ref.3) | copy-start | bytes 3538948
  90.9 5.8 %collective-permute-start.30 = (bf16[4,16,1152]{2,1,0:T(8,128)(2,1)S(1)}, bf16[4,16,1152]{2,1,0:T(8,128)(2,1)S(1)}, u32[]{:S(2)}, u32[]{:S(2)}) collective-permute-start(bf16[4,16,1152]{2,1,0:T(8,128)(2,1)S(1)} %get-tuple-element.104), channel_id=1, source_target_pairs={{0,4},{1,5},{2,6},{3,7},{4,0},{5,1},{6,2},{7,3},{8,12},{9,13},{10,... | collective-permute-start | bytes 442376 | tf_op jit(solution)/shard_map/ppermute | solution.py:256
  91.5 12.2 %collective-permute-start.31 = (bf16[4,16,1152]{2,1,0:T(8,128)(2,1)S(1)}, bf16[4,16,1152]{2,1,0:T(8,128)(2,1)S(1)}, u32[]{:S(2)}, u32[]{:S(2)}) collective-permute-start(bf16[4,16,1152]{2,1,0:T(8,128)(2,1)S(1)} %get-tuple-element.103), channel_id=1, source_target_pairs={{0,5},{1,4},{2,7},{3,6},{4,1},{5,0},{6,3},{7,2},{8,13},{9,12},{10,... | collective-permute-start | bytes 442376 | tf_op jit(solution)/shard_map/ppermute | solution.py:256
  94.7 23.6 %collective-permute-start.29 = (bf16[2,4,16,1152]{3,2,1,0:T(8,128)(2,1)S(1)}, bf16[2,4,16,1152]{3,2,1,0:T(8,128)(2,1)S(1)}, u32[]{:S(2)}, u32[]{:S(2)}) collective-permute-start(bf16[2,4,16,1152]{3,2,1,0:T(8,128)(2,1)S(1)} %get-tuple-element.80), channel_id=1, source_target_pairs={{0,2},{1,3},{2,0},{3,1},{4,6},{5,7},{6,4},{7,5},{8,10},{9,11},{10,... | collective-permute-start | bytes 884744 | tf_op jit(solution)/shard_map/ppermute | solution.py:256
  95.0 23.9 %collective-permute-start.28 = (bf16[2,144,1152]{2,1,0:T(8,128)(2,1)S(1)}, bf16[2,144,1152]{2,1,0:T(8,128)(2,1)S(1)}, u32[]{:S(2)}, u32[]{:S(2)}) collective-permute-start(bf16[2,144,1152]{2,1,0:T(8,128)(2,1)S(1)} %collective-permute-done.23.refs_4_), channel_id=1, source_target_pairs={{0,1},{1,0},{2,3},{3,2},{4,5},{5,4},{6,7},{7,6},{8,9},{9,8},{10,11... | collective-permute-start | bytes 1990664 | tf_op jit(solution)/shard_map/ppermute | solution.py:256
  95.2 18.9 %collective-permute-start.32 = (bf16[4,16,1152]{2,1,0:T(8,128)(2,1)S(1)}, bf16[4,16,1152]{2,1,0:T(8,128)(2,1)S(1)}, u32[]{:S(2)}, u32[]{:S(2)}) collective-permute-start(bf16[4,16,1152]{2,1,0:T(8,128)(2,1)S(1)} %get-tuple-element.102), channel_id=1, source_target_pairs={{0,6},{1,7},{2,4},{3,5},{4,2},{5,3},{6,0},{7,1},{8,14},{9,15},{10,... | collective-permute-start | bytes 442376 | tf_op jit(solution)/shard_map/ppermute | solution.py:256
  96.7 21.6 %collective-permute-start.33 = (bf16[4,16,1152]{2,1,0:T(8,128)(2,1)S(1)}, bf16[4,16,1152]{2,1,0:T(8,128)(2,1)S(1)}, u32[]{:S(2)}, u32[]{:S(2)}) collective-permute-start(bf16[4,16,1152]{2,1,0:T(8,128)(2,1)S(1)} %get-tuple-element.101), channel_id=1, source_target_pairs={{0,7},{1,6},{2,5},{3,4},{4,3},{5,2},{6,1},{7,0},{8,15},{9,14},{10,... | collective-permute-start | bytes 442376 | tf_op jit(solution)/shard_map/ppermute | solution.py:256
  103.7 15.1 %collective-permute-start.5 = (bf16[144,1152]{1,0:T(8,128)(2,1)S(1)}, bf16[144,1152]{1,0:T(8,128)(2,1)S(1)}, u32[]{:S(2)}, u32[]{:S(2)}) collective-permute-start(bf16[144,1152]{1,0:T(8,128)(2,1)S(1)} %bitcast.41), channel_id=1, source_target_pairs={{0,1},{1,0},{2,3},{3,2},{4,5},{5,4},{6,7},{7,6},{8,9},{9,8},{10,11... | collective-permute-start | bytes 995336 | tf_op jit(solution)/shard_map/ppermute | solution.py:256
  114.0 4.8 %collective-permute-start.22 = (bf16[144,1152]{1,0:T(8,128)(2,1)S(1)}, bf16[144,1152]{1,0:T(8,128)(2,1)S(1)}, u32[]{:S(2)}, u32[]{:S(2)}) collective-permute-start(bf16[144,1152]{1,0:T(8,128)(2,1)S(1)} %bitcast.44), channel_id=1, source_target_pairs={{0,1},{1,0},{2,3},{3,2},{4,5},{5,4},{6,7},{7,6},{8,9},{9,8},{10,11... | collective-permute-start | bytes 995336 | tf_op jit(solution)/shard_map/ppermute | solution.py:256
  118.3 2.0 %collective-permute-start.34 = (bf16[2,4,16,1152]{3,2,1,0:T(8,128)(2,1)S(1)}, bf16[2,4,16,1152]{3,2,1,0:T(8,128)(2,1)S(1)}, u32[]{:S(2)}, u32[]{:S(2)}) collective-permute-start(bf16[2,4,16,1152]{3,2,1,0:T(8,128)(2,1)S(1)} %get-tuple-element.85.refs_0_), channel_id=1, source_target_pairs={{0,1},{1,0},{2,3},{3,2},{4,5},{5,4},{6,7},{7,6},{8,9},{9,8},{10,11... | collective-permute-start | bytes 884744 | tf_op jit(solution)/shard_map/ppermute | solution.py:256
  118.3 2.0 %collective-permute-start.35 = (bf16[2,4,16,1152]{3,2,1,0:T(8,128)(2,1)S(1)}, bf16[2,4,16,1152]{3,2,1,0:T(8,128)(2,1)S(1)}, u32[]{:S(2)}, u32[]{:S(2)}) collective-permute-start(bf16[2,4,16,1152]{3,2,1,0:T(8,128)(2,1)S(1)} %collective-permute-done.29.refs_2_), channel_id=1, source_target_pairs={{0,1},{1,0},{2,3},{3,2},{4,5},{5,4},{6,7},{7,6},{8,9},{9,8},{10,11... | collective-permute-start | bytes 884744 | tf_op jit(solution)/shard_map/ppermute | solution.py:256
